TPU v7x, 32 devices: a whole 2x2x4 slice. The times are simulated.
32 devices in a mesh: grp: 2 (over x), sx: 16 (over z, y, core).
Axes of the slice: x: 2, y: 2, z: 4, core: 2. Of those that a mesh axis runs over, the one named last changes fastest.
Arguments:
- pieces: bfloat16 [6144, 4096], P(('grp', 'sx')), parts along dimension 0, may hold values from -6 to 6
- potential: float32 [128, 1024], P(('grp', 'sx')), parts along dimension 0, may hold values from -1.5 to 1.5
- centers: int32 [2048, 4], P('grp'), parts along dimension 0, may hold values from 0 to 63, as said below
- pattern: int32 [32, 2], P('grp'), parts along dimension 0, may hold values 0 or 1
Outputs:
- direction: bfloat16 [6144, 4096], P(('grp', 'sx')), parts along dimension 0
There are 2 independent parts, one for each index of `grp`. A program takes and returns all parts, laid end to end along the dimension named above; each array names one. Nothing has to cross between parts.
Inputs may be any that keep to these rules, and one draw needn't show every extreme that they name: `centers`: row j holds orbital j's center (x, y, z) and sphere radius r: 4 * (j // 64) <= x < 4 * (j // 64 + 1), 0 <= y < 32, 0 <= z < 32, and 2 <= r <= 4, so orbital j is zero outside slabs j // 64 - 1 to j // 64 + 1.
All inputs are finite; a program needn't handle non-finite values.
Results may differ from a plain program's by a relative error of at most 0.0097.
Values may be sent and summed in bfloat16 or wider, within the bound.
No kernel may reach another device: no remote copies, remote signals or barrier semaphores. Data moves between devices by JAX's collectives and lax.ppermute only.
A program may use at most 64 MiB of HBM per device.

v0:
```python
import jax
import jax.numpy as jnp
from jax import lax
from jax.sharding import PartitionSpec as P

ORB = 64
CX = 4
NY = 32
NZ = 32


mass_term = 1.0
jacobi_diag = 3.0 + mass_term


def extended_2(block, sides, width):
    for axis, dim in sides:
        count = lax.axis_size(axis)
        forward = [(i, i + 1) for i in range(count - 1)]
        backward = [(target, source) for source, target in forward]
        low = lax.ppermute(
            lax.slice_in_dim(block, block.shape[dim] - width, None, axis=dim), axis, forward
        )
        high = lax.ppermute(lax.slice_in_dim(block, 0, width, axis=dim), axis, backward)
        block = jnp.concatenate([low, block, high], axis=dim)
    return block


def passed_along(value, axis, steps):
    count = lax.axis_size(axis)
    initial, last = (max(0, -steps), min(count, count - steps))
    return lax.ppermute(value, axis, [(source, source + steps) for source in range(initial, last)])


def sphere_mask(centers, slab_id, slab_count):
    padded = jnp.pad(centers, ((ORB, ORB), (0, 0)))
    nearby = lax.dynamic_slice_in_dim(padded, slab_id * ORB, 3 * ORB, 0)
    blocks = slab_id - 1 + jnp.arange(3 * ORB, dtype=jnp.int32) // ORB
    in_range = (blocks >= 0) & (blocks < slab_count)
    plane_x = slab_id * CX + jnp.arange(CX, dtype=jnp.int32)
    dist_x = (plane_x[None, :] - nearby[:, 0:1]) ** 2
    dist_y = (jnp.arange(NY, dtype=jnp.int32)[None, :] - nearby[:, 1:2]) ** 2
    dist_z = (jnp.arange(NZ, dtype=jnp.int32)[None, :] - nearby[:, 2:3]) ** 2
    reach_sq = dist_x[:, :, None, None] + dist_y[:, None, :, None] + dist_z[:, None, None, :]
    radius_sq = (nearby[:, 3] ** 2)[:, None, None, None]
    inside = (reach_sq <= radius_sq) & in_range[:, None, None, None]
    return inside.reshape(3 * ORB, CX, NY * NZ)


def kinetic(values, plane_low, plane_high):
    row_count = values.shape[0]
    extended = jnp.concatenate([plane_low[:, None], values, plane_high[:, None]], axis=1)
    beside_all = extended[:, :-2] + extended[:, 2:]
    cube_view = values.reshape(row_count, CX, NY, NZ)
    padded_y = jnp.pad(cube_view, ((0, 0), (0, 0), (1, 1), (0, 0)))
    padded_z = jnp.pad(cube_view, ((0, 0), (0, 0), (0, 0), (1, 1)))
    sideways = (
        padded_y[:, :, :-2] + padded_y[:, :, 2:] + padded_z[:, :, :, :-2] + padded_z[:, :, :, 2:]
    )
    beside_all = beside_all + sideways.reshape(row_count, CX, NY * NZ)
    return 0.5 * (6.0 * values - beside_all)


def boundary(grouped):
    extended = extended_2(grouped, (("sx", 2),), 1)
    from_below = extended[:, :, 0]
    from_above = extended[:, :, -1]
    plane_low = jnp.concatenate([from_below[1:], jnp.zeros_like(from_below[:1])], axis=0)
    plane_high = jnp.concatenate([jnp.zeros_like(from_above[:1]), from_above[:2]], axis=0)
    return (plane_low, plane_high)


def per_device(pieces, potential, centers, pattern):
    slab_id = lax.axis_index("sx")
    slab_count = lax.axis_size("sx")
    row_count = pieces.shape[0]
    section = NY * NZ
    volume = 1.0 / (4.0 * CX**3)
    inside = sphere_mask(centers, slab_id, slab_count)
    orbitals = jnp.where(
        inside, pieces.reshape(row_count, CX, section), jnp.zeros((), pieces.dtype)
    )
    grouped = orbitals.reshape(3, ORB, CX, section)
    slot_masks = inside.reshape(3, ORB, CX, section)
    plane_low, plane_high = boundary(grouped)

    def apply_ham(items):
        slot_values, low_side, high_side, region = items
        values = slot_values.astype(jnp.float32)
        applied = (
            kinetic(values, low_side.astype(jnp.float32), high_side.astype(jnp.float32))
            + potential[None] * values
        )
        return jnp.where(region, applied, 0.0).astype(jnp.bfloat16)

    energy = lax.map(apply_ham, (grouped, plane_low, plane_high, slot_masks))
    flat_orbit = orbitals.reshape(row_count, -1)
    flat_energy = energy.reshape(row_count, -1)
    contract_cells = (((1,), (1,)), ((), ()))
    correlation_local = (
        lax.dot_general(flat_orbit, flat_orbit, contract_cells, preferred_element_type=jnp.float32)
        * volume
    )
    ham_local = (
        lax.dot_general(flat_orbit, flat_energy, contract_cells, preferred_element_type=jnp.float32)
        * volume
    )
    stacked = jnp.stack(
        [correlation_local.reshape(3, ORB * row_count), ham_local.reshape(3, ORB * row_count)],
        axis=1,
    )
    received = extended_2(stacked, (("sx", 0),), 1)
    from_below = jnp.pad(received[0].reshape(2, ORB, 3, ORB), ((0, 0), (0, 0), (0, 2), (0, 0)))
    from_self = jnp.pad(received[2].reshape(2, ORB, 3, ORB), ((0, 0), (0, 0), (1, 1), (0, 0)))
    from_above = jnp.pad(received[4].reshape(2, ORB, 3, ORB), ((0, 0), (0, 0), (2, 0), (0, 0)))
    band_pair = from_below + from_self + from_above
    padded_pattern = jnp.pad(pattern, ((2, 2), (0, 0))).astype(jnp.float32)
    near_pattern = lax.dynamic_slice_in_dim(padded_pattern, slab_id, 3, 0)
    weights = jnp.stack(
        [
            near_pattern[0, 1],
            near_pattern[1, 0],
            jnp.ones((), jnp.float32),
            near_pattern[2, 0],
            near_pattern[2, 1],
        ]
    )
    band_pair = band_pair * weights[None, None, :, None]
    inverse_band = (-band_pair[0]).at[:, 2, :].add(2.0 * jnp.eye(ORB, dtype=jnp.float32))
    band_tiles = jnp.stack([inverse_band, band_pair[1]]).reshape(1, 2, ORB * 5 * ORB)
    nearby = []
    for offset in range(-3, 4):
        if offset == 0:
            nearby.append(band_tiles[0])
        else:
            nearby.append(passed_along(band_tiles, "sx", -offset)[0])
    window = jnp.stack(nearby)
    window = window.reshape(7, 2, ORB, 5, ORB)
    theta_rows = []
    for row_slot in range(3):
        theta_cols = []
        for col_slot in range(3):
            summed = jnp.zeros((ORB, ORB), jnp.float32)
            for step_off in range(-2, 3):
                band_off = col_slot - row_slot - step_off
                if abs(band_off) > 2:
                    continue
                x_block = window[row_slot + 2, 0, :, step_off + 2, :]
                h_block = window[row_slot + 2 + step_off, 1, :, band_off + 2, :]
                summed = summed + jnp.dot(
                    x_block,
                    h_block,
                    precision=lax.Precision.HIGHEST,
                    preferred_element_type=jnp.float32,
                )
            theta_cols.append(summed)
        theta_rows.append(jnp.stack(theta_cols, axis=1))
    theta_full = jnp.stack(theta_rows).astype(jnp.bfloat16).reshape(row_count, row_count)
    theta_slots = jnp.moveaxis(theta_full.reshape(row_count, 3, ORB), 1, 0)

    def correct(items):
        theta_part, energy_part, region = items
        correction = lax.dot_general(
            theta_part, flat_orbit, (((0,), (0,)), ((), ())), preferred_element_type=jnp.float32
        )
        result = jnp.where(
            region.reshape(ORB, -1),
            energy_part.reshape(ORB, -1).astype(jnp.float32) - correction,
            0.0,
        )
        return result.astype(jnp.bfloat16).reshape(ORB, CX, section)

    gradient = lax.map(correct, (theta_slots, energy, slot_masks))
    grad_low, grad_high = boundary(gradient)

    def smooth(items):
        slot_values, low_side, high_side, region = items
        values = slot_values.astype(jnp.float32)
        applied = (
            kinetic(values, low_side.astype(jnp.float32), high_side.astype(jnp.float32))
            + mass_term * values
        )
        smoothed = (2.0 * values - applied / jacobi_diag) / jacobi_diag
        return jnp.where(region, smoothed, 0.0).astype(jnp.bfloat16)

    direction = lax.map(smooth, (gradient, grad_low, grad_high, slot_masks))
    return direction.reshape(row_count, CX * section)


def solution(mesh):
    return jax.shard_map(
        per_device,
        mesh=mesh,
        in_specs=(P(("grp", "sx"), None), P(("grp", "sx"), None), P("grp", None), P("grp", None)),
        out_specs=P(("grp", "sx"), None),
        check_vma=False,
    )
```

profile of v0, /device:TPU:11, one launch (start us, length us, event | category | flops | bytes accessed | tf_op | source)
XLA Modules:
  0.0 221.3 jit_solution(16793476513872011293)
XLA Ops:
  4.5 9.5 %add.311 = s32[3,64,4,1024]{1,0,3,2:T(4,128)} reshape(s32[192,4,32,32]{0,3,2,1:T(8,128)} %add.310) | data formatting | bytes 6291456 | tf_op jit(solution)/shard_map/add | solution.py:44
  15.9 2.4 %reshape.308 = bf16[3,64,4,1024]{3,2,1,0:T(4,128)(2,1)} reshape(bf16[192,4096]{1,0:T(8,128)(2,1)S(1)} %copy-done.3) | data formatting | bytes 3145728 | tf_op jit(solution)/shard_map/reshape | solution.py:81
  18.3 7.4 %copy.56 = bf16[3,64,4,1024]{1,0,3,2:T(4,128)(2,1)} copy(bf16[3,64,4,1024]{3,2,1,0:T(4,128)(2,1)} %reshape.308) | data formatting | bytes 3145728 | tf_op jit(solution)/shard_map/reshape | solution.py:81
  25.8 9.2 %broadcast_select_fusion = (bf16[3,64,4,1024]{1,0,3,2:T(4,128)(2,1)S(1)}, pred[3,64,4,1024]{1,0,3,2:T(4,128)(4,1)}) fusion(bf16[3,64,4,1024]{1,0,3,2:T(4,128)(2,1)} %copy.56, pred[3,64]{1,0:T(4,128)(4,1)S(1)} %compare_and_fusion.1, s32[3,64]{1,0:T(4,128)S(1)} %integer_pow.39, s32[3,64,4,1024]{1,0,3,2:T(4,128)} %add.311, s32[3,64,1024]{1,0,2:T(4,128)} %add.313), kind=kLoop, calls=%fused_computation.64 | loop fusion | flops 3145728 | bytes 7865280 | tf_op jit(solution)/shard_map/jit(_where)/select_n | solution.py:80
  35.0 2.5 %fusion.76 = (bf16[3,64,1,1024]{1,0,3,2:T(4,128)(2,1)}, bf16[3,64,1,1024]{1,0,3,2:T(4,128)(2,1)}) fusion(bf16[3,64,4,1024]{1,0,3,2:T(4,128)(2,1)S(1)} %get-tuple-element.320), kind=kLoop, calls=%fused_computation.156 | loop fusion | bytes 1572864 | tf_op jit(solution)/shard_map/slice | solution.py:24
  39.2 3.7 %collective-permute-start = (bf16[3,64,1,1024]{3,1,2,0:T(8,128)(2,1)S(1)}, bf16[3,64,1,1024]{3,1,2,0:T(8,128)(2,1)}, u32[]{:S(2)}, u32[]{:S(2)}) collective-permute-start(bf16[3,64,1,1024]{3,1,2,0:T(8,128)(2,1)S(1)} %copy.57), channel_id=1, source_target_pairs={{0,1},{1,2},{2,3},{3,4},{4,5},{5,6},{6,7},{7,8},{8,9},{9,10},{10,1... | collective-permute-start | bytes 1179656 | tf_op jit(solution)/shard_map/ppermute | solution.py:21
  47.2 2.5 %copy.66 = bf16[192,4096]{0,1:T(8,128)(2,1)} copy(bf16[192,4096]{1,0:T(8,128)(2,1)S(1)} %copy-done.3) | data formatting | bytes 3145728 | tf_op args[0]
  49.7 2.6 %fusion.32 = bf16[192,4096]{0,1:T(8,128)(2,1)S(1)} fusion(bf16[192,4096]{0,1:T(8,128)(2,1)} %copy.66, s32[192]{0:T(256)S(1)} %bitcast.350, s32[192,1024]{0,1:T(8,128)S(1)} %bitcast.271, s32[192,4,32]{0,2,1:T(8,128)S(1)} %broadcast_add_fusion, pred[192]{0:T(512)(128)(4,1)S(1)} %compare_and_fusion), kind=kLoop, calls=%fused_computation.63 | loop fusion | flops 3145728 | bytes 4031424 | tf_op jit(solution)/shard_map/jit(_where)/select_n | solution.py:80
  55.3 4.5 %copy.63 = bf16[3,64,4,1024]{1,3,2,0:T(8,128)(2,1)} copy(bf16[3,64,4,1024]{1,0,3,2:T(4,128)(2,1)} %copy-done) | data formatting | bytes 3145728 | tf_op jit(solution)/shard_map/while | solution.py:96
  59.8 3.6 %copy.78 = pred[3,64,4,1024]{1,3,2,0:T(8,128)(4,1)} copy(pred[3,64,4,1024]{1,0,3,2:T(4,128)(4,1)} %get-tuple-element.321) | data formatting | bytes 1572864 | tf_op jit(solution)/shard_map/while | solution.py:186
  63.4 6.5 %copy.72 = pred[3,64,4,1024]{3,2,1,0:T(4,128)(4,1)} copy(pred[3,64,4,1024]{1,0,3,2:T(4,128)(4,1)} %get-tuple-element.321) | data formatting | bytes 1572864 | tf_op jit(solution)/shard_map/while | solution.py:173
  69.9 2.9 %copy.74 = bf16[192,4096]{1,0:T(8,128)(2,1)S(1)} copy(bf16[192,4096]{0,1:T(8,128)(2,1)} %copy-done.1) | data formatting | bytes 3145728 | tf_op jit(solution)/shard_map/while | solution.py:173
  77.9 21.8 %while.35 = (s32[]{:T(128)}, bf16[3,64,4,1024]{3,2,1,0:T(4,128)(2,1)}, pred[3,64,4,1024]{1,3,2,0:T(8,128)(4,1)}, bf16[3,64,4,1024]{1,3,2,0:T(8,128)(2,1)}, bf16[...) while((s32[]{:T(128)}, ...), condition=%wide.region_1.2_spmd, body=%wide.region_0.1_spmd.sunk | while | flops 4063234 | bytes 12075617 | solution.py:96
  103.4 3.4 %collective-permute-start.3 = (f32[1,2,12288]{2,0,1:T(1,128)S(1)}, f32[1,2,12288]{2,0,1:T(1,128)S(1)}, u32[]{:S(2)}, u32[]{:S(2)}) collective-permute-start(f32[1,2,12288]{2,0,1:T(1,128)S(1)} %get-tuple-element.367), channel_id=1, source_target_pairs={{1,0},{2,1},{3,2},{4,3},{5,4},{6,5},{7,6},{8,7},{9,8},{10,9},{11,1... | collective-permute-start | bytes 294920 | tf_op jit(solution)/shard_map/ppermute | solution.py:24
  109.7 2.6 %stack.92 = f32[5]{0:T(128)S(1)} concatenate(f32[1]{0:T(128)} %bitcast.26, f32[1]{0:T(128)} %bitcast.27, f32[1]{0:T(128)} %constant.180.clone.1, f32[1]{0:T(128)} %bitcast.28, f32[1]{0:T(128)} %bitcast.29), dimensions={0} | concatenate | bytes 40 | tf_op jit(solution)/shard_map/stack | solution.py:119
  114.3 2.4 %collective-permute-start.4 = (f32[1,2,20480]{2,1,0:T(2,128)S(1)}, f32[1,2,20480]{2,1,0:T(2,128)S(1)}, u32[]{:S(2)}, u32[]{:S(2)}) collective-permute-start(f32[1,2,20480]{2,1,0:T(2,128)S(1)} %reshape.310), channel_id=1, source_target_pairs={{0,1},{1,2},{2,3},{3,4},{4,5},{5,6},{6,7},{7,8},{8,9},{9,10},{10,1... | collective-permute-start | bytes 491528 | tf_op jit(solution)/shard_map/ppermute | solution.py:32
  116.7 4.5 %collective-permute-start.6 = (f32[1,2,20480]{2,1,0:T(2,128)S(1)}, f32[1,2,20480]{2,1,0:T(2,128)S(1)}, u32[]{:S(2)}, u32[]{:S(2)}) collective-permute-start(f32[1,2,20480]{2,1,0:T(2,128)S(1)} %reshape.310), channel_id=1, source_target_pairs={{0,2},{1,3},{2,4},{3,5},{4,6},{5,7},{6,8},{7,9},{8,10},{9,11},{10,... | collective-permute-start | bytes 491528 | tf_op jit(solution)/shard_map/ppermute | solution.py:32
  125.4 5.0 %collective-permute-start.5 = (f32[1,2,20480]{2,1,0:T(2,128)S(1)}, f32[1,2,20480]{2,1,0:T(2,128)S(1)}, u32[]{:S(2)}, u32[]{:S(2)}) collective-permute-start(f32[1,2,20480]{2,1,0:T(2,128)S(1)} %reshape.310), channel_id=1, source_target_pairs={{0,3},{1,4},{2,5},{3,6},{4,7},{5,8},{6,9},{7,10},{8,11},{9,12},{10... | collective-permute-start | bytes 491528 | tf_op jit(solution)/shard_map/ppermute | solution.py:32
  162.9 15.0 %while.36 = (s32[]{:T(128)}, bf16[3,64,4,1024]{3,2,1,0:T(4,128)(2,1)}, pred[3,64,4,1024]{3,2,1,0:T(4,128)(4,1)}, bf16[3,64,4,1024]{3,2,1,0:T(4,128)(2,1)}, bf16[...) while((s32[]{:T(128)}, bf16[3,64,4,1024]{3,2,1,0:T(4,128)(2,1)}, ...), condition=%wide.region_3.4_spmd, body=%wide.region_2.3_spmd.sunk | while | flops 101711872 | bytes 10273369 | solution.py:173
  179.9 2.4 %collective-permute-start.10 = (bf16[3,64,1,1024]{3,1,2,0:T(8,128)(2,1)S(1)}, bf16[3,64,1,1024]{3,1,2,0:T(8,128)(2,1)S(1)}, u32[]{:S(2)}, u32[]{:S(2)}) collective-permute-start(bf16[3,64,1,1024]{3,1,2,0:T(8,128)(2,1)S(1)} %get-tuple-element.333), channel_id=1, source_target_pairs={{0,1},{1,2},{2,3},{3,4},{4,5},{5,6},{6,7},{7,8},{8,9},{9,10},{10,1... | collective-permute-start | bytes 1179656 | tf_op jit(solution)/shard_map/ppermute | solution.py:21
  184.6 2.4 %collective-permute-done.10 = bf16[3,64,1,1024]{3,1,2,0:T(8,128)(2,1)S(1)} collective-permute-done((bf16[3,64,1,1024]{3,1,2,0:T(8,128)(2,1)S(1)}, bf16[3,64,1,1024]{3,1,2,0:T(8,128)(2,1)S(1)}, u32[]{:S(2)}, u32[]{:S(2)}) %collective-permute-start.10) | collective-permute-done | bytes 393248 | tf_op jit(solution)/shard_map/ppermute | solution.py:21
  187.0 7.0 %collective-permute-done.11 = bf16[3,64,1,1024]{3,1,2,0:T(8,128)(2,1)S(1)} collective-permute-done((bf16[3,64,1,1024]{3,1,2,0:T(8,128)(2,1)S(1)}, bf16[3,64,1,1024]{3,1,2,0:T(8,128)(2,1)S(1)}, u32[]{:S(2)}, u32[]{:S(2)}) %collective-permute-start.11) | collective-permute-done | bytes 393248 | tf_op jit(solution)/shard_map/ppermute | solution.py:24
  195.7 22.4 %while.37 = (s32[]{:T(128)}, bf16[3,64,4,1024]{3,2,1,0:T(4,128)(2,1)}, pred[3,64,4,1024]{1,3,2,0:T(8,128)(4,1)}, bf16[3,64,4,1024]{3,2,1,0:T(4,128)(2,1)}, bf16[...) while((s32[]{:T(128)}, bf16[3,64,4,1024]{3,2,1,0:T(4,128)(2,1)}, ...), condition=%wide.region_5.6_spmd, body=%wide.region_4.5_spmd.sunk | while | flops 5111810 | bytes 14680665 | solution.py:186
  218.1 3.2 %copy.100 = bf16[24,8,4,1024]{3,1,2,0:T(8,128)(2,1)} copy(bf16[24,8,4,1024]{3,2,1,0:T(4,128)(2,1)} %bitcast.272) | data formatting | bytes 3145728
  (249 shorter events, 129.9 us)
Async XLA Ops:
  35.0 2.6 %copy-start = (bf16[3,64,4,1024]{1,0,3,2:T(4,128)(2,1)}, bf16[3,64,4,1024]{1,0,3,2:T(4,128)(2,1)S(1)}, u32[]{:S(2)}) copy-start(bf16[3,64,4,1024]{1,0,3,2:T(4,128)(2,1)S(1)} %get-tuple-element.320) | copy-start | bytes 4718596
  39.2 34.4 %collective-permute-start = (bf16[3,64,1,1024]{3,1,2,0:T(8,128)(2,1)S(1)}, bf16[3,64,1,1024]{3,1,2,0:T(8,128)(2,1)}, u32[]{:S(2)}, u32[]{:S(2)}) collective-permute-start(bf16[3,64,1,1024]{3,1,2,0:T(8,128)(2,1)S(1)} %copy.57), channel_id=1, source_target_pairs={{0,1},{1,2},{2,3},{3,4},{4,5},{5,6},{6,7},{7,8},{8,9},{9,10},{10,1... | collective-permute-start | bytes 1179656 | tf_op jit(solution)/shard_map/ppermute | solution.py:21
  45.1 29.4 %collective-permute-start.1 = (bf16[3,64,1,1024]{3,1,2,0:T(8,128)(2,1)}, bf16[3,64,1,1024]{3,1,2,0:T(8,128)(2,1)}, u32[]{:S(2)}, u32[]{:S(2)}) collective-permute-start(bf16[3,64,1,1024]{3,1,2,0:T(8,128)(2,1)} %copy.59), channel_id=1, source_target_pairs={{1,0},{2,1},{3,2},{4,3},{5,4},{6,5},{7,6},{8,7},{9,8},{10,9},{11,1... | collective-permute-start | bytes 1179656 | tf_op jit(solution)/shard_map/ppermute | solution.py:24
  72.8 5.1 %copy-start.5 = (f32[4,1024]{1,0:T(4,128)S(1)}, f32[4,1024]{1,0:T(4,128)}, u32[]{:S(2)}) copy-start(f32[4,1024]{1,0:T(4,128)} %param.13) | copy-start | bytes 49156
  101.9 7.1 %copy-start.16 = (f32[3,2]{0,1:T(2,128)S(1)}, f32[3,2]{0,1:T(2,128)}, u32[]{:S(2)}) copy-start(f32[3,2]{0,1:T(2,128)} %constant_dynamic-slice_fusion.6) | copy-start | bytes 76
  103.4 9.0 %collective-permute-start.3 = (f32[1,2,12288]{2,0,1:T(1,128)S(1)}, f32[1,2,12288]{2,0,1:T(1,128)S(1)}, u32[]{:S(2)}, u32[]{:S(2)}) collective-permute-start(f32[1,2,12288]{2,0,1:T(1,128)S(1)} %get-tuple-element.367), channel_id=1, source_target_pairs={{1,0},{2,1},{3,2},{4,3},{5,4},{6,5},{7,6},{8,7},{9,8},{10,9},{11,1... | collective-permute-start | bytes 294920 | tf_op jit(solution)/shard_map/ppermute | solution.py:24
  106.8 6.1 %collective-permute-start.2 = (f32[1,2,12288]{2,0,1:T(1,128)S(1)}, f32[1,2,12288]{2,0,1:T(1,128)S(1)}, u32[]{:S(2)}, u32[]{:S(2)}) collective-permute-start(f32[1,2,12288]{2,0,1:T(1,128)S(1)} %get-tuple-element.366), channel_id=1, source_target_pairs={{0,1},{1,2},{2,3},{3,4},{4,5},{5,6},{6,7},{7,8},{8,9},{9,10},{10,1... | collective-permute-start | bytes 294920 | tf_op jit(solution)/shard_map/ppermute | solution.py:21
  114.3 17.4 %collective-permute-start.4 = (f32[1,2,20480]{2,1,0:T(2,128)S(1)}, f32[1,2,20480]{2,1,0:T(2,128)S(1)}, u32[]{:S(2)}, u32[]{:S(2)}) collective-permute-start(f32[1,2,20480]{2,1,0:T(2,128)S(1)} %reshape.310), channel_id=1, source_target_pairs={{0,1},{1,2},{2,3},{3,4},{4,5},{5,6},{6,7},{7,8},{8,9},{9,10},{10,1... | collective-permute-start | bytes 491528 | tf_op jit(solution)/shard_map/ppermute | solution.py:32
  116.7 36.4 %collective-permute-start.6 = (f32[1,2,20480]{2,1,0:T(2,128)S(1)}, f32[1,2,20480]{2,1,0:T(2,128)S(1)}, u32[]{:S(2)}, u32[]{:S(2)}) collective-permute-start(f32[1,2,20480]{2,1,0:T(2,128)S(1)} %reshape.310), channel_id=1, source_target_pairs={{0,2},{1,3},{2,4},{3,5},{4,6},{5,7},{6,8},{7,9},{8,10},{9,11},{10,... | collective-permute-start | bytes 491528 | tf_op jit(solution)/shard_map/ppermute | solution.py:32
  121.3 19.8 %collective-permute-start.7 = (f32[1,2,20480]{2,1,0:T(2,128)S(1)}, f32[1,2,20480]{2,1,0:T(2,128)}, u32[]{:S(2)}, u32[]{:S(2)}) collective-permute-start(f32[1,2,20480]{2,1,0:T(2,128)S(1)} %reshape.310), channel_id=1, source_target_pairs={{1,0},{2,1},{3,2},{4,3},{5,4},{6,5},{7,6},{8,7},{9,8},{10,9},{11,1... | collective-permute-start | bytes 491528 | tf_op jit(solution)/shard_map/ppermute | solution.py:32
  123.2 25.6 %collective-permute-start.8 = (f32[1,2,20480]{2,1,0:T(2,128)S(1)}, f32[1,2,20480]{2,1,0:T(2,128)}, u32[]{:S(2)}, u32[]{:S(2)}) collective-permute-start(f32[1,2,20480]{2,1,0:T(2,128)S(1)} %reshape.310), channel_id=1, source_target_pairs={{2,0},{3,1},{4,2},{5,3},{6,4},{7,5},{8,6},{9,7},{10,8},{11,9},{12,... | collective-permute-start | bytes 491528 | tf_op jit(solution)/shard_map/ppermute | solution.py:32
  125.4 29.3 %collective-permute-start.5 = (f32[1,2,20480]{2,1,0:T(2,128)S(1)}, f32[1,2,20480]{2,1,0:T(2,128)S(1)}, u32[]{:S(2)}, u32[]{:S(2)}) collective-permute-start(f32[1,2,20480]{2,1,0:T(2,128)S(1)} %reshape.310), channel_id=1, source_target_pairs={{0,3},{1,4},{2,5},{3,6},{4,7},{5,8},{6,9},{7,10},{8,11},{9,12},{10... | collective-permute-start | bytes 491528 | tf_op jit(solution)/shard_map/ppermute | solution.py:32
  132.4 22.7 %collective-permute-start.9 = (f32[1,2,20480]{2,1,0:T(2,128)S(1)}, f32[1,2,20480]{2,1,0:T(2,128)S(1)}, u32[]{:S(2)}, u32[]{:S(2)}) collective-permute-start(f32[1,2,20480]{2,1,0:T(2,128)S(1)} %reshape.310), channel_id=1, source_target_pairs={{3,0},{4,1},{5,2},{6,3},{7,4},{8,5},{9,6},{10,7},{11,8},{12,9},{13... | collective-permute-start | bytes 491528 | tf_op jit(solution)/shard_map/ppermute | solution.py:32
  149.9 7.0 %copy-start.10 = (f32[64,64]{1,0:T(8,128)S(1)}, f32[64,64]{1,0:T(8,128)}, u32[]{:S(2)}) copy-start(f32[64,64]{1,0:T(8,128)} %fusion.100) | copy-start | bytes 49156
  149.9 7.2 %copy-start.11 = (f32[64,64]{1,0:T(8,128)S(1)}, f32[64,64]{1,0:T(8,128)}, u32[]{:S(2)}) copy-start(f32[64,64]{1,0:T(8,128)} %fusion.90) | copy-start | bytes 49156
  153.1 7.9 %copy-start.7 = (f32[1,1,64,1,64]{4,3,2,1,0:T(1,128)S(1)}, f32[1,1,64,1,64]{4,3,2,1,0:T(1,128)}, u32[]{:S(2)}) copy-start(f32[1,1,64,1,64]{4,3,2,1,0:T(1,128)} %get-tuple-element.334) | copy-start | bytes 49156
  153.1 7.9 %copy-start.8 = (f32[64,64]{1,0:T(8,128)S(1)}, f32[64,64]{1,0:T(8,128)}, u32[]{:S(2)}) copy-start(f32[64,64]{1,0:T(8,128)} %fusion.87) | copy-start | bytes 49156
  153.1 7.9 %copy-start.9 = (f32[64,64]{1,0:T(8,128)S(1)}, f32[64,64]{1,0:T(8,128)}, u32[]{:S(2)}) copy-start(f32[64,64]{1,0:T(8,128)} %fusion.88) | copy-start | bytes 49156
  153.3 2.3 %copy-start.15 = (f32[64,64]{1,0:T(8,128)S(1)}, f32[64,64]{1,0:T(8,128)}, u32[]{:S(2)}) copy-start(f32[64,64]{1,0:T(8,128)} %fusion.99) | copy-start | bytes 49156
  153.4 3.6 %copy-start.14 = (f32[64,64]{1,0:T(8,128)S(1)}, f32[64,64]{1,0:T(8,128)}, u32[]{:S(2)}) copy-start(f32[64,64]{1,0:T(8,128)} %fusion.102) | copy-start | bytes 49156
  153.4 5.7 %copy-start.13 = (f32[64,64]{1,0:T(8,128)S(1)}, f32[64,64]{1,0:T(8,128)}, u32[]{:S(2)}) copy-start(f32[64,64]{1,0:T(8,128)} %fusion.107) | copy-start | bytes 49156
  153.4 6.6 %copy-start.12 = (f32[64,64]{1,0:T(8,128)S(1)}, f32[64,64]{1,0:T(8,128)}, u32[]{:S(2)}) copy-start(f32[64,64]{1,0:T(8,128)} %fusion.110) | copy-start | bytes 49156
  179.9 7.1 %collective-permute-start.10 = (bf16[3,64,1,1024]{3,1,2,0:T(8,128)(2,1)S(1)}, bf16[3,64,1,1024]{3,1,2,0:T(8,128)(2,1)S(1)}, u32[]{:S(2)}, u32[]{:S(2)}) collective-permute-start(bf16[3,64,1,1024]{3,1,2,0:T(8,128)(2,1)S(1)} %get-tuple-element.333), channel_id=1, source_target_pairs={{0,1},{1,2},{2,3},{3,4},{4,5},{5,6},{6,7},{7,8},{8,9},{9,10},{10,1... | collective-permute-start | bytes 1179656 | tf_op jit(solution)/shard_map/ppermute | solution.py:21
  182.3 11.7 %collective-permute-start.11 = (bf16[3,64,1,1024]{3,1,2,0:T(8,128)(2,1)S(1)}, bf16[3,64,1,1024]{3,1,2,0:T(8,128)(2,1)S(1)}, u32[]{:S(2)}, u32[]{:S(2)}) collective-permute-start(bf16[3,64,1,1024]{3,1,2,0:T(8,128)(2,1)S(1)} %get-tuple-element.332), channel_id=1, source_target_pairs={{1,0},{2,1},{3,2},{4,3},{5,4},{6,5},{7,6},{8,7},{9,8},{10,9},{11,1... | collective-permute-start | bytes 1179656 | tf_op jit(solution)/shard_map/ppermute | solution.py:24
  (6 other events, 8.7 us)
where the time goes:
time: 224 us; the launch traced here: 221 us
  local copies, waits for them, and re-layouts  110 us (49%)
  other arithmetic  41.5 us (19%)
  starting transfers between devices  34 us (15%)
  matrix products  25.2 us (11%)
  waiting for transfers between devices  9.38 us (4%)
    dot_general x37, matrix products, per_device(): jnp.dot(x_block, h_block, precision=lax.Precision.HIGHEST, preferred_elem...  22.3 us
    ppermute x6, starting transfers between devices, passed_along(): lax.ppermute(value, axis, [(source, source + steps) for source in range(i...  18 us
    dynamic_slice x27, local copies, waits for them, and re-layouts, per_device(): energy = lax.map(apply_ham, (grouped, plane_low, plane_high, slot_masks))  14.4 us
    add x4, local copies, waits for them, and re-layouts, sphere_mask(): dist_x[:, :, None, None] + dist_y[:, None, :, None]  13.6 us
    dynamic_update_slice x15, local copies, waits for them, and re-layouts, per_device(): energy = lax.map(apply_ham, (grouped, plane_low, plane_high, slot_masks))  12.7 us
    select_n x2, other arithmetic, per_device(): jnp.where(inside, pieces.reshape(row_count, CX, section), jnp.zeros((), p...  11.9 us
    while x3, local copies, waits for them, and re-layouts, per_device(): gradient = lax.map(correct, (theta_slots, energy, slot_masks))  11.3 us
    unnamed x40, local copies, waits for them, and re-layouts  10.9 us
  transfers between devices with their start and end apart: 12, of which 2 were waited for; matrix products, arithmetic and copies ran while one was open for 24% of the time, Pallas kernels for 0%

commit v1 on v0

v1 whole, which is shorter than its diff:
```python
import functools

import jax
import jax.numpy as jnp
from jax import lax
from jax.experimental import pallas as pl
from jax.experimental.pallas import tpu as pltpu
from jax.sharding import PartitionSpec as P

ORB = 64
CX = 4
NY = 32
NZ = 32
ROWS = 3 * ORB
PLANE = NY * NZ
TILE = 256
HALF = PLANE // 4
F32 = jnp.float32
BF16 = jnp.bfloat16


def iota(shape, dim):
    return lax.broadcasted_iota(jnp.int32, shape, dim)


def row_features(ct_ref):
    slab = lax.axis_index("sx")
    count = lax.axis_size("sx")
    width = ct_ref.shape[1]
    first = jnp.clip(slab * ORB - ORB, 0, width - 4 * ORB) // 128 * 128
    first = pl.multiple_of(first, 128)
    window = ct_ref[:, pl.ds(first, 4 * ORB)]
    shift = slab * ORB - ORB - first
    window = pltpu.roll(jnp.concatenate([window, window], axis=0), lax.rem(4 * ORB - shift, 4 * ORB), 1)
    lane = iota((1, 4 * ORB), 1)
    block = slab - 1 + lane // ORB
    valid = (block >= 0) & (block < count)
    cx = window[0:1] - slab * CX
    cy = window[1:2]
    cz = window[2:3]
    r = window[3:4]
    const = cx * cx + cy * cy + cz * cz - r * r
    const = jnp.where(valid, const, 65535)
    cx = jnp.where(valid, cx, 0)
    cy = jnp.where(valid, cy, 0)
    cz = jnp.where(valid, cz, 0)
    k = iota((16, 4 * ORB), 0)
    feats = jnp.where(k == 0, 1, 0)
    feats = jnp.where(k == 1, 256, feats)
    feats = jnp.where(k == 2, cy, feats)
    feats = jnp.where(k == 3, cz, feats)
    feats = jnp.where(k == 4, const & 255, feats)
    feats = jnp.where(k == 5, const >> 8, feats)
    feats = jnp.where(k == 6, cx, feats)
    return jnp.transpose(feats.astype(F32))[:ROWS].astype(BF16)


def cell_features(plane):
    k = iota((16, PLANE), 0)
    cell = iota((16, PLANE), 1)
    y = cell >> 5
    z = cell & 31
    sq = y * y + z * z + plane * plane
    feats = jnp.where(k == 0, sq & 255, 0)
    feats = jnp.where(k == 1, sq >> 8, feats)
    feats = jnp.where(k == 2, -2 * y, feats)
    feats = jnp.where(k == 3, -2 * z, feats)
    feats = jnp.where(k == 4, 1, feats)
    feats = jnp.where(k == 5, 256, feats)
    feats = jnp.where(k == 6, -2 * plane, feats)
    return feats.astype(F32).astype(BF16)


def sphere(rows, plane):
    reach = jnp.dot(rows, cell_features(plane), preferred_element_type=F32)
    return jnp.where(reach <= 0.0, 1.0, 0.0).astype(BF16)


def in_plane(center, beside):
    k = iota((2 * TILE, TILE), 0) - 128
    n = iota((2 * TILE, TILE), 1)
    diff = k - n
    near_y = (diff == NZ) | (diff == -NZ)
    near_z = ((diff == 1) | (diff == -1)) & ((k >> 5) == (n >> 5))
    w = jnp.where(near_y | near_z, float(beside), 0.0)
    return jnp.where(diff == 0, float(center), w).astype(BF16)


def plane_product(values, weights, t):
    low = max(0, TILE * t - 128)
    high = min(PLANE, TILE * t + TILE + 128)
    shift = 128 - TILE * t
    return jnp.dot(
        values[:, low:high], weights[low + shift : high + shift], preferred_element_type=F32
    )


def fold(values):
    half = values[:, : PLANE // 2] + values[:, PLANE // 2 :]
    low_z = (iota((1, 128), 1) & 31) < 16
    out = []
    for i in range(2):
        a = half[:, 256 * i : 256 * i + 128]
        b = half[:, 256 * i + 128 : 256 * i + 256]
        out.append(jnp.where(low_z, a + pltpu.roll(a, 112, 1), b + pltpu.roll(b, 16, 1)))
    return out


def unfold(packed):
    low_z = (iota((1, 128), 1) & 31) < 16
    tiles = []
    for i in range(2):
        p = packed[:, 128 * i : 128 * i + 128]
        tiles.append(jnp.where(low_z, p, pltpu.roll(p, 16, 1)))
        tiles.append(jnp.where(low_z, pltpu.roll(p, 112, 1), p))
    return tiles


def put_fold(ref, values):
    a, b = fold(values)
    ref[:, 0:128] = a.astype(BF16)
    ref[:, 128:256] = b.astype(BF16)


def edges_kernel(ct_ref, first_ref, last_ref, phi_ref, mask_ref, up_ref, down_ref):
    rows = row_features(ct_ref)
    for i, (plane, ref) in enumerate(((0, first_ref), (CX - 1, last_ref))):
        mask = sphere(rows, plane)
        value = ref[...] * mask
        mask_ref[i] = mask
        phi_ref[i] = value
        if i == 0:
            put_fold(down_ref, value[: 2 * ORB].astype(F32))
        else:
            put_fold(up_ref, value[ORB:].astype(F32))


def rows_product(a, b):
    return lax.dot_general(a, b, (((1,), (1,)), ((), ())), preferred_element_type=F32)


def energy_kernel(
    ct_ref, mid1_ref, mid2_ref, pot_ref, edge_ref,
    phi_ref, mask_ref, energy_ref, part_ref, corr_ref, ham_ref,
):
    rows = row_features(ct_ref)
    for i, ref in enumerate((mid1_ref, mid2_ref)):
        mask = sphere(rows, 1 + i)
        mask_ref[i] = mask
        phi_ref[i] = ref[...] * mask
    weights = in_plane(6, -1)
    for t in range(PLANE // TILE):
        lanes = slice(TILE * t, TILE * t + TILE)
        edge = edge_ref[:, :, lanes].astype(F32)
        mid = phi_ref[:, :, lanes].astype(F32)
        inner = plane_product(phi_ref[...].reshape(2 * ROWS, PLANE), weights, t).reshape(2, ROWS, TILE)
        outer = plane_product(edge_ref[...].reshape(2 * ROWS, PLANE), weights, t).reshape(2, ROWS, TILE)
        for i in range(2):
            value = 0.5 * (inner[i] - (edge[i] + mid[1 - i])) + pot_ref[1 + i : 2 + i, lanes] * mid[i]
            energy_ref[i, :, lanes] = value.astype(BF16) * mask_ref[i, :, lanes]
            plane = (CX - 1) * i
            part_ref[i, :, lanes] = 0.5 * (outer[i] - mid[i]) + pot_ref[plane : plane + 1, lanes] * edge[i]
    corr = jnp.zeros((ROWS, ROWS), F32)
    ham = jnp.zeros((ROWS, ROWS), F32)
    for i in range(2):
        corr = corr + rows_product(phi_ref[i], phi_ref[i]) + rows_product(edge_ref[i], edge_ref[i])
        ham = ham + rows_product(energy_ref[i], phi_ref[i])
    corr_ref[...] = corr
    ham_ref[...] = ham


def halo_rows(i):
    return slice(0, 2 * ORB) if i == 0 else slice(ORB, ROWS)


def bands_kernel(
    below_ref, above_ref, part_ref, mask_ref, phi_ref, corr_ref, ham_ref,
    energy_ref, own_ref, up1_ref, down1_ref, up2_ref, down2_ref,
):
    volume = 1.0 / (4.0 * CX**3)
    ham = ham_ref[...]
    for i, ref in enumerate((below_ref, above_ref)):
        tiles = unfold(ref[...].astype(F32))
        rest = slice(2 * ORB, ROWS) if i == 0 else slice(0, ORB)
        for t in range(PLANE // 128):
            lanes = slice(128 * t, 128 * t + 128)
            value = part_ref[i, halo_rows(i), lanes] - 0.5 * tiles[t % 4]
            energy_ref[i, halo_rows(i), lanes] = value.astype(BF16) * mask_ref[i, halo_rows(i), lanes]
            energy_ref[i, rest, lanes] = part_ref[i, rest, lanes].astype(BF16) * mask_ref[i, rest, lanes]
        ham = ham + rows_product(energy_ref[i], phi_ref[i])
    own_ref[:, :, ROWS:] = jnp.zeros((2, ROWS, TILE - ROWS), F32)
    own_ref[0, :, :ROWS] = ham * volume
    own_ref[1, :, :ROWS] = corr_ref[...] * volume
    low = iota((1, 128), 1) < 64
    h0 = own_ref[0, :, 0:128]
    h1 = own_ref[0, :, 128:256]
    c0 = own_ref[1, :, 0:128]
    c1 = own_ref[1, :, 128:256]
    h0r = pltpu.roll(h0, 64, 1)
    h1r = pltpu.roll(h1, 64, 1)
    c1r = pltpu.roll(c1, 64, 1)
    near = (
        jnp.where(low, h0r, h1r),
        jnp.where(low, pltpu.roll(c0, 64, 1), c1r),
        jnp.where(low, c0, h0r),
    )
    far = (h0, c0, jnp.where(low, h1, c1r))
    for i in range(3):
        value = near[i].astype(BF16)
        up1_ref[i] = value[ORB:]
        down1_ref[i] = value[: 2 * ORB]
        value = far[i].astype(BF16)
        up2_ref[i] = value[2 * ORB :]
        down2_ref[i] = value[:ORB]


def gradient_kernel(
    pattern_ref, own_ref, below1_ref, above1_ref, below2_ref, above2_ref,
    edge_ref, phi_ref, edge_energy_ref, energy_ref, edge_mask_ref, mask_ref,
    edge_grad_ref, grad_ref, up_ref, down_ref,
    ham_ref, inv_ref,
):
    slab = lax.axis_index("sx")
    last = pattern_ref.shape[1] - 1
    low = iota((1, 128), 1) < 64
    for which, band_ref in enumerate((ham_ref, inv_ref)):

        def near(ref):
            head = ref[2].astype(F32)
            if which == 1:
                head = pltpu.roll(head, 64, 1)
            return (jnp.where(low, 0.0, head), ref[which].astype(F32))

        def far(ref):
            tail = ref[2].astype(F32)
            if which == 1:
                tail = pltpu.roll(tail, 64, 1)
            return (ref[which].astype(F32), jnp.where(low, tail, 0.0))

        own = (own_ref[which, :, 0:128], own_ref[which, :, 128:256])
        below1 = near(below1_ref)
        above1 = near(above1_ref)
        below2 = far(below2_ref)
        above2 = far(above2_ref)
        zero = jnp.zeros((ORB, 128), F32)
        s0, s1, s2 = (slice(ORB * i, ORB * i + ORB) for i in range(3))
        tiles = (
            (
                below1[0][s0] + below2[0],
                own[0][s0] + below1[1][s0] + below2[1],
                own[1][s0],
                zero,
            ),
            (
                below1[0][s1],
                own[0][s1] + below1[1][s1] + above1[0][s0],
                own[1][s1] + above1[1][s0],
                zero,
            ),
            (
                zero,
                own[0][s2] + above1[0][s1],
                own[1][s2] + above1[1][s1] + above2[0],
                above2[1],
            ),
        )
        for r in range(3):
            for q in range(4):
                kept = []
                for col in (2 * q, 2 * q + 1):
                    apart = abs(col - r - 2)
                    if apart == 0:
                        kept.append(1.0)
                    elif apart > 2:
                        kept.append(0.0)
                    else:
                        at = jnp.clip(slab - 3 + min(col, r + 2), 0, last)
                        kept.append(pattern_ref[apart - 1, at].astype(F32))
                value = tiles[r][q] * jnp.where(low, kept[0], kept[1])
                if which == 1:
                    on = iota((ORB, 128), 0) + (ORB * (r + 2) - 128 * q) == iota((ORB, 128), 1)
                    value = jnp.where(on, 2.0, 0.0) - value
                band_ref[ORB * r : ORB * r + ORB, 128 * q : 128 * q + 128] = value
    theta = lax.dot_general(
        ham_ref[...], inv_ref[...], (((1,), (1,)), ((), ())),
        precision=lax.Precision.HIGHEST, preferred_element_type=F32,
    ).astype(BF16)
    for orb_ref, en_ref, m_ref, out_ref in (
        (edge_ref, edge_energy_ref, edge_mask_ref, edge_grad_ref),
        (phi_ref, energy_ref, mask_ref, grad_ref),
    ):
        for i in range(2):
            for t in range(PLANE // TILE):
                lanes = slice(TILE * t, TILE * t + TILE)
                fix = jnp.dot(theta, orb_ref[i, :, lanes], preferred_element_type=F32)
                value = en_ref[i, :, lanes].astype(F32) - fix
                out_ref[i, :, lanes] = value.astype(BF16) * m_ref[i, :, lanes]
    put_fold(down_ref, edge_grad_ref[0, : 2 * ORB].astype(F32))
    put_fold(up_ref, edge_grad_ref[1, ORB:].astype(F32))


def smooth_kernel(edge_ref, grad_ref, edge_mask_ref, mask_ref, out_ref, part_ref):
    weights = in_plane(8, 1)
    for t in range(PLANE // TILE):
        lanes = slice(TILE * t, TILE * t + TILE)
        edge = edge_ref[:, :, lanes].astype(F32)
        mid = grad_ref[:, :, lanes].astype(F32)
        inner = plane_product(grad_ref[...].reshape(2 * ROWS, PLANE), weights, t).reshape(2, ROWS, TILE)
        outer = plane_product(edge_ref[...].reshape(2 * ROWS, PLANE), weights, t).reshape(2, ROWS, TILE)
        for i in range(2):
            value = (inner[i] + (edge[i] + mid[1 - i])) * (1.0 / 32.0)
            start = PLANE * (1 + i) + TILE * t
            out_ref[:, start : start + TILE] = value.astype(BF16) * mask_ref[i, :, lanes]
            part_ref[i, :, lanes] = outer[i] + mid[i]


def finish_kernel(below_ref, above_ref, part_ref, mask_ref, inner_ref, out_ref):
    for i, ref in enumerate((below_ref, above_ref)):
        tiles = unfold(ref[...].astype(F32))
        rest = slice(2 * ORB, ROWS) if i == 0 else slice(0, ORB)
        for t in range(PLANE // 128):
            lanes = slice(128 * t, 128 * t + 128)
            start = PLANE * (CX - 1) * i + 128 * t
            put = slice(start, start + 128)
            value = (part_ref[i, halo_rows(i), lanes] + tiles[t % 4]) * (1.0 / 32.0)
            out_ref[halo_rows(i), put] = value.astype(BF16) * mask_ref[i, halo_rows(i), lanes]
            value = part_ref[i, rest, lanes] * (1.0 / 32.0)
            out_ref[rest, put] = value.astype(BF16) * mask_ref[i, rest, lanes]
    out_ref[:, PLANE : (CX - 1) * PLANE] = inner_ref[:, PLANE : (CX - 1) * PLANE]


def shape(*dims, dtype=BF16):
    return jax.ShapeDtypeStruct(dims, dtype)


def cost(flops, moved):
    return pl.CostEstimate(flops=flops, bytes_accessed=moved, transcendentals=0)


PARAMS = pltpu.CompilerParams(vmem_limit_bytes=32 * 1024 * 1024)
WHOLE = pl.BlockSpec(memory_space=pltpu.VMEM)


def per_device(pieces, potential, centers, pattern):
    count = lax.axis_size("sx")

    def moved(value, steps):
        first, end = max(0, -steps), min(count, count - steps)
        return lax.ppermute(value, "sx", [(i, i + steps) for i in range(first, end)])

    table = centers.T
    pair = shape(2, ROWS, PLANE)

    def plane_spec(plane):
        return pl.BlockSpec((ROWS, PLANE), lambda i: (0, plane))

    def whole_spec(*dims):
        return pl.BlockSpec(dims, lambda i: (0,) * len(dims))

    edge, edge_mask, up, down = pl.pallas_call(
        edges_kernel,
        grid=(1,),
        out_shape=(pair, pair, shape(2 * ORB, HALF), shape(2 * ORB, HALF)),
        in_specs=[whole_spec(*table.shape), plane_spec(0), plane_spec(CX - 1)],
        out_specs=(
            whole_spec(2, ROWS, PLANE), whole_spec(2, ROWS, PLANE),
            whole_spec(2 * ORB, HALF), whole_spec(2 * ORB, HALF),
        ),
        compiler_params=PARAMS,
        cost_estimate=cost(10**8, 10**6),
        name="edges",
    )(table, pieces, pieces)
    below = moved(up, 1)
    above = moved(down, -1)

    mid, mid_mask, mid_energy, part, corr, ham = pl.pallas_call(
        energy_kernel,
        grid=(1,),
        out_shape=(
            pair, pair, pair, shape(2, ROWS, PLANE, dtype=F32),
            shape(ROWS, ROWS, dtype=F32), shape(ROWS, ROWS, dtype=F32),
        ),
        in_specs=[
            whole_spec(*table.shape), plane_spec(1), plane_spec(2),
            whole_spec(CX, PLANE), whole_spec(2, ROWS, PLANE),
        ],
        out_specs=(
            whole_spec(2, ROWS, PLANE), whole_spec(2, ROWS, PLANE), whole_spec(2, ROWS, PLANE),
            whole_spec(2, ROWS, PLANE), whole_spec(ROWS, ROWS), whole_spec(ROWS, ROWS),
        ),
        compiler_params=PARAMS,
        cost_estimate=cost(4 * 10**9, 10**7),
        name="energy",
    )(table, pieces, pieces, potential, edge)

    edge_energy, own, up1, down1, up2, down2 = pl.pallas_call(
        bands_kernel,
        out_shape=(
            pair, shape(2, ROWS, TILE, dtype=F32),
            shape(3, 2 * ORB, 128), shape(3, 2 * ORB, 128),
            shape(3, ORB, 128), shape(3, ORB, 128),
        ),
        in_specs=[WHOLE] * 7,
        out_specs=(WHOLE,) * 6,
        compiler_params=PARAMS,
        cost_estimate=cost(10**9, 10**7),
        name="bands",
    )(below, above, part, edge_mask, edge, corr, ham)
    below1 = moved(up1, 1)
    above1 = moved(down1, -1)
    below2 = moved(up2, 2)
    above2 = moved(down2, -2)

    edge_grad, mid_grad, up, down = pl.pallas_call(
        gradient_kernel,
        out_shape=(pair, pair, shape(2 * ORB, HALF), shape(2 * ORB, HALF)),
        in_specs=[pl.BlockSpec(memory_space=pltpu.SMEM)] + [WHOLE] * 11,
        out_specs=(WHOLE,) * 4,
        scratch_shapes=[pltpu.VMEM((ROWS, 512), F32), pltpu.VMEM((ROWS, 512), F32)],
        compiler_params=PARAMS,
        cost_estimate=cost(10**9, 10**7),
        name="gradient",
    )(
        pattern.T, own, below1, above1, below2, above2,
        edge, mid, edge_energy, mid_energy, edge_mask, mid_mask,
    )
    below = moved(up, 1)
    above = moved(down, -1)

    inner, part = pl.pallas_call(
        smooth_kernel,
        out_shape=(shape(ROWS, CX * PLANE), shape(2, ROWS, PLANE, dtype=F32)),
        in_specs=[WHOLE] * 4,
        out_specs=(WHOLE,) * 2,
        compiler_params=PARAMS,
        cost_estimate=cost(2 * 10**9, 10**7),
        name="smooth",
    )(edge_grad, mid_grad, edge_mask, mid_mask)

    return pl.pallas_call(
        finish_kernel,
        out_shape=shape(ROWS, CX * PLANE),
        in_specs=[WHOLE] * 5,
        out_specs=WHOLE,
        compiler_params=PARAMS,
        cost_estimate=cost(10**7, 10**7),
        name="finish",
    )(below, above, part, edge_mask, inner)


def solution(mesh):
    return jax.shard_map(
        per_device,
        mesh=mesh,
        in_specs=(P(("grp", "sx"), None), P(("grp", "sx"), None), P("grp", None), P("grp", None)),
        out_specs=P(("grp", "sx"), None),
        check_vma=False,
    )
```

time: 224 us -> 43.6 us (0.19)
  the two profiles are of different devices: /device:TPU:11 before, /device:TPU:1 now
where the time goes in v1:
time: 43.6 us; the launch traced here: 43.2 us
  starting transfers between devices  25 us (57%)
  Pallas kernels  8.74 us (20%)
  waiting for transfers between devices  7.22 us (17%)
  local copies, waits for them, and re-layouts  2.13 us (5%)
    ppermute x8, starting transfers between devices, moved(): lax.ppermute(value, 'sx', [(i, i + steps) for i in range(first, end)])  25 us
    ppermute x8, waiting for transfers between devices, moved(): lax.ppermute(value, 'sx', [(i, i + steps) for i in range(first, end)])  7.22 us
    pallas_call x1, Pallas kernels, per_device(): pl.pallas_call(energy_kernel, grid=(1,), out_shape=(pair, pair, pair, sha...  2.44 us
    pallas_call x1, Pallas kernels, per_device(): pl.pallas_call(gradient_kernel, out_shape=(pair, pair, shape(2 * ORB, HAL...  2.27 us
    unnamed x8, local copies, waits for them, and re-layouts  2.13 us
    pallas_call x1, Pallas kernels, per_device(): pl.pallas_call(finish_kernel, out_shape=shape(ROWS, CX * PLANE), in_specs...  1.56 us
    pallas_call x1, Pallas kernels, per_device(): pl.pallas_call(smooth_kernel, out_shape=(shape(ROWS, CX * PLANE), shape(2...  1.16 us
  transfers between devices with their start and end apart: 8, of which 4 were waited for; matrix products, arithmetic and copies ran while one was open for 0% of the time, Pallas kernels for 8%

profile of v1, /device:TPU:1, one launch (start us, length us, event | category | flops | bytes accessed | tf_op | source)
XLA Modules:
  0.0 43.2 jit_solution(17616719741338447333)
XLA Ops:
  0.0 1.4 %copy-done = bf16[192,4096]{1,0:T(8,128)(2,1)S(1)} copy-done((bf16[192,4096]{1,0:T(8,128)(2,1)S(1)}, bf16[192,4096]{1,0:T(8,128)(2,1)}, u32[]{:S(2)}) %copy-start) | copy-done | bytes 1572888
  1.4 0.7 %copy-done.1 = s32[1024,4]{0,1:T(4,128)S(1)} copy-done((s32[1024,4]{0,1:T(4,128)S(1)}, s32[1024,4]{0,1:T(4,128)}, u32[]{:S(2)}) %copy-start.1) | copy-done | bytes 16408
  2.1 0.6 %edges.1 = (bf16[2,192,1024]{2,1,0:T(8,128)(2,1)S(1)}, bf16[2,192,1024]{2,1,0:T(8,128)(2,1)S(1)}, bf16[128,256]{1,0:T(8,128)(2,1)S(1)}, bf16[128,256]{1,0:T(8,128)(2,1)S(1)}) custom-call(s32[4,1024]{1,0:T(4,128)S(1)} %bitcast.2, bf16[192,4096]{1,0:T(8,128)(2,1)S(1)} %copy-done, bf16[192,4096]{1,0:T(8,128)(2,1)S(1)} %copy-done), custom_call_target="tpu_custom_call" | custom-call | flops 100000000 | bytes 1000000 | tf_op jit(solution)/shard_map/edges/pallas_call | solution.py:360
  2.8 4.5 %collective-permute-start = (bf16[128,256]{1,0:T(8,128)(2,1)S(1)}, bf16[128,256]{1,0:T(8,128)(2,1)S(1)}, u32[]{:S(2)}, u32[]{:S(2)}) collective-permute-start(bf16[128,256]{1,0:T(8,128)(2,1)S(1)} %get-tuple-element.27), channel_id=1, source_target_pairs={{0,1},{1,2},{2,3},{3,4},{4,5},{5,6},{6,7},{7,8},{8,9},{9,10},{10,1... | collective-permute-start | bytes 196616 | tf_op jit(solution)/shard_map/ppermute | solution.py:349
  7.3 1.9 %collective-permute-start.1 = (bf16[128,256]{1,0:T(8,128)(2,1)S(1)}, bf16[128,256]{1,0:T(8,128)(2,1)S(1)}, u32[]{:S(2)}, u32[]{:S(2)}) collective-permute-start(bf16[128,256]{1,0:T(8,128)(2,1)S(1)} %get-tuple-element.28), channel_id=1, source_target_pairs={{1,0},{2,1},{3,2},{4,3},{5,4},{6,5},{7,6},{8,7},{9,8},{10,9},{11,1... | collective-permute-start | bytes 196616 | tf_op jit(solution)/shard_map/ppermute | solution.py:349
  9.2 2.4 %energy.1 = (bf16[2,192,1024]{2,1,0:T(8,128)(2,1)S(1)}, bf16[2,192,1024]{2,1,0:T(8,128)(2,1)S(1)}, bf16[2,192,1024]{2,1,0:T(8,128)(2,1)S(1)}, f32[2,192,1024]{2,...) custom-call(s32[4,1024]{1,0:T(4,128)S(1)} %bitcast.3, bf16[192,4096]{1,0:T(8,128)(2,1)S(1)} %copy-done, ...), custom_call_target="tpu_custom_call" | custom-call | flops 4000000000 | bytes 10000000 | tf_op jit(solution)/shard_map/energy/pallas_call | solution.py:376
  11.7 0.0 collective-permute-done.below_ref
  11.7 1.2 %collective-permute-done.1.above_ref = bf16[128,256]{1,0:T(8,128)(2,1)S(1)} collective-permute-done((bf16[128,256]{1,0:T(8,128)(2,1)S(1)}, bf16[128,256]{1,0:T(8,128)(2,1)S(1)}, u32[]{:S(2)}, u32[]{:S(2)}) %collective-permute-start.1) | collective-permute-done | bytes 65568 | tf_op jit(solution)/shard_map/ppermute | solution.py:349
  12.9 0.7 %bands.1 = (bf16[2,192,1024]{2,1,0:T(8,128)(2,1)S(1)}, f32[2,192,256]{2,1,0:T(8,128)S(1)}, bf16[3,128,128]{2,1,0:T(8,128)(2,1)S(1)}, bf16[3,128,128]{2,1,0:T(8,1...) custom-call(bf16[128,256]{1,0:T(8,128)(2,1)S(1)} %collective-permute-done.below_ref, ...), custom_call_target="tpu_custom_call" | custom-call | flops 1000000000 | bytes 10000000 | tf_op jit(solution)/shard_map/bands/pallas_call | solution.py:396
  13.6 2.5 %collective-permute-start.2 = (bf16[3,128,128]{2,1,0:T(8,128)(2,1)S(1)}, bf16[3,128,128]{2,1,0:T(8,128)(2,1)S(1)}, u32[]{:S(2)}, u32[]{:S(2)}) collective-permute-start(bf16[3,128,128]{2,1,0:T(8,128)(2,1)S(1)} %get-tuple-element.35), channel_id=1, source_target_pairs={{0,1},{1,2},{2,3},{3,4},{4,5},{5,6},{6,7},{7,8},{8,9},{9,10},{10,1... | collective-permute-start | bytes 294920 | tf_op jit(solution)/shard_map/ppermute | solution.py:349
  16.1 1.9 %collective-permute-start.3 = (bf16[3,128,128]{2,1,0:T(8,128)(2,1)S(1)}, bf16[3,128,128]{2,1,0:T(8,128)(2,1)S(1)}, u32[]{:S(2)}, u32[]{:S(2)}) collective-permute-start(bf16[3,128,128]{2,1,0:T(8,128)(2,1)S(1)} %get-tuple-element.36), channel_id=1, source_target_pairs={{1,0},{2,1},{3,2},{4,3},{5,4},{6,5},{7,6},{8,7},{9,8},{10,9},{11,1... | collective-permute-start | bytes 294920 | tf_op jit(solution)/shard_map/ppermute | solution.py:349
  18.0 4.0 %collective-permute-start.4 = (bf16[3,64,128]{2,1,0:T(8,128)(2,1)S(1)}, bf16[3,64,128]{2,1,0:T(8,128)(2,1)S(1)}, u32[]{:S(2)}, u32[]{:S(2)}) collective-permute-start(bf16[3,64,128]{2,1,0:T(8,128)(2,1)S(1)} %get-tuple-element.37), channel_id=1, source_target_pairs={{0,2},{1,3},{2,4},{3,5},{4,6},{5,7},{6,8},{7,9},{8,10},{9,11},{10,... | collective-permute-start | bytes 147464 | tf_op jit(solution)/shard_map/ppermute | solution.py:349
  22.1 1.3 %collective-permute-start.5 = (bf16[3,64,128]{2,1,0:T(8,128)(2,1)S(1)}, bf16[3,64,128]{2,1,0:T(8,128)(2,1)S(1)}, u32[]{:S(2)}, u32[]{:S(2)}) collective-permute-start(bf16[3,64,128]{2,1,0:T(8,128)(2,1)S(1)} %get-tuple-element.38), channel_id=1, source_target_pairs={{2,0},{3,1},{4,2},{5,3},{6,4},{7,5},{8,6},{9,7},{10,8},{11,9},{12,... | collective-permute-start | bytes 147464 | tf_op jit(solution)/shard_map/ppermute | solution.py:349
  23.4 0.8 %collective-permute-done.4.below2_ref = bf16[3,64,128]{2,1,0:T(8,128)(2,1)S(1)} collective-permute-done((bf16[3,64,128]{2,1,0:T(8,128)(2,1)S(1)}, bf16[3,64,128]{2,1,0:T(8,128)(2,1)S(1)}, u32[]{:S(2)}, u32[]{:S(2)}) %collective-permute-start.4) | collective-permute-done | bytes 49184 | tf_op jit(solution)/shard_map/ppermute | solution.py:349
  24.2 2.7 %collective-permute-done.5.above2_ref = bf16[3,64,128]{2,1,0:T(8,128)(2,1)S(1)} collective-permute-done((bf16[3,64,128]{2,1,0:T(8,128)(2,1)S(1)}, bf16[3,64,128]{2,1,0:T(8,128)(2,1)S(1)}, u32[]{:S(2)}, u32[]{:S(2)}) %collective-permute-start.5) | collective-permute-done | bytes 49184 | tf_op jit(solution)/shard_map/ppermute | solution.py:349
  26.9 0.0 collective-permute-done.2.below1_ref
  26.9 0.0 collective-permute-done.3.above1_ref
  26.9 2.3 %gradient.1 = (bf16[2,192,1024]{2,1,0:T(8,128)(2,1)S(1)}, bf16[2,192,1024]{2,1,0:T(8,128)(2,1)S(1)}, bf16[128,256]{1,0:T(8,128)(2,1)S(1)}, bf16[128,256]{1,0:T(8,128)(2,1)S(1)}) custom-call(s32[2,16]{1,0:T(2,128)S(1)} %bitcast.4, f32[2,192,256]{2,1,0:T(8,128)S(1)} %get-tuple-element.34.own_ref, bf16[3,128,128]{2,1,0:T(8,128)(2,1)S(1)} %collective-permute-done.2.below1_ref, ...), custom_call_target="tpu_custom_call" | custom-call | flops 1000000000 | bytes 10000000 | tf_op jit(solution)/shard_map/gradient/pallas_call | solution.py:414
  29.2 6.9 %collective-permute-start.6 = (bf16[128,256]{1,0:T(8,128)(2,1)S(1)}, bf16[128,256]{1,0:T(8,128)(2,1)S(1)}, u32[]{:S(2)}, u32[]{:S(2)}) collective-permute-start(bf16[128,256]{1,0:T(8,128)(2,1)S(1)} %get-tuple-element.43), channel_id=1, source_target_pairs={{0,1},{1,2},{2,3},{3,4},{4,5},{5,6},{6,7},{7,8},{8,9},{9,10},{10,1... | collective-permute-start | bytes 196616 | tf_op jit(solution)/shard_map/ppermute | solution.py:349
  36.1 1.9 %collective-permute-start.7 = (bf16[128,256]{1,0:T(8,128)(2,1)S(1)}, bf16[128,256]{1,0:T(8,128)(2,1)S(1)}, u32[]{:S(2)}, u32[]{:S(2)}) collective-permute-start(bf16[128,256]{1,0:T(8,128)(2,1)S(1)} %get-tuple-element.44), channel_id=1, source_target_pairs={{1,0},{2,1},{3,2},{4,3},{5,4},{6,5},{7,6},{8,7},{9,8},{10,9},{11,1... | collective-permute-start | bytes 196616 | tf_op jit(solution)/shard_map/ppermute | solution.py:349
  38.0 1.2 %smooth.1 = (bf16[192,4096]{1,0:T(8,128)(2,1)S(1)}, f32[2,192,1024]{2,1,0:T(8,128)S(1)}) custom-call(bf16[2,192,1024]{2,1,0:T(8,128)(2,1)S(1)} %get-tuple-element.45.edge_ref, bf16[2,192,1024]{2,1,0:T(8,128)(2,1)S(1)} %get-tuple-element.46.grad_ref, bf16[2,192,1024]{2,1,0:T(8,128)(2,1)S(1)} %get-tuple-element.31.mask_ref.edge_mask_ref, ...), custom_call_target="tpu_custom_call" | custom-call | flops 2000000000 | bytes 10000000 | tf_op jit(solution)/shard_map/smooth/pallas_call | solution.py:430
  39.1 0.0 collective-permute-done.6.below_ref
  39.2 2.5 %collective-permute-done.7.above_ref = bf16[128,256]{1,0:T(8,128)(2,1)S(1)} collective-permute-done((bf16[128,256]{1,0:T(8,128)(2,1)S(1)}, bf16[128,256]{1,0:T(8,128)(2,1)S(1)}, u32[]{:S(2)}, u32[]{:S(2)}) %collective-permute-start.7) | collective-permute-done | bytes 65568 | tf_op jit(solution)/shard_map/ppermute | solution.py:349
  41.6 1.6 %finish.1 = bf16[192,4096]{1,0:T(8,128)(2,1)} custom-call(bf16[128,256]{1,0:T(8,128)(2,1)S(1)} %collective-permute-done.6.below_ref, bf16[128,256]{1,0:T(8,128)(2,1)S(1)} %collective-permute-done.7.above_ref, f32[2,192,1024]{2,1,0:T(8,128)S(1)} %get-tuple-element.47.part_ref, bf16[2,192,1024]{2,1,0:T(8,128)(2,1)S(1)} %get-tuple-element.31.mask_ref.edge_mask_ref, ...), custom_call_target="tpu_custom_call" | custom-call | flops 10000000 | bytes 10000000 | tf_op jit(solution)/shard_map/finish/pallas_call | solution.py:440
  (6 shorter events, 0.0 us)
Async XLA Ops:
  0.0 1.4 %copy-start = (bf16[192,4096]{1,0:T(8,128)(2,1)S(1)}, bf16[192,4096]{1,0:T(8,128)(2,1)}, u32[]{:S(2)}) copy-start(bf16[192,4096]{1,0:T(8,128)(2,1)} %mid2_ref.1) | copy-start | bytes 4718596
  1.4 0.7 %copy-start.1 = (s32[1024,4]{0,1:T(4,128)S(1)}, s32[1024,4]{0,1:T(4,128)}, u32[]{:S(2)}) copy-start(s32[1024,4]{0,1:T(4,128)} %param.6) | copy-start | bytes 49156
  2.1 7.1 %copy-start.3 = (f32[4,1024]{1,0:T(4,128)S(1)}, f32[4,1024]{1,0:T(4,128)}, u32[]{:S(2)}) copy-start(f32[4,1024]{1,0:T(4,128)} %pot_ref.1) | copy-start | bytes 49156
  2.8 8.9 %collective-permute-start = (bf16[128,256]{1,0:T(8,128)(2,1)S(1)}, bf16[128,256]{1,0:T(8,128)(2,1)S(1)}, u32[]{:S(2)}, u32[]{:S(2)}) collective-permute-start(bf16[128,256]{1,0:T(8,128)(2,1)S(1)} %get-tuple-element.27), channel_id=1, source_target_pairs={{0,1},{1,2},{2,3},{3,4},{4,5},{5,6},{6,7},{7,8},{8,9},{9,10},{10,1... | collective-permute-start | bytes 196616 | tf_op jit(solution)/shard_map/ppermute | solution.py:349
  7.3 5.6 %collective-permute-start.1 = (bf16[128,256]{1,0:T(8,128)(2,1)S(1)}, bf16[128,256]{1,0:T(8,128)(2,1)S(1)}, u32[]{:S(2)}, u32[]{:S(2)}) collective-permute-start(bf16[128,256]{1,0:T(8,128)(2,1)S(1)} %get-tuple-element.28), channel_id=1, source_target_pairs={{1,0},{2,1},{3,2},{4,3},{5,4},{6,5},{7,6},{8,7},{9,8},{10,9},{11,1... | collective-permute-start | bytes 196616 | tf_op jit(solution)/shard_map/ppermute | solution.py:349
  12.9 14.0 %copy-start.2 = (s32[16,2]{0,1:T(2,128)S(1)}, s32[16,2]{0,1:T(2,128)}, u32[]{:S(2)}) copy-start(s32[16,2]{0,1:T(2,128)} %param.7) | copy-start | bytes 388
  13.6 13.3 %collective-permute-start.2 = (bf16[3,128,128]{2,1,0:T(8,128)(2,1)S(1)}, bf16[3,128,128]{2,1,0:T(8,128)(2,1)S(1)}, u32[]{:S(2)}, u32[]{:S(2)}) collective-permute-start(bf16[3,128,128]{2,1,0:T(8,128)(2,1)S(1)} %get-tuple-element.35), channel_id=1, source_target_pairs={{0,1},{1,2},{2,3},{3,4},{4,5},{5,6},{6,7},{7,8},{8,9},{9,10},{10,1... | collective-permute-start | bytes 294920 | tf_op jit(solution)/shard_map/ppermute | solution.py:349
  16.1 10.8 %collective-permute-start.3 = (bf16[3,128,128]{2,1,0:T(8,128)(2,1)S(1)}, bf16[3,128,128]{2,1,0:T(8,128)(2,1)S(1)}, u32[]{:S(2)}, u32[]{:S(2)}) collective-permute-start(bf16[3,128,128]{2,1,0:T(8,128)(2,1)S(1)} %get-tuple-element.36), channel_id=1, source_target_pairs={{1,0},{2,1},{3,2},{4,3},{5,4},{6,5},{7,6},{8,7},{9,8},{10,9},{11,1... | collective-permute-start | bytes 294920 | tf_op jit(solution)/shard_map/ppermute | solution.py:349
  18.0 6.1 %collective-permute-start.4 = (bf16[3,64,128]{2,1,0:T(8,128)(2,1)S(1)}, bf16[3,64,128]{2,1,0:T(8,128)(2,1)S(1)}, u32[]{:S(2)}, u32[]{:S(2)}) collective-permute-start(bf16[3,64,128]{2,1,0:T(8,128)(2,1)S(1)} %get-tuple-element.37), channel_id=1, source_target_pairs={{0,2},{1,3},{2,4},{3,5},{4,6},{5,7},{6,8},{7,9},{8,10},{9,11},{10,... | collective-permute-start | bytes 147464 | tf_op jit(solution)/shard_map/ppermute | solution.py:349
  22.1 4.8 %collective-permute-start.5 = (bf16[3,64,128]{2,1,0:T(8,128)(2,1)S(1)}, bf16[3,64,128]{2,1,0:T(8,128)(2,1)S(1)}, u32[]{:S(2)}, u32[]{:S(2)}) collective-permute-start(bf16[3,64,128]{2,1,0:T(8,128)(2,1)S(1)} %get-tuple-element.38), channel_id=1, source_target_pairs={{2,0},{3,1},{4,2},{5,3},{6,4},{7,5},{8,6},{9,7},{10,8},{11,9},{12,... | collective-permute-start | bytes 147464 | tf_op jit(solution)/shard_map/ppermute | solution.py:349
  29.2 10.0 %collective-permute-start.6 = (bf16[128,256]{1,0:T(8,128)(2,1)S(1)}, bf16[128,256]{1,0:T(8,128)(2,1)S(1)}, u32[]{:S(2)}, u32[]{:S(2)}) collective-permute-start(bf16[128,256]{1,0:T(8,128)(2,1)S(1)} %get-tuple-element.43), channel_id=1, source_target_pairs={{0,1},{1,2},{2,3},{3,4},{4,5},{5,6},{6,7},{7,8},{8,9},{9,10},{10,1... | collective-permute-start | bytes 196616 | tf_op jit(solution)/shard_map/ppermute | solution.py:349
  36.1 5.6 %collective-permute-start.7 = (bf16[128,256]{1,0:T(8,128)(2,1)S(1)}, bf16[128,256]{1,0:T(8,128)(2,1)S(1)}, u32[]{:S(2)}, u32[]{:S(2)}) collective-permute-start(bf16[128,256]{1,0:T(8,128)(2,1)S(1)} %get-tuple-element.44), channel_id=1, source_target_pairs={{1,0},{2,1},{3,2},{4,3},{5,4},{6,5},{7,6},{8,7},{9,8},{10,9},{11,1... | collective-permute-start | bytes 196616 | tf_op jit(solution)/shard_map/ppermute | solution.py:349

commit v2 on v1

--- a/solution.py
+++ b/solution.py
@@ -116,23 +116,34 @@
     return tiles
 
 
-def put_fold(ref, values):
-    a, b = fold(values)
-    ref[:, 0:128] = a.astype(BF16)
-    ref[:, 128:256] = b.astype(BF16)
-
-
-def edges_kernel(ct_ref, first_ref, last_ref, phi_ref, mask_ref, up_ref, down_ref):
+def is_even():
+    return lax.rem(lax.axis_index("sx"), 2) == 0
+
+
+def put_messages(planes, mate_ref, across_ref):
+    down = fold(planes[0, : 2 * ORB].astype(F32))
+    up = fold(planes[1, ORB:].astype(F32))
+    even = is_even()
+    for i in range(2):
+        lanes = slice(128 * i, 128 * i + 128)
+        mate_ref[:, lanes] = jnp.where(even, up[i], down[i]).astype(BF16)
+        across_ref[:, lanes] = jnp.where(even, down[i], up[i]).astype(BF16)
+
+
+def sides(mate_ref, across_ref):
+    mate = mate_ref[...].astype(F32)
+    across = across_ref[...].astype(F32)
+    even = is_even()
+    return (jnp.where(even, across, mate), jnp.where(even, mate, across))
+
+
+def edges_kernel(ct_ref, first_ref, last_ref, phi_ref, mask_ref, mate_ref, across_ref):
     rows = row_features(ct_ref)
     for i, (plane, ref) in enumerate(((0, first_ref), (CX - 1, last_ref))):
         mask = sphere(rows, plane)
-        value = ref[...] * mask
         mask_ref[i] = mask
-        phi_ref[i] = value
-        if i == 0:
-            put_fold(down_ref, value[: 2 * ORB].astype(F32))
-        else:
-            put_fold(up_ref, value[ORB:].astype(F32))
+        phi_ref[i] = ref[...] * mask
+    put_messages(phi_ref, mate_ref, across_ref)
 
 
 def rows_product(a, b):
@@ -174,13 +185,13 @@
 
 
 def bands_kernel(
-    below_ref, above_ref, part_ref, mask_ref, phi_ref, corr_ref, ham_ref,
-    energy_ref, own_ref, up1_ref, down1_ref, up2_ref, down2_ref,
+    mate_ref, across_ref, part_ref, mask_ref, phi_ref, corr_ref, ham_ref,
+    energy_ref, own_ref, rows_ref,
 ):
     volume = 1.0 / (4.0 * CX**3)
     ham = ham_ref[...]
-    for i, ref in enumerate((below_ref, above_ref)):
-        tiles = unfold(ref[...].astype(F32))
+    for i, side in enumerate(sides(mate_ref, across_ref)):
+        tiles = unfold(side)
         rest = slice(2 * ORB, ROWS) if i == 0 else slice(0, ORB)
         for t in range(PLANE // 128):
             lanes = slice(128 * t, 128 * t + 128)
@@ -191,78 +202,76 @@
     own_ref[:, :, ROWS:] = jnp.zeros((2, ROWS, TILE - ROWS), F32)
     own_ref[0, :, :ROWS] = ham * volume
     own_ref[1, :, :ROWS] = corr_ref[...] * volume
-    low = iota((1, 128), 1) < 64
-    h0 = own_ref[0, :, 0:128]
-    h1 = own_ref[0, :, 128:256]
-    c0 = own_ref[1, :, 0:128]
-    c1 = own_ref[1, :, 128:256]
-    h0r = pltpu.roll(h0, 64, 1)
-    h1r = pltpu.roll(h1, 64, 1)
-    c1r = pltpu.roll(c1, 64, 1)
-    near = (
-        jnp.where(low, h0r, h1r),
-        jnp.where(low, pltpu.roll(c0, 64, 1), c1r),
-        jnp.where(low, c0, h0r),
-    )
-    far = (h0, c0, jnp.where(low, h1, c1r))
-    for i in range(3):
-        value = near[i].astype(BF16)
-        up1_ref[i] = value[ORB:]
-        down1_ref[i] = value[: 2 * ORB]
-        value = far[i].astype(BF16)
-        up2_ref[i] = value[2 * ORB :]
-        down2_ref[i] = value[:ORB]
+    tail = jnp.where(low_half(), own_ref[0, :, 128:256], swapped(own_ref[1, :, 128:256]))
+    even = is_even()
+    for i, value in enumerate((own_ref[0, :, 0:128], own_ref[1, :, 0:128], tail)):
+        rows_ref[i] = jnp.where(even, value[ORB:], value[: 2 * ORB]).astype(BF16)
+
+
+def low_half():
+    return iota((1, 128), 1) < 64
+
+
+def swapped(value):
+    return pltpu.roll(value, 64, 1)
+
+
+def mate_blocks(rows_ref, which):
+    tail = rows_ref[2].astype(F32)
+    if which == 1:
+        tail = swapped(tail)
+    return rows_ref[which].astype(F32), jnp.where(low_half(), tail, 0.0)
+
+
+def shifted(c01, c2x):
+    low = low_half()
+    turned = swapped(c01)
+    return jnp.where(low, 0.0, turned), jnp.where(low, turned, swapped(c2x))
+
+
+def relay_kernel(own_ref, rows_ref, out_ref):
+    even = is_even()
+    for which in range(2):
+        head, rest = shifted(own_ref[which, :, 0:128], own_ref[which, :, 128:256])
+        c01, c2x = mate_blocks(rows_ref, which)
+        c01 = jnp.where(even, c01[:ORB], c01[ORB:])
+        c2x = jnp.where(even, c2x[:ORB], c2x[ORB:])
+        own = slice(ORB, 2 * ORB)
+        out_ref[which, :ORB, 0:128] = (head[own] + jnp.where(even, c2x, c01)).astype(BF16)
+        out_ref[which, :ORB, 128:256] = (rest[own] + jnp.where(even, c01, c2x)).astype(BF16)
+        out_ref[which, ORB:, 0:128] = jnp.where(even, head[:ORB], head[2 * ORB :]).astype(BF16)
+        out_ref[which, ORB:, 128:256] = jnp.where(even, rest[:ORB], rest[2 * ORB :]).astype(BF16)
 
 
 def gradient_kernel(
-    pattern_ref, own_ref, below1_ref, above1_ref, below2_ref, above2_ref,
+    pattern_ref, own_ref, rows_ref, across_in_ref, relayed_ref,
     edge_ref, phi_ref, edge_energy_ref, energy_ref, edge_mask_ref, mask_ref,
-    edge_grad_ref, grad_ref, up_ref, down_ref,
+    edge_grad_ref, grad_ref, mate_ref, across_ref,
     ham_ref, inv_ref,
 ):
     slab = lax.axis_index("sx")
+    even = is_even()
     last = pattern_ref.shape[1] - 1
-    low = iota((1, 128), 1) < 64
+    low = low_half()
+    zero = jnp.zeros((ORB, 128), F32)
     for which, band_ref in enumerate((ham_ref, inv_ref)):
-
-        def near(ref):
-            head = ref[2].astype(F32)
-            if which == 1:
-                head = pltpu.roll(head, 64, 1)
-            return (jnp.where(low, 0.0, head), ref[which].astype(F32))
-
-        def far(ref):
-            tail = ref[2].astype(F32)
-            if which == 1:
-                tail = pltpu.roll(tail, 64, 1)
-            return (ref[which].astype(F32), jnp.where(low, tail, 0.0))
-
-        own = (own_ref[which, :, 0:128], own_ref[which, :, 128:256])
-        below1 = near(below1_ref)
-        above1 = near(above1_ref)
-        below2 = far(below2_ref)
-        above2 = far(above2_ref)
-        zero = jnp.zeros((ORB, 128), F32)
-        s0, s1, s2 = (slice(ORB * i, ORB * i + ORB) for i in range(3))
-        tiles = (
-            (
-                below1[0][s0] + below2[0],
-                own[0][s0] + below1[1][s0] + below2[1],
-                own[1][s0],
-                zero,
-            ),
-            (
-                below1[0][s1],
-                own[0][s1] + below1[1][s1] + above1[0][s0],
-                own[1][s1] + above1[1][s0],
-                zero,
-            ),
-            (
-                zero,
-                own[0][s2] + above1[0][s1],
-                own[1][s2] + above1[1][s1] + above2[0],
-                above2[1],
-            ),
+        near, rest = shifted(*mate_blocks(rows_ref, which))
+        ahead = across_in_ref[which, :, 0:128].astype(F32)
+        beside = across_in_ref[which, :, 128:256].astype(F32)
+        turned = swapped(relayed_ref[which, ORB:, 128:256].astype(F32))
+        far0 = jnp.where(low, swapped(relayed_ref[which, ORB:, 0:128].astype(F32)), turned)
+        far1 = jnp.where(low, turned, 0.0)
+        got_even = (
+            (ahead[:ORB], beside[:ORB], zero, zero),
+            (ahead[ORB:], beside[ORB:] + near[:ORB], rest[:ORB], zero),
+            (zero, near[ORB:], rest[ORB:] + far0, far1),
+        )
+        ahead_high = jnp.where(low, 0.0, ahead)
+        ahead_low = jnp.where(low, ahead, 0.0)
+        got_odd = (
+            (near[:ORB] + far0, rest[:ORB] + far1, zero, zero),
+            (near[ORB:], rest[ORB:] + ahead_high[ORB:], beside[ORB:], zero),
+            (zero, ahead_high[:ORB], beside[:ORB], ahead_low[:ORB]),
         )
         for r in range(3):
             for q in range(4):
@@ -276,7 +285,10 @@
                     else:
                         at = jnp.clip(slab - 3 + min(col, r + 2), 0, last)
                         kept.append(pattern_ref[apart - 1, at].astype(F32))
-                value = tiles[r][q] * jnp.where(low, kept[0], kept[1])
+                value = jnp.where(even, got_even[r][q], got_odd[r][q])
+                if q in (1, 2):
+                    value = value + own_ref[which, ORB * r : ORB * r + ORB, 128 * q - 128 : 128 * q]
+                value = value * jnp.where(low, kept[0], kept[1])
                 if which == 1:
                     on = iota((ORB, 128), 0) + (ORB * (r + 2) - 128 * q) == iota((ORB, 128), 1)
                     value = jnp.where(on, 2.0, 0.0) - value
@@ -295,8 +307,7 @@
                 fix = jnp.dot(theta, orb_ref[i, :, lanes], preferred_element_type=F32)
                 value = en_ref[i, :, lanes].astype(F32) - fix
                 out_ref[i, :, lanes] = value.astype(BF16) * m_ref[i, :, lanes]
-    put_fold(down_ref, edge_grad_ref[0, : 2 * ORB].astype(F32))
-    put_fold(up_ref, edge_grad_ref[1, ORB:].astype(F32))
+    put_messages(edge_grad_ref, mate_ref, across_ref)
 
 
 def smooth_kernel(edge_ref, grad_ref, edge_mask_ref, mask_ref, out_ref, part_ref):
@@ -314,9 +325,9 @@
             part_ref[i, :, lanes] = outer[i] + mid[i]
 
 
-def finish_kernel(below_ref, above_ref, part_ref, mask_ref, inner_ref, out_ref):
-    for i, ref in enumerate((below_ref, above_ref)):
-        tiles = unfold(ref[...].astype(F32))
+def finish_kernel(mate_ref, across_ref, part_ref, mask_ref, inner_ref, out_ref):
+    for i, side in enumerate(sides(mate_ref, across_ref)):
+        tiles = unfold(side)
         rest = slice(2 * ORB, ROWS) if i == 0 else slice(0, ORB)
         for t in range(PLANE // 128):
             lanes = slice(128 * t, 128 * t + 128)
@@ -343,10 +354,14 @@
 
 def per_device(pieces, potential, centers, pattern):
     count = lax.axis_size("sx")
-
-    def moved(value, steps):
-        first, end = max(0, -steps), min(count, count - steps)
-        return lax.ppermute(value, "sx", [(i, i + steps) for i in range(first, end)])
+    mates = [(i, i ^ 1) for i in range(count)]
+    others = [(i, i + 1 if i % 2 else i - 1) for i in range(1, count - 1)]
+
+    def to_mate(value):
+        return lax.ppermute(value, "sx", mates)
+
+    def across(value):
+        return lax.ppermute(value, "sx", others)
 
     table = centers.T
     pair = shape(2, ROWS, PLANE)
@@ -357,7 +372,7 @@
     def whole_spec(*dims):
         return pl.BlockSpec(dims, lambda i: (0,) * len(dims))
 
-    edge, edge_mask, up, down = pl.pallas_call(
+    edge, edge_mask, for_mate, for_other = pl.pallas_call(
         edges_kernel,
         grid=(1,),
         out_shape=(pair, pair, shape(2 * ORB, HALF), shape(2 * ORB, HALF)),
@@ -370,8 +385,8 @@
         cost_estimate=cost(10**8, 10**6),
         name="edges",
     )(table, pieces, pieces)
-    below = moved(up, 1)
-    above = moved(down, -1)
+    other_side = across(for_other)
+    mate_side = to_mate(for_mate)
 
     mid, mid_mask, mid_energy, part, corr, ham = pl.pallas_call(
         energy_kernel,
@@ -393,39 +408,43 @@
         name="energy",
     )(table, pieces, pieces, potential, edge)
 
-    edge_energy, own, up1, down1, up2, down2 = pl.pallas_call(
+    edge_energy, own, for_mate = pl.pallas_call(
         bands_kernel,
-        out_shape=(
-            pair, shape(2, ROWS, TILE, dtype=F32),
-            shape(3, 2 * ORB, 128), shape(3, 2 * ORB, 128),
-            shape(3, ORB, 128), shape(3, ORB, 128),
-        ),
+        out_shape=(pair, shape(2, ROWS, TILE, dtype=F32), shape(3, 2 * ORB, 128)),
         in_specs=[WHOLE] * 7,
-        out_specs=(WHOLE,) * 6,
+        out_specs=(WHOLE,) * 3,
         compiler_params=PARAMS,
         cost_estimate=cost(10**9, 10**7),
         name="bands",
-    )(below, above, part, edge_mask, edge, corr, ham)
-    below1 = moved(up1, 1)
-    above1 = moved(down1, -1)
-    below2 = moved(up2, 2)
-    above2 = moved(down2, -2)
-
-    edge_grad, mid_grad, up, down = pl.pallas_call(
+    )(mate_side, other_side, part, edge_mask, edge, corr, ham)
+    mate_rows = to_mate(for_mate)
+    for_other = pl.pallas_call(
+        relay_kernel,
+        out_shape=shape(2, 2 * ORB, TILE),
+        in_specs=[WHOLE] * 2,
+        out_specs=WHOLE,
+        compiler_params=PARAMS,
+        cost_estimate=cost(10**6, 10**6),
+        name="relay",
+    )(own, mate_rows)
+    other_rows = across(for_other)
+    relayed = to_mate(other_rows)
+
+    edge_grad, mid_grad, for_mate, for_other = pl.pallas_call(
         gradient_kernel,
         out_shape=(pair, pair, shape(2 * ORB, HALF), shape(2 * ORB, HALF)),
-        in_specs=[pl.BlockSpec(memory_space=pltpu.SMEM)] + [WHOLE] * 11,
+        in_specs=[pl.BlockSpec(memory_space=pltpu.SMEM)] + [WHOLE] * 10,
         out_specs=(WHOLE,) * 4,
         scratch_shapes=[pltpu.VMEM((ROWS, 512), F32), pltpu.VMEM((ROWS, 512), F32)],
         compiler_params=PARAMS,
         cost_estimate=cost(10**9, 10**7),
         name="gradient",
     )(
-        pattern.T, own, below1, above1, below2, above2,
+        pattern.T, own, mate_rows, other_rows, relayed,
         edge, mid, edge_energy, mid_energy, edge_mask, mid_mask,
     )
-    below = moved(up, 1)
-    above = moved(down, -1)
+    other_side = across(for_other)
+    mate_side = to_mate(for_mate)
 
     inner, part = pl.pallas_call(
         smooth_kernel,
@@ -445,7 +464,7 @@
         compiler_params=PARAMS,
         cost_estimate=cost(10**7, 10**7),
         name="finish",
-    )(below, above, part, edge_mask, inner)
+    )(mate_side, other_side, part, edge_mask, inner)
 
 
 def solution(mesh):

time: 43.6 us -> 31.8 us (0.73)
  the two profiles are of different devices: /device:TPU:1 before, /device:TPU:9 now
where the time goes in v2:
time: 31.8 us; the launch traced here: 31.6 us
  starting transfers between devices  10.8 us (34%)
  waiting for transfers between devices  9.59 us (30%)
  Pallas kernels  8.89 us (28%)
  local copies, waits for them, and re-layouts  2.13 us (7%)
    ppermute x3, starting transfers between devices, across(): return lax.ppermute(value, 'sx', others)  9.5 us
    ppermute x3, waiting for transfers between devices, across(): return lax.ppermute(value, 'sx', others)  7.27 us
    pallas_call x1, Pallas kernels, per_device(): pl.pallas_call(energy_kernel, grid=(1,), out_shape=(pair, pair, pair, sha...  2.44 us
    pallas_call x1, Pallas kernels, per_device(): pl.pallas_call(gradient_kernel, out_shape=(pair, pair, shape(2 * ORB, HAL...  2.37 us
    ppermute x4, waiting for transfers between devices, to_mate(): return lax.ppermute(value, 'sx', mates)  2.32 us
    unnamed x8, local copies, waits for them, and re-layouts  2.13 us
    pallas_call x1, Pallas kernels, per_device(): pl.pallas_call(finish_kernel, out_shape=shape(ROWS, CX * PLANE), in_specs...  1.57 us
    ppermute x4, starting transfers between devices, to_mate(): return lax.ppermute(value, 'sx', mates)  1.35 us
  transfers between devices with their start and end apart: 7, of which 5 were waited for; matrix products, arithmetic and copies ran while one was open for 0% of the time, Pallas kernels for 11%

profile of v2, /device:TPU:9, one launch (start us, length us, event | category | flops | bytes accessed | tf_op | source)
XLA Modules:
  0.0 31.6 jit_solution(10100087585645749899)
XLA Ops:
  0.0 1.4 %copy-done = bf16[192,4096]{1,0:T(8,128)(2,1)S(1)} copy-done((bf16[192,4096]{1,0:T(8,128)(2,1)S(1)}, bf16[192,4096]{1,0:T(8,128)(2,1)}, u32[]{:S(2)}) %copy-start) | copy-done | bytes 1572888
  1.4 0.7 %copy-done.1 = s32[1024,4]{0,1:T(4,128)S(1)} copy-done((s32[1024,4]{0,1:T(4,128)S(1)}, s32[1024,4]{0,1:T(4,128)}, u32[]{:S(2)}) %copy-start.1) | copy-done | bytes 16408
  2.1 0.6 %edges.1 = (bf16[2,192,1024]{2,1,0:T(8,128)(2,1)S(1)}, bf16[2,192,1024]{2,1,0:T(8,128)(2,1)S(1)}, bf16[128,256]{1,0:T(8,128)(2,1)S(1)}, bf16[128,256]{1,0:T(8,128)(2,1)S(1)}) custom-call(s32[4,1024]{1,0:T(4,128)S(1)} %bitcast.2, bf16[192,4096]{1,0:T(8,128)(2,1)S(1)} %copy-done, bf16[192,4096]{1,0:T(8,128)(2,1)S(1)} %copy-done), custom_call_target="tpu_custom_call" | custom-call | flops 100000000 | bytes 1000000 | tf_op jit(solution)/shard_map/edges/pallas_call | solution.py:375
  2.8 0.7 %collective-permute-start = (bf16[128,256]{1,0:T(8,128)(2,1)S(1)}, bf16[128,256]{1,0:T(8,128)(2,1)S(1)}, u32[]{:S(2)}, u32[]{:S(2)}) collective-permute-start(bf16[128,256]{1,0:T(8,128)(2,1)S(1)} %get-tuple-element.24), channel_id=1, source_target_pairs={{0,1},{1,0},{2,3},{3,2},{4,5},{5,4},{6,7},{7,6},{8,9},{9,8},{10,11... | collective-permute-start | bytes 196616 | tf_op jit(solution)/shard_map/ppermute | solution.py:361
  3.5 3.0 %collective-permute-start.1 = (bf16[128,256]{1,0:T(8,128)(2,1)S(1)}, bf16[128,256]{1,0:T(8,128)(2,1)S(1)}, u32[]{:S(2)}, u32[]{:S(2)}) collective-permute-start(bf16[128,256]{1,0:T(8,128)(2,1)S(1)} %get-tuple-element.25), channel_id=1, source_target_pairs={{1,2},{2,1},{3,4},{4,3},{5,6},{6,5},{7,8},{8,7},{9,10},{10,9},{11,... | collective-permute-start | bytes 196616 | tf_op jit(solution)/shard_map/ppermute | solution.py:364
  6.6 0.0 copy-done.3
  6.6 2.4 %energy.1 = (bf16[2,192,1024]{2,1,0:T(8,128)(2,1)S(1)}, bf16[2,192,1024]{2,1,0:T(8,128)(2,1)S(1)}, bf16[2,192,1024]{2,1,0:T(8,128)(2,1)S(1)}, f32[2,192,1024]{2,...) custom-call(s32[4,1024]{1,0:T(4,128)S(1)} %bitcast.3, bf16[192,4096]{1,0:T(8,128)(2,1)S(1)} %copy-done, ...), custom_call_target="tpu_custom_call" | custom-call | flops 4000000000 | bytes 10000000 | tf_op jit(solution)/shard_map/energy/pallas_call | solution.py:391
  9.0 0.0 collective-permute-done.mate_ref
  9.0 0.8 %collective-permute-done.1.across_ref = bf16[128,256]{1,0:T(8,128)(2,1)S(1)} collective-permute-done((bf16[128,256]{1,0:T(8,128)(2,1)S(1)}, bf16[128,256]{1,0:T(8,128)(2,1)S(1)}, u32[]{:S(2)}, u32[]{:S(2)}) %collective-permute-start.1) | collective-permute-done | bytes 65568 | tf_op jit(solution)/shard_map/ppermute | solution.py:364
  9.8 0.6 %bands.1 = (bf16[2,192,1024]{2,1,0:T(8,128)(2,1)S(1)}, f32[2,192,256]{2,1,0:T(8,128)S(1)}, bf16[3,128,128]{2,1,0:T(8,128)(2,1)S(1)}) custom-call(bf16[128,256]{1,0:T(8,128)(2,1)S(1)} %collective-permute-done.mate_ref, bf16[128,256]{1,0:T(8,128)(2,1)S(1)} %collective-permute-done.1.across_ref, f32[2,192,1024]{2,1,0:T(8,128)S(1)} %get-tuple-element.27.part_ref, ...), custom_call_target="tpu_custom_call" | custom-call | flops 1000000000 | bytes 10000000 | tf_op jit(solution)/shard_map/bands/pallas_call | solution.py:411
  10.4 0.4 %collective-permute-start.2 = (bf16[3,128,128]{2,1,0:T(8,128)(2,1)S(1)}, bf16[3,128,128]{2,1,0:T(8,128)(2,1)S(1)}, u32[]{:S(2)}, u32[]{:S(2)}) collective-permute-start(bf16[3,128,128]{2,1,0:T(8,128)(2,1)S(1)} %get-tuple-element.32), channel_id=1, source_target_pairs={{0,1},{1,0},{2,3},{3,2},{4,5},{5,4},{6,7},{7,6},{8,9},{9,8},{10,11... | collective-permute-start | bytes 294920 | tf_op jit(solution)/shard_map/ppermute | solution.py:361
  10.8 1.0 %collective-permute-done.2.rows_ref = bf16[3,128,128]{2,1,0:T(8,128)(2,1)S(1)} collective-permute-done((bf16[3,128,128]{2,1,0:T(8,128)(2,1)S(1)}, bf16[3,128,128]{2,1,0:T(8,128)(2,1)S(1)}, u32[]{:S(2)}, u32[]{:S(2)}) %collective-permute-start.2) | collective-permute-done | bytes 98336 | tf_op jit(solution)/shard_map/ppermute | solution.py:361
  11.8 0.1 relay.1
  11.9 3.4 %collective-permute-start.3 = (bf16[2,128,256]{2,1,0:T(8,128)(2,1)S(1)}, bf16[2,128,256]{2,1,0:T(8,128)(2,1)S(1)}, u32[]{:S(2)}, u32[]{:S(2)}) collective-permute-start(bf16[2,128,256]{2,1,0:T(8,128)(2,1)S(1)} %relay.1), channel_id=1, source_target_pairs={{1,2},{2,1},{3,4},{4,3},{5,6},{6,5},{7,8},{8,7},{9,10},{10,9},{11,... | collective-permute-start | bytes 393224 | tf_op jit(solution)/shard_map/ppermute | solution.py:364
  15.3 4.3 %collective-permute-done.3.across_in_ref = bf16[2,128,256]{2,1,0:T(8,128)(2,1)S(1)} collective-permute-done((bf16[2,128,256]{2,1,0:T(8,128)(2,1)S(1)}, bf16[2,128,256]{2,1,0:T(8,128)(2,1)S(1)}, u32[]{:S(2)}, u32[]{:S(2)}) %collective-permute-start.3) | collective-permute-done | bytes 131104 | tf_op jit(solution)/shard_map/ppermute | solution.py:364
  19.6 0.0 collective-permute-start.4
  19.6 1.3 %collective-permute-done.4.relayed_ref = bf16[2,128,256]{2,1,0:T(8,128)(2,1)S(1)} collective-permute-done((bf16[2,128,256]{2,1,0:T(8,128)(2,1)S(1)}, bf16[2,128,256]{2,1,0:T(8,128)(2,1)S(1)}, u32[]{:S(2)}, u32[]{:S(2)}) %collective-permute-start.4) | collective-permute-done | bytes 131104 | tf_op jit(solution)/shard_map/ppermute | solution.py:361
  21.0 2.4 %gradient.1 = (bf16[2,192,1024]{2,1,0:T(8,128)(2,1)S(1)}, bf16[2,192,1024]{2,1,0:T(8,128)(2,1)S(1)}, bf16[128,256]{1,0:T(8,128)(2,1)S(1)}, bf16[128,256]{1,0:T(8,128)(2,1)S(1)}) custom-call(s32[2,16]{1,0:T(2,128)S(1)} %bitcast.4, f32[2,192,256]{2,1,0:T(8,128)S(1)} %get-tuple-element.31.own_ref, bf16[3,128,128]{2,1,0:T(8,128)(2,1)S(1)} %collective-permute-done.2.rows_ref, ...), custom_call_target="tpu_custom_call" | custom-call | flops 1000000000 | bytes 10000000 | tf_op jit(solution)/shard_map/gradient/pallas_call | solution.py:433
  23.3 0.2 collective-permute-start.5
  23.6 3.1 %collective-permute-start.6 = (bf16[128,256]{1,0:T(8,128)(2,1)S(1)}, bf16[128,256]{1,0:T(8,128)(2,1)S(1)}, u32[]{:S(2)}, u32[]{:S(2)}) collective-permute-start(bf16[128,256]{1,0:T(8,128)(2,1)S(1)} %get-tuple-element.38), channel_id=1, source_target_pairs={{1,2},{2,1},{3,4},{4,3},{5,6},{6,5},{7,8},{8,7},{9,10},{10,9},{11,... | collective-permute-start | bytes 196616 | tf_op jit(solution)/shard_map/ppermute | solution.py:364
  26.6 1.1 %smooth.1 = (bf16[192,4096]{1,0:T(8,128)(2,1)S(1)}, f32[2,192,1024]{2,1,0:T(8,128)S(1)}) custom-call(bf16[2,192,1024]{2,1,0:T(8,128)(2,1)S(1)} %get-tuple-element.39.edge_ref, bf16[2,192,1024]{2,1,0:T(8,128)(2,1)S(1)} %get-tuple-element.40.grad_ref, bf16[2,192,1024]{2,1,0:T(8,128)(2,1)S(1)} %get-tuple-element.28.mask_ref.edge_mask_ref, ...), custom_call_target="tpu_custom_call" | custom-call | flops 2000000000 | bytes 10000000 | tf_op jit(solution)/shard_map/smooth/pallas_call | solution.py:449
  27.8 0.0 collective-permute-done.5.mate_ref
  27.8 2.2 %collective-permute-done.6.across_ref = bf16[128,256]{1,0:T(8,128)(2,1)S(1)} collective-permute-done((bf16[128,256]{1,0:T(8,128)(2,1)S(1)}, bf16[128,256]{1,0:T(8,128)(2,1)S(1)}, u32[]{:S(2)}, u32[]{:S(2)}) %collective-permute-start.6) | collective-permute-done | bytes 65568 | tf_op jit(solution)/shard_map/ppermute | solution.py:364
  30.0 1.6 %finish.1 = bf16[192,4096]{1,0:T(8,128)(2,1)} custom-call(bf16[128,256]{1,0:T(8,128)(2,1)S(1)} %collective-permute-done.5.mate_ref, bf16[128,256]{1,0:T(8,128)(2,1)S(1)} %collective-permute-done.6.across_ref, f32[2,192,1024]{2,1,0:T(8,128)S(1)} %get-tuple-element.41.part_ref, bf16[2,192,1024]{2,1,0:T(8,128)(2,1)S(1)} %get-tuple-element.28.mask_ref.edge_mask_ref, ...), custom_call_target="tpu_custom_call" | custom-call | flops 10000000 | bytes 10000000 | tf_op jit(solution)/shard_map/finish/pallas_call | solution.py:459
  (5 shorter events, 0.0 us)
Async XLA Ops:
  0.0 1.4 %copy-start = (bf16[192,4096]{1,0:T(8,128)(2,1)S(1)}, bf16[192,4096]{1,0:T(8,128)(2,1)}, u32[]{:S(2)}) copy-start(bf16[192,4096]{1,0:T(8,128)(2,1)} %mid2_ref.1) | copy-start | bytes 4718596
  1.4 0.7 %copy-start.1 = (s32[1024,4]{0,1:T(4,128)S(1)}, s32[1024,4]{0,1:T(4,128)}, u32[]{:S(2)}) copy-start(s32[1024,4]{0,1:T(4,128)} %param.6) | copy-start | bytes 49156
  2.1 4.4 %copy-start.3 = (f32[4,1024]{1,0:T(4,128)S(1)}, f32[4,1024]{1,0:T(4,128)}, u32[]{:S(2)}) copy-start(f32[4,1024]{1,0:T(4,128)} %pot_ref.1) | copy-start | bytes 49156
  2.8 6.3 %collective-permute-start = (bf16[128,256]{1,0:T(8,128)(2,1)S(1)}, bf16[128,256]{1,0:T(8,128)(2,1)S(1)}, u32[]{:S(2)}, u32[]{:S(2)}) collective-permute-start(bf16[128,256]{1,0:T(8,128)(2,1)S(1)} %get-tuple-element.24), channel_id=1, source_target_pairs={{0,1},{1,0},{2,3},{3,2},{4,5},{5,4},{6,7},{7,6},{8,9},{9,8},{10,11... | collective-permute-start | bytes 196616 | tf_op jit(solution)/shard_map/ppermute | solution.py:361
  3.5 6.3 %collective-permute-start.1 = (bf16[128,256]{1,0:T(8,128)(2,1)S(1)}, bf16[128,256]{1,0:T(8,128)(2,1)S(1)}, u32[]{:S(2)}, u32[]{:S(2)}) collective-permute-start(bf16[128,256]{1,0:T(8,128)(2,1)S(1)} %get-tuple-element.25), channel_id=1, source_target_pairs={{1,2},{2,1},{3,4},{4,3},{5,6},{6,5},{7,8},{8,7},{9,10},{10,9},{11,... | collective-permute-start | bytes 196616 | tf_op jit(solution)/shard_map/ppermute | solution.py:364
  9.8 11.2 %copy-start.2 = (s32[16,2]{0,1:T(2,128)S(1)}, s32[16,2]{0,1:T(2,128)}, u32[]{:S(2)}) copy-start(s32[16,2]{0,1:T(2,128)} %param.7) | copy-start | bytes 388
  10.4 1.4 %collective-permute-start.2 = (bf16[3,128,128]{2,1,0:T(8,128)(2,1)S(1)}, bf16[3,128,128]{2,1,0:T(8,128)(2,1)S(1)}, u32[]{:S(2)}, u32[]{:S(2)}) collective-permute-start(bf16[3,128,128]{2,1,0:T(8,128)(2,1)S(1)} %get-tuple-element.32), channel_id=1, source_target_pairs={{0,1},{1,0},{2,3},{3,2},{4,5},{5,4},{6,7},{7,6},{8,9},{9,8},{10,11... | collective-permute-start | bytes 294920 | tf_op jit(solution)/shard_map/ppermute | solution.py:361
  11.9 7.7 %collective-permute-start.3 = (bf16[2,128,256]{2,1,0:T(8,128)(2,1)S(1)}, bf16[2,128,256]{2,1,0:T(8,128)(2,1)S(1)}, u32[]{:S(2)}, u32[]{:S(2)}) collective-permute-start(bf16[2,128,256]{2,1,0:T(8,128)(2,1)S(1)} %relay.1), channel_id=1, source_target_pairs={{1,2},{2,1},{3,4},{4,3},{5,6},{6,5},{7,8},{8,7},{9,10},{10,9},{11,... | collective-permute-start | bytes 393224 | tf_op jit(solution)/shard_map/ppermute | solution.py:364
  19.6 1.3 %collective-permute-start.4 = (bf16[2,128,256]{2,1,0:T(8,128)(2,1)S(1)}, bf16[2,128,256]{2,1,0:T(8,128)(2,1)S(1)}, u32[]{:S(2)}, u32[]{:S(2)}) collective-permute-start(bf16[2,128,256]{2,1,0:T(8,128)(2,1)S(1)} %collective-permute-done.3.across_in_ref), channel_id=1, source_target_pairs={{0,1},{1,0},{2,3},{3,2},{4,5},{5,4},{6,7},{7,6},{8,9},{9,8},{10,11... | collective-permute-start | bytes 393224 | tf_op jit(solution)/shard_map/ppermute | solution.py:361
  23.3 4.4 %collective-permute-start.5 = (bf16[128,256]{1,0:T(8,128)(2,1)S(1)}, bf16[128,256]{1,0:T(8,128)(2,1)S(1)}, u32[]{:S(2)}, u32[]{:S(2)}) collective-permute-start(bf16[128,256]{1,0:T(8,128)(2,1)S(1)} %get-tuple-element.37), channel_id=1, source_target_pairs={{0,1},{1,0},{2,3},{3,2},{4,5},{5,4},{6,7},{7,6},{8,9},{9,8},{10,11... | collective-permute-start | bytes 196616 | tf_op jit(solution)/shard_map/ppermute | solution.py:361
  23.6 6.4 %collective-permute-start.6 = (bf16[128,256]{1,0:T(8,128)(2,1)S(1)}, bf16[128,256]{1,0:T(8,128)(2,1)S(1)}, u32[]{:S(2)}, u32[]{:S(2)}) collective-permute-start(bf16[128,256]{1,0:T(8,128)(2,1)S(1)} %get-tuple-element.38), channel_id=1, source_target_pairs={{1,2},{2,1},{3,4},{4,3},{5,6},{6,5},{7,8},{8,7},{9,10},{10,9},{11,... | collective-permute-start | bytes 196616 | tf_op jit(solution)/shard_map/ppermute | solution.py:364

commit v3 on v2

--- a/solution.py
+++ b/solution.py
@@ -23,13 +23,16 @@
     return lax.broadcasted_iota(jnp.int32, shape, dim)
 
 
-def row_features(ct_ref):
+def window_start(width):
+    slab = lax.axis_index("sx")
+    first = jnp.clip(slab * ORB - ORB, 0, width - 4 * ORB) // 128 * 128
+    return pl.multiple_of(first, 128)
+
+
+def row_features(window_ref, first):
     slab = lax.axis_index("sx")
     count = lax.axis_size("sx")
-    width = ct_ref.shape[1]
-    first = jnp.clip(slab * ORB - ORB, 0, width - 4 * ORB) // 128 * 128
-    first = pl.multiple_of(first, 128)
-    window = ct_ref[:, pl.ds(first, 4 * ORB)]
+    window = window_ref[...]
     shift = slab * ORB - ORB - first
     window = pltpu.roll(jnp.concatenate([window, window], axis=0), lax.rem(4 * ORB - shift, 4 * ORB), 1)
     lane = iota((1, 4 * ORB), 1)
@@ -120,6 +123,11 @@
     return lax.rem(lax.axis_index("sx"), 2) == 0
 
 
+def at_end():
+    slab = lax.axis_index("sx")
+    return (slab == 0) | (slab == lax.axis_size("sx") - 1)
+
+
 def put_messages(planes, mate_ref, across_ref):
     down = fold(planes[0, : 2 * ORB].astype(F32))
     up = fold(planes[1, ORB:].astype(F32))
@@ -132,17 +140,34 @@
 
 def sides(mate_ref, across_ref):
     mate = mate_ref[...].astype(F32)
-    across = across_ref[...].astype(F32)
+    across = jnp.where(at_end(), 0.0, across_ref[...].astype(F32))
     even = is_even()
     return (jnp.where(even, across, mate), jnp.where(even, mate, across))
 
 
-def edges_kernel(ct_ref, first_ref, last_ref, phi_ref, mask_ref, mate_ref, across_ref):
-    rows = row_features(ct_ref)
-    for i, (plane, ref) in enumerate(((0, first_ref), (CX - 1, last_ref))):
-        mask = sphere(rows, plane)
-        mask_ref[i] = mask
-        phi_ref[i] = ref[...] * mask
+def edges_kernel(
+    table_ref, pieces_ref,
+    phi_ref, mask_ref, rows_ref, mate_ref, across_ref,
+    window_ref, raw_ref, sems,
+):
+    first = window_start(table_ref.shape[1])
+    table_copy = pltpu.make_async_copy(table_ref.at[:, pl.ds(first, 4 * ORB)], window_ref, sems.at[2])
+    table_copy.start()
+    copies = []
+    for i in range(2):
+        start = (CX - 1) * PLANE * i
+        copies.append(
+            pltpu.make_async_copy(pieces_ref.at[:, start : start + PLANE], raw_ref.at[i], sems.at[i])
+        )
+        copies[i].start()
+    table_copy.wait()
+    rows = row_features(window_ref, first)
+    rows_ref[...] = rows
+    for i in range(2):
+        mask_ref[i] = sphere(rows, (CX - 1) * i)
+    for i in range(2):
+        copies[i].wait()
+        phi_ref[i] = raw_ref[i] * mask_ref[i]
     put_messages(phi_ref, mate_ref, across_ref)
 
 
@@ -151,14 +176,14 @@
 
 
 def energy_kernel(
-    ct_ref, mid1_ref, mid2_ref, pot_ref, edge_ref,
+    rows_ref, pieces_ref, pot_ref, edge_ref,
     phi_ref, mask_ref, energy_ref, part_ref, corr_ref, ham_ref,
 ):
-    rows = row_features(ct_ref)
-    for i, ref in enumerate((mid1_ref, mid2_ref)):
+    rows = rows_ref[...]
+    for i in range(2):
         mask = sphere(rows, 1 + i)
         mask_ref[i] = mask
-        phi_ref[i] = ref[...] * mask
+        phi_ref[i] = pieces_ref[:, PLANE * (1 + i) : PLANE * (2 + i)] * mask
     weights = in_plane(6, -1)
     for t in range(PLANE // TILE):
         lanes = slice(TILE * t, TILE * t + TILE)
@@ -185,7 +210,7 @@
 
 
 def bands_kernel(
-    mate_ref, across_ref, part_ref, mask_ref, phi_ref, corr_ref, ham_ref,
+    across_ref, mate_ref, part_ref, mask_ref, phi_ref, corr_ref, ham_ref,
     energy_ref, own_ref, rows_ref,
 ):
     volume = 1.0 / (4.0 * CX**3)
@@ -237,16 +262,29 @@
         c01 = jnp.where(even, c01[:ORB], c01[ORB:])
         c2x = jnp.where(even, c2x[:ORB], c2x[ORB:])
         own = slice(ORB, 2 * ORB)
-        out_ref[which, :ORB, 0:128] = (head[own] + jnp.where(even, c2x, c01)).astype(BF16)
-        out_ref[which, :ORB, 128:256] = (rest[own] + jnp.where(even, c01, c2x)).astype(BF16)
-        out_ref[which, ORB:, 0:128] = jnp.where(even, head[:ORB], head[2 * ORB :]).astype(BF16)
-        out_ref[which, ORB:, 128:256] = jnp.where(even, rest[:ORB], rest[2 * ORB :]).astype(BF16)
+        parts = (
+            (head[own] + jnp.where(even, c2x, c01), rest[own] + jnp.where(even, c01, c2x)),
+            (jnp.where(even, head[:ORB], head[2 * ORB :]), jnp.where(even, rest[:ORB], rest[2 * ORB :])),
+        )
+        for i in range(2):
+            for q in range(2):
+                value = jnp.where(at_end(), 0.0, parts[i][q]).astype(BF16)
+                out_ref[which, ORB * i : ORB * i + ORB, 128 * q : 128 * q + 128] = value
+
+
+def put_gradient(theta, orbital_ref, energy_ref, mask_ref, out_ref):
+    for i in range(2):
+        for t in range(PLANE // TILE):
+            lanes = slice(TILE * t, TILE * t + TILE)
+            fix = jnp.dot(theta, orbital_ref[i, :, lanes], preferred_element_type=F32)
+            value = energy_ref[i, :, lanes].astype(F32) - fix
+            out_ref[i, :, lanes] = value.astype(BF16) * mask_ref[i, :, lanes]
 
 
 def gradient_kernel(
     pattern_ref, own_ref, rows_ref, across_in_ref, relayed_ref,
-    edge_ref, phi_ref, edge_energy_ref, energy_ref, edge_mask_ref, mask_ref,
-    edge_grad_ref, grad_ref, mate_ref, across_ref,
+    edge_ref, edge_energy_ref, edge_mask_ref,
+    edge_grad_ref, theta_ref, mate_ref, across_ref,
     ham_ref, inv_ref,
 ):
     slab = lax.axis_index("sx")
@@ -297,20 +335,17 @@
         ham_ref[...], inv_ref[...], (((1,), (1,)), ((), ())),
         precision=lax.Precision.HIGHEST, preferred_element_type=F32,
     ).astype(BF16)
-    for orb_ref, en_ref, m_ref, out_ref in (
-        (edge_ref, edge_energy_ref, edge_mask_ref, edge_grad_ref),
-        (phi_ref, energy_ref, mask_ref, grad_ref),
-    ):
-        for i in range(2):
-            for t in range(PLANE // TILE):
-                lanes = slice(TILE * t, TILE * t + TILE)
-                fix = jnp.dot(theta, orb_ref[i, :, lanes], preferred_element_type=F32)
-                value = en_ref[i, :, lanes].astype(F32) - fix
-                out_ref[i, :, lanes] = value.astype(BF16) * m_ref[i, :, lanes]
+    theta_ref[...] = theta
+    put_gradient(theta, edge_ref, edge_energy_ref, edge_mask_ref, edge_grad_ref)
     put_messages(edge_grad_ref, mate_ref, across_ref)
 
 
-def smooth_kernel(edge_ref, grad_ref, edge_mask_ref, mask_ref, out_ref, part_ref):
+def smooth_kernel(
+    theta_ref, phi_ref, energy_ref, edge_ref, mask_ref,
+    out_ref, part_ref,
+    grad_ref, done_ref, sems,
+):
+    put_gradient(theta_ref[...], phi_ref, energy_ref, mask_ref, grad_ref)
     weights = in_plane(8, 1)
     for t in range(PLANE // TILE):
         lanes = slice(TILE * t, TILE * t + TILE)
@@ -320,24 +355,37 @@
         outer = plane_product(edge_ref[...].reshape(2 * ROWS, PLANE), weights, t).reshape(2, ROWS, TILE)
         for i in range(2):
             value = (inner[i] + (edge[i] + mid[1 - i])) * (1.0 / 32.0)
-            start = PLANE * (1 + i) + TILE * t
-            out_ref[:, start : start + TILE] = value.astype(BF16) * mask_ref[i, :, lanes]
+            done_ref[i, :, lanes] = value.astype(BF16) * mask_ref[i, :, lanes]
             part_ref[i, :, lanes] = outer[i] + mid[i]
-
-
-def finish_kernel(mate_ref, across_ref, part_ref, mask_ref, inner_ref, out_ref):
+    copies = []
+    for i in range(2):
+        start = PLANE * (1 + i)
+        copies.append(
+            pltpu.make_async_copy(done_ref.at[i], out_ref.at[:, start : start + PLANE], sems.at[i])
+        )
+        copies[i].start()
+    for copy in copies:
+        copy.wait()
+
+
+def finish_kernel(across_ref, mate_ref, part_ref, mask_ref, inner_ref, out_ref, done_ref, sems):
+    copies = []
     for i, side in enumerate(sides(mate_ref, across_ref)):
         tiles = unfold(side)
         rest = slice(2 * ORB, ROWS) if i == 0 else slice(0, ORB)
         for t in range(PLANE // 128):
             lanes = slice(128 * t, 128 * t + 128)
-            start = PLANE * (CX - 1) * i + 128 * t
-            put = slice(start, start + 128)
             value = (part_ref[i, halo_rows(i), lanes] + tiles[t % 4]) * (1.0 / 32.0)
-            out_ref[halo_rows(i), put] = value.astype(BF16) * mask_ref[i, halo_rows(i), lanes]
+            done_ref[i, halo_rows(i), lanes] = value.astype(BF16) * mask_ref[i, halo_rows(i), lanes]
             value = part_ref[i, rest, lanes] * (1.0 / 32.0)
-            out_ref[rest, put] = value.astype(BF16) * mask_ref[i, rest, lanes]
-    out_ref[:, PLANE : (CX - 1) * PLANE] = inner_ref[:, PLANE : (CX - 1) * PLANE]
+            done_ref[i, rest, lanes] = value.astype(BF16) * mask_ref[i, rest, lanes]
+        start = PLANE * (CX - 1) * i
+        copies.append(
+            pltpu.make_async_copy(done_ref.at[i], out_ref.at[:, start : start + PLANE], sems.at[i])
+        )
+        copies[i].start()
+    for copy in copies:
+        copy.wait()
 
 
 def shape(*dims, dtype=BF16):
@@ -350,12 +398,18 @@
 
 PARAMS = pltpu.CompilerParams(vmem_limit_bytes=32 * 1024 * 1024)
 WHOLE = pl.BlockSpec(memory_space=pltpu.VMEM)
+FAR = pl.BlockSpec(memory_space=pltpu.HBM)
+
+
+def far(value):
+    return pltpu.with_memory_space_constraint(value, pltpu.HBM)
 
 
 def per_device(pieces, potential, centers, pattern):
     count = lax.axis_size("sx")
     mates = [(i, i ^ 1) for i in range(count)]
-    others = [(i, i + 1 if i % 2 else i - 1) for i in range(1, count - 1)]
+    others = [(0, 0), (count - 1, count - 1)]
+    others += [(i, i + 1 if i % 2 else i - 1) for i in range(1, count - 1)]
 
     def to_mate(value):
         return lax.ppermute(value, "sx", mates)
@@ -366,47 +420,35 @@
     table = centers.T
     pair = shape(2, ROWS, PLANE)
 
-    def plane_spec(plane):
-        return pl.BlockSpec((ROWS, PLANE), lambda i: (0, plane))
-
-    def whole_spec(*dims):
-        return pl.BlockSpec(dims, lambda i: (0,) * len(dims))
-
-    edge, edge_mask, for_mate, for_other = pl.pallas_call(
+    edge, edge_mask, rows, for_mate, for_other = pl.pallas_call(
         edges_kernel,
-        grid=(1,),
-        out_shape=(pair, pair, shape(2 * ORB, HALF), shape(2 * ORB, HALF)),
-        in_specs=[whole_spec(*table.shape), plane_spec(0), plane_spec(CX - 1)],
-        out_specs=(
-            whole_spec(2, ROWS, PLANE), whole_spec(2, ROWS, PLANE),
-            whole_spec(2 * ORB, HALF), whole_spec(2 * ORB, HALF),
-        ),
+        out_shape=(pair, pair, shape(ROWS, 16), shape(2 * ORB, HALF), shape(2 * ORB, HALF)),
+        in_specs=[FAR, FAR],
+        out_specs=(WHOLE,) * 5,
+        scratch_shapes=[
+            pltpu.VMEM((4, 4 * ORB), jnp.int32),
+            pltpu.VMEM((2, ROWS, PLANE), BF16),
+            pltpu.SemaphoreType.DMA((3,)),
+        ],
         compiler_params=PARAMS,
         cost_estimate=cost(10**8, 10**6),
         name="edges",
-    )(table, pieces, pieces)
+    )(far(table), far(pieces))
     other_side = across(for_other)
     mate_side = to_mate(for_mate)
 
     mid, mid_mask, mid_energy, part, corr, ham = pl.pallas_call(
         energy_kernel,
-        grid=(1,),
         out_shape=(
             pair, pair, pair, shape(2, ROWS, PLANE, dtype=F32),
             shape(ROWS, ROWS, dtype=F32), shape(ROWS, ROWS, dtype=F32),
         ),
-        in_specs=[
-            whole_spec(*table.shape), plane_spec(1), plane_spec(2),
-            whole_spec(CX, PLANE), whole_spec(2, ROWS, PLANE),
-        ],
-        out_specs=(
-            whole_spec(2, ROWS, PLANE), whole_spec(2, ROWS, PLANE), whole_spec(2, ROWS, PLANE),
-            whole_spec(2, ROWS, PLANE), whole_spec(ROWS, ROWS), whole_spec(ROWS, ROWS),
-        ),
+        in_specs=[WHOLE] * 4,
+        out_specs=(WHOLE,) * 6,
         compiler_params=PARAMS,
         cost_estimate=cost(4 * 10**9, 10**7),
         name="energy",
-    )(table, pieces, pieces, potential, edge)
+    )(rows, pieces, potential, edge)
 
     edge_energy, own, for_mate = pl.pallas_call(
         bands_kernel,
@@ -416,7 +458,7 @@
         compiler_params=PARAMS,
         cost_estimate=cost(10**9, 10**7),
         name="bands",
-    )(mate_side, other_side, part, edge_mask, edge, corr, ham)
+    )(other_side, mate_side, part, edge_mask, edge, corr, ham)
     mate_rows = to_mate(for_mate)
     for_other = pl.pallas_call(
         relay_kernel,
@@ -430,41 +472,45 @@
     other_rows = across(for_other)
     relayed = to_mate(other_rows)
 
-    edge_grad, mid_grad, for_mate, for_other = pl.pallas_call(
+    edge_grad, theta, for_mate, for_other = pl.pallas_call(
         gradient_kernel,
-        out_shape=(pair, pair, shape(2 * ORB, HALF), shape(2 * ORB, HALF)),
-        in_specs=[pl.BlockSpec(memory_space=pltpu.SMEM)] + [WHOLE] * 10,
+        out_shape=(pair, shape(ROWS, ROWS), shape(2 * ORB, HALF), shape(2 * ORB, HALF)),
+        in_specs=[pl.BlockSpec(memory_space=pltpu.SMEM)] + [WHOLE] * 7,
         out_specs=(WHOLE,) * 4,
         scratch_shapes=[pltpu.VMEM((ROWS, 512), F32), pltpu.VMEM((ROWS, 512), F32)],
         compiler_params=PARAMS,
         cost_estimate=cost(10**9, 10**7),
         name="gradient",
-    )(
-        pattern.T, own, mate_rows, other_rows, relayed,
-        edge, mid, edge_energy, mid_energy, edge_mask, mid_mask,
-    )
+    )(pattern.T, own, mate_rows, other_rows, relayed, edge, edge_energy, edge_mask)
     other_side = across(for_other)
     mate_side = to_mate(for_mate)
 
     inner, part = pl.pallas_call(
         smooth_kernel,
-        out_shape=(shape(ROWS, CX * PLANE), shape(2, ROWS, PLANE, dtype=F32)),
-        in_specs=[WHOLE] * 4,
-        out_specs=(WHOLE,) * 2,
+        out_shape=(pltpu.HBM((ROWS, CX * PLANE), BF16), shape(2, ROWS, PLANE, dtype=F32)),
+        in_specs=[WHOLE] * 5,
+        out_specs=(FAR, WHOLE),
+        scratch_shapes=[
+            pltpu.VMEM((2, ROWS, PLANE), BF16),
+            pltpu.VMEM((2, ROWS, PLANE), BF16),
+            pltpu.SemaphoreType.DMA((2,)),
+        ],
         compiler_params=PARAMS,
         cost_estimate=cost(2 * 10**9, 10**7),
         name="smooth",
-    )(edge_grad, mid_grad, edge_mask, mid_mask)
+    )(theta, mid, mid_energy, edge_grad, mid_mask)
 
     return pl.pallas_call(
         finish_kernel,
-        out_shape=shape(ROWS, CX * PLANE),
-        in_specs=[WHOLE] * 5,
-        out_specs=WHOLE,
+        out_shape=pltpu.HBM((ROWS, CX * PLANE), BF16),
+        in_specs=[WHOLE] * 4 + [FAR],
+        out_specs=FAR,
+        scratch_shapes=[pltpu.VMEM((2, ROWS, PLANE), BF16), pltpu.SemaphoreType.DMA((2,))],
+        input_output_aliases={4: 0},
         compiler_params=PARAMS,
         cost_estimate=cost(10**7, 10**7),
         name="finish",
-    )(mate_side, other_side, part, edge_mask, inner)
+    )(other_side, mate_side, part, edge_mask, inner)
 
 
 def solution(mesh):

time: 31.8 us -> 29.1 us (0.915)
  the two profiles are of different devices: /device:TPU:9 before, /device:TPU:0 now
where the time goes in v3:
time: 29.1 us; the launch traced here: 28.6 us
  starting transfers between devices  16.4 us (56%)
  Pallas kernels  9.76 us (34%)
  waiting for transfers between devices  2.27 us (8%)
    ppermute x4, starting transfers between devices, to_mate(): return lax.ppermute(value, 'sx', mates)  14.4 us
    ppermute x4, waiting for transfers between devices, to_mate(): return lax.ppermute(value, 'sx', mates)  2.26 us
    pallas_call x1, Pallas kernels, per_device(): pl.pallas_call(energy_kernel, out_shape=(pair, pair, pair, shape(2, ROWS,...  2.16 us
    pallas_call x1, Pallas kernels, per_device(): pl.pallas_call(smooth_kernel, out_shape=(pltpu.HBM((ROWS, CX * PLANE), BF...  2.16 us
    ppermute x3, starting transfers between devices, across(): return lax.ppermute(value, 'sx', others)  2 us
    pallas_call x1, Pallas kernels, per_device(): pl.pallas_call(gradient_kernel, out_shape=(pair, shape(ROWS, ROWS), shape...  1.97 us
    pallas_call x1, Pallas kernels, per_device(): pl.pallas_call(edges_kernel, out_shape=(pair, pair, shape(ROWS, 16), shap...  1.59 us
    pallas_call x1, Pallas kernels, per_device(): pl.pallas_call(finish_kernel, out_shape=pltpu.HBM((ROWS, CX * PLANE), BF1...  1.14 us
  transfers between devices with their start and end apart: 7, of which 2 were waited for; matrix products, arithmetic and copies ran while one was open for 0% of the time, Pallas kernels for 15%

profile of v3, /device:TPU:0, one launch (start us, length us, event | category | flops | bytes accessed | tf_op | source)
XLA Modules:
  0.0 28.6 jit_solution(3700969901105833253)
XLA Ops:
  0.0 1.6 %edges.1 = (bf16[2,192,1024]{2,1,0:T(8,128)(2,1)S(1)}, bf16[2,192,1024]{2,1,0:T(8,128)(2,1)S(1)}, bf16[192,16]{1,0:T(8,128)(2,1)S(1)}, bf16[128,256]{1,0:T(8,128)(2,1)S(1)}, bf16[128,256]{1,0:T(8,128)(2,1)S(1)}) custom-call(s32[4,1024]{1,0:T(4,128)} %bitcast.3, bf16[192,4096]{1,0:T(8,128)(2,1)} %pieces_ref.3), custom_call_target="tpu_custom_call" | custom-call | flops 100000000 | bytes 1000000 | tf_op jit(solution)/shard_map/edges/pallas_call | solution.py:423
  1.6 0.7 %collective-permute-start = (bf16[128,256]{1,0:T(8,128)(2,1)S(1)}, bf16[128,256]{1,0:T(8,128)(2,1)S(1)}, u32[]{:S(2)}, u32[]{:S(2)}) collective-permute-start(bf16[128,256]{1,0:T(8,128)(2,1)S(1)} %get-tuple-element.25), channel_id=1, source_target_pairs={{0,0},{15,15},{1,2},{2,1},{3,4},{4,3},{5,6},{6,5},{7,8},{8,7},{9,1... | collective-permute-start | bytes 196616 | tf_op jit(solution)/shard_map/ppermute | solution.py:418
  2.3 4.4 %collective-permute-start.1 = (bf16[128,256]{1,0:T(8,128)(2,1)S(1)}, bf16[128,256]{1,0:T(8,128)(2,1)S(1)}, u32[]{:S(2)}, u32[]{:S(2)}) collective-permute-start(bf16[128,256]{1,0:T(8,128)(2,1)S(1)} %get-tuple-element.26), channel_id=1, source_target_pairs={{0,1},{1,0},{2,3},{3,2},{4,5},{5,4},{6,7},{7,6},{8,9},{9,8},{10,11... | collective-permute-start | bytes 196616 | tf_op jit(solution)/shard_map/ppermute | solution.py:415
  6.7 0.0 copy-done
  6.7 0.0 copy-done.1
  6.7 2.2 %energy.1 = (bf16[2,192,1024]{2,1,0:T(8,128)(2,1)S(1)}, bf16[2,192,1024]{2,1,0:T(8,128)(2,1)S(1)}, bf16[2,192,1024]{2,1,0:T(8,128)(2,1)S(1)}, f32[2,192,1024]{2,...) custom-call(bf16[192,16]{1,0:T(8,128)(2,1)S(1)} %get-tuple-element.27.rows_ref, ...), custom_call_target="tpu_custom_call" | custom-call | flops 4000000000 | bytes 10000000 | tf_op jit(solution)/shard_map/energy/pallas_call | solution.py:440
  8.8 0.0 collective-permute-done.across_ref
  8.8 0.0 collective-permute-done.1.mate_ref
  8.9 0.0 copy-start.2
  8.9 0.6 %bands.1 = (bf16[2,192,1024]{2,1,0:T(8,128)(2,1)S(1)}, f32[2,192,256]{2,1,0:T(8,128)S(1)}, bf16[3,128,128]{2,1,0:T(8,128)(2,1)S(1)}) custom-call(bf16[128,256]{1,0:T(8,128)(2,1)S(1)} %collective-permute-done.across_ref, bf16[128,256]{1,0:T(8,128)(2,1)S(1)} %collective-permute-done.1.mate_ref, f32[2,192,1024]{2,1,0:T(8,128)S(1)} %get-tuple-element.29.part_ref, ...), custom_call_target="tpu_custom_call" | custom-call | flops 1000000000 | bytes 10000000 | tf_op jit(solution)/shard_map/bands/pallas_call | solution.py:453
  9.5 0.1 collective-permute-start.2
  9.6 1.3 %collective-permute-done.2.rows_ref = bf16[3,128,128]{2,1,0:T(8,128)(2,1)S(1)} collective-permute-done((bf16[3,128,128]{2,1,0:T(8,128)(2,1)S(1)}, bf16[3,128,128]{2,1,0:T(8,128)(2,1)S(1)}, u32[]{:S(2)}, u32[]{:S(2)}) %collective-permute-start.2) | collective-permute-done | bytes 98336 | tf_op jit(solution)/shard_map/ppermute | solution.py:415
  10.8 0.1 relay.1
  11.0 0.7 %collective-permute-start.3 = (bf16[2,128,256]{2,1,0:T(8,128)(2,1)S(1)}, bf16[2,128,256]{2,1,0:T(8,128)(2,1)S(1)}, u32[]{:S(2)}, u32[]{:S(2)}) collective-permute-start(bf16[2,128,256]{2,1,0:T(8,128)(2,1)S(1)} %relay.1), channel_id=1, source_target_pairs={{0,0},{15,15},{1,2},{2,1},{3,4},{4,3},{5,6},{6,5},{7,8},{8,7},{9,1... | collective-permute-start | bytes 393224 | tf_op jit(solution)/shard_map/ppermute | solution.py:418
  11.7 0.0 collective-permute-done.3.across_in_ref
  11.7 5.8 %collective-permute-start.4 = (bf16[2,128,256]{2,1,0:T(8,128)(2,1)S(1)}, bf16[2,128,256]{2,1,0:T(8,128)(2,1)S(1)}, u32[]{:S(2)}, u32[]{:S(2)}) collective-permute-start(bf16[2,128,256]{2,1,0:T(8,128)(2,1)S(1)} %collective-permute-done.3.across_in_ref), channel_id=1, source_target_pairs={{0,1},{1,0},{2,3},{3,2},{4,5},{5,4},{6,7},{7,6},{8,9},{9,8},{10,11... | collective-permute-start | bytes 393224 | tf_op jit(solution)/shard_map/ppermute | solution.py:415
  17.4 1.0 %collective-permute-done.4.relayed_ref = bf16[2,128,256]{2,1,0:T(8,128)(2,1)S(1)} collective-permute-done((bf16[2,128,256]{2,1,0:T(8,128)(2,1)S(1)}, bf16[2,128,256]{2,1,0:T(8,128)(2,1)S(1)}, u32[]{:S(2)}, u32[]{:S(2)}) %collective-permute-start.4) | collective-permute-done | bytes 131104 | tf_op jit(solution)/shard_map/ppermute | solution.py:415
  18.4 2.0 %gradient.1 = (bf16[2,192,1024]{2,1,0:T(8,128)(2,1)S(1)}, bf16[192,192]{1,0:T(8,128)(2,1)S(1)}, bf16[128,256]{1,0:T(8,128)(2,1)S(1)}, bf16[128,256]{1,0:T(8,128)(2,1)S(1)}) custom-call(s32[2,16]{1,0:T(2,128)S(1)} %bitcast.2, f32[2,192,256]{2,1,0:T(8,128)S(1)} %get-tuple-element.33.own_ref, bf16[3,128,128]{2,1,0:T(8,128)(2,1)S(1)} %collective-permute-done.2.rows_ref, ...), custom_call_target="tpu_custom_call" | custom-call | flops 1000000000 | bytes 10000000 | tf_op jit(solution)/shard_map/gradient/pallas_call | solution.py:475
  20.4 0.7 %collective-permute-start.5 = (bf16[128,256]{1,0:T(8,128)(2,1)S(1)}, bf16[128,256]{1,0:T(8,128)(2,1)S(1)}, u32[]{:S(2)}, u32[]{:S(2)}) collective-permute-start(bf16[128,256]{1,0:T(8,128)(2,1)S(1)} %get-tuple-element.36), channel_id=1, source_target_pairs={{0,0},{15,15},{1,2},{2,1},{3,4},{4,3},{5,6},{6,5},{7,8},{8,7},{9,1... | collective-permute-start | bytes 196616 | tf_op jit(solution)/shard_map/ppermute | solution.py:418
  21.1 4.2 %collective-permute-start.6 = (bf16[128,256]{1,0:T(8,128)(2,1)S(1)}, bf16[128,256]{1,0:T(8,128)(2,1)S(1)}, u32[]{:S(2)}, u32[]{:S(2)}) collective-permute-start(bf16[128,256]{1,0:T(8,128)(2,1)S(1)} %get-tuple-element.37), channel_id=1, source_target_pairs={{0,1},{1,0},{2,3},{3,2},{4,5},{5,4},{6,7},{7,6},{8,9},{9,8},{10,11... | collective-permute-start | bytes 196616 | tf_op jit(solution)/shard_map/ppermute | solution.py:415
  25.3 2.2 %smooth.1 = (bf16[192,4096]{1,0:T(8,128)(2,1)}, f32[2,192,1024]{2,1,0:T(8,128)S(1)}) custom-call(bf16[192,192]{1,0:T(8,128)(2,1)S(1)} %get-tuple-element.38.theta_ref, bf16[2,192,1024]{2,1,0:T(8,128)(2,1)S(1)} %get-tuple-element.39.phi_ref, bf16[2,192,1024]{2,1,0:T(8,128)(2,1)S(1)} %get-tuple-element.40.energy_ref, ...), custom_call_target="tpu_custom_call" | custom-call | flops 2000000000 | bytes 10000000 | tf_op jit(solution)/shard_map/smooth/pallas_call | solution.py:488
  27.4 0.0 collective-permute-done.5.across_ref
  27.4 0.0 collective-permute-done.6.mate_ref
  27.5 1.1 %finish.1 = bf16[192,4096]{1,0:T(8,128)(2,1)} custom-call(bf16[128,256]{1,0:T(8,128)(2,1)S(1)} %collective-permute-done.5.across_ref, bf16[128,256]{1,0:T(8,128)(2,1)S(1)} %collective-permute-done.6.mate_ref, f32[2,192,1024]{2,1,0:T(8,128)S(1)} %get-tuple-element.43.part_ref, ...), custom_call_target="tpu_custom_call", output_to_operand_aliasing={{}: (4, {})} | custom-call | flops 10000000 | bytes 10000000 | tf_op jit(solution)/shard_map/finish/pallas_call | solution.py:503
  (3 shorter events, 0.0 us)
Async XLA Ops:
  0.0 6.7 %copy-start = (bf16[192,4096]{1,0:T(8,128)(2,1)S(1)}, bf16[192,4096]{1,0:T(8,128)(2,1)}, u32[]{:S(2)}) copy-start(bf16[192,4096]{1,0:T(8,128)(2,1)} %pieces_ref.3) | copy-start | bytes 4718596
  0.0 6.7 %copy-start.1 = (f32[4,1024]{1,0:T(4,128)S(1)}, f32[4,1024]{1,0:T(4,128)}, u32[]{:S(2)}) copy-start(f32[4,1024]{1,0:T(4,128)} %pot_ref.1) | copy-start | bytes 49156
  1.6 7.2 %collective-permute-start = (bf16[128,256]{1,0:T(8,128)(2,1)S(1)}, bf16[128,256]{1,0:T(8,128)(2,1)S(1)}, u32[]{:S(2)}, u32[]{:S(2)}) collective-permute-start(bf16[128,256]{1,0:T(8,128)(2,1)S(1)} %get-tuple-element.25), channel_id=1, source_target_pairs={{0,0},{15,15},{1,2},{2,1},{3,4},{4,3},{5,6},{6,5},{7,8},{8,7},{9,1... | collective-permute-start | bytes 196616 | tf_op jit(solution)/shard_map/ppermute | solution.py:418
  2.3 6.6 %collective-permute-start.1 = (bf16[128,256]{1,0:T(8,128)(2,1)S(1)}, bf16[128,256]{1,0:T(8,128)(2,1)S(1)}, u32[]{:S(2)}, u32[]{:S(2)}) collective-permute-start(bf16[128,256]{1,0:T(8,128)(2,1)S(1)} %get-tuple-element.26), channel_id=1, source_target_pairs={{0,1},{1,0},{2,3},{3,2},{4,5},{5,4},{6,7},{7,6},{8,9},{9,8},{10,11... | collective-permute-start | bytes 196616 | tf_op jit(solution)/shard_map/ppermute | solution.py:415
  8.9 9.6 %copy-start.2 = (s32[16,2]{0,1:T(2,128)S(1)}, s32[16,2]{0,1:T(2,128)}, u32[]{:S(2)}) copy-start(s32[16,2]{0,1:T(2,128)} %param.7) | copy-start | bytes 388
  9.5 1.4 %collective-permute-start.2 = (bf16[3,128,128]{2,1,0:T(8,128)(2,1)S(1)}, bf16[3,128,128]{2,1,0:T(8,128)(2,1)S(1)}, u32[]{:S(2)}, u32[]{:S(2)}) collective-permute-start(bf16[3,128,128]{2,1,0:T(8,128)(2,1)S(1)} %get-tuple-element.34), channel_id=1, source_target_pairs={{0,1},{1,0},{2,3},{3,2},{4,5},{5,4},{6,7},{7,6},{8,9},{9,8},{10,11... | collective-permute-start | bytes 294920 | tf_op jit(solution)/shard_map/ppermute | solution.py:415
  11.0 0.7 %collective-permute-start.3 = (bf16[2,128,256]{2,1,0:T(8,128)(2,1)S(1)}, bf16[2,128,256]{2,1,0:T(8,128)(2,1)S(1)}, u32[]{:S(2)}, u32[]{:S(2)}) collective-permute-start(bf16[2,128,256]{2,1,0:T(8,128)(2,1)S(1)} %relay.1), channel_id=1, source_target_pairs={{0,0},{15,15},{1,2},{2,1},{3,4},{4,3},{5,6},{6,5},{7,8},{8,7},{9,1... | collective-permute-start | bytes 393224 | tf_op jit(solution)/shard_map/ppermute | solution.py:418
  11.7 6.7 %collective-permute-start.4 = (bf16[2,128,256]{2,1,0:T(8,128)(2,1)S(1)}, bf16[2,128,256]{2,1,0:T(8,128)(2,1)S(1)}, u32[]{:S(2)}, u32[]{:S(2)}) collective-permute-start(bf16[2,128,256]{2,1,0:T(8,128)(2,1)S(1)} %collective-permute-done.3.across_in_ref), channel_id=1, source_target_pairs={{0,1},{1,0},{2,3},{3,2},{4,5},{5,4},{6,7},{7,6},{8,9},{9,8},{10,11... | collective-permute-start | bytes 393224 | tf_op jit(solution)/shard_map/ppermute | solution.py:415
  20.4 7.0 %collective-permute-start.5 = (bf16[128,256]{1,0:T(8,128)(2,1)S(1)}, bf16[128,256]{1,0:T(8,128)(2,1)S(1)}, u32[]{:S(2)}, u32[]{:S(2)}) collective-permute-start(bf16[128,256]{1,0:T(8,128)(2,1)S(1)} %get-tuple-element.36), channel_id=1, source_target_pairs={{0,0},{15,15},{1,2},{2,1},{3,4},{4,3},{5,6},{6,5},{7,8},{8,7},{9,1... | collective-permute-start | bytes 196616 | tf_op jit(solution)/shard_map/ppermute | solution.py:418
  21.1 6.4 %collective-permute-start.6 = (bf16[128,256]{1,0:T(8,128)(2,1)S(1)}, bf16[128,256]{1,0:T(8,128)(2,1)S(1)}, u32[]{:S(2)}, u32[]{:S(2)}) collective-permute-start(bf16[128,256]{1,0:T(8,128)(2,1)S(1)} %get-tuple-element.37), channel_id=1, source_target_pairs={{0,1},{1,0},{2,3},{3,2},{4,5},{5,4},{6,7},{7,6},{8,9},{9,8},{10,11... | collective-permute-start | bytes 196616 | tf_op jit(solution)/shard_map/ppermute | solution.py:415

commit v4 on v3

--- a/solution.py
+++ b/solution.py
@@ -408,14 +408,15 @@
 def per_device(pieces, potential, centers, pattern):
     count = lax.axis_size("sx")
     mates = [(i, i ^ 1) for i in range(count)]
-    others = [(0, 0), (count - 1, count - 1)]
-    others += [(i, i + 1 if i % 2 else i - 1) for i in range(1, count - 1)]
+    pairs = [[0, count - 1]] + [[i, i + 1] for i in range(1, count - 1, 2)]
 
     def to_mate(value):
         return lax.ppermute(value, "sx", mates)
 
     def across(value):
-        return lax.ppermute(value, "sx", others)
+        both = lax.all_gather(value, "sx", axis_index_groups=pairs)
+        first = (lax.axis_index("sx") % 2) == 1
+        return jnp.where(first, both[1], both[0])
 
     table = centers.T
     pair = shape(2, ROWS, PLANE)

time: 29.1 us -> 36.6 us (1.26)
  blocking collectives: 0 us -> 23.1 us
  starting transfers between devices: 16.4 us -> 0.73 us
    all_gather x0 -> x3, blocking collectives: none -> 23.1 us  [across(): both = lax.all_gather(value, 'sx', axis_index_groups=pairs)]
    ppermute x4, starting transfers between devices: 14.4 us -> 0.73 us  [to_mate(): return lax.ppermute(value, 'sx', mates)]
    ppermute x3 -> x0, starting transfers between devices: 2 us -> none  [across(): return lax.ppermute(value, 'sx', others)]
  transfers between devices with their start and end apart: 7 -> 4, of which waited for: 2 -> 2; matrix products, arithmetic and copies ran while one was open for 0% -> 0% of each run, Pallas kernels for 15% -> 12%
where the time goes in v4:
time: 36.6 us; the launch traced here: 36.4 us
  blocking collectives  23.1 us (63%)
  Pallas kernels  9.82 us (27%)
  waiting for transfers between devices  2.63 us (7%)
  starting transfers between devices  0.73 us (2%)
    all_gather x3, blocking collectives, across(): both = lax.all_gather(value, 'sx', axis_index_groups=pairs)  23.1 us
    ppermute x4, waiting for transfers between devices, to_mate(): return lax.ppermute(value, 'sx', mates)  2.63 us
    pallas_call x1, Pallas kernels, per_device(): pl.pallas_call(smooth_kernel, out_shape=(pltpu.HBM((ROWS, CX * PLANE), BF...  2.16 us
    pallas_call x1, Pallas kernels, per_device(): pl.pallas_call(energy_kernel, out_shape=(pair, pair, pair, shape(2, ROWS,...  2.16 us
    pallas_call x1, Pallas kernels, per_device(): pl.pallas_call(gradient_kernel, out_shape=(pair, shape(ROWS, ROWS), shape...  1.97 us
    pallas_call x1, Pallas kernels, per_device(): pl.pallas_call(edges_kernel, out_shape=(pair, pair, shape(ROWS, 16), shap...  1.59 us
    pallas_call x1, Pallas kernels, per_device(): pl.pallas_call(finish_kernel, out_shape=pltpu.HBM((ROWS, CX * PLANE), BF1...  1.14 us
  transfers between devices with their start and end apart: 4, of which 2 were waited for; matrix products, arithmetic and copies ran while one was open for 0% of the time, Pallas kernels for 12%

profile of v4, /device:TPU:0, one launch (start us, length us, event | category | flops | bytes accessed | tf_op | source)
XLA Modules:
  0.0 36.4 jit_solution(13432412711316290779)
XLA Ops:
  0.0 0.0 copy-start
  0.0 0.0 copy-start.1
  0.0 1.6 %edges.1 = (bf16[2,192,1024]{2,1,0:T(8,128)(2,1)S(1)}, bf16[2,192,1024]{2,1,0:T(8,128)(2,1)S(1)}, bf16[192,16]{1,0:T(8,128)(2,1)S(1)}, bf16[128,256]{1,0:T(8,128)(2,1)S(1)}, bf16[128,256]{1,0:T(8,128)(2,1)S(1)}) custom-call(s32[4,1024]{1,0:T(4,128)} %bitcast.3, bf16[192,4096]{1,0:T(8,128)(2,1)} %pieces_ref.3), custom_call_target="tpu_custom_call" | custom-call | flops 100000000 | bytes 1000000 | tf_op jit(solution)/shard_map/edges/pallas_call | solution.py:424
  1.6 0.5 %collective-permute-start = (bf16[128,256]{1,0:T(8,128)(2,1)S(1)}, bf16[128,256]{1,0:T(8,128)(2,1)S(1)}, u32[]{:S(2)}, u32[]{:S(2)}) collective-permute-start(bf16[128,256]{1,0:T(8,128)(2,1)S(1)} %get-tuple-element.26), channel_id=1, source_target_pairs={{0,1},{1,0},{2,3},{3,2},{4,5},{5,4},{6,7},{7,6},{8,9},{9,8},{10,11... | collective-permute-start | bytes 196616 | tf_op jit(solution)/shard_map/ppermute | solution.py:414
  2.1 8.3 %all-gather = bf16[256,256]{1,0:T(8,128)(2,1)S(1)} all-gather(bf16[128,256]{1,0:T(8,128)(2,1)S(1)} %get-tuple-element.25), channel_id=2, replica_groups={{0,15},{1,2},{3,4},{5,6},{7,8},{9,10},{11,12},{13,14},{16,31},{17,18},{..., dimensions={0}, use_global_device_ids=true | all-gather | bytes 196608 | tf_op jit(solution)/shard_map/all_gather | solution.py:417
  10.4 0.0 copy-done
  10.4 0.0 copy-done.1
  10.4 2.2 %energy.1 = (bf16[2,192,1024]{2,1,0:T(8,128)(2,1)S(1)}, bf16[2,192,1024]{2,1,0:T(8,128)(2,1)S(1)}, bf16[2,192,1024]{2,1,0:T(8,128)(2,1)S(1)}, f32[2,192,1024]{2,...) custom-call(bf16[192,16]{1,0:T(8,128)(2,1)S(1)} %get-tuple-element.27.rows_ref, ...), custom_call_target="tpu_custom_call" | custom-call | flops 4000000000 | bytes 10000000 | tf_op jit(solution)/shard_map/energy/pallas_call | solution.py:441
  12.6 0.0 collective-permute-done.mate_ref
  12.6 0.0 copy-start.2
  12.6 0.7 %bands.1 = (bf16[2,192,1024]{2,1,0:T(8,128)(2,1)S(1)}, f32[2,192,256]{2,1,0:T(8,128)S(1)}, bf16[3,128,128]{2,1,0:T(8,128)(2,1)S(1)}) custom-call(bf16[128,256]{1,0:T(8,128)(2,1)S(1)} %slice_select_fusion.2.across_ref, bf16[128,256]{1,0:T(8,128)(2,1)S(1)} %collective-permute-done.mate_ref, f32[2,192,1024]{2,1,0:T(8,128)S(1)} %get-tuple-element.29.part_ref, ...), custom_call_target="tpu_custom_call" | custom-call | flops 1000000000 | bytes 10000000 | tf_op jit(solution)/shard_map/bands/pallas_call | solution.py:454
  13.2 0.1 collective-permute-start.1
  13.3 1.3 %collective-permute-done.1.rows_ref = bf16[3,128,128]{2,1,0:T(8,128)(2,1)S(1)} collective-permute-done((bf16[3,128,128]{2,1,0:T(8,128)(2,1)S(1)}, bf16[3,128,128]{2,1,0:T(8,128)(2,1)S(1)}, u32[]{:S(2)}, u32[]{:S(2)}) %collective-permute-start.1) | collective-permute-done | bytes 98336 | tf_op jit(solution)/shard_map/ppermute | solution.py:414
  14.6 0.1 relay.1
  14.8 7.8 %all-gather.1 = bf16[4,128,256]{2,1,0:T(8,128)(2,1)S(1)} all-gather(bf16[2,128,256]{2,1,0:T(8,128)(2,1)S(1)} %relay.1), channel_id=3, replica_groups={{0,15},{1,2},{3,4},{5,6},{7,8},{9,10},{11,12},{13,14},{16,31},{17,18},{..., dimensions={0}, use_global_device_ids=true | all-gather | bytes 393216 | tf_op jit(solution)/shard_map/all_gather | solution.py:417
  22.6 0.1 collective-permute-start.2
  22.6 1.3 %collective-permute-done.2.relayed_ref = bf16[2,128,256]{2,1,0:T(8,128)(2,1)S(1)} collective-permute-done((bf16[2,128,256]{2,1,0:T(8,128)(2,1)S(1)}, bf16[2,128,256]{2,1,0:T(8,128)(2,1)S(1)}, u32[]{:S(2)}, u32[]{:S(2)}) %collective-permute-start.2) | collective-permute-done | bytes 131104 | tf_op jit(solution)/shard_map/ppermute | solution.py:414
  24.0 0.0 copy-done.2
  24.0 2.0 %gradient.1 = (bf16[2,192,1024]{2,1,0:T(8,128)(2,1)S(1)}, bf16[192,192]{1,0:T(8,128)(2,1)S(1)}, bf16[128,256]{1,0:T(8,128)(2,1)S(1)}, bf16[128,256]{1,0:T(8,128)(2,1)S(1)}) custom-call(s32[2,16]{1,0:T(2,128)S(1)} %bitcast.2, f32[2,192,256]{2,1,0:T(8,128)S(1)} %get-tuple-element.33.own_ref, bf16[3,128,128]{2,1,0:T(8,128)(2,1)S(1)} %collective-permute-done.1.rows_ref, ...), custom_call_target="tpu_custom_call" | custom-call | flops 1000000000 | bytes 10000000 | tf_op jit(solution)/shard_map/gradient/pallas_call | solution.py:476
  26.0 7.1 %all-gather.2 = bf16[256,256]{1,0:T(8,128)(2,1)S(1)} all-gather(bf16[128,256]{1,0:T(8,128)(2,1)S(1)} %get-tuple-element.36), channel_id=4, replica_groups={{0,15},{1,2},{3,4},{5,6},{7,8},{9,10},{11,12},{13,14},{16,31},{17,18},{..., dimensions={0}, use_global_device_ids=true | all-gather | bytes 196608 | tf_op jit(solution)/shard_map/all_gather | solution.py:417
  33.0 0.1 collective-permute-start.3
  33.1 2.2 %smooth.1 = (bf16[192,4096]{1,0:T(8,128)(2,1)}, f32[2,192,1024]{2,1,0:T(8,128)S(1)}) custom-call(bf16[192,192]{1,0:T(8,128)(2,1)S(1)} %get-tuple-element.38.theta_ref, bf16[2,192,1024]{2,1,0:T(8,128)(2,1)S(1)} %get-tuple-element.39.phi_ref, bf16[2,192,1024]{2,1,0:T(8,128)(2,1)S(1)} %get-tuple-element.40.energy_ref, ...), custom_call_target="tpu_custom_call" | custom-call | flops 2000000000 | bytes 10000000 | tf_op jit(solution)/shard_map/smooth/pallas_call | solution.py:489
  35.3 0.0 collective-permute-done.3.mate_ref
  35.3 1.1 %finish.1 = bf16[192,4096]{1,0:T(8,128)(2,1)} custom-call(bf16[128,256]{1,0:T(8,128)(2,1)S(1)} %slice_select_fusion.1.across_ref, bf16[128,256]{1,0:T(8,128)(2,1)S(1)} %collective-permute-done.3.mate_ref, f32[2,192,1024]{2,1,0:T(8,128)S(1)} %get-tuple-element.43.part_ref, ...), custom_call_target="tpu_custom_call", output_to_operand_aliasing={{}: (4, {})} | custom-call | flops 10000000 | bytes 10000000 | tf_op jit(solution)/shard_map/finish/pallas_call | solution.py:504
  (3 shorter events, 0.0 us)
Async XLA Ops:
  0.0 10.4 %copy-start = (bf16[192,4096]{1,0:T(8,128)(2,1)S(1)}, bf16[192,4096]{1,0:T(8,128)(2,1)}, u32[]{:S(2)}) copy-start(bf16[192,4096]{1,0:T(8,128)(2,1)} %pieces_ref.3) | copy-start | bytes 4718596
  0.0 10.4 %copy-start.1 = (f32[4,1024]{1,0:T(4,128)S(1)}, f32[4,1024]{1,0:T(4,128)}, u32[]{:S(2)}) copy-start(f32[4,1024]{1,0:T(4,128)} %pot_ref.1) | copy-start | bytes 49156
  1.6 11.0 %collective-permute-start = (bf16[128,256]{1,0:T(8,128)(2,1)S(1)}, bf16[128,256]{1,0:T(8,128)(2,1)S(1)}, u32[]{:S(2)}, u32[]{:S(2)}) collective-permute-start(bf16[128,256]{1,0:T(8,128)(2,1)S(1)} %get-tuple-element.26), channel_id=1, source_target_pairs={{0,1},{1,0},{2,3},{3,2},{4,5},{5,4},{6,7},{7,6},{8,9},{9,8},{10,11... | collective-permute-start | bytes 196616 | tf_op jit(solution)/shard_map/ppermute | solution.py:414
  12.6 11.4 %copy-start.2 = (s32[16,2]{0,1:T(2,128)S(1)}, s32[16,2]{0,1:T(2,128)}, u32[]{:S(2)}) copy-start(s32[16,2]{0,1:T(2,128)} %param.7) | copy-start | bytes 388
  13.2 1.4 %collective-permute-start.1 = (bf16[3,128,128]{2,1,0:T(8,128)(2,1)S(1)}, bf16[3,128,128]{2,1,0:T(8,128)(2,1)S(1)}, u32[]{:S(2)}, u32[]{:S(2)}) collective-permute-start(bf16[3,128,128]{2,1,0:T(8,128)(2,1)S(1)} %get-tuple-element.34), channel_id=1, source_target_pairs={{0,1},{1,0},{2,3},{3,2},{4,5},{5,4},{6,7},{7,6},{8,9},{9,8},{10,11... | collective-permute-start | bytes 294920 | tf_op jit(solution)/shard_map/ppermute | solution.py:414
  22.6 1.4 %collective-permute-start.2 = (bf16[2,128,256]{2,1,0:T(8,128)(2,1)S(1)}, bf16[2,128,256]{2,1,0:T(8,128)(2,1)S(1)}, u32[]{:S(2)}, u32[]{:S(2)}) collective-permute-start(bf16[2,128,256]{2,1,0:T(8,128)(2,1)S(1)} %slice_select_fusion.across_in_ref), channel_id=1, source_target_pairs={{0,1},{1,0},{2,3},{3,2},{4,5},{5,4},{6,7},{7,6},{8,9},{9,8},{10,11... | collective-permute-start | bytes 393224 | tf_op jit(solution)/shard_map/ppermute | solution.py:414
  33.0 2.3 %collective-permute-start.3 = (bf16[128,256]{1,0:T(8,128)(2,1)S(1)}, bf16[128,256]{1,0:T(8,128)(2,1)S(1)}, u32[]{:S(2)}, u32[]{:S(2)}) collective-permute-start(bf16[128,256]{1,0:T(8,128)(2,1)S(1)} %get-tuple-element.37), channel_id=1, source_target_pairs={{0,1},{1,0},{2,3},{3,2},{4,5},{5,4},{6,7},{7,6},{8,9},{9,8},{10,11... | collective-permute-start | bytes 196616 | tf_op jit(solution)/shard_map/ppermute | solution.py:414

commit v5 on v3

--- a/solution.py
+++ b/solution.py
@@ -135,13 +135,16 @@
     for i in range(2):
         lanes = slice(128 * i, 128 * i + 128)
         mate_ref[:, lanes] = jnp.where(even, up[i], down[i]).astype(BF16)
-        across_ref[:, lanes] = jnp.where(even, down[i], up[i]).astype(BF16)
+        value = jnp.where(even, down[i], up[i]).astype(BF16)
+        across_ref[0, :, lanes] = value
+        across_ref[1, :, lanes] = value
 
 
 def sides(mate_ref, across_ref):
     mate = mate_ref[...].astype(F32)
-    across = jnp.where(at_end(), 0.0, across_ref[...].astype(F32))
     even = is_even()
+    across = jnp.where(even, across_ref[0].astype(F32), across_ref[1].astype(F32))
+    across = jnp.where(at_end(), 0.0, across)
     return (jnp.where(even, across, mate), jnp.where(even, mate, across))
 
 
@@ -254,6 +257,13 @@
     return jnp.where(low, 0.0, turned), jnp.where(low, turned, swapped(c2x))
 
 
+def picked(both_ref, even, which, rows, lanes):
+    slab = lax.axis_index("sx")
+    owner = jnp.where(even == is_even(), slab, slab + 1 - 2 * lax.rem(slab, 2))
+    value = jnp.where(even, both_ref[0, which, rows, lanes].astype(F32), both_ref[1, which, rows, lanes].astype(F32))
+    return jnp.where((owner == 0) | (owner == lax.axis_size("sx") - 1), 0.0, value)
+
+
 def relay_kernel(own_ref, rows_ref, out_ref):
     even = is_even()
     for which in range(2):
@@ -268,7 +278,7 @@
         )
         for i in range(2):
             for q in range(2):
-                value = jnp.where(at_end(), 0.0, parts[i][q]).astype(BF16)
+                value = parts[i][q].astype(BF16)
                 out_ref[which, ORB * i : ORB * i + ORB, 128 * q : 128 * q + 128] = value
 
 
@@ -294,10 +304,15 @@
     zero = jnp.zeros((ORB, 128), F32)
     for which, band_ref in enumerate((ham_ref, inv_ref)):
         near, rest = shifted(*mate_blocks(rows_ref, which))
-        ahead = across_in_ref[which, :, 0:128].astype(F32)
-        beside = across_in_ref[which, :, 128:256].astype(F32)
-        turned = swapped(relayed_ref[which, ORB:, 128:256].astype(F32))
-        far0 = jnp.where(low, swapped(relayed_ref[which, ORB:, 0:128].astype(F32)), turned)
+        ahead, beside = (
+            picked(across_in_ref, even, which, slice(0, 2 * ORB), slice(128 * i, 128 * i + 128))
+            for i in range(2)
+        )
+        front, turned = (
+            swapped(picked(relayed_ref, ~even, which, slice(ORB, 2 * ORB), slice(128 * i, 128 * i + 128)))
+            for i in range(2)
+        )
+        far0 = jnp.where(low, front, turned)
         far1 = jnp.where(low, turned, 0.0)
         got_even = (
             (ahead[:ORB], beside[:ORB], zero, zero),
@@ -408,21 +423,29 @@
 def per_device(pieces, potential, centers, pattern):
     count = lax.axis_size("sx")
     mates = [(i, i ^ 1) for i in range(count)]
-    others = [(0, 0), (count - 1, count - 1)]
-    others += [(i, i + 1 if i % 2 else i - 1) for i in range(1, count - 1)]
+    groups = lax.axis_size("grp")
+    pairs = []
+    for g in range(0, groups, 2):
+        for end in (0, count - 1):
+            pairs.append([g * count + end, g * count + count + end])
+    for g in range(groups):
+        pairs += [[g * count + i, g * count + i + 1] for i in range(1, count - 1, 2)]
 
     def to_mate(value):
         return lax.ppermute(value, "sx", mates)
 
     def across(value):
-        return lax.ppermute(value, "sx", others)
+        return lax.all_to_all(value, ("grp", "sx"), 0, 0, axis_index_groups=pairs)
+
+    def gathered(value):
+        return lax.all_gather(value, ("grp", "sx"), axis_index_groups=pairs)
 
     table = centers.T
     pair = shape(2, ROWS, PLANE)
 
     edge, edge_mask, rows, for_mate, for_other = pl.pallas_call(
         edges_kernel,
-        out_shape=(pair, pair, shape(ROWS, 16), shape(2 * ORB, HALF), shape(2 * ORB, HALF)),
+        out_shape=(pair, pair, shape(ROWS, 16), shape(2 * ORB, HALF), shape(2, 2 * ORB, HALF)),
         in_specs=[FAR, FAR],
         out_specs=(WHOLE,) * 5,
         scratch_shapes=[
@@ -469,19 +492,19 @@
         cost_estimate=cost(10**6, 10**6),
         name="relay",
     )(own, mate_rows)
-    other_rows = across(for_other)
-    relayed = to_mate(other_rows)
+    both_rows = gathered(for_other)
+    relayed = to_mate(both_rows)
 
     edge_grad, theta, for_mate, for_other = pl.pallas_call(
         gradient_kernel,
-        out_shape=(pair, shape(ROWS, ROWS), shape(2 * ORB, HALF), shape(2 * ORB, HALF)),
+        out_shape=(pair, shape(ROWS, ROWS), shape(2 * ORB, HALF), shape(2, 2 * ORB, HALF)),
         in_specs=[pl.BlockSpec(memory_space=pltpu.SMEM)] + [WHOLE] * 7,
         out_specs=(WHOLE,) * 4,
         scratch_shapes=[pltpu.VMEM((ROWS, 512), F32), pltpu.VMEM((ROWS, 512), F32)],
         compiler_params=PARAMS,
         cost_estimate=cost(10**9, 10**7),
         name="gradient",
-    )(pattern.T, own, mate_rows, other_rows, relayed, edge, edge_energy, edge_mask)
+    )(pattern.T, own, mate_rows, both_rows, relayed, edge, edge_energy, edge_mask)
     other_side = across(for_other)
     mate_side = to_mate(for_mate)
 

time: 29.1 us -> 41.9 us (1.44)
  the two profiles are of different devices: /device:TPU:0 before, /device:TPU:9 now
where the time goes in v5:
time: 41.9 us; the launch traced here: 41.4 us
  local copies, waits for them, and re-layouts  11.9 us (28%)
  Pallas kernels  11 us (26%)
  starting transfers between devices  9.01 us (22%)
  blocking collectives  6.47 us (15%)
  waiting for transfers between devices  2.83 us (7%)
    unnamed x30, local copies, waits for them, and re-layouts  11.9 us
    all_to_all x2, starting transfers between devices, across(): return lax.all_to_all(value, ('grp', 'sx'), 0, 0, axis_index_groups=pairs)  6.76 us
    all_gather x1, blocking collectives, gathered(): return lax.all_gather(value, ('grp', 'sx'), axis_index_groups=pairs)  6.47 us
    ppermute x4, waiting for transfers between devices, to_mate(): return lax.ppermute(value, 'sx', mates)  2.83 us
    pallas_call x1, Pallas kernels, per_device(): pl.pallas_call(gradient_kernel, out_shape=(pair, shape(ROWS, ROWS), shape...  2.63 us
    ppermute x4, starting transfers between devices, to_mate(): return lax.ppermute(value, 'sx', mates)  2.24 us
    pallas_call x1, Pallas kernels, per_device(): pl.pallas_call(edges_kernel, out_shape=(pair, pair, shape(ROWS, 16), shap...  2.17 us
    pallas_call x1, Pallas kernels, per_device(): pl.pallas_call(energy_kernel, out_shape=(pair, pair, pair, shape(2, ROWS,...  2.16 us
  transfers between devices with their start and end apart: 6, of which 2 were waited for; matrix products, arithmetic and copies ran while one was open for 0% of the time, Pallas kernels for 10%

profile of v5, /device:TPU:9, one launch (start us, length us, event | category | flops | bytes accessed | tf_op | source)
XLA Modules:
  0.0 41.4 jit_solution(11480202438267366163)
XLA Ops:
  0.0 2.2 %edges.1 = (bf16[2,192,1024]{2,1,0:T(8,128)(2,1)S(1)}, bf16[2,192,1024]{2,1,0:T(8,128)(2,1)S(1)}, bf16[192,16]{1,0:T(8,128)(2,1)S(1)}, bf16[128,256]{1,0:T(8,128)(2,1)}, bf16[2,128,256]{2,1,0:T(8,128)(2,1)}) custom-call(s32[4,1024]{1,0:T(4,128)} %bitcast.6, bf16[192,4096]{1,0:T(8,128)(2,1)} %pieces_ref.3), custom_call_target="tpu_custom_call" | custom-call | flops 100000000 | bytes 1000000 | tf_op jit(solution)/shard_map/edges/pallas_call | solution.py:446
  2.2 3.4 %all-to-all-start = ((bf16[2,128,256]{2,1,0:T(8,128)(2,1)}), bf16[2,128,256]{2,1,0:T(8,128)(2,1)S(1)}, u32[]{:S(2)}, u32[]{:S(2)}) async-start(bf16[2,128,256]{2,1,0:T(8,128)(2,1)} %get-tuple-element.25), calls=%async_computation | async-start | bytes 262144 | tf_op jit(solution)/shard_map/all_to_all | solution.py:438
  5.6 1.5 %collective-permute-start = (bf16[128,256]{1,0:T(8,128)(2,1)}, bf16[128,256]{1,0:T(8,128)(2,1)S(1)}, u32[]{:S(2)}, u32[]{:S(2)}) collective-permute-start(bf16[128,256]{1,0:T(8,128)(2,1)} %get-tuple-element.26), channel_id=1, source_target_pairs={{0,1},{1,0},{2,3},{3,2},{4,5},{5,4},{6,7},{7,6},{8,9},{9,8},{10,11... | collective-permute-start | bytes 196616 | tf_op jit(solution)/shard_map/ppermute | solution.py:435
  7.1 1.4 %copy-done = bf16[192,4096]{1,0:T(8,128)(2,1)S(1)} copy-done((bf16[192,4096]{1,0:T(8,128)(2,1)S(1)}, bf16[192,4096]{1,0:T(8,128)(2,1)}, u32[]{:S(2)}) %copy-start) | copy-done | bytes 1572888
  8.5 0.8 %copy-done.4 = bf16[192,16]{1,0:T(8,128)(2,1)S(1)} copy-done((bf16[192,16]{1,0:T(8,128)(2,1)S(1)}, bf16[192,16]{1,0:T(8,128)(2,1)}, u32[]{:S(2)}) %copy-start.4) | copy-done | bytes 6168
  9.3 2.2 %energy.1 = (bf16[2,192,1024]{2,1,0:T(8,128)(2,1)S(1)}, bf16[2,192,1024]{2,1,0:T(8,128)(2,1)S(1)}, bf16[2,192,1024]{2,1,0:T(8,128)(2,1)S(1)}, f32[2,192,1024]{2,...) custom-call(bf16[192,16]{1,0:T(8,128)(2,1)S(1)} %copy-done.4, bf16[192,4096]{1,0:T(8,128)(2,1)S(1)} %copy-done, ...), custom_call_target="tpu_custom_call" | custom-call | flops 4000000000 | bytes 10000000 | tf_op jit(solution)/shard_map/energy/pallas_call | solution.py:463
  11.5 0.7 %copy-done.1 = f32[192,192]{1,0:T(8,128)} copy-done((f32[192,192]{1,0:T(8,128)}, f32[192,192]{1,0:T(8,128)S(1)}, u32[]{:S(2)}) %copy-start.1) | copy-done | bytes 147480
  12.2 0.9 %copy-done.9 = bf16[2,192,1024]{2,1,0:T(8,128)(2,1)} copy-done((bf16[2,192,1024]{2,1,0:T(8,128)(2,1)}, bf16[2,192,1024]{2,1,0:T(8,128)(2,1)S(1)}, u32[]{:S(2)}) %copy-start.9) | copy-done | bytes 786456
  13.0 0.9 %copy-done.11 = bf16[2,192,1024]{2,1,0:T(8,128)(2,1)} copy-done((bf16[2,192,1024]{2,1,0:T(8,128)(2,1)}, bf16[2,192,1024]{2,1,0:T(8,128)(2,1)S(1)}, u32[]{:S(2)}) %copy-start.11) | copy-done | bytes 786456
  14.0 0.9 %copy-done.13 = bf16[2,192,1024]{2,1,0:T(8,128)(2,1)} copy-done((bf16[2,192,1024]{2,1,0:T(8,128)(2,1)}, bf16[2,192,1024]{2,1,0:T(8,128)(2,1)S(1)}, u32[]{:S(2)}) %copy-start.13) | copy-done | bytes 786456
  14.9 0.9 %copy-done.2 = f32[192,192]{1,0:T(8,128)S(1)} copy-done((f32[192,192]{1,0:T(8,128)S(1)}, f32[192,192]{1,0:T(8,128)}, u32[]{:S(2)}) %copy-start.2) | copy-done | bytes 147480
  16.5 1.3 %collective-permute-done.1.rows_ref = bf16[3,128,128]{2,1,0:T(8,128)(2,1)S(1)} collective-permute-done((bf16[3,128,128]{2,1,0:T(8,128)(2,1)S(1)}, bf16[3,128,128]{2,1,0:T(8,128)(2,1)S(1)}, u32[]{:S(2)}, u32[]{:S(2)}) %collective-permute-start.1) | collective-permute-done | bytes 98336 | tf_op jit(solution)/shard_map/ppermute | solution.py:435
  17.9 6.5 %all-gather = bf16[4,128,256]{2,1,0:T(8,128)(2,1)S(1)} all-gather(bf16[2,128,256]{2,1,0:T(8,128)(2,1)S(1)} %relay.1), channel_id=2, replica_groups={{0,16},{15,31},{1,2},{3,4},{5,6},{7,8},{9,10},{11,12},{13,14},{17,18},{..., dimensions={0}, use_global_device_ids=true | all-gather | bytes 393216 | tf_op jit(solution)/shard_map/all_gather | solution.py:441
  24.4 1.5 %collective-permute-done.2.relayed_ref = bf16[2,2,128,256]{3,2,1,0:T(8,128)(2,1)S(1)} collective-permute-done((bf16[2,2,128,256]{3,2,1,0:T(8,128)(2,1)S(1)}, bf16[2,2,128,256]{3,2,1,0:T(8,128)(2,1)S(1)}, u32[]{:S(2)}, u32[]{:S(2)}) %collective-permute-start.2) | collective-permute-done | bytes 262176 | tf_op jit(solution)/shard_map/ppermute | solution.py:435
  25.9 2.6 %gradient.1 = (bf16[2,192,1024]{2,1,0:T(8,128)(2,1)S(1)}, bf16[192,192]{1,0:T(8,128)(2,1)S(1)}, bf16[128,256]{1,0:T(8,128)(2,1)S(1)}, bf16[2,128,256]{2,1,0:T(8,128)(2,1)}) custom-call(s32[2,16]{1,0:T(2,128)S(1)} %bitcast.5, f32[2,192,256]{2,1,0:T(8,128)S(1)} %get-tuple-element.33.own_ref, bf16[3,128,128]{2,1,0:T(8,128)(2,1)S(1)} %collective-permute-done.1.rows_ref, ...), custom_call_target="tpu_custom_call" | custom-call | flops 1000000000 | bytes 10000000 | tf_op jit(solution)/shard_map/gradient/pallas_call | solution.py:498
  28.6 0.9 %copy-done.7 = bf16[2,192,1024]{2,1,0:T(8,128)(2,1)} copy-done((bf16[2,192,1024]{2,1,0:T(8,128)(2,1)}, bf16[2,192,1024]{2,1,0:T(8,128)(2,1)S(1)}, u32[]{:S(2)}) %copy-start.7) | copy-done | bytes 786456
  29.4 3.4 %all-to-all-start.1 = ((bf16[2,128,256]{2,1,0:T(8,128)(2,1)}), bf16[2,128,256]{2,1,0:T(8,128)(2,1)S(1)}, u32[]{:S(2)}, u32[]{:S(2)}) async-start(bf16[2,128,256]{2,1,0:T(8,128)(2,1)} %get-tuple-element.36), calls=%async_computation.1 | async-start | bytes 262144 | tf_op jit(solution)/shard_map/all_to_all | solution.py:438
  32.8 0.7 %collective-permute-start.3 = (bf16[128,256]{1,0:T(8,128)(2,1)S(1)}, bf16[128,256]{1,0:T(8,128)(2,1)S(1)}, u32[]{:S(2)}, u32[]{:S(2)}) collective-permute-start(bf16[128,256]{1,0:T(8,128)(2,1)S(1)} %get-tuple-element.37), channel_id=1, source_target_pairs={{0,1},{1,0},{2,3},{3,2},{4,5},{5,4},{6,7},{7,6},{8,9},{9,8},{10,11... | collective-permute-start | bytes 196616 | tf_op jit(solution)/shard_map/ppermute | solution.py:435
  33.5 1.1 %copy-done.8 = bf16[2,192,1024]{2,1,0:T(8,128)(2,1)S(1)} copy-done((bf16[2,192,1024]{2,1,0:T(8,128)(2,1)S(1)}, bf16[2,192,1024]{2,1,0:T(8,128)(2,1)}, u32[]{:S(2)}) %copy-start.8) | copy-done | bytes 786456
  34.6 1.1 %copy-done.10 = bf16[2,192,1024]{2,1,0:T(8,128)(2,1)S(1)} copy-done((bf16[2,192,1024]{2,1,0:T(8,128)(2,1)S(1)}, bf16[2,192,1024]{2,1,0:T(8,128)(2,1)}, u32[]{:S(2)}) %copy-start.10) | copy-done | bytes 786456
  35.8 1.1 %copy-done.12 = bf16[2,192,1024]{2,1,0:T(8,128)(2,1)S(1)} copy-done((bf16[2,192,1024]{2,1,0:T(8,128)(2,1)S(1)}, bf16[2,192,1024]{2,1,0:T(8,128)(2,1)}, u32[]{:S(2)}) %copy-start.12) | copy-done | bytes 786456
  36.9 1.1 %copy-done.14 = bf16[2,192,1024]{2,1,0:T(8,128)(2,1)S(1)} copy-done((bf16[2,192,1024]{2,1,0:T(8,128)(2,1)S(1)}, bf16[2,192,1024]{2,1,0:T(8,128)(2,1)}, u32[]{:S(2)}) %copy-start.14) | copy-done | bytes 786456
  38.0 2.2 %smooth.1 = (bf16[192,4096]{1,0:T(8,128)(2,1)}, f32[2,192,1024]{2,1,0:T(8,128)S(1)}) custom-call(bf16[192,192]{1,0:T(8,128)(2,1)S(1)} %get-tuple-element.38.theta_ref, bf16[2,192,1024]{2,1,0:T(8,128)(2,1)S(1)} %copy-done.10, bf16[2,192,1024]{2,1,0:T(8,128)(2,1)S(1)} %copy-done.14, bf16[2,192,1024]{2,1,0:T(8,128)(2,1)S(1)} %copy-done.8, ...), custom_call_target="tpu_custom_call" | custom-call | flops 2000000000 | bytes 10000000 | tf_op jit(solution)/shard_map/smooth/pallas_call | solution.py:511
  40.2 1.1 %finish.1 = bf16[192,4096]{1,0:T(8,128)(2,1)} custom-call(bf16[2,128,256]{2,1,0:T(8,128)(2,1)S(1)} %all-to-all-done.1.across_ref, bf16[128,256]{1,0:T(8,128)(2,1)S(1)} %collective-permute-done.3.mate_ref, f32[2,192,1024]{2,1,0:T(8,128)S(1)} %get-tuple-element.43.part_ref, ...), custom_call_target="tpu_custom_call", output_to_operand_aliasing={{}: (4, {})} | custom-call | flops 10000000 | bytes 10000000 | tf_op jit(solution)/shard_map/finish/pallas_call | solution.py:526
  (26 shorter events, 0.9 us)
Async XLA Ops:
  0.0 7.1 %copy-start.5 = (f32[4,1024]{1,0:T(4,128)S(1)}, f32[4,1024]{1,0:T(4,128)}, u32[]{:S(2)}) copy-start(f32[4,1024]{1,0:T(4,128)} %pot_ref.1) | copy-start | bytes 49156
  2.2 4.9 %copy-start.3 = (bf16[192,16]{1,0:T(8,128)(2,1)}, bf16[192,16]{1,0:T(8,128)(2,1)S(1)}, u32[]{:S(2)}) copy-start(bf16[192,16]{1,0:T(8,128)(2,1)S(1)} %get-tuple-element.27.rows_ref) | copy-start | bytes 18436
  2.2 12.7 %all-to-all-start = ((bf16[2,128,256]{2,1,0:T(8,128)(2,1)}), bf16[2,128,256]{2,1,0:T(8,128)(2,1)S(1)}, u32[]{:S(2)}, u32[]{:S(2)}) async-start(bf16[2,128,256]{2,1,0:T(8,128)(2,1)} %get-tuple-element.25), calls=%async_computation | async-start | bytes 262144 | tf_op jit(solution)/shard_map/all_to_all | solution.py:438
  5.6 9.3 %collective-permute-start = (bf16[128,256]{1,0:T(8,128)(2,1)}, bf16[128,256]{1,0:T(8,128)(2,1)S(1)}, u32[]{:S(2)}, u32[]{:S(2)}) collective-permute-start(bf16[128,256]{1,0:T(8,128)(2,1)} %get-tuple-element.26), channel_id=1, source_target_pairs={{0,1},{1,0},{2,3},{3,2},{4,5},{5,4},{6,7},{7,6},{8,9},{9,8},{10,11... | collective-permute-start | bytes 196616 | tf_op jit(solution)/shard_map/ppermute | solution.py:435
  7.1 1.4 %copy-start = (bf16[192,4096]{1,0:T(8,128)(2,1)S(1)}, bf16[192,4096]{1,0:T(8,128)(2,1)}, u32[]{:S(2)}) copy-start(bf16[192,4096]{1,0:T(8,128)(2,1)} %pieces_ref.3) | copy-start | bytes 4718596
  8.5 0.8 %copy-start.4 = (bf16[192,16]{1,0:T(8,128)(2,1)S(1)}, bf16[192,16]{1,0:T(8,128)(2,1)}, u32[]{:S(2)}) copy-start(bf16[192,16]{1,0:T(8,128)(2,1)} %copy-done.3) | copy-start | bytes 18436
  11.5 0.7 %copy-start.1 = (f32[192,192]{1,0:T(8,128)}, f32[192,192]{1,0:T(8,128)S(1)}, u32[]{:S(2)}) copy-start(f32[192,192]{1,0:T(8,128)S(1)} %get-tuple-element.32.ham_ref) | copy-start | bytes 442372
  12.2 0.9 %copy-start.9 = (bf16[2,192,1024]{2,1,0:T(8,128)(2,1)}, bf16[2,192,1024]{2,1,0:T(8,128)(2,1)S(1)}, u32[]{:S(2)}) copy-start(bf16[2,192,1024]{2,1,0:T(8,128)(2,1)S(1)} %get-tuple-element.39.phi_ref) | copy-start | bytes 2359300
  13.0 0.9 %copy-start.11 = (bf16[2,192,1024]{2,1,0:T(8,128)(2,1)}, bf16[2,192,1024]{2,1,0:T(8,128)(2,1)S(1)}, u32[]{:S(2)}) copy-start(bf16[2,192,1024]{2,1,0:T(8,128)(2,1)S(1)} %get-tuple-element.42.mask_ref) | copy-start | bytes 2359300
  14.0 0.9 %copy-start.13 = (bf16[2,192,1024]{2,1,0:T(8,128)(2,1)}, bf16[2,192,1024]{2,1,0:T(8,128)(2,1)S(1)}, u32[]{:S(2)}) copy-start(bf16[2,192,1024]{2,1,0:T(8,128)(2,1)S(1)} %get-tuple-element.40.energy_ref) | copy-start | bytes 2359300
  14.9 0.9 %copy-start.2 = (f32[192,192]{1,0:T(8,128)S(1)}, f32[192,192]{1,0:T(8,128)}, u32[]{:S(2)}) copy-start(f32[192,192]{1,0:T(8,128)} %copy-done.1) | copy-start | bytes 442372
  15.8 10.1 %copy-start.6 = (s32[16,2]{0,1:T(2,128)S(1)}, s32[16,2]{0,1:T(2,128)}, u32[]{:S(2)}) copy-start(s32[16,2]{0,1:T(2,128)} %param.7) | copy-start | bytes 388
  16.4 1.4 %collective-permute-start.1 = (bf16[3,128,128]{2,1,0:T(8,128)(2,1)S(1)}, bf16[3,128,128]{2,1,0:T(8,128)(2,1)S(1)}, u32[]{:S(2)}, u32[]{:S(2)}) collective-permute-start(bf16[3,128,128]{2,1,0:T(8,128)(2,1)S(1)} %get-tuple-element.34), channel_id=1, source_target_pairs={{0,1},{1,0},{2,3},{3,2},{4,5},{5,4},{6,7},{7,6},{8,9},{9,8},{10,11... | collective-permute-start | bytes 294920 | tf_op jit(solution)/shard_map/ppermute | solution.py:435
  24.4 1.5 %collective-permute-start.2 = (bf16[2,2,128,256]{3,2,1,0:T(8,128)(2,1)S(1)}, bf16[2,2,128,256]{3,2,1,0:T(8,128)(2,1)S(1)}, u32[]{:S(2)}, u32[]{:S(2)}) collective-permute-start(bf16[2,2,128,256]{3,2,1,0:T(8,128)(2,1)S(1)} %bitcast.3), channel_id=1, source_target_pairs={{0,1},{1,0},{2,3},{3,2},{4,5},{5,4},{6,7},{7,6},{8,9},{9,8},{10,11... | collective-permute-start | bytes 786440 | tf_op jit(solution)/shard_map/ppermute | solution.py:435
  28.6 0.9 %copy-start.7 = (bf16[2,192,1024]{2,1,0:T(8,128)(2,1)}, bf16[2,192,1024]{2,1,0:T(8,128)(2,1)S(1)}, u32[]{:S(2)}) copy-start(bf16[2,192,1024]{2,1,0:T(8,128)(2,1)S(1)} %get-tuple-element.41.edge_ref) | copy-start | bytes 2359300
  29.4 10.8 %all-to-all-start.1 = ((bf16[2,128,256]{2,1,0:T(8,128)(2,1)}), bf16[2,128,256]{2,1,0:T(8,128)(2,1)S(1)}, u32[]{:S(2)}, u32[]{:S(2)}) async-start(bf16[2,128,256]{2,1,0:T(8,128)(2,1)} %get-tuple-element.36), calls=%async_computation.1 | async-start | bytes 262144 | tf_op jit(solution)/shard_map/all_to_all | solution.py:438
  32.8 7.4 %collective-permute-start.3 = (bf16[128,256]{1,0:T(8,128)(2,1)S(1)}, bf16[128,256]{1,0:T(8,128)(2,1)S(1)}, u32[]{:S(2)}, u32[]{:S(2)}) collective-permute-start(bf16[128,256]{1,0:T(8,128)(2,1)S(1)} %get-tuple-element.37), channel_id=1, source_target_pairs={{0,1},{1,0},{2,3},{3,2},{4,5},{5,4},{6,7},{7,6},{8,9},{9,8},{10,11... | collective-permute-start | bytes 196616 | tf_op jit(solution)/shard_map/ppermute | solution.py:435
  33.5 1.1 %copy-start.8 = (bf16[2,192,1024]{2,1,0:T(8,128)(2,1)S(1)}, bf16[2,192,1024]{2,1,0:T(8,128)(2,1)}, u32[]{:S(2)}) copy-start(bf16[2,192,1024]{2,1,0:T(8,128)(2,1)} %copy-done.7) | copy-start | bytes 2359300
  34.6 1.1 %copy-start.10 = (bf16[2,192,1024]{2,1,0:T(8,128)(2,1)S(1)}, bf16[2,192,1024]{2,1,0:T(8,128)(2,1)}, u32[]{:S(2)}) copy-start(bf16[2,192,1024]{2,1,0:T(8,128)(2,1)} %copy-done.9) | copy-start | bytes 2359300
  35.8 1.1 %copy-start.12 = (bf16[2,192,1024]{2,1,0:T(8,128)(2,1)S(1)}, bf16[2,192,1024]{2,1,0:T(8,128)(2,1)}, u32[]{:S(2)}) copy-start(bf16[2,192,1024]{2,1,0:T(8,128)(2,1)} %copy-done.11) | copy-start | bytes 2359300
  36.9 1.1 %copy-start.14 = (bf16[2,192,1024]{2,1,0:T(8,128)(2,1)S(1)}, bf16[2,192,1024]{2,1,0:T(8,128)(2,1)}, u32[]{:S(2)}) copy-start(bf16[2,192,1024]{2,1,0:T(8,128)(2,1)} %copy-done.13) | copy-start | bytes 2359300

commit v6 on v3

--- a/solution.py
+++ b/solution.py
@@ -123,11 +123,6 @@
     return lax.rem(lax.axis_index("sx"), 2) == 0
 
 
-def at_end():
-    slab = lax.axis_index("sx")
-    return (slab == 0) | (slab == lax.axis_size("sx") - 1)
-
-
 def put_messages(planes, mate_ref, across_ref):
     down = fold(planes[0, : 2 * ORB].astype(F32))
     up = fold(planes[1, ORB:].astype(F32))
@@ -140,7 +135,7 @@
 
 def sides(mate_ref, across_ref):
     mate = mate_ref[...].astype(F32)
-    across = jnp.where(at_end(), 0.0, across_ref[...].astype(F32))
+    across = across_ref[...].astype(F32)
     even = is_even()
     return (jnp.where(even, across, mate), jnp.where(even, mate, across))
 
@@ -209,6 +204,10 @@
     return slice(0, 2 * ORB) if i == 0 else slice(ORB, ROWS)
 
 
+def rest_rows(i):
+    return slice(2 * ORB, ROWS) if i == 0 else slice(0, ORB)
+
+
 def bands_kernel(
     across_ref, mate_ref, part_ref, mask_ref, phi_ref, corr_ref, ham_ref,
     energy_ref, own_ref, rows_ref,
@@ -217,7 +216,7 @@
     ham = ham_ref[...]
     for i, side in enumerate(sides(mate_ref, across_ref)):
         tiles = unfold(side)
-        rest = slice(2 * ORB, ROWS) if i == 0 else slice(0, ORB)
+        rest = rest_rows(i)
         for t in range(PLANE // 128):
             lanes = slice(128 * t, 128 * t + 128)
             value = part_ref[i, halo_rows(i), lanes] - 0.5 * tiles[t % 4]
@@ -256,20 +255,25 @@
 
 def relay_kernel(own_ref, rows_ref, out_ref):
     even = is_even()
+    heads = []
     for which in range(2):
         head, rest = shifted(own_ref[which, :, 0:128], own_ref[which, :, 128:256])
         c01, c2x = mate_blocks(rows_ref, which)
         c01 = jnp.where(even, c01[:ORB], c01[ORB:])
         c2x = jnp.where(even, c2x[:ORB], c2x[ORB:])
         own = slice(ORB, 2 * ORB)
-        parts = (
-            (head[own] + jnp.where(even, c2x, c01), rest[own] + jnp.where(even, c01, c2x)),
-            (jnp.where(even, head[:ORB], head[2 * ORB :]), jnp.where(even, rest[:ORB], rest[2 * ORB :])),
-        )
-        for i in range(2):
-            for q in range(2):
-                value = jnp.where(at_end(), 0.0, parts[i][q]).astype(BF16)
-                out_ref[which, ORB * i : ORB * i + ORB, 128 * q : 128 * q + 128] = value
+        out_ref[2 * which] = (head[own] + jnp.where(even, c2x, c01)).astype(BF16)
+        out_ref[2 * which + 1] = (rest[own] + jnp.where(even, c01, c2x)).astype(BF16)
+        out_ref[5 + which] = jnp.where(even, rest[:ORB], rest[2 * ORB :]).astype(BF16)
+        heads.append(jnp.where(even, head[:ORB], head[2 * ORB :]))
+    out_ref[4] = jnp.where(low_half(), swapped(heads[1]), heads[0]).astype(BF16)
+
+
+def shared_head(tile, which):
+    tile = tile.astype(F32)
+    if which == 1:
+        tile = swapped(tile)
+    return jnp.where(low_half(), 0.0, tile)
 
 
 def put_gradient(theta, orbital_ref, energy_ref, mask_ref, out_ref):
@@ -281,69 +285,97 @@
             out_ref[i, :, lanes] = value.astype(BF16) * mask_ref[i, :, lanes]
 
 
-def gradient_kernel(
-    pattern_ref, own_ref, rows_ref, across_in_ref, relayed_ref,
-    edge_ref, edge_energy_ref, edge_mask_ref,
-    edge_grad_ref, theta_ref, mate_ref, across_ref,
-    ham_ref, inv_ref,
-):
+def kept(pattern_ref, r, q):
     slab = lax.axis_index("sx")
+    last = pattern_ref.shape[1] - 1
+    values = []
+    for col in (2 * q, 2 * q + 1):
+        apart = abs(col - r - 2)
+        if apart == 0:
+            values.append(1.0)
+        elif apart > 2:
+            values.append(0.0)
+        else:
+            at = jnp.clip(slab - 3 + min(col, r + 2), 0, last)
+            values.append(pattern_ref[apart - 1, at].astype(F32))
+    return jnp.where(low_half(), values[0], values[1])
+
+
+def split(value):
+    high = value.astype(BF16)
+    return high, (value - high.astype(F32)).astype(BF16)
+
+
+def fine_product(a, b):
+    return rows_product(a[0], b[0]) + (rows_product(a[0], b[1]) + rows_product(a[1], b[0]))
+
+
+def theta_kernel(pattern_ref, own_ref, rows_ref, other_ref, ham_ref, inv_ref, theta_ref):
     even = is_even()
-    last = pattern_ref.shape[1] - 1
     low = low_half()
     zero = jnp.zeros((ORB, 128), F32)
     for which, band_ref in enumerate((ham_ref, inv_ref)):
         near, rest = shifted(*mate_blocks(rows_ref, which))
-        ahead = across_in_ref[which, :, 0:128].astype(F32)
-        beside = across_in_ref[which, :, 128:256].astype(F32)
-        turned = swapped(relayed_ref[which, ORB:, 128:256].astype(F32))
-        far0 = jnp.where(low, swapped(relayed_ref[which, ORB:, 0:128].astype(F32)), turned)
-        far1 = jnp.where(low, turned, 0.0)
+        ahead = other_ref[2 * which].astype(F32)
+        beside = other_ref[2 * which + 1].astype(F32)
+        head = shared_head(other_ref[4], which)
+        tail = other_ref[5 + which].astype(F32)
         got_even = (
-            (ahead[:ORB], beside[:ORB], zero, zero),
-            (ahead[ORB:], beside[ORB:] + near[:ORB], rest[:ORB], zero),
-            (zero, near[ORB:], rest[ORB:] + far0, far1),
+            (ahead, beside, zero, zero),
+            (head, tail + near[:ORB], rest[:ORB], zero),
+            (zero, near[ORB:], rest[ORB:], zero),
         )
-        ahead_high = jnp.where(low, 0.0, ahead)
-        ahead_low = jnp.where(low, ahead, 0.0)
         got_odd = (
-            (near[:ORB] + far0, rest[:ORB] + far1, zero, zero),
-            (near[ORB:], rest[ORB:] + ahead_high[ORB:], beside[ORB:], zero),
-            (zero, ahead_high[:ORB], beside[:ORB], ahead_low[:ORB]),
+            (near[:ORB], rest[:ORB], zero, zero),
+            (near[ORB:], rest[ORB:] + head, tail, zero),
+            (zero, jnp.where(low, 0.0, ahead), beside, jnp.where(low, ahead, 0.0)),
         )
         for r in range(3):
             for q in range(4):
-                kept = []
-                for col in (2 * q, 2 * q + 1):
-                    apart = abs(col - r - 2)
-                    if apart == 0:
-                        kept.append(1.0)
-                    elif apart > 2:
-                        kept.append(0.0)
-                    else:
-                        at = jnp.clip(slab - 3 + min(col, r + 2), 0, last)
-                        kept.append(pattern_ref[apart - 1, at].astype(F32))
                 value = jnp.where(even, got_even[r][q], got_odd[r][q])
                 if q in (1, 2):
                     value = value + own_ref[which, ORB * r : ORB * r + ORB, 128 * q - 128 : 128 * q]
-                value = value * jnp.where(low, kept[0], kept[1])
+                value = value * kept(pattern_ref, r, q)
                 if which == 1:
                     on = iota((ORB, 128), 0) + (ORB * (r + 2) - 128 * q) == iota((ORB, 128), 1)
                     value = jnp.where(on, 2.0, 0.0) - value
                 band_ref[ORB * r : ORB * r + ORB, 128 * q : 128 * q + 128] = value
-    theta = lax.dot_general(
-        ham_ref[...], inv_ref[...], (((1,), (1,)), ((), ())),
-        precision=lax.Precision.HIGHEST, preferred_element_type=F32,
-    ).astype(BF16)
+    theta_ref[...] = fine_product(split(ham_ref[...]), split(inv_ref[...]))
+
+
+def gradient_kernel(
+    pattern_ref, relayed_ref, ham_ref, inv_ref, base_ref,
+    edge_ref, edge_energy_ref, edge_mask_ref,
+    edge_grad_ref, theta_ref, mate_ref, across_ref,
+    more_ref,
+):
+    even = is_even()
+    low = low_half()
+    for which in range(2):
+        front = swapped(shared_head(relayed_ref[0], which))
+        turned = swapped(relayed_ref[1 + which].astype(F32))
+        for q, value in enumerate((jnp.where(low, front, turned), jnp.where(low, turned, 0.0))):
+            value = value * jnp.where(even, kept(pattern_ref, 2, 2 + q), kept(pattern_ref, 0, q))
+            if which == 1:
+                value = -value
+            lanes = slice(128 * q, 128 * q + 128)
+            more_ref[which, :ORB, lanes] = jnp.where(even, 0.0, value)
+            more_ref[which, ORB : 2 * ORB, lanes] = jnp.zeros((ORB, 128), F32)
+            more_ref[which, 2 * ORB :, lanes] = jnp.where(even, value, 0.0)
+    ham = jnp.where(even, ham_ref[:, 256:512], ham_ref[:, 0:256]) + more_ref[0]
+    inv = jnp.where(even, inv_ref[:, 256:512], inv_ref[:, 0:256])
+    theta = base_ref[...] + fine_product(split(ham), split(more_ref[1]))
+    theta = theta + fine_product(split(more_ref[0]), split(inv))
+    theta = theta.astype(BF16)
     theta_ref[...] = theta
     put_gradient(theta, edge_ref, edge_energy_ref, edge_mask_ref, edge_grad_ref)
     put_messages(edge_grad_ref, mate_ref, across_ref)
 
 
 def smooth_kernel(
-    theta_ref, phi_ref, energy_ref, edge_ref, mask_ref,
+    theta_ref, phi_ref, energy_ref, edge_ref, mask_ref, edge_mask_ref,
     out_ref, part_ref,
-    grad_ref, done_ref, sems,
+    grad_ref, done_ref, rest_ref, sems,
 ):
     put_gradient(theta_ref[...], phi_ref, energy_ref, mask_ref, grad_ref)
     weights = in_plane(8, 1)
@@ -357,13 +389,24 @@
             value = (inner[i] + (edge[i] + mid[1 - i])) * (1.0 / 32.0)
             done_ref[i, :, lanes] = value.astype(BF16) * mask_ref[i, :, lanes]
             part_ref[i, :, lanes] = outer[i] + mid[i]
+        for i in range(2):
+            rows = rest_rows(i)
+            value = part_ref[i, rows, lanes] * (1.0 / 32.0)
+            rest_ref[i, :, lanes] = value.astype(BF16) * edge_mask_ref[i, rows, lanes]
     copies = []
     for i in range(2):
         start = PLANE * (1 + i)
         copies.append(
             pltpu.make_async_copy(done_ref.at[i], out_ref.at[:, start : start + PLANE], sems.at[i])
         )
-        copies[i].start()
+        start = PLANE * (CX - 1) * i
+        copies.append(
+            pltpu.make_async_copy(
+                rest_ref.at[i], out_ref.at[rest_rows(i), start : start + PLANE], sems.at[2 + i]
+            )
+        )
+    for copy in copies:
+        copy.start()
     for copy in copies:
         copy.wait()
 
@@ -372,18 +415,20 @@
     copies = []
     for i, side in enumerate(sides(mate_ref, across_ref)):
         tiles = unfold(side)
-        rest = slice(2 * ORB, ROWS) if i == 0 else slice(0, ORB)
-        for t in range(PLANE // 128):
-            lanes = slice(128 * t, 128 * t + 128)
-            value = (part_ref[i, halo_rows(i), lanes] + tiles[t % 4]) * (1.0 / 32.0)
-            done_ref[i, halo_rows(i), lanes] = value.astype(BF16) * mask_ref[i, halo_rows(i), lanes]
-            value = part_ref[i, rest, lanes] * (1.0 / 32.0)
-            done_ref[i, rest, lanes] = value.astype(BF16) * mask_ref[i, rest, lanes]
-        start = PLANE * (CX - 1) * i
-        copies.append(
-            pltpu.make_async_copy(done_ref.at[i], out_ref.at[:, start : start + PLANE], sems.at[i])
-        )
-        copies[i].start()
+        for half in range(2):
+            rows = slice(ORB * (half + i), ORB * (half + i) + ORB)
+            got = slice(ORB * half, ORB * half + ORB)
+            for t in range(PLANE // 128):
+                lanes = slice(128 * t, 128 * t + 128)
+                value = (part_ref[i, rows, lanes] + tiles[t % 4][got]) * (1.0 / 32.0)
+                done_ref[2 * i + half, :, lanes] = value.astype(BF16) * mask_ref[i, rows, lanes]
+            start = PLANE * (CX - 1) * i
+            copies.append(
+                pltpu.make_async_copy(
+                    done_ref.at[2 * i + half], out_ref.at[rows, start : start + PLANE], sems.at[2 * i + half]
+                )
+            )
+            copies[-1].start()
     for copy in copies:
         copy.wait()
 
@@ -408,14 +453,25 @@
 def per_device(pieces, potential, centers, pattern):
     count = lax.axis_size("sx")
     mates = [(i, i ^ 1) for i in range(count)]
-    others = [(0, 0), (count - 1, count - 1)]
-    others += [(i, i + 1 if i % 2 else i - 1) for i in range(1, count - 1)]
+    others = [(i, i + 1 if i % 2 else i - 1) for i in range(1, count - 1)]
+    groups = lax.axis_size("grp")
+    pairs = [[g * count + i, g * count + i + 1] for g in range(groups) for i in range(1, count - 1, 2)]
+    ends = [g * count + end for g in range(groups) for end in (0, count - 1)]
+    pairs += [[ends[i], ends[i + 2]] for i in range(len(ends)) if i % 4 < 2] if groups % 2 == 0 else [
+        [ends[2 * i], ends[2 * i + 1]] for i in range(groups)
+    ]
+    slab = lax.axis_index("sx")
 
     def to_mate(value):
         return lax.ppermute(value, "sx", mates)
 
     def across(value):
         return lax.ppermute(value, "sx", others)
+
+    def gathered(value):
+        both = lax.all_gather(value, ("grp", "sx"), axis_index_groups=pairs)
+        got = jnp.where(slab % 2 == 1, both[1], both[0])
+        return jnp.where((slab == 0) | (slab == count - 1), jnp.zeros((), value.dtype), got)
 
     table = centers.T
     pair = shape(2, ROWS, PLANE)
@@ -462,50 +518,63 @@
     mate_rows = to_mate(for_mate)
     for_other = pl.pallas_call(
         relay_kernel,
-        out_shape=shape(2, 2 * ORB, TILE),
+        out_shape=shape(7, ORB, 128),
         in_specs=[WHOLE] * 2,
         out_specs=WHOLE,
         compiler_params=PARAMS,
         cost_estimate=cost(10**6, 10**6),
         name="relay",
     )(own, mate_rows)
-    other_rows = across(for_other)
-    relayed = to_mate(other_rows)
-
+    other_rows = gathered(for_other)
+    relayed = to_mate(other_rows[4:])
+
+    patterns = pattern.T
+    scalars = pl.BlockSpec(memory_space=pltpu.SMEM)
+    band = shape(ROWS, 8 * ORB, dtype=F32)
+    ham_band, inv_band, base = pl.pallas_call(
+        theta_kernel,
+        out_shape=(band, band, shape(ROWS, ROWS, dtype=F32)),
+        in_specs=[scalars] + [WHOLE] * 3,
+        out_specs=(WHOLE,) * 3,
+        compiler_params=PARAMS,
+        cost_estimate=cost(10**9, 4 * 10**6),
+        name="theta",
+    )(patterns, own, mate_rows, other_rows)
     edge_grad, theta, for_mate, for_other = pl.pallas_call(
         gradient_kernel,
         out_shape=(pair, shape(ROWS, ROWS), shape(2 * ORB, HALF), shape(2 * ORB, HALF)),
-        in_specs=[pl.BlockSpec(memory_space=pltpu.SMEM)] + [WHOLE] * 7,
+        in_specs=[scalars] + [WHOLE] * 7,
         out_specs=(WHOLE,) * 4,
-        scratch_shapes=[pltpu.VMEM((ROWS, 512), F32), pltpu.VMEM((ROWS, 512), F32)],
+        scratch_shapes=[pltpu.VMEM((2, ROWS, TILE), F32)],
         compiler_params=PARAMS,
         cost_estimate=cost(10**9, 10**7),
         name="gradient",
-    )(pattern.T, own, mate_rows, other_rows, relayed, edge, edge_energy, edge_mask)
+    )(patterns, relayed, ham_band, inv_band, base, edge, edge_energy, edge_mask)
     other_side = across(for_other)
     mate_side = to_mate(for_mate)
 
     inner, part = pl.pallas_call(
         smooth_kernel,
         out_shape=(pltpu.HBM((ROWS, CX * PLANE), BF16), shape(2, ROWS, PLANE, dtype=F32)),
-        in_specs=[WHOLE] * 5,
+        in_specs=[WHOLE] * 6,
         out_specs=(FAR, WHOLE),
         scratch_shapes=[
             pltpu.VMEM((2, ROWS, PLANE), BF16),
             pltpu.VMEM((2, ROWS, PLANE), BF16),
-            pltpu.SemaphoreType.DMA((2,)),
+            pltpu.VMEM((2, ORB, PLANE), BF16),
+            pltpu.SemaphoreType.DMA((4,)),
         ],
         compiler_params=PARAMS,
         cost_estimate=cost(2 * 10**9, 10**7),
         name="smooth",
-    )(theta, mid, mid_energy, edge_grad, mid_mask)
+    )(theta, mid, mid_energy, edge_grad, mid_mask, edge_mask)
 
     return pl.pallas_call(
         finish_kernel,
         out_shape=pltpu.HBM((ROWS, CX * PLANE), BF16),
         in_specs=[WHOLE] * 4 + [FAR],
         out_specs=FAR,
-        scratch_shapes=[pltpu.VMEM((2, ROWS, PLANE), BF16), pltpu.SemaphoreType.DMA((2,))],
+        scratch_shapes=[pltpu.VMEM((4, ORB, PLANE), BF16), pltpu.SemaphoreType.DMA((4,))],
         input_output_aliases={4: 0},
         compiler_params=PARAMS,
         cost_estimate=cost(10**7, 10**7),

time: 29.1 us -> 27.7 us (0.952); the launches traced: 28.6 us -> 27.6 us
  starting transfers between devices: 16.4 us -> 9.11 us
  blocking collectives: 0 us -> 5.46 us
  Pallas kernels: 9.76 us -> 10.7 us
  waiting for transfers between devices: 2.27 us -> 1.43 us
  local copies, waits for them, and re-layouts: 0.01 us -> 0.74 us
    ppermute x4, starting transfers between devices: 14.4 us -> 7.78 us  [to_mate(): return lax.ppermute(value, 'sx', mates)]
    all_gather x0 -> x1, blocking collectives: none -> 5.46 us  [gathered(): both = lax.all_gather(value, ('grp', 'sx'), axis_index_groups=pairs)]
    pallas_call x1 -> x2, Pallas kernels: 0.15 us -> 1.24 us  [the longest x1 1.06 us: per_device(): pl.pallas_call(theta_kernel, out_shape=(band, band, shape(ROWS, ROWS, dty...]
    ppermute x4, waiting for transfers between devices: 2.26 us -> 1.42 us  [to_mate(): return lax.ppermute(value, 'sx', mates)]
    unnamed x6 -> x18, local copies, waits for them, and re-layouts: 0.01 us -> 0.74 us
    ppermute x3 -> x2, starting transfers between devices: 2 us -> 1.33 us  [across(): return lax.ppermute(value, 'sx', others)]
  transfers between devices with their start and end apart: 7 -> 6, of which waited for: 2 -> 2; matrix products, arithmetic and copies ran while one was open for 0% -> 0% of each run, Pallas kernels for 15% -> 20%
where the time goes in v6:
time: 27.7 us; the launch traced here: 27.6 us
  Pallas kernels  10.7 us (39%)
  starting transfers between devices  9.11 us (33%)
  blocking collectives  5.46 us (20%)
  waiting for transfers between devices  1.43 us (5%)
  local copies, waits for them, and re-layouts  0.74 us (3%)
    ppermute x4, starting transfers between devices, to_mate(): return lax.ppermute(value, 'sx', mates)  7.78 us
    all_gather x1, blocking collectives, gathered(): both = lax.all_gather(value, ('grp', 'sx'), axis_index_groups=pairs)  5.46 us
    pallas_call x1, Pallas kernels, per_device(): pl.pallas_call(smooth_kernel, out_shape=(pltpu.HBM((ROWS, CX * PLANE), BF...  2.34 us
    pallas_call x1, Pallas kernels, per_device(): pl.pallas_call(energy_kernel, out_shape=(pair, pair, pair, shape(2, ROWS,...  2.16 us
    pallas_call x1, Pallas kernels, per_device(): pl.pallas_call(gradient_kernel, out_shape=(pair, shape(ROWS, ROWS), shape...  1.7 us
    pallas_call x1, Pallas kernels, per_device(): pl.pallas_call(edges_kernel, out_shape=(pair, pair, shape(ROWS, 16), shap...  1.59 us
    ppermute x4, waiting for transfers between devices, to_mate(): return lax.ppermute(value, 'sx', mates)  1.42 us
    ppermute x2, starting transfers between devices, across(): return lax.ppermute(value, 'sx', others)  1.33 us
  transfers between devices with their start and end apart: 6, of which 2 were waited for; matrix products, arithmetic and copies ran while one was open for 0% of the time, Pallas kernels for 20%

profile of v6, /device:TPU:0, one launch (start us, length us, event | category | flops | bytes accessed | tf_op | source)
XLA Modules:
  0.0 27.6 jit_solution(7424583228423690353)
XLA Ops:
  0.0 1.6 %edges.1 = (bf16[2,192,1024]{2,1,0:T(8,128)(2,1)S(1)}, bf16[2,192,1024]{2,1,0:T(8,128)(2,1)S(1)}, bf16[192,16]{1,0:T(8,128)(2,1)S(1)}, bf16[128,256]{1,0:T(8,128)(2,1)S(1)}, bf16[128,256]{1,0:T(8,128)(2,1)S(1)}) custom-call(s32[4,1024]{1,0:T(4,128)} %bitcast.8, bf16[192,4096]{1,0:T(8,128)(2,1)} %pieces_ref.3), custom_call_target="tpu_custom_call" | custom-call | flops 100000000 | bytes 1000000 | tf_op jit(solution)/shard_map/edges/pallas_call | solution.py:479
  1.6 0.7 %collective-permute-start = (bf16[128,256]{1,0:T(8,128)(2,1)S(1)}, bf16[128,256]{1,0:T(8,128)(2,1)S(1)}, u32[]{:S(2)}, u32[]{:S(2)}) collective-permute-start(bf16[128,256]{1,0:T(8,128)(2,1)S(1)} %get-tuple-element.28), channel_id=1, source_target_pairs={{1,2},{2,1},{3,4},{4,3},{5,6},{6,5},{7,8},{8,7},{9,10},{10,9},{11,... | collective-permute-start | bytes 196616 | tf_op jit(solution)/shard_map/ppermute | solution.py:469
  2.3 4.4 %collective-permute-start.1 = (bf16[128,256]{1,0:T(8,128)(2,1)S(1)}, bf16[128,256]{1,0:T(8,128)(2,1)S(1)}, u32[]{:S(2)}, u32[]{:S(2)}) collective-permute-start(bf16[128,256]{1,0:T(8,128)(2,1)S(1)} %get-tuple-element.29), channel_id=1, source_target_pairs={{0,1},{1,0},{2,3},{3,2},{4,5},{5,4},{6,7},{7,6},{8,9},{9,8},{10,11... | collective-permute-start | bytes 196616 | tf_op jit(solution)/shard_map/ppermute | solution.py:466
  6.7 2.2 %energy.1 = (bf16[2,192,1024]{2,1,0:T(8,128)(2,1)S(1)}, bf16[2,192,1024]{2,1,0:T(8,128)(2,1)S(1)}, bf16[2,192,1024]{2,1,0:T(8,128)(2,1)S(1)}, f32[2,192,1024]{2,...) custom-call(bf16[192,16]{1,0:T(8,128)(2,1)S(1)} %get-tuple-element.30.rows_ref, ...), custom_call_target="tpu_custom_call" | custom-call | flops 4000000000 | bytes 10000000 | tf_op jit(solution)/shard_map/energy/pallas_call | solution.py:496
  8.8 0.0 copy-start.3
  8.9 0.0 collective-permute-done.across_ref
  8.9 0.0 collective-permute-done.1.mate_ref
  8.9 0.6 %bands.1 = (bf16[2,192,1024]{2,1,0:T(8,128)(2,1)S(1)}, f32[2,192,256]{2,1,0:T(8,128)S(1)}, bf16[3,128,128]{2,1,0:T(8,128)(2,1)S(1)}) custom-call(bf16[128,256]{1,0:T(8,128)(2,1)S(1)} %collective-permute-done.across_ref, bf16[128,256]{1,0:T(8,128)(2,1)S(1)} %collective-permute-done.1.mate_ref, f32[2,192,1024]{2,1,0:T(8,128)S(1)} %get-tuple-element.32.part_ref, ...), custom_call_target="tpu_custom_call" | custom-call | flops 1000000000 | bytes 10000000 | tf_op jit(solution)/shard_map/bands/pallas_call | solution.py:509
  9.5 0.2 copy-done.3
  9.7 0.3 %copy-done.5 = bf16[2,192,1024]{2,1,0:T(8,128)(2,1)} copy-done((bf16[2,192,1024]{2,1,0:T(8,128)(2,1)}, bf16[2,192,1024]{2,1,0:T(8,128)(2,1)S(1)}, u32[]{:S(2)}) %copy-start.5) | copy-done | bytes 786456
  10.0 0.2 copy-done.7
  10.2 0.0 collective-permute-start.2
  10.3 1.3 %collective-permute-done.2.rows_ref = bf16[3,128,128]{2,1,0:T(8,128)(2,1)S(1)} collective-permute-done((bf16[3,128,128]{2,1,0:T(8,128)(2,1)S(1)}, bf16[3,128,128]{2,1,0:T(8,128)(2,1)S(1)}, u32[]{:S(2)}, u32[]{:S(2)}) %collective-permute-start.2) | collective-permute-done | bytes 98336 | tf_op jit(solution)/shard_map/ppermute | solution.py:466
  11.5 0.2 relay.1
  11.7 5.5 %all-gather = bf16[14,64,128]{2,1,0:T(8,128)(2,1)S(1)} all-gather(bf16[7,64,128]{2,1,0:T(8,128)(2,1)S(1)} %relay.1), channel_id=2, replica_groups={{1,2},{3,4},{5,6},{7,8},{9,10},{11,12},{13,14},{17,18},{19,20},{21,22},..., dimensions={0}, use_global_device_ids=true | all-gather | bytes 344064 | tf_op jit(solution)/shard_map/all_gather | solution.py:472
  17.2 0.1 collective-permute-start.3
  17.3 1.1 %theta.1 = (f32[192,512]{1,0:T(8,128)S(1)}, f32[192,512]{1,0:T(8,128)S(1)}, f32[192,192]{1,0:T(8,128)S(1)}) custom-call(s32[2,16]{1,0:T(2,128)S(1)} %bitcast.6, f32[2,192,256]{2,1,0:T(8,128)S(1)} %get-tuple-element.36.own_ref, bf16[3,128,128]{2,1,0:T(8,128)(2,1)S(1)} %collective-permute-done.2.rows_ref, bf16[7,64,128]{2,1,0:T(8,128)(2,1)S(1)} %fusion.other_ref), custom_call_target="tpu_custom_call" | custom-call | flops 1000000000 | bytes 4000000 | tf_op jit(solution)/shard_map/theta/pallas_call | solution.py:534
  18.4 0.1 collective-permute-done.3.relayed_ref
  18.6 1.7 %gradient.1 = (bf16[2,192,1024]{2,1,0:T(8,128)(2,1)S(1)}, bf16[192,192]{1,0:T(8,128)(2,1)S(1)}, bf16[128,256]{1,0:T(8,128)(2,1)S(1)}, bf16[128,256]{1,0:T(8,128)(2,1)S(1)}) custom-call(s32[2,16]{1,0:T(2,128)S(1)} %bitcast.7, bf16[3,64,128]{2,1,0:T(8,128)(2,1)S(1)} %collective-permute-done.3.relayed_ref, f32[192,512]{1,0:T(8,128)S(1)} %get-tuple-element.38.ham_ref, ...), custom_call_target="tpu_custom_call" | custom-call | flops 1000000000 | bytes 10000000 | tf_op jit(solution)/shard_map/gradient/pallas_call | solution.py:543
  20.3 0.7 %collective-permute-start.4 = (bf16[128,256]{1,0:T(8,128)(2,1)S(1)}, bf16[128,256]{1,0:T(8,128)(2,1)S(1)}, u32[]{:S(2)}, u32[]{:S(2)}) collective-permute-start(bf16[128,256]{1,0:T(8,128)(2,1)S(1)} %get-tuple-element.42), channel_id=1, source_target_pairs={{1,2},{2,1},{3,4},{4,3},{5,6},{6,5},{7,8},{8,7},{9,10},{10,9},{11,... | collective-permute-start | bytes 196616 | tf_op jit(solution)/shard_map/ppermute | solution.py:469
  20.9 3.3 %collective-permute-start.5 = (bf16[128,256]{1,0:T(8,128)(2,1)S(1)}, bf16[128,256]{1,0:T(8,128)(2,1)S(1)}, u32[]{:S(2)}, u32[]{:S(2)}) collective-permute-start(bf16[128,256]{1,0:T(8,128)(2,1)S(1)} %get-tuple-element.43), channel_id=1, source_target_pairs={{0,1},{1,0},{2,3},{3,2},{4,5},{5,4},{6,7},{7,6},{8,9},{9,8},{10,11... | collective-permute-start | bytes 196616 | tf_op jit(solution)/shard_map/ppermute | solution.py:466
  24.2 2.3 %smooth.1 = (bf16[192,4096]{1,0:T(8,128)(2,1)}, f32[2,192,1024]{2,1,0:T(8,128)S(1)}) custom-call(bf16[192,192]{1,0:T(8,128)(2,1)S(1)} %get-tuple-element.44.theta_ref, bf16[2,192,1024]{2,1,0:T(8,128)(2,1)S(1)} %copy-done.4, bf16[2,192,1024]{2,1,0:T(8,128)(2,1)S(1)} %copy-done.8, bf16[2,192,1024]{2,1,0:T(8,128)(2,1)S(1)} %get-tuple-element.47.edge_ref, ...), custom_call_target="tpu_custom_call" | custom-call | flops 2000000000 | bytes 10000000 | tf_op jit(solution)/shard_map/smooth/pallas_call | solution.py:556
  26.6 0.0 collective-permute-done.4.across_ref
  26.6 1.0 %finish.1 = bf16[192,4096]{1,0:T(8,128)(2,1)} custom-call(bf16[128,256]{1,0:T(8,128)(2,1)S(1)} %collective-permute-done.4.across_ref, bf16[128,256]{1,0:T(8,128)(2,1)S(1)} %collective-permute-done.5.mate_ref, f32[2,192,1024]{2,1,0:T(8,128)S(1)} %get-tuple-element.49.part_ref, ...), custom_call_target="tpu_custom_call", output_to_operand_aliasing={{}: (4, {})} | custom-call | flops 10000000 | bytes 10000000 | tf_op jit(solution)/shard_map/finish/pallas_call | solution.py:572
  (18 shorter events, 0.1 us)
Async XLA Ops:
  0.0 6.7 %copy-start = (bf16[192,4096]{1,0:T(8,128)(2,1)S(1)}, bf16[192,4096]{1,0:T(8,128)(2,1)}, u32[]{:S(2)}) copy-start(bf16[192,4096]{1,0:T(8,128)(2,1)} %pieces_ref.3) | copy-start | bytes 4718596
  0.0 6.7 %copy-start.1 = (f32[4,1024]{1,0:T(4,128)S(1)}, f32[4,1024]{1,0:T(4,128)}, u32[]{:S(2)}) copy-start(f32[4,1024]{1,0:T(4,128)} %pot_ref.1) | copy-start | bytes 49156
  1.6 7.3 %collective-permute-start = (bf16[128,256]{1,0:T(8,128)(2,1)S(1)}, bf16[128,256]{1,0:T(8,128)(2,1)S(1)}, u32[]{:S(2)}, u32[]{:S(2)}) collective-permute-start(bf16[128,256]{1,0:T(8,128)(2,1)S(1)} %get-tuple-element.28), channel_id=1, source_target_pairs={{1,2},{2,1},{3,4},{4,3},{5,6},{6,5},{7,8},{8,7},{9,10},{10,9},{11,... | collective-permute-start | bytes 196616 | tf_op jit(solution)/shard_map/ppermute | solution.py:469
  2.3 6.6 %collective-permute-start.1 = (bf16[128,256]{1,0:T(8,128)(2,1)S(1)}, bf16[128,256]{1,0:T(8,128)(2,1)S(1)}, u32[]{:S(2)}, u32[]{:S(2)}) collective-permute-start(bf16[128,256]{1,0:T(8,128)(2,1)S(1)} %get-tuple-element.29), channel_id=1, source_target_pairs={{0,1},{1,0},{2,3},{3,2},{4,5},{5,4},{6,7},{7,6},{8,9},{9,8},{10,11... | collective-permute-start | bytes 196616 | tf_op jit(solution)/shard_map/ppermute | solution.py:466
  8.8 0.9 %copy-start.3 = (bf16[2,192,1024]{2,1,0:T(8,128)(2,1)}, bf16[2,192,1024]{2,1,0:T(8,128)(2,1)S(1)}, u32[]{:S(2)}) copy-start(bf16[2,192,1024]{2,1,0:T(8,128)(2,1)S(1)} %get-tuple-element.45.phi_ref) | copy-start | bytes 2359300
  8.9 1.2 %copy-start.5 = (bf16[2,192,1024]{2,1,0:T(8,128)(2,1)}, bf16[2,192,1024]{2,1,0:T(8,128)(2,1)S(1)}, u32[]{:S(2)}) copy-start(bf16[2,192,1024]{2,1,0:T(8,128)(2,1)S(1)} %get-tuple-element.48.mask_ref) | copy-start | bytes 2359300
  8.9 1.4 %copy-start.7 = (bf16[2,192,1024]{2,1,0:T(8,128)(2,1)}, bf16[2,192,1024]{2,1,0:T(8,128)(2,1)S(1)}, u32[]{:S(2)}) copy-start(bf16[2,192,1024]{2,1,0:T(8,128)(2,1)S(1)} %get-tuple-element.46.energy_ref) | copy-start | bytes 2359300
  10.2 7.1 %copy-start.2 = (s32[16,2]{0,1:T(2,128)S(1)}, s32[16,2]{0,1:T(2,128)}, u32[]{:S(2)}) copy-start(s32[16,2]{0,1:T(2,128)} %param.7) | copy-start | bytes 388
  10.2 1.3 %collective-permute-start.2 = (bf16[3,128,128]{2,1,0:T(8,128)(2,1)S(1)}, bf16[3,128,128]{2,1,0:T(8,128)(2,1)S(1)}, u32[]{:S(2)}, u32[]{:S(2)}) collective-permute-start(bf16[3,128,128]{2,1,0:T(8,128)(2,1)S(1)} %get-tuple-element.37), channel_id=1, source_target_pairs={{0,1},{1,0},{2,3},{3,2},{4,5},{5,4},{6,7},{7,6},{8,9},{9,8},{10,11... | collective-permute-start | bytes 294920 | tf_op jit(solution)/shard_map/ppermute | solution.py:466
  17.2 1.3 %collective-permute-start.3 = (bf16[3,64,128]{2,1,0:T(8,128)(2,1)S(1)}, bf16[3,64,128]{2,1,0:T(8,128)(2,1)S(1)}, u32[]{:S(2)}, u32[]{:S(2)}) collective-permute-start(bf16[3,64,128]{2,1,0:T(8,128)(2,1)S(1)} %slice_bitcast_fusion), channel_id=1, source_target_pairs={{0,1},{1,0},{2,3},{3,2},{4,5},{5,4},{6,7},{7,6},{8,9},{9,8},{10,11... | collective-permute-start | bytes 147464 | tf_op jit(solution)/shard_map/ppermute | solution.py:466
  18.5 5.7 %copy-start.4 = (bf16[2,192,1024]{2,1,0:T(8,128)(2,1)S(1)}, bf16[2,192,1024]{2,1,0:T(8,128)(2,1)}, u32[]{:S(2)}) copy-start(bf16[2,192,1024]{2,1,0:T(8,128)(2,1)} %copy-done.3) | copy-start | bytes 2359300
  18.5 5.7 %copy-start.6 = (bf16[2,192,1024]{2,1,0:T(8,128)(2,1)S(1)}, bf16[2,192,1024]{2,1,0:T(8,128)(2,1)}, u32[]{:S(2)}) copy-start(bf16[2,192,1024]{2,1,0:T(8,128)(2,1)} %copy-done.5) | copy-start | bytes 2359300
  18.5 5.7 %copy-start.8 = (bf16[2,192,1024]{2,1,0:T(8,128)(2,1)S(1)}, bf16[2,192,1024]{2,1,0:T(8,128)(2,1)}, u32[]{:S(2)}) copy-start(bf16[2,192,1024]{2,1,0:T(8,128)(2,1)} %copy-done.7) | copy-start | bytes 2359300
  20.3 6.3 %collective-permute-start.4 = (bf16[128,256]{1,0:T(8,128)(2,1)S(1)}, bf16[128,256]{1,0:T(8,128)(2,1)S(1)}, u32[]{:S(2)}, u32[]{:S(2)}) collective-permute-start(bf16[128,256]{1,0:T(8,128)(2,1)S(1)} %get-tuple-element.42), channel_id=1, source_target_pairs={{1,2},{2,1},{3,4},{4,3},{5,6},{6,5},{7,8},{8,7},{9,10},{10,9},{11,... | collective-permute-start | bytes 196616 | tf_op jit(solution)/shard_map/ppermute | solution.py:469
  20.9 5.7 %collective-permute-start.5 = (bf16[128,256]{1,0:T(8,128)(2,1)S(1)}, bf16[128,256]{1,0:T(8,128)(2,1)S(1)}, u32[]{:S(2)}, u32[]{:S(2)}) collective-permute-start(bf16[128,256]{1,0:T(8,128)(2,1)S(1)} %get-tuple-element.43), channel_id=1, source_target_pairs={{0,1},{1,0},{2,3},{3,2},{4,5},{5,4},{6,7},{7,6},{8,9},{9,8},{10,11... | collective-permute-start | bytes 196616 | tf_op jit(solution)/shard_map/ppermute | solution.py:466

commit v7 on v6

--- a/solution.py
+++ b/solution.py
@@ -14,7 +14,6 @@
 ROWS = 3 * ORB
 PLANE = NY * NZ
 TILE = 256
-HALF = PLANE // 4
 F32 = jnp.float32
 BF16 = jnp.bfloat16
 
@@ -99,24 +98,26 @@
 
 
 def fold(values):
-    half = values[:, : PLANE // 2] + values[:, PLANE // 2 :]
+    tiles = [values[:, 128 * t : 128 * t + 128] for t in range(PLANE // 128)]
+    a, b, c = (sum(tiles[t::3][1:], tiles[t]) for t in range(3))
     low_z = (iota((1, 128), 1) & 31) < 16
-    out = []
-    for i in range(2):
-        a = half[:, 256 * i : 256 * i + 128]
-        b = half[:, 256 * i + 128 : 256 * i + 256]
-        out.append(jnp.where(low_z, a + pltpu.roll(a, 112, 1), b + pltpu.roll(b, 16, 1)))
-    return out
+    top, bottom = c[:ORB], c[ORB:]
+    return (
+        jnp.where(low_z, a + pltpu.roll(a, 112, 1), b + pltpu.roll(b, 16, 1)),
+        jnp.where(low_z, top + pltpu.roll(top, 112, 1), bottom + pltpu.roll(bottom, 16, 1)),
+    )
 
 
 def unfold(packed):
     low_z = (iota((1, 128), 1) & 31) < 16
-    tiles = []
-    for i in range(2):
-        p = packed[:, 128 * i : 128 * i + 128]
-        tiles.append(jnp.where(low_z, p, pltpu.roll(p, 16, 1)))
-        tiles.append(jnp.where(low_z, pltpu.roll(p, 112, 1), p))
-    return tiles
+    p, q = packed[: 2 * ORB], packed[2 * ORB :]
+    return (
+        jnp.where(low_z, p, pltpu.roll(p, 16, 1)),
+        jnp.where(low_z, pltpu.roll(p, 112, 1), p),
+        jnp.concatenate(
+            [jnp.where(low_z, q, pltpu.roll(q, 16, 1)), jnp.where(low_z, pltpu.roll(q, 112, 1), q)], axis=0
+        ),
+    )
 
 
 def is_even():
@@ -127,10 +128,9 @@
     down = fold(planes[0, : 2 * ORB].astype(F32))
     up = fold(planes[1, ORB:].astype(F32))
     even = is_even()
-    for i in range(2):
-        lanes = slice(128 * i, 128 * i + 128)
-        mate_ref[:, lanes] = jnp.where(even, up[i], down[i]).astype(BF16)
-        across_ref[:, lanes] = jnp.where(even, down[i], up[i]).astype(BF16)
+    for i, rows in enumerate((slice(0, 2 * ORB), slice(2 * ORB, ROWS))):
+        mate_ref[rows] = jnp.where(even, up[i], down[i]).astype(BF16)
+        across_ref[rows] = jnp.where(even, down[i], up[i]).astype(BF16)
 
 
 def sides(mate_ref, across_ref):
@@ -172,7 +172,8 @@
 
 def energy_kernel(
     rows_ref, pieces_ref, pot_ref, edge_ref,
-    phi_ref, mask_ref, energy_ref, part_ref, corr_ref, ham_ref,
+    edge_mask_ref,
+    phi_ref, mask_ref, energy_ref, part_ref, edge_energy_ref, corr_ref, ham_ref,
 ):
     rows = rows_ref[...]
     for i in range(2):
@@ -190,7 +191,10 @@
             value = 0.5 * (inner[i] - (edge[i] + mid[1 - i])) + pot_ref[1 + i : 2 + i, lanes] * mid[i]
             energy_ref[i, :, lanes] = value.astype(BF16) * mask_ref[i, :, lanes]
             plane = (CX - 1) * i
-            part_ref[i, :, lanes] = 0.5 * (outer[i] - mid[i]) + pot_ref[plane : plane + 1, lanes] * edge[i]
+            value = 0.5 * (outer[i] - mid[i]) + pot_ref[plane : plane + 1, lanes] * edge[i]
+            part_ref[i, :, lanes] = value
+            rest = rest_rows(i)
+            edge_energy_ref[i, rest, lanes] = value[rest].astype(BF16) * edge_mask_ref[i, rest, lanes]
     corr = jnp.zeros((ROWS, ROWS), F32)
     ham = jnp.zeros((ROWS, ROWS), F32)
     for i in range(2):
@@ -198,6 +202,9 @@
         ham = ham + rows_product(energy_ref[i], phi_ref[i])
     corr_ref[...] = corr
     ham_ref[...] = ham
+    for i in range(2):
+        rest = rest_rows(i)
+        ham_ref[rest] += rows_product(edge_energy_ref[i, rest], edge_ref[i])
 
 
 def halo_rows(i):
@@ -209,22 +216,22 @@
 
 
 def bands_kernel(
-    across_ref, mate_ref, part_ref, mask_ref, phi_ref, corr_ref, ham_ref,
+    across_ref, mate_ref, part_ref, mask_ref, phi_ref, corr_ref, ham_ref, rest_ref,
     energy_ref, own_ref, rows_ref,
 ):
     volume = 1.0 / (4.0 * CX**3)
-    ham = ham_ref[...]
+    gram = []
     for i, side in enumerate(sides(mate_ref, across_ref)):
         tiles = unfold(side)
-        rest = rest_rows(i)
         for t in range(PLANE // 128):
             lanes = slice(128 * t, 128 * t + 128)
-            value = part_ref[i, halo_rows(i), lanes] - 0.5 * tiles[t % 4]
+            value = part_ref[i, halo_rows(i), lanes] - 0.5 * tiles[t % 3]
             energy_ref[i, halo_rows(i), lanes] = value.astype(BF16) * mask_ref[i, halo_rows(i), lanes]
-            energy_ref[i, rest, lanes] = part_ref[i, rest, lanes].astype(BF16) * mask_ref[i, rest, lanes]
-        ham = ham + rows_product(energy_ref[i], phi_ref[i])
+        gram.append(rows_product(energy_ref[i, halo_rows(i)], phi_ref[i]))
     own_ref[:, :, ROWS:] = jnp.zeros((2, ROWS, TILE - ROWS), F32)
-    own_ref[0, :, :ROWS] = ham * volume
+    own_ref[0, :ORB, :ROWS] = (ham_ref[:ORB] + gram[0][:ORB]) * volume
+    own_ref[0, ORB : 2 * ORB, :ROWS] = (ham_ref[ORB : 2 * ORB] + gram[0][ORB:] + gram[1][:ORB]) * volume
+    own_ref[0, 2 * ORB :, :ROWS] = (ham_ref[2 * ORB :] + gram[1][ORB:]) * volume
     own_ref[1, :, :ROWS] = corr_ref[...] * volume
     tail = jnp.where(low_half(), own_ref[0, :, 128:256], swapped(own_ref[1, :, 128:256]))
     even = is_even()
@@ -274,6 +281,18 @@
     if which == 1:
         tile = swapped(tile)
     return jnp.where(low_half(), 0.0, tile)
+
+
+def pick_kernel(both_ref, other_ref, forward_ref):
+    slab = lax.axis_index("sx")
+    even = is_even()
+    end = (slab == 0) | (slab == lax.axis_size("sx") - 1)
+    for i in range(7):
+        value = jnp.where(even, both_ref[0, i].astype(F32), both_ref[1, i].astype(F32))
+        value = jnp.where(end, 0.0, value).astype(BF16)
+        other_ref[i] = value
+        if i >= 4:
+            forward_ref[i - 4] = value
 
 
 def put_gradient(theta, orbital_ref, energy_ref, mask_ref, out_ref):
@@ -347,26 +366,33 @@
     pattern_ref, relayed_ref, ham_ref, inv_ref, base_ref,
     edge_ref, edge_energy_ref, edge_mask_ref,
     edge_grad_ref, theta_ref, mate_ref, across_ref,
-    more_ref,
+    window_ref, total_ref,
 ):
     even = is_even()
     low = low_half()
+    more = []
     for which in range(2):
         front = swapped(shared_head(relayed_ref[0], which))
         turned = swapped(relayed_ref[1 + which].astype(F32))
+        tiles = []
         for q, value in enumerate((jnp.where(low, front, turned), jnp.where(low, turned, 0.0))):
-            value = value * jnp.where(even, kept(pattern_ref, 2, 2 + q), kept(pattern_ref, 0, q))
-            if which == 1:
-                value = -value
-            lanes = slice(128 * q, 128 * q + 128)
-            more_ref[which, :ORB, lanes] = jnp.where(even, 0.0, value)
-            more_ref[which, ORB : 2 * ORB, lanes] = jnp.zeros((ORB, 128), F32)
-            more_ref[which, 2 * ORB :, lanes] = jnp.where(even, value, 0.0)
-    ham = jnp.where(even, ham_ref[:, 256:512], ham_ref[:, 0:256]) + more_ref[0]
-    inv = jnp.where(even, inv_ref[:, 256:512], inv_ref[:, 0:256])
-    theta = base_ref[...] + fine_product(split(ham), split(more_ref[1]))
-    theta = theta + fine_product(split(more_ref[0]), split(inv))
-    theta = theta.astype(BF16)
+            tiles.append(value * jnp.where(even, kept(pattern_ref, 2, 2 + q), kept(pattern_ref, 0, q)))
+        more.append(jnp.concatenate(tiles, axis=1))
+    first, third = slice(0, ORB), slice(2 * ORB, ROWS)
+    window_ref[...] = jnp.where(even, ham_ref[:, 256:512], ham_ref[:, 0:256])
+    window_ref[first] += jnp.where(even, 0.0, more[0])
+    window_ref[third] += jnp.where(even, more[0], 0.0)
+    ham = jnp.concatenate(split(window_ref[...]), axis=1)
+    inv = jnp.concatenate(split(jnp.where(even, inv_ref[:, 256:512], inv_ref[:, 0:256])), axis=1)
+    more = [jnp.concatenate([value.astype(BF16)] * 2, axis=1) for value in more]
+    column = rows_product(ham, more[1])
+    row = rows_product(more[0], inv)
+    total_ref[...] = base_ref[...]
+    total_ref[first] += jnp.where(even, 0.0, row)
+    total_ref[third] += jnp.where(even, row, 0.0)
+    total_ref[:, first] -= jnp.where(even, 0.0, column)
+    total_ref[:, third] -= jnp.where(even, column, 0.0)
+    theta = total_ref[...].astype(BF16)
     theta_ref[...] = theta
     put_gradient(theta, edge_ref, edge_energy_ref, edge_mask_ref, edge_grad_ref)
     put_messages(edge_grad_ref, mate_ref, across_ref)
@@ -420,7 +446,7 @@
             got = slice(ORB * half, ORB * half + ORB)
             for t in range(PLANE // 128):
                 lanes = slice(128 * t, 128 * t + 128)
-                value = (part_ref[i, rows, lanes] + tiles[t % 4][got]) * (1.0 / 32.0)
+                value = (part_ref[i, rows, lanes] + tiles[t % 3][got]) * (1.0 / 32.0)
                 done_ref[2 * i + half, :, lanes] = value.astype(BF16) * mask_ref[i, rows, lanes]
             start = PLANE * (CX - 1) * i
             copies.append(
@@ -460,7 +486,6 @@
     pairs += [[ends[i], ends[i + 2]] for i in range(len(ends)) if i % 4 < 2] if groups % 2 == 0 else [
         [ends[2 * i], ends[2 * i + 1]] for i in range(groups)
     ]
-    slab = lax.axis_index("sx")
 
     def to_mate(value):
         return lax.ppermute(value, "sx", mates)
@@ -469,16 +494,14 @@
         return lax.ppermute(value, "sx", others)
 
     def gathered(value):
-        both = lax.all_gather(value, ("grp", "sx"), axis_index_groups=pairs)
-        got = jnp.where(slab % 2 == 1, both[1], both[0])
-        return jnp.where((slab == 0) | (slab == count - 1), jnp.zeros((), value.dtype), got)
+        return lax.all_gather(value, ("grp", "sx"), axis_index_groups=pairs)
 
     table = centers.T
     pair = shape(2, ROWS, PLANE)
 
     edge, edge_mask, rows, for_mate, for_other = pl.pallas_call(
         edges_kernel,
-        out_shape=(pair, pair, shape(ROWS, 16), shape(2 * ORB, HALF), shape(2 * ORB, HALF)),
+        out_shape=(pair, pair, shape(ROWS, 16), shape(ROWS, 128), shape(ROWS, 128)),
         in_specs=[FAR, FAR],
         out_specs=(WHOLE,) * 5,
         scratch_shapes=[
@@ -493,28 +516,29 @@
     other_side = across(for_other)
     mate_side = to_mate(for_mate)
 
-    mid, mid_mask, mid_energy, part, corr, ham = pl.pallas_call(
+    mid, mid_mask, mid_energy, part, rest_energy, corr, ham = pl.pallas_call(
         energy_kernel,
         out_shape=(
-            pair, pair, pair, shape(2, ROWS, PLANE, dtype=F32),
+            pair, pair, pair, shape(2, ROWS, PLANE, dtype=F32), pair,
             shape(ROWS, ROWS, dtype=F32), shape(ROWS, ROWS, dtype=F32),
         ),
-        in_specs=[WHOLE] * 4,
-        out_specs=(WHOLE,) * 6,
+        in_specs=[WHOLE] * 5,
+        out_specs=(WHOLE,) * 7,
         compiler_params=PARAMS,
         cost_estimate=cost(4 * 10**9, 10**7),
         name="energy",
-    )(rows, pieces, potential, edge)
+    )(rows, pieces, potential, edge, edge_mask)
 
     edge_energy, own, for_mate = pl.pallas_call(
         bands_kernel,
         out_shape=(pair, shape(2, ROWS, TILE, dtype=F32), shape(3, 2 * ORB, 128)),
-        in_specs=[WHOLE] * 7,
+        in_specs=[WHOLE] * 8,
         out_specs=(WHOLE,) * 3,
+        input_output_aliases={7: 0},
         compiler_params=PARAMS,
         cost_estimate=cost(10**9, 10**7),
         name="bands",
-    )(other_side, mate_side, part, edge_mask, edge, corr, ham)
+    )(other_side, mate_side, part, edge_mask, edge, corr, ham, rest_energy)
     mate_rows = to_mate(for_mate)
     for_other = pl.pallas_call(
         relay_kernel,
@@ -525,8 +549,16 @@
         cost_estimate=cost(10**6, 10**6),
         name="relay",
     )(own, mate_rows)
-    other_rows = gathered(for_other)
-    relayed = to_mate(other_rows[4:])
+    other_rows, forward = pl.pallas_call(
+        pick_kernel,
+        out_shape=(shape(7, ORB, 128), shape(3, ORB, 128)),
+        in_specs=[WHOLE],
+        out_specs=(WHOLE,) * 2,
+        compiler_params=PARAMS,
+        cost_estimate=cost(10**6, 10**6),
+        name="pick",
+    )(gathered(for_other))
+    relayed = to_mate(forward)
 
     patterns = pattern.T
     scalars = pl.BlockSpec(memory_space=pltpu.SMEM)
@@ -542,10 +574,10 @@
     )(patterns, own, mate_rows, other_rows)
     edge_grad, theta, for_mate, for_other = pl.pallas_call(
         gradient_kernel,
-        out_shape=(pair, shape(ROWS, ROWS), shape(2 * ORB, HALF), shape(2 * ORB, HALF)),
+        out_shape=(pair, shape(ROWS, ROWS), shape(ROWS, 128), shape(ROWS, 128)),
         in_specs=[scalars] + [WHOLE] * 7,
         out_specs=(WHOLE,) * 4,
-        scratch_shapes=[pltpu.VMEM((2, ROWS, TILE), F32)],
+        scratch_shapes=[pltpu.VMEM((ROWS, TILE), F32), pltpu.VMEM((ROWS, ROWS), F32)],
         compiler_params=PARAMS,
         cost_estimate=cost(10**9, 10**7),
         name="gradient",

time: 27.7 us -> 26.8 us (0.968)
  local copies, waits for them, and re-layouts: 0.74 us -> 0.01 us
    unnamed x18 -> x6, local copies, waits for them, and re-layouts: 0.74 us -> 0.01 us
    pallas_call x1, Pallas kernels: 1.7 us -> 1.41 us  [per_device(): pl.pallas_call(gradient_kernel, out_shape=(pair, shape(ROWS, ROWS), shape...]
  transfers between devices with their start and end apart: 6 -> 6, of which waited for: 2 -> 2; matrix products, arithmetic and copies ran while one was open for 0% -> 0% of each run, Pallas kernels for 20% -> 21%
where the time goes in v7:
time: 26.8 us; the launch traced here: 26.7 us
  Pallas kernels  10.5 us (39%)
  starting transfers between devices  9.15 us (34%)
  blocking collectives  5.46 us (20%)
  waiting for transfers between devices  1.43 us (5%)
    ppermute x4, starting transfers between devices, to_mate(): return lax.ppermute(value, 'sx', mates)  7.82 us
    all_gather x1, blocking collectives, gathered(): return lax.all_gather(value, ('grp', 'sx'), axis_index_groups=pairs)  5.46 us
    pallas_call x1, Pallas kernels, per_device(): pl.pallas_call(energy_kernel, out_shape=(pair, pair, pair, shape(2, ROWS,...  2.41 us
    pallas_call x1, Pallas kernels, per_device(): pl.pallas_call(smooth_kernel, out_shape=(pltpu.HBM((ROWS, CX * PLANE), BF...  2.27 us
    pallas_call x1, Pallas kernels, per_device(): pl.pallas_call(edges_kernel, out_shape=(pair, pair, shape(ROWS, 16), shap...  1.56 us
    ppermute x4, waiting for transfers between devices, to_mate(): return lax.ppermute(value, 'sx', mates)  1.42 us
    pallas_call x1, Pallas kernels, per_device(): pl.pallas_call(gradient_kernel, out_shape=(pair, shape(ROWS, ROWS), shape...  1.41 us
    ppermute x2, starting transfers between devices, across(): return lax.ppermute(value, 'sx', others)  1.33 us
  transfers between devices with their start and end apart: 6, of which 2 were waited for; matrix products, arithmetic and copies ran while one was open for 0% of the time, Pallas kernels for 21%

profile of v7, /device:TPU:0, one launch (start us, length us, event | category | flops | bytes accessed | tf_op | source)
XLA Modules:
  0.0 26.7 jit_solution(8205396228674408326)
XLA Ops:
  0.0 1.6 %edges.1 = (bf16[2,192,1024]{2,1,0:T(8,128)(2,1)S(1)}, bf16[2,192,1024]{2,1,0:T(8,128)(2,1)S(1)}, bf16[192,16]{1,0:T(8,128)(2,1)S(1)}, bf16[192,128]{1,0:T(8,128)(2,1)S(1)}, bf16[192,128]{1,0:T(8,128)(2,1)S(1)}) custom-call(s32[4,1024]{1,0:T(4,128)} %bitcast.6, bf16[192,4096]{1,0:T(8,128)(2,1)} %pieces_ref.3), custom_call_target="tpu_custom_call" | custom-call | flops 100000000 | bytes 1000000 | tf_op jit(solution)/shard_map/edges/pallas_call | solution.py:502
  1.6 0.7 %collective-permute-start = (bf16[192,128]{1,0:T(8,128)(2,1)S(1)}, bf16[192,128]{1,0:T(8,128)(2,1)S(1)}, u32[]{:S(2)}, u32[]{:S(2)}) collective-permute-start(bf16[192,128]{1,0:T(8,128)(2,1)S(1)} %get-tuple-element.31), channel_id=1, source_target_pairs={{1,2},{2,1},{3,4},{4,3},{5,6},{6,5},{7,8},{8,7},{9,10},{10,9},{11,... | collective-permute-start | bytes 147464 | tf_op jit(solution)/shard_map/ppermute | solution.py:494
  2.2 4.4 %collective-permute-start.1 = (bf16[192,128]{1,0:T(8,128)(2,1)S(1)}, bf16[192,128]{1,0:T(8,128)(2,1)S(1)}, u32[]{:S(2)}, u32[]{:S(2)}) collective-permute-start(bf16[192,128]{1,0:T(8,128)(2,1)S(1)} %get-tuple-element.32), channel_id=1, source_target_pairs={{0,1},{1,0},{2,3},{3,2},{4,5},{5,4},{6,7},{7,6},{8,9},{9,8},{10,11... | collective-permute-start | bytes 147464 | tf_op jit(solution)/shard_map/ppermute | solution.py:491
  6.6 0.0 copy-done
  6.6 2.4 %energy.1 = (bf16[2,192,1024]{2,1,0:T(8,128)(2,1)S(1)}, bf16[2,192,1024]{2,1,0:T(8,128)(2,1)S(1)}, bf16[2,192,1024]{2,1,0:T(8,128)(2,1)S(1)}, f32[2,192,1024]{2,...) custom-call(bf16[192,16]{1,0:T(8,128)(2,1)S(1)} %get-tuple-element.33.rows_ref, ...), custom_call_target="tpu_custom_call" | custom-call | flops 4000000000 | bytes 10000000 | tf_op jit(solution)/shard_map/energy/pallas_call | solution.py:519
  9.1 0.0 collective-permute-done.across_ref
  9.1 0.0 collective-permute-done.1.mate_ref
  9.1 0.0 copy-start.2
  9.1 0.6 %bands.1 = (bf16[2,192,1024]{2,1,0:T(8,128)(2,1)S(1)}, f32[2,192,256]{2,1,0:T(8,128)S(1)}, bf16[3,128,128]{2,1,0:T(8,128)(2,1)S(1)}) custom-call(bf16[192,128]{1,0:T(8,128)(2,1)S(1)} %collective-permute-done.across_ref, bf16[192,128]{1,0:T(8,128)(2,1)S(1)} %collective-permute-done.1.mate_ref, ...), custom_call_target="tpu_custom_call", output_to_operand_aliasing={{0}: (7, {})} | custom-call | flops 1000000000 | bytes 10000000 | tf_op jit(solution)/shard_map/bands/pallas_call | solution.py:532
  9.7 0.1 collective-permute-start.2
  9.8 1.3 %collective-permute-done.2.rows_ref = bf16[3,128,128]{2,1,0:T(8,128)(2,1)S(1)} collective-permute-done((bf16[3,128,128]{2,1,0:T(8,128)(2,1)S(1)}, bf16[3,128,128]{2,1,0:T(8,128)(2,1)S(1)}, u32[]{:S(2)}, u32[]{:S(2)}) %collective-permute-start.2) | collective-permute-done | bytes 98336 | tf_op jit(solution)/shard_map/ppermute | solution.py:491
  11.0 0.2 relay.1
  11.2 5.5 %all-gather = bf16[14,64,128]{2,1,0:T(8,128)(2,1)S(1)} all-gather(bf16[7,64,128]{2,1,0:T(8,128)(2,1)S(1)} %relay.1), channel_id=2, replica_groups={{1,2},{3,4},{5,6},{7,8},{9,10},{11,12},{13,14},{17,18},{19,20},{21,22},..., dimensions={0}, use_global_device_ids=true | all-gather | bytes 344064 | tf_op jit(solution)/shard_map/all_gather | solution.py:497
  16.7 0.1 collective-permute-start.3
  16.8 0.0 copy-done.2
  16.8 1.1 %theta.1 = (f32[192,512]{1,0:T(8,128)S(1)}, f32[192,512]{1,0:T(8,128)S(1)}, f32[192,192]{1,0:T(8,128)S(1)}) custom-call(s32[2,16]{1,0:T(2,128)S(1)} %bitcast.4, f32[2,192,256]{2,1,0:T(8,128)S(1)} %get-tuple-element.40.own_ref, bf16[3,128,128]{2,1,0:T(8,128)(2,1)S(1)} %collective-permute-done.2.rows_ref, bf16[7,64,128]{2,1,0:T(8,128)(2,1)S(1)} %get-tuple-element.43.other_ref), custom_call_target="tpu_custom_call" | custom-call | flops 1000000000 | bytes 4000000 | tf_op jit(solution)/shard_map/theta/pallas_call | solution.py:566
  17.9 0.1 collective-permute-done.3.relayed_ref
  18.0 1.4 %gradient.1 = (bf16[2,192,1024]{2,1,0:T(8,128)(2,1)S(1)}, bf16[192,192]{1,0:T(8,128)(2,1)S(1)}, bf16[192,128]{1,0:T(8,128)(2,1)S(1)}, bf16[192,128]{1,0:T(8,128)(2,1)S(1)}) custom-call(s32[2,16]{1,0:T(2,128)S(1)} %bitcast.5, bf16[3,64,128]{2,1,0:T(8,128)(2,1)S(1)} %collective-permute-done.3.relayed_ref, f32[192,512]{1,0:T(8,128)S(1)} %get-tuple-element.44.ham_ref, ...), custom_call_target="tpu_custom_call" | custom-call | flops 1000000000 | bytes 10000000 | tf_op jit(solution)/shard_map/gradient/pallas_call | solution.py:575
  19.5 0.7 %collective-permute-start.4 = (bf16[192,128]{1,0:T(8,128)(2,1)S(1)}, bf16[192,128]{1,0:T(8,128)(2,1)S(1)}, u32[]{:S(2)}, u32[]{:S(2)}) collective-permute-start(bf16[192,128]{1,0:T(8,128)(2,1)S(1)} %get-tuple-element.48), channel_id=1, source_target_pairs={{1,2},{2,1},{3,4},{4,3},{5,6},{6,5},{7,8},{8,7},{9,10},{10,9},{11,... | collective-permute-start | bytes 147464 | tf_op jit(solution)/shard_map/ppermute | solution.py:494
  20.1 3.3 %collective-permute-start.5 = (bf16[192,128]{1,0:T(8,128)(2,1)S(1)}, bf16[192,128]{1,0:T(8,128)(2,1)S(1)}, u32[]{:S(2)}, u32[]{:S(2)}) collective-permute-start(bf16[192,128]{1,0:T(8,128)(2,1)S(1)} %get-tuple-element.49), channel_id=1, source_target_pairs={{0,1},{1,0},{2,3},{3,2},{4,5},{5,4},{6,7},{7,6},{8,9},{9,8},{10,11... | collective-permute-start | bytes 147464 | tf_op jit(solution)/shard_map/ppermute | solution.py:491
  23.4 2.3 %smooth.1 = (bf16[192,4096]{1,0:T(8,128)(2,1)}, f32[2,192,1024]{2,1,0:T(8,128)S(1)}) custom-call(bf16[192,192]{1,0:T(8,128)(2,1)S(1)} %get-tuple-element.50.theta_ref, bf16[2,192,1024]{2,1,0:T(8,128)(2,1)S(1)} %get-tuple-element.51.phi_ref, bf16[2,192,1024]{2,1,0:T(8,128)(2,1)S(1)} %get-tuple-element.52.energy_ref, ...), custom_call_target="tpu_custom_call" | custom-call | flops 2000000000 | bytes 10000000 | tf_op jit(solution)/shard_map/smooth/pallas_call | solution.py:588
  25.7 0.0 collective-permute-done.4.across_ref
  25.7 0.0 collective-permute-done.5.mate_ref
  25.7 1.0 %finish.1 = bf16[192,4096]{1,0:T(8,128)(2,1)} custom-call(bf16[192,128]{1,0:T(8,128)(2,1)S(1)} %collective-permute-done.4.across_ref, bf16[192,128]{1,0:T(8,128)(2,1)S(1)} %collective-permute-done.5.mate_ref, f32[2,192,1024]{2,1,0:T(8,128)S(1)} %get-tuple-element.55.part_ref, ...), custom_call_target="tpu_custom_call", output_to_operand_aliasing={{}: (4, {})} | custom-call | flops 10000000 | bytes 10000000 | tf_op jit(solution)/shard_map/finish/pallas_call | solution.py:604
  (4 shorter events, 0.0 us)
Async XLA Ops:
  0.0 6.6 %copy-start = (bf16[192,4096]{1,0:T(8,128)(2,1)S(1)}, bf16[192,4096]{1,0:T(8,128)(2,1)}, u32[]{:S(2)}) copy-start(bf16[192,4096]{1,0:T(8,128)(2,1)} %pieces_ref.3) | copy-start | bytes 4718596
  0.0 6.6 %copy-start.1 = (f32[4,1024]{1,0:T(4,128)S(1)}, f32[4,1024]{1,0:T(4,128)}, u32[]{:S(2)}) copy-start(f32[4,1024]{1,0:T(4,128)} %pot_ref.1) | copy-start | bytes 49156
  1.6 7.5 %collective-permute-start = (bf16[192,128]{1,0:T(8,128)(2,1)S(1)}, bf16[192,128]{1,0:T(8,128)(2,1)S(1)}, u32[]{:S(2)}, u32[]{:S(2)}) collective-permute-start(bf16[192,128]{1,0:T(8,128)(2,1)S(1)} %get-tuple-element.31), channel_id=1, source_target_pairs={{1,2},{2,1},{3,4},{4,3},{5,6},{6,5},{7,8},{8,7},{9,10},{10,9},{11,... | collective-permute-start | bytes 147464 | tf_op jit(solution)/shard_map/ppermute | solution.py:494
  2.2 6.8 %collective-permute-start.1 = (bf16[192,128]{1,0:T(8,128)(2,1)S(1)}, bf16[192,128]{1,0:T(8,128)(2,1)S(1)}, u32[]{:S(2)}, u32[]{:S(2)}) collective-permute-start(bf16[192,128]{1,0:T(8,128)(2,1)S(1)} %get-tuple-element.32), channel_id=1, source_target_pairs={{0,1},{1,0},{2,3},{3,2},{4,5},{5,4},{6,7},{7,6},{8,9},{9,8},{10,11... | collective-permute-start | bytes 147464 | tf_op jit(solution)/shard_map/ppermute | solution.py:491
  9.1 7.7 %copy-start.2 = (s32[16,2]{0,1:T(2,128)S(1)}, s32[16,2]{0,1:T(2,128)}, u32[]{:S(2)}) copy-start(s32[16,2]{0,1:T(2,128)} %param.7) | copy-start | bytes 388
  9.7 1.4 %collective-permute-start.2 = (bf16[3,128,128]{2,1,0:T(8,128)(2,1)S(1)}, bf16[3,128,128]{2,1,0:T(8,128)(2,1)S(1)}, u32[]{:S(2)}, u32[]{:S(2)}) collective-permute-start(bf16[3,128,128]{2,1,0:T(8,128)(2,1)S(1)} %get-tuple-element.41), channel_id=1, source_target_pairs={{0,1},{1,0},{2,3},{3,2},{4,5},{5,4},{6,7},{7,6},{8,9},{9,8},{10,11... | collective-permute-start | bytes 294920 | tf_op jit(solution)/shard_map/ppermute | solution.py:491
  16.7 1.3 %collective-permute-start.3 = (bf16[3,64,128]{2,1,0:T(8,128)(2,1)S(1)}, bf16[3,64,128]{2,1,0:T(8,128)(2,1)S(1)}, u32[]{:S(2)}, u32[]{:S(2)}) collective-permute-start(bf16[3,64,128]{2,1,0:T(8,128)(2,1)S(1)} %get-tuple-element.42), channel_id=1, source_target_pairs={{0,1},{1,0},{2,3},{3,2},{4,5},{5,4},{6,7},{7,6},{8,9},{9,8},{10,11... | collective-permute-start | bytes 147464 | tf_op jit(solution)/shard_map/ppermute | solution.py:491
  19.5 6.2 %collective-permute-start.4 = (bf16[192,128]{1,0:T(8,128)(2,1)S(1)}, bf16[192,128]{1,0:T(8,128)(2,1)S(1)}, u32[]{:S(2)}, u32[]{:S(2)}) collective-permute-start(bf16[192,128]{1,0:T(8,128)(2,1)S(1)} %get-tuple-element.48), channel_id=1, source_target_pairs={{1,2},{2,1},{3,4},{4,3},{5,6},{6,5},{7,8},{8,7},{9,10},{10,9},{11,... | collective-permute-start | bytes 147464 | tf_op jit(solution)/shard_map/ppermute | solution.py:494
  20.1 5.6 %collective-permute-start.5 = (bf16[192,128]{1,0:T(8,128)(2,1)S(1)}, bf16[192,128]{1,0:T(8,128)(2,1)S(1)}, u32[]{:S(2)}, u32[]{:S(2)}) collective-permute-start(bf16[192,128]{1,0:T(8,128)(2,1)S(1)} %get-tuple-element.49), channel_id=1, source_target_pairs={{0,1},{1,0},{2,3},{3,2},{4,5},{5,4},{6,7},{7,6},{8,9},{9,8},{10,11... | collective-permute-start | bytes 147464 | tf_op jit(solution)/shard_map/ppermute | solution.py:491

commit v8 on v7

--- a/solution.py
+++ b/solution.py
@@ -57,30 +57,29 @@
     return jnp.transpose(feats.astype(F32))[:ROWS].astype(BF16)
 
 
-def cell_features(plane):
+def cell_features():
     k = iota((16, PLANE), 0)
     cell = iota((16, PLANE), 1)
     y = cell >> 5
     z = cell & 31
-    sq = y * y + z * z + plane * plane
+    sq = y * y + z * z
     feats = jnp.where(k == 0, sq & 255, 0)
     feats = jnp.where(k == 1, sq >> 8, feats)
     feats = jnp.where(k == 2, -2 * y, feats)
     feats = jnp.where(k == 3, -2 * z, feats)
     feats = jnp.where(k == 4, 1, feats)
     feats = jnp.where(k == 5, 256, feats)
-    feats = jnp.where(k == 6, -2 * plane, feats)
     return feats.astype(F32).astype(BF16)
 
 
-def sphere(rows, plane):
-    reach = jnp.dot(rows, cell_features(plane), preferred_element_type=F32)
-    return jnp.where(reach <= 0.0, 1.0, 0.0).astype(BF16)
+def sphere(reach, rows, plane):
+    bound = rows[:, 6:7].astype(F32) * (2.0 * plane) - float(plane * plane)
+    return jnp.where(reach <= bound, 1.0, 0.0).astype(BF16)
 
 
 def in_plane(center, beside):
-    k = iota((2 * TILE, TILE), 0) - 128
-    n = iota((2 * TILE, TILE), 1)
+    k = iota((TILE, TILE), 0)
+    n = iota((TILE, TILE), 1)
     diff = k - n
     near_y = (diff == NZ) | (diff == -NZ)
     near_z = ((diff == 1) | (diff == -1)) & ((k >> 5) == (n >> 5))
@@ -88,13 +87,19 @@
     return jnp.where(diff == 0, float(center), w).astype(BF16)
 
 
-def plane_product(values, weights, t):
-    low = max(0, TILE * t - 128)
-    high = min(PLANE, TILE * t + TILE + 128)
-    shift = 128 - TILE * t
-    return jnp.dot(
-        values[:, low:high], weights[low + shift : high + shift], preferred_element_type=F32
-    )
+def plane_product(ref, weights, beside, t):
+    start = TILE * t
+    values = ref[:, :, start : start + TILE].reshape(2 * ROWS, TILE)
+    out = jnp.dot(values, weights, preferred_element_type=F32).reshape(2, ROWS, TILE)
+    lane = iota((1, 1, 128), 2)
+    first, last = out[:, :, :128], out[:, :, 128:]
+    if t > 0:
+        turned = pltpu.roll(ref[:, :, start - 128 : start].astype(F32), NZ, 2)
+        first = first + jnp.where(lane < NZ, turned * beside, 0.0)
+    if start + TILE < PLANE:
+        turned = pltpu.roll(ref[:, :, start + TILE : start + TILE + 128].astype(F32), 128 - NZ, 2)
+        last = last + jnp.where(lane >= 128 - NZ, turned * beside, 0.0)
+    return jnp.concatenate([first, last], axis=2)
 
 
 def fold(values):
@@ -133,16 +138,19 @@
         across_ref[rows] = jnp.where(even, down[i], up[i]).astype(BF16)
 
 
-def sides(mate_ref, across_ref):
-    mate = mate_ref[...].astype(F32)
-    across = across_ref[...].astype(F32)
+def sides(mate, across):
     even = is_even()
     return (jnp.where(even, across, mate), jnp.where(even, mate, across))
+
+
+def at_end():
+    slab = lax.axis_index("sx")
+    return (slab == 0) | (slab == lax.axis_size("sx") - 1)
 
 
 def edges_kernel(
     table_ref, pieces_ref,
-    phi_ref, mask_ref, rows_ref, mate_ref, across_ref,
+    phi_ref, mask_ref, rows_ref, reach_ref, mate_ref, across_ref,
     window_ref, raw_ref, sems,
 ):
     first = window_start(table_ref.shape[1])
@@ -158,8 +166,10 @@
     table_copy.wait()
     rows = row_features(window_ref, first)
     rows_ref[...] = rows
+    reach = jnp.dot(rows, cell_features(), preferred_element_type=F32)
+    reach_ref[...] = reach
     for i in range(2):
-        mask_ref[i] = sphere(rows, (CX - 1) * i)
+        mask_ref[i] = sphere(reach, rows, (CX - 1) * i)
     for i in range(2):
         copies[i].wait()
         phi_ref[i] = raw_ref[i] * mask_ref[i]
@@ -171,13 +181,12 @@
 
 
 def energy_kernel(
-    rows_ref, pieces_ref, pot_ref, edge_ref,
-    edge_mask_ref,
+    rows_ref, reach_ref, pieces_ref, pot_ref, edge_ref, edge_mask_ref,
     phi_ref, mask_ref, energy_ref, part_ref, edge_energy_ref, corr_ref, ham_ref,
 ):
     rows = rows_ref[...]
     for i in range(2):
-        mask = sphere(rows, 1 + i)
+        mask = sphere(reach_ref[...], rows, 1 + i)
         mask_ref[i] = mask
         phi_ref[i] = pieces_ref[:, PLANE * (1 + i) : PLANE * (2 + i)] * mask
     weights = in_plane(6, -1)
@@ -185,8 +194,8 @@
         lanes = slice(TILE * t, TILE * t + TILE)
         edge = edge_ref[:, :, lanes].astype(F32)
         mid = phi_ref[:, :, lanes].astype(F32)
-        inner = plane_product(phi_ref[...].reshape(2 * ROWS, PLANE), weights, t).reshape(2, ROWS, TILE)
-        outer = plane_product(edge_ref[...].reshape(2 * ROWS, PLANE), weights, t).reshape(2, ROWS, TILE)
+        inner = plane_product(phi_ref, weights, -1.0, t)
+        outer = plane_product(edge_ref, weights, -1.0, t)
         for i in range(2):
             value = 0.5 * (inner[i] - (edge[i] + mid[1 - i])) + pot_ref[1 + i : 2 + i, lanes] * mid[i]
             energy_ref[i, :, lanes] = value.astype(BF16) * mask_ref[i, :, lanes]
@@ -195,16 +204,17 @@
             part_ref[i, :, lanes] = value
             rest = rest_rows(i)
             edge_energy_ref[i, rest, lanes] = value[rest].astype(BF16) * edge_mask_ref[i, rest, lanes]
-    corr = jnp.zeros((ROWS, ROWS), F32)
-    ham = jnp.zeros((ROWS, ROWS), F32)
-    for i in range(2):
-        corr = corr + rows_product(phi_ref[i], phi_ref[i]) + rows_product(edge_ref[i], edge_ref[i])
-        ham = ham + rows_product(energy_ref[i], phi_ref[i])
-    corr_ref[...] = corr
-    ham_ref[...] = ham
+    mid = jnp.concatenate([phi_ref[0], phi_ref[1]], axis=1)
+    both = jnp.concatenate([energy_ref[0], energy_ref[1]], axis=1)
+    gram = rows_product(jnp.concatenate([mid, both], axis=0), mid)
+    corr = gram[:ROWS]
+    ham_ref[...] = gram[ROWS:]
     for i in range(2):
         rest = rest_rows(i)
-        ham_ref[rest] += rows_product(edge_energy_ref[i, rest], edge_ref[i])
+        gram = rows_product(jnp.concatenate([edge_ref[i], edge_energy_ref[i, rest]], axis=0), edge_ref[i])
+        corr = corr + gram[:ROWS]
+        ham_ref[rest] += gram[ROWS:]
+    corr_ref[...] = corr
 
 
 def halo_rows(i):
@@ -221,7 +231,7 @@
 ):
     volume = 1.0 / (4.0 * CX**3)
     gram = []
-    for i, side in enumerate(sides(mate_ref, across_ref)):
+    for i, side in enumerate(sides(mate_ref[...].astype(F32), across_ref[...].astype(F32))):
         tiles = unfold(side)
         for t in range(PLANE // 128):
             lanes = slice(128 * t, 128 * t + 128)
@@ -284,12 +294,10 @@
 
 
 def pick_kernel(both_ref, other_ref, forward_ref):
-    slab = lax.axis_index("sx")
-    even = is_even()
-    end = (slab == 0) | (slab == lax.axis_size("sx") - 1)
+    even = is_even()
     for i in range(7):
         value = jnp.where(even, both_ref[0, i].astype(F32), both_ref[1, i].astype(F32))
-        value = jnp.where(end, 0.0, value).astype(BF16)
+        value = jnp.where(at_end(), 0.0, value).astype(BF16)
         other_ref[i] = value
         if i >= 4:
             forward_ref[i - 4] = value
@@ -398,60 +406,37 @@
     put_messages(edge_grad_ref, mate_ref, across_ref)
 
 
-def smooth_kernel(
-    theta_ref, phi_ref, energy_ref, edge_ref, mask_ref, edge_mask_ref,
-    out_ref, part_ref,
-    grad_ref, done_ref, rest_ref, sems,
+def final_kernel(
+    both_ref, mate_ref, theta_ref, phi_ref, energy_ref, edge_ref, mask_ref, edge_mask_ref,
+    out_ref,
+    grad_ref, done_ref, sems,
 ):
     put_gradient(theta_ref[...], phi_ref, energy_ref, mask_ref, grad_ref)
     weights = in_plane(8, 1)
+    across = jnp.where(is_even(), both_ref[0].astype(F32), both_ref[1].astype(F32))
+    halos = [unfold(side) for side in sides(mate_ref[...].astype(F32), jnp.where(at_end(), 0.0, across))]
+    copies = []
     for t in range(PLANE // TILE):
         lanes = slice(TILE * t, TILE * t + TILE)
         edge = edge_ref[:, :, lanes].astype(F32)
         mid = grad_ref[:, :, lanes].astype(F32)
-        inner = plane_product(grad_ref[...].reshape(2 * ROWS, PLANE), weights, t).reshape(2, ROWS, TILE)
-        outer = plane_product(edge_ref[...].reshape(2 * ROWS, PLANE), weights, t).reshape(2, ROWS, TILE)
+        inner = plane_product(grad_ref, weights, 1.0, t)
+        outer = plane_product(edge_ref, weights, 1.0, t)
         for i in range(2):
             value = (inner[i] + (edge[i] + mid[1 - i])) * (1.0 / 32.0)
-            done_ref[i, :, lanes] = value.astype(BF16) * mask_ref[i, :, lanes]
-            part_ref[i, :, lanes] = outer[i] + mid[i]
-        for i in range(2):
-            rows = rest_rows(i)
-            value = part_ref[i, rows, lanes] * (1.0 / 32.0)
-            rest_ref[i, :, lanes] = value.astype(BF16) * edge_mask_ref[i, rows, lanes]
-    copies = []
-    for i in range(2):
-        start = PLANE * (1 + i)
-        copies.append(
-            pltpu.make_async_copy(done_ref.at[i], out_ref.at[:, start : start + PLANE], sems.at[i])
-        )
-        start = PLANE * (CX - 1) * i
-        copies.append(
-            pltpu.make_async_copy(
-                rest_ref.at[i], out_ref.at[rest_rows(i), start : start + PLANE], sems.at[2 + i]
-            )
-        )
-    for copy in copies:
-        copy.start()
-    for copy in copies:
-        copy.wait()
-
-
-def finish_kernel(across_ref, mate_ref, part_ref, mask_ref, inner_ref, out_ref, done_ref, sems):
-    copies = []
-    for i, side in enumerate(sides(mate_ref, across_ref)):
-        tiles = unfold(side)
-        for half in range(2):
-            rows = slice(ORB * (half + i), ORB * (half + i) + ORB)
-            got = slice(ORB * half, ORB * half + ORB)
-            for t in range(PLANE // 128):
-                lanes = slice(128 * t, 128 * t + 128)
-                value = (part_ref[i, rows, lanes] + tiles[t % 3][got]) * (1.0 / 32.0)
-                done_ref[2 * i + half, :, lanes] = value.astype(BF16) * mask_ref[i, rows, lanes]
-            start = PLANE * (CX - 1) * i
+            done_ref[1 + i, :, lanes] = value.astype(BF16) * mask_ref[i, :, lanes]
+            plane = (CX - 1) * i
+            halo = jnp.concatenate([halos[i][2 * t % 3], halos[i][(2 * t + 1) % 3]], axis=1)
+            base = outer[i] + mid[i]
+            value = (base[halo_rows(i)] + halo) * (1.0 / 32.0)
+            done_ref[plane, halo_rows(i), lanes] = value.astype(BF16) * edge_mask_ref[i, halo_rows(i), lanes]
+            value = base[rest_rows(i)] * (1.0 / 32.0)
+            done_ref[plane, rest_rows(i), lanes] = value.astype(BF16) * edge_mask_ref[i, rest_rows(i), lanes]
+        for plane in range(CX):
+            start = PLANE * plane + TILE * t
             copies.append(
                 pltpu.make_async_copy(
-                    done_ref.at[2 * i + half], out_ref.at[rows, start : start + PLANE], sems.at[2 * i + half]
+                    done_ref.at[plane, :, lanes], out_ref.at[:, start : start + TILE], sems.at[t, plane]
                 )
             )
             copies[-1].start()
@@ -499,11 +484,13 @@
     table = centers.T
     pair = shape(2, ROWS, PLANE)
 
-    edge, edge_mask, rows, for_mate, for_other = pl.pallas_call(
+    edge, edge_mask, rows, reach, for_mate, for_other = pl.pallas_call(
         edges_kernel,
-        out_shape=(pair, pair, shape(ROWS, 16), shape(ROWS, 128), shape(ROWS, 128)),
+        out_shape=(
+            pair, pair, shape(ROWS, 16), shape(ROWS, PLANE, dtype=F32), shape(ROWS, 128), shape(ROWS, 128),
+        ),
         in_specs=[FAR, FAR],
-        out_specs=(WHOLE,) * 5,
+        out_specs=(WHOLE,) * 6,
         scratch_shapes=[
             pltpu.VMEM((4, 4 * ORB), jnp.int32),
             pltpu.VMEM((2, ROWS, PLANE), BF16),
@@ -522,12 +509,12 @@
             pair, pair, pair, shape(2, ROWS, PLANE, dtype=F32), pair,
             shape(ROWS, ROWS, dtype=F32), shape(ROWS, ROWS, dtype=F32),
         ),
-        in_specs=[WHOLE] * 5,
+        in_specs=[WHOLE] * 6,
         out_specs=(WHOLE,) * 7,
         compiler_params=PARAMS,
         cost_estimate=cost(4 * 10**9, 10**7),
         name="energy",
-    )(rows, pieces, potential, edge, edge_mask)
+    )(rows, reach, pieces, potential, edge, edge_mask)
 
     edge_energy, own, for_mate = pl.pallas_call(
         bands_kernel,
@@ -582,36 +569,23 @@
         cost_estimate=cost(10**9, 10**7),
         name="gradient",
     )(patterns, relayed, ham_band, inv_band, base, edge, edge_energy, edge_mask)
-    other_side = across(for_other)
     mate_side = to_mate(for_mate)
-
-    inner, part = pl.pallas_call(
-        smooth_kernel,
-        out_shape=(pltpu.HBM((ROWS, CX * PLANE), BF16), shape(2, ROWS, PLANE, dtype=F32)),
-        in_specs=[WHOLE] * 6,
-        out_specs=(FAR, WHOLE),
+    both_sides = gathered(for_other)
+
+    return pl.pallas_call(
+        final_kernel,
+        out_shape=pltpu.HBM((ROWS, CX * PLANE), BF16),
+        in_specs=[WHOLE] * 8,
+        out_specs=FAR,
         scratch_shapes=[
             pltpu.VMEM((2, ROWS, PLANE), BF16),
-            pltpu.VMEM((2, ROWS, PLANE), BF16),
-            pltpu.VMEM((2, ORB, PLANE), BF16),
-            pltpu.SemaphoreType.DMA((4,)),
+            pltpu.VMEM((CX, ROWS, PLANE), BF16),
+            pltpu.SemaphoreType.DMA((PLANE // TILE, CX)),
         ],
         compiler_params=PARAMS,
         cost_estimate=cost(2 * 10**9, 10**7),
-        name="smooth",
-    )(theta, mid, mid_energy, edge_grad, mid_mask, edge_mask)
-
-    return pl.pallas_call(
-        finish_kernel,
-        out_shape=pltpu.HBM((ROWS, CX * PLANE), BF16),
-        in_specs=[WHOLE] * 4 + [FAR],
-        out_specs=FAR,
-        scratch_shapes=[pltpu.VMEM((4, ORB, PLANE), BF16), pltpu.SemaphoreType.DMA((4,))],
-        input_output_aliases={4: 0},
-        compiler_params=PARAMS,
-        cost_estimate=cost(10**7, 10**7),
-        name="finish",
-    )(other_side, mate_side, part, edge_mask, inner)
+        name="final",
+    )(both_sides, mate_side, theta, mid, mid_energy, edge_grad, mid_mask, edge_mask)
 
 
 def solution(mesh):

time: 26.8 us -> 27 us (level)
  blocking collectives: 5.46 us -> 10.2 us
  starting transfers between devices: 9.15 us -> 5.64 us
  Pallas kernels: 10.5 us -> 9.21 us
    all_gather x1 -> x2, blocking collectives: 5.46 us -> 10.2 us  [gathered(): return lax.all_gather(value, ('grp', 'sx'), axis_index_groups=pairs)]
    ppermute x4, starting transfers between devices: 7.82 us -> 4.98 us  [to_mate(): return lax.ppermute(value, 'sx', mates)]
    pallas_call x2 -> x1, Pallas kernels: 3.25 us -> 2.39 us  [per_device(): pl.pallas_call(final_kernel, out_shape=pltpu.HBM((ROWS, CX * PLANE), BF16...]
    ppermute x2 -> x1, starting transfers between devices: 1.33 us -> 0.66 us  [across(): return lax.ppermute(value, 'sx', others)]
    pallas_call x1, Pallas kernels: 2.41 us -> 2.07 us  [per_device(): pl.pallas_call(energy_kernel, out_shape=(pair, pair, pair, shape(2, ROWS,...]
  transfers between devices with their start and end apart: 6 -> 5, of which waited for: 2 -> 2; matrix products, arithmetic and copies ran while one was open for 0% -> 0% of each run, Pallas kernels for 21% -> 12%
where the time goes in v8:
time: 27 us; the launch traced here: 26.6 us
  blocking collectives  10.2 us (38%)
  Pallas kernels  9.21 us (34%)
  starting transfers between devices  5.64 us (21%)
  waiting for transfers between devices  1.42 us (5%)
    all_gather x2, blocking collectives, gathered(): return lax.all_gather(value, ('grp', 'sx'), axis_index_groups=pairs)  10.2 us
    ppermute x4, starting transfers between devices, to_mate(): return lax.ppermute(value, 'sx', mates)  4.98 us
    pallas_call x1, Pallas kernels, per_device(): pl.pallas_call(final_kernel, out_shape=pltpu.HBM((ROWS, CX * PLANE), BF16...  2.39 us
    pallas_call x1, Pallas kernels, per_device(): pl.pallas_call(energy_kernel, out_shape=(pair, pair, pair, shape(2, ROWS,...  2.07 us
    pallas_call x1, Pallas kernels, per_device(): pl.pallas_call(edges_kernel, out_shape=(pair, pair, shape(ROWS, 16), shap...  1.49 us
    ppermute x4, waiting for transfers between devices, to_mate(): return lax.ppermute(value, 'sx', mates)  1.42 us
    pallas_call x1, Pallas kernels, per_device(): pl.pallas_call(gradient_kernel, out_shape=(pair, shape(ROWS, ROWS), shape...  1.41 us
    pallas_call x1, Pallas kernels, per_device(): pl.pallas_call(theta_kernel, out_shape=(band, band, shape(ROWS, ROWS, dty...  1.05 us
  transfers between devices with their start and end apart: 5, of which 2 were waited for; matrix products, arithmetic and copies ran while one was open for 0% of the time, Pallas kernels for 12%

profile of v8, /device:TPU:0, one launch (start us, length us, event | category | flops | bytes accessed | tf_op | source)
XLA Modules:
  0.0 26.6 jit_solution(3270497476650164332)
XLA Ops:
  0.0 0.0 copy-start
  0.0 1.5 %edges.1 = (bf16[2,192,1024]{2,1,0:T(8,128)(2,1)S(1)}, bf16[2,192,1024]{2,1,0:T(8,128)(2,1)S(1)}, bf16[192,16]{1,0:T(8,128)(2,1)S(1)}, f32[192,1024]{1,0:T(8,128...) custom-call(s32[4,1024]{1,0:T(4,128)} %bitcast.8, bf16[192,4096]{1,0:T(8,128)(2,1)} %pieces_ref.3), custom_call_target="tpu_custom_call" | custom-call | flops 100000000 | bytes 1000000 | tf_op jit(solution)/shard_map/edges/pallas_call | solution.py:487
  1.5 0.7 %collective-permute-start = (bf16[192,128]{1,0:T(8,128)(2,1)S(1)}, bf16[192,128]{1,0:T(8,128)(2,1)S(1)}, u32[]{:S(2)}, u32[]{:S(2)}) collective-permute-start(bf16[192,128]{1,0:T(8,128)(2,1)S(1)} %get-tuple-element.30), channel_id=1, source_target_pairs={{1,2},{2,1},{3,4},{4,3},{5,6},{6,5},{7,8},{8,7},{9,10},{10,9},{11,... | collective-permute-start | bytes 147464 | tf_op jit(solution)/shard_map/ppermute | solution.py:479
  2.2 4.4 %collective-permute-start.1 = (bf16[192,128]{1,0:T(8,128)(2,1)S(1)}, bf16[192,128]{1,0:T(8,128)(2,1)S(1)}, u32[]{:S(2)}, u32[]{:S(2)}) collective-permute-start(bf16[192,128]{1,0:T(8,128)(2,1)S(1)} %get-tuple-element.31), channel_id=1, source_target_pairs={{0,1},{1,0},{2,3},{3,2},{4,5},{5,4},{6,7},{7,6},{8,9},{9,8},{10,11... | collective-permute-start | bytes 147464 | tf_op jit(solution)/shard_map/ppermute | solution.py:476
  6.6 0.0 copy-done
  6.6 0.0 copy-done.1
  6.6 2.1 %energy.1 = (bf16[2,192,1024]{2,1,0:T(8,128)(2,1)S(1)}, bf16[2,192,1024]{2,1,0:T(8,128)(2,1)S(1)}, bf16[2,192,1024]{2,1,0:T(8,128)(2,1)S(1)}, f32[2,192,1024]{2,...) custom-call(bf16[192,16]{1,0:T(8,128)(2,1)S(1)} %get-tuple-element.32.rows_ref, ...), custom_call_target="tpu_custom_call" | custom-call | flops 4000000000 | bytes 10000000 | tf_op jit(solution)/shard_map/energy/pallas_call | solution.py:506
  8.7 0.0 collective-permute-done.across_ref
  8.7 0.0 collective-permute-done.1.mate_ref
  8.7 0.0 copy-start.2
  8.7 0.6 %bands.1 = (bf16[2,192,1024]{2,1,0:T(8,128)(2,1)S(1)}, f32[2,192,256]{2,1,0:T(8,128)S(1)}, bf16[3,128,128]{2,1,0:T(8,128)(2,1)S(1)}) custom-call(bf16[192,128]{1,0:T(8,128)(2,1)S(1)} %collective-permute-done.across_ref, bf16[192,128]{1,0:T(8,128)(2,1)S(1)} %collective-permute-done.1.mate_ref, ...), custom_call_target="tpu_custom_call", output_to_operand_aliasing={{0}: (7, {})} | custom-call | flops 1000000000 | bytes 10000000 | tf_op jit(solution)/shard_map/bands/pallas_call | solution.py:519
  9.3 0.1 collective-permute-start.2
  9.4 1.3 %collective-permute-done.2.rows_ref = bf16[3,128,128]{2,1,0:T(8,128)(2,1)S(1)} collective-permute-done((bf16[3,128,128]{2,1,0:T(8,128)(2,1)S(1)}, bf16[3,128,128]{2,1,0:T(8,128)(2,1)S(1)}, u32[]{:S(2)}, u32[]{:S(2)}) %collective-permute-start.2) | collective-permute-done | bytes 98336 | tf_op jit(solution)/shard_map/ppermute | solution.py:476
  10.6 0.2 relay.1
  10.8 5.5 %all-gather = bf16[14,64,128]{2,1,0:T(8,128)(2,1)S(1)} all-gather(bf16[7,64,128]{2,1,0:T(8,128)(2,1)S(1)} %relay.1), channel_id=2, replica_groups={{1,2},{3,4},{5,6},{7,8},{9,10},{11,12},{13,14},{17,18},{19,20},{21,22},..., dimensions={0}, use_global_device_ids=true | all-gather | bytes 344064 | tf_op jit(solution)/shard_map/all_gather | solution.py:482
  16.3 0.1 collective-permute-start.3
  16.4 0.0 copy-done.2
  16.4 1.1 %theta.1 = (f32[192,512]{1,0:T(8,128)S(1)}, f32[192,512]{1,0:T(8,128)S(1)}, f32[192,192]{1,0:T(8,128)S(1)}) custom-call(s32[2,16]{1,0:T(2,128)S(1)} %bitcast.6, f32[2,192,256]{2,1,0:T(8,128)S(1)} %get-tuple-element.40.own_ref, bf16[3,128,128]{2,1,0:T(8,128)(2,1)S(1)} %collective-permute-done.2.rows_ref, bf16[7,64,128]{2,1,0:T(8,128)(2,1)S(1)} %get-tuple-element.43.other_ref), custom_call_target="tpu_custom_call" | custom-call | flops 1000000000 | bytes 4000000 | tf_op jit(solution)/shard_map/theta/pallas_call | solution.py:553
  17.5 0.1 collective-permute-done.3.relayed_ref
  17.6 1.4 %gradient.1 = (bf16[2,192,1024]{2,1,0:T(8,128)(2,1)S(1)}, bf16[192,192]{1,0:T(8,128)(2,1)S(1)}, bf16[192,128]{1,0:T(8,128)(2,1)S(1)}, bf16[192,128]{1,0:T(8,128)(2,1)S(1)}) custom-call(s32[2,16]{1,0:T(2,128)S(1)} %bitcast.7, bf16[3,64,128]{2,1,0:T(8,128)(2,1)S(1)} %collective-permute-done.3.relayed_ref, f32[192,512]{1,0:T(8,128)S(1)} %get-tuple-element.44.ham_ref, ...), custom_call_target="tpu_custom_call" | custom-call | flops 1000000000 | bytes 10000000 | tf_op jit(solution)/shard_map/gradient/pallas_call | solution.py:562
  19.0 0.4 %collective-permute-start.4 = (bf16[192,128]{1,0:T(8,128)(2,1)S(1)}, bf16[192,128]{1,0:T(8,128)(2,1)S(1)}, u32[]{:S(2)}, u32[]{:S(2)}) collective-permute-start(bf16[192,128]{1,0:T(8,128)(2,1)S(1)} %get-tuple-element.49), channel_id=1, source_target_pairs={{0,1},{1,0},{2,3},{3,2},{4,5},{5,4},{6,7},{7,6},{8,9},{9,8},{10,11... | collective-permute-start | bytes 147464 | tf_op jit(solution)/shard_map/ppermute | solution.py:476
  19.5 4.8 %all-gather.1 = bf16[384,128]{1,0:T(8,128)(2,1)S(1)} all-gather(bf16[192,128]{1,0:T(8,128)(2,1)S(1)} %get-tuple-element.48), channel_id=3, replica_groups={{1,2},{3,4},{5,6},{7,8},{9,10},{11,12},{13,14},{17,18},{19,20},{21,22},..., dimensions={0}, use_global_device_ids=true | all-gather | bytes 147456 | tf_op jit(solution)/shard_map/all_gather | solution.py:482
  24.2 0.0 collective-permute-done.4.mate_ref
  24.2 2.4 %final.1 = bf16[192,4096]{1,0:T(8,128)(2,1)} custom-call(bf16[2,192,128]{2,1,0:T(8,128)(2,1)S(1)} %bitcast.5, bf16[192,128]{1,0:T(8,128)(2,1)S(1)} %collective-permute-done.4.mate_ref, bf16[192,192]{1,0:T(8,128)(2,1)S(1)} %get-tuple-element.50.theta_ref, bf16[2,192,1024]{2,1,0:T(8,128)(2,1)S(1)} %get-tuple-element.51.phi_ref, ...), custom_call_target="tpu_custom_call" | custom-call | flops 2000000000 | bytes 10000000 | tf_op jit(solution)/shard_map/final/pallas_call | solution.py:575
  (2 shorter events, 0.0 us)
Async XLA Ops:
  0.0 6.6 %copy-start = (bf16[192,4096]{1,0:T(8,128)(2,1)S(1)}, bf16[192,4096]{1,0:T(8,128)(2,1)}, u32[]{:S(2)}) copy-start(bf16[192,4096]{1,0:T(8,128)(2,1)} %pieces_ref.3) | copy-start | bytes 4718596
  0.0 6.6 %copy-start.1 = (f32[4,1024]{1,0:T(4,128)S(1)}, f32[4,1024]{1,0:T(4,128)}, u32[]{:S(2)}) copy-start(f32[4,1024]{1,0:T(4,128)} %pot_ref.1) | copy-start | bytes 49156
  1.5 7.2 %collective-permute-start = (bf16[192,128]{1,0:T(8,128)(2,1)S(1)}, bf16[192,128]{1,0:T(8,128)(2,1)S(1)}, u32[]{:S(2)}, u32[]{:S(2)}) collective-permute-start(bf16[192,128]{1,0:T(8,128)(2,1)S(1)} %get-tuple-element.30), channel_id=1, source_target_pairs={{1,2},{2,1},{3,4},{4,3},{5,6},{6,5},{7,8},{8,7},{9,10},{10,9},{11,... | collective-permute-start | bytes 147464 | tf_op jit(solution)/shard_map/ppermute | solution.py:479
  2.2 6.5 %collective-permute-start.1 = (bf16[192,128]{1,0:T(8,128)(2,1)S(1)}, bf16[192,128]{1,0:T(8,128)(2,1)S(1)}, u32[]{:S(2)}, u32[]{:S(2)}) collective-permute-start(bf16[192,128]{1,0:T(8,128)(2,1)S(1)} %get-tuple-element.31), channel_id=1, source_target_pairs={{0,1},{1,0},{2,3},{3,2},{4,5},{5,4},{6,7},{7,6},{8,9},{9,8},{10,11... | collective-permute-start | bytes 147464 | tf_op jit(solution)/shard_map/ppermute | solution.py:476
  8.7 7.7 %copy-start.2 = (s32[16,2]{0,1:T(2,128)S(1)}, s32[16,2]{0,1:T(2,128)}, u32[]{:S(2)}) copy-start(s32[16,2]{0,1:T(2,128)} %param.7) | copy-start | bytes 388
  9.3 1.4 %collective-permute-start.2 = (bf16[3,128,128]{2,1,0:T(8,128)(2,1)S(1)}, bf16[3,128,128]{2,1,0:T(8,128)(2,1)S(1)}, u32[]{:S(2)}, u32[]{:S(2)}) collective-permute-start(bf16[3,128,128]{2,1,0:T(8,128)(2,1)S(1)} %get-tuple-element.41), channel_id=1, source_target_pairs={{0,1},{1,0},{2,3},{3,2},{4,5},{5,4},{6,7},{7,6},{8,9},{9,8},{10,11... | collective-permute-start | bytes 294920 | tf_op jit(solution)/shard_map/ppermute | solution.py:476
  16.3 1.3 %collective-permute-start.3 = (bf16[3,64,128]{2,1,0:T(8,128)(2,1)S(1)}, bf16[3,64,128]{2,1,0:T(8,128)(2,1)S(1)}, u32[]{:S(2)}, u32[]{:S(2)}) collective-permute-start(bf16[3,64,128]{2,1,0:T(8,128)(2,1)S(1)} %get-tuple-element.42), channel_id=1, source_target_pairs={{0,1},{1,0},{2,3},{3,2},{4,5},{5,4},{6,7},{7,6},{8,9},{9,8},{10,11... | collective-permute-start | bytes 147464 | tf_op jit(solution)/shard_map/ppermute | solution.py:476
  19.0 5.2 %collective-permute-start.4 = (bf16[192,128]{1,0:T(8,128)(2,1)S(1)}, bf16[192,128]{1,0:T(8,128)(2,1)S(1)}, u32[]{:S(2)}, u32[]{:S(2)}) collective-permute-start(bf16[192,128]{1,0:T(8,128)(2,1)S(1)} %get-tuple-element.49), channel_id=1, source_target_pairs={{0,1},{1,0},{2,3},{3,2},{4,5},{5,4},{6,7},{7,6},{8,9},{9,8},{10,11... | collective-permute-start | bytes 147464 | tf_op jit(solution)/shard_map/ppermute | solution.py:476

commit v9 on v8

--- a/solution.py
+++ b/solution.py
@@ -95,10 +95,12 @@
     first, last = out[:, :, :128], out[:, :, 128:]
     if t > 0:
         turned = pltpu.roll(ref[:, :, start - 128 : start].astype(F32), NZ, 2)
-        first = first + jnp.where(lane < NZ, turned * beside, 0.0)
+        turned = jnp.where(lane < NZ, turned, 0.0)
+        first = first + turned if beside > 0 else first - turned
     if start + TILE < PLANE:
         turned = pltpu.roll(ref[:, :, start + TILE : start + TILE + 128].astype(F32), 128 - NZ, 2)
-        last = last + jnp.where(lane >= 128 - NZ, turned * beside, 0.0)
+        turned = jnp.where(lane >= 128 - NZ, turned, 0.0)
+        last = last + turned if beside > 0 else last - turned
     return jnp.concatenate([first, last], axis=2)
 
 
@@ -163,10 +165,11 @@
             pltpu.make_async_copy(pieces_ref.at[:, start : start + PLANE], raw_ref.at[i], sems.at[i])
         )
         copies[i].start()
+    cells = cell_features()
     table_copy.wait()
     rows = row_features(window_ref, first)
     rows_ref[...] = rows
-    reach = jnp.dot(rows, cell_features(), preferred_element_type=F32)
+    reach = jnp.dot(rows, cells, preferred_element_type=F32)
     reach_ref[...] = reach
     for i in range(2):
         mask_ref[i] = sphere(reach, rows, (CX - 1) * i)
@@ -337,7 +340,11 @@
     return rows_product(a[0], b[0]) + (rows_product(a[0], b[1]) + rows_product(a[1], b[0]))
 
 
-def theta_kernel(pattern_ref, own_ref, rows_ref, other_ref, ham_ref, inv_ref, theta_ref):
+def theta_kernel(
+    pattern_ref, own_ref, rows_ref, other_ref,
+    window_ref, theta_ref,
+    ham_ref, inv_ref,
+):
     even = is_even()
     low = low_half()
     zero = jnp.zeros((ORB, 128), F32)
@@ -367,11 +374,14 @@
                     on = iota((ORB, 128), 0) + (ORB * (r + 2) - 128 * q) == iota((ORB, 128), 1)
                     value = jnp.where(on, 2.0, 0.0) - value
                 band_ref[ORB * r : ORB * r + ORB, 128 * q : 128 * q + 128] = value
-    theta_ref[...] = fine_product(split(ham_ref[...]), split(inv_ref[...]))
+    ham, inv = split(ham_ref[...]), split(inv_ref[...])
+    theta_ref[...] = fine_product(ham, inv)
+    for which, (high, _) in enumerate((ham, inv)):
+        window_ref[which] = jnp.where(even, high[:, 256:512].astype(F32), high[:, 0:256].astype(F32)).astype(BF16)
 
 
 def gradient_kernel(
-    pattern_ref, relayed_ref, ham_ref, inv_ref, base_ref,
+    pattern_ref, relayed_ref, bands_ref, base_ref,
     edge_ref, edge_energy_ref, edge_mask_ref,
     edge_grad_ref, theta_ref, mate_ref, across_ref,
     window_ref, total_ref,
@@ -387,14 +397,12 @@
             tiles.append(value * jnp.where(even, kept(pattern_ref, 2, 2 + q), kept(pattern_ref, 0, q)))
         more.append(jnp.concatenate(tiles, axis=1))
     first, third = slice(0, ORB), slice(2 * ORB, ROWS)
-    window_ref[...] = jnp.where(even, ham_ref[:, 256:512], ham_ref[:, 0:256])
-    window_ref[first] += jnp.where(even, 0.0, more[0])
-    window_ref[third] += jnp.where(even, more[0], 0.0)
-    ham = jnp.concatenate(split(window_ref[...]), axis=1)
-    inv = jnp.concatenate(split(jnp.where(even, inv_ref[:, 256:512], inv_ref[:, 0:256])), axis=1)
-    more = [jnp.concatenate([value.astype(BF16)] * 2, axis=1) for value in more]
-    column = rows_product(ham, more[1])
-    row = rows_product(more[0], inv)
+    window_ref[...] = bands_ref[0]
+    window_ref[first] = (bands_ref[0, first].astype(F32) + jnp.where(even, 0.0, more[0])).astype(BF16)
+    window_ref[third] = (bands_ref[0, third].astype(F32) + jnp.where(even, more[0], 0.0)).astype(BF16)
+    more = [value.astype(BF16) for value in more]
+    column = rows_product(window_ref[...], more[1])
+    row = rows_product(more[0], bands_ref[1])
     total_ref[...] = base_ref[...]
     total_ref[first] += jnp.where(even, 0.0, row)
     total_ref[third] += jnp.where(even, row, 0.0)
@@ -406,16 +414,19 @@
     put_messages(edge_grad_ref, mate_ref, across_ref)
 
 
-def final_kernel(
-    both_ref, mate_ref, theta_ref, phi_ref, energy_ref, edge_ref, mask_ref, edge_mask_ref,
-    out_ref,
-    grad_ref, done_ref, sems,
+def smooth_kernel(
+    theta_ref, phi_ref, energy_ref, edge_ref, mask_ref, edge_mask_ref,
+    out_ref, part_ref,
+    grad_ref, done_ref, rest_ref, sems,
 ):
     put_gradient(theta_ref[...], phi_ref, energy_ref, mask_ref, grad_ref)
     weights = in_plane(8, 1)
-    across = jnp.where(is_even(), both_ref[0].astype(F32), both_ref[1].astype(F32))
-    halos = [unfold(side) for side in sides(mate_ref[...].astype(F32), jnp.where(at_end(), 0.0, across))]
     copies = []
+
+    def send(source, rows, start, sem):
+        copies.append(pltpu.make_async_copy(source, out_ref.at[rows, start : start + TILE], sem))
+        copies[-1].start()
+
     for t in range(PLANE // TILE):
         lanes = slice(TILE * t, TILE * t + TILE)
         edge = edge_ref[:, :, lanes].astype(F32)
@@ -424,19 +435,34 @@
         outer = plane_product(edge_ref, weights, 1.0, t)
         for i in range(2):
             value = (inner[i] + (edge[i] + mid[1 - i])) * (1.0 / 32.0)
-            done_ref[1 + i, :, lanes] = value.astype(BF16) * mask_ref[i, :, lanes]
-            plane = (CX - 1) * i
-            halo = jnp.concatenate([halos[i][2 * t % 3], halos[i][(2 * t + 1) % 3]], axis=1)
-            base = outer[i] + mid[i]
-            value = (base[halo_rows(i)] + halo) * (1.0 / 32.0)
-            done_ref[plane, halo_rows(i), lanes] = value.astype(BF16) * edge_mask_ref[i, halo_rows(i), lanes]
-            value = base[rest_rows(i)] * (1.0 / 32.0)
-            done_ref[plane, rest_rows(i), lanes] = value.astype(BF16) * edge_mask_ref[i, rest_rows(i), lanes]
-        for plane in range(CX):
-            start = PLANE * plane + TILE * t
+            done_ref[i, :, lanes] = value.astype(BF16) * mask_ref[i, :, lanes]
+            value = outer[i] + mid[i]
+            part_ref[i, :, lanes] = value
+            rest = rest_rows(i)
+            value = value[rest] * (1.0 / 32.0)
+            rest_ref[i, :, lanes] = value.astype(BF16) * edge_mask_ref[i, rest, lanes]
+        for i in range(2):
+            send(done_ref.at[i, :, lanes], slice(0, ROWS), PLANE * (1 + i) + TILE * t, sems.at[t, i])
+            send(rest_ref.at[i, :, lanes], rest_rows(i), PLANE * (CX - 1) * i + TILE * t, sems.at[t, 2 + i])
+    for copy in copies:
+        copy.wait()
+
+
+def finish_kernel(across_ref, mate_ref, part_ref, mask_ref, inner_ref, out_ref, done_ref, sems):
+    halos = [unfold(side) for side in sides(mate_ref[...].astype(F32), across_ref[...].astype(F32))]
+    copies = []
+    for h in range(4):
+        for i in range(2):
+            for t in (2 * h, 2 * h + 1):
+                lanes = slice(128 * t, 128 * t + 128)
+                value = (part_ref[i, halo_rows(i), lanes] + halos[i][t % 3]) * (1.0 / 32.0)
+                done_ref[i, :, lanes] = value.astype(BF16) * mask_ref[i, halo_rows(i), lanes]
+            start = PLANE * (CX - 1) * i + TILE * h
             copies.append(
                 pltpu.make_async_copy(
-                    done_ref.at[plane, :, lanes], out_ref.at[:, start : start + TILE], sems.at[t, plane]
+                    done_ref.at[i, :, TILE * h : TILE * h + TILE],
+                    out_ref.at[halo_rows(i), start : start + TILE],
+                    sems.at[i, h],
                 )
             )
             copies[-1].start()
@@ -549,12 +575,12 @@
 
     patterns = pattern.T
     scalars = pl.BlockSpec(memory_space=pltpu.SMEM)
-    band = shape(ROWS, 8 * ORB, dtype=F32)
-    ham_band, inv_band, base = pl.pallas_call(
+    bands, base = pl.pallas_call(
         theta_kernel,
-        out_shape=(band, band, shape(ROWS, ROWS, dtype=F32)),
+        out_shape=(shape(2, ROWS, TILE), shape(ROWS, ROWS, dtype=F32)),
         in_specs=[scalars] + [WHOLE] * 3,
-        out_specs=(WHOLE,) * 3,
+        out_specs=(WHOLE,) * 2,
+        scratch_shapes=[pltpu.VMEM((ROWS, 8 * ORB), F32), pltpu.VMEM((ROWS, 8 * ORB), F32)],
         compiler_params=PARAMS,
         cost_estimate=cost(10**9, 4 * 10**6),
         name="theta",
@@ -562,30 +588,43 @@
     edge_grad, theta, for_mate, for_other = pl.pallas_call(
         gradient_kernel,
         out_shape=(pair, shape(ROWS, ROWS), shape(ROWS, 128), shape(ROWS, 128)),
-        in_specs=[scalars] + [WHOLE] * 7,
+        in_specs=[scalars] + [WHOLE] * 6,
         out_specs=(WHOLE,) * 4,
-        scratch_shapes=[pltpu.VMEM((ROWS, TILE), F32), pltpu.VMEM((ROWS, ROWS), F32)],
+        scratch_shapes=[pltpu.VMEM((ROWS, TILE), BF16), pltpu.VMEM((ROWS, ROWS), F32)],
         compiler_params=PARAMS,
         cost_estimate=cost(10**9, 10**7),
         name="gradient",
-    )(patterns, relayed, ham_band, inv_band, base, edge, edge_energy, edge_mask)
+    )(patterns, relayed, bands, base, edge, edge_energy, edge_mask)
+    other_side = across(for_other)
     mate_side = to_mate(for_mate)
-    both_sides = gathered(for_other)
-
-    return pl.pallas_call(
-        final_kernel,
-        out_shape=pltpu.HBM((ROWS, CX * PLANE), BF16),
-        in_specs=[WHOLE] * 8,
-        out_specs=FAR,
+
+    inner, part = pl.pallas_call(
+        smooth_kernel,
+        out_shape=(pltpu.HBM((ROWS, CX * PLANE), BF16), shape(2, ROWS, PLANE, dtype=F32)),
+        in_specs=[WHOLE] * 6,
+        out_specs=(FAR, WHOLE),
         scratch_shapes=[
             pltpu.VMEM((2, ROWS, PLANE), BF16),
-            pltpu.VMEM((CX, ROWS, PLANE), BF16),
-            pltpu.SemaphoreType.DMA((PLANE // TILE, CX)),
+            pltpu.VMEM((2, ROWS, PLANE), BF16),
+            pltpu.VMEM((2, ORB, PLANE), BF16),
+            pltpu.SemaphoreType.DMA((PLANE // TILE, 4)),
         ],
         compiler_params=PARAMS,
         cost_estimate=cost(2 * 10**9, 10**7),
-        name="final",
-    )(both_sides, mate_side, theta, mid, mid_energy, edge_grad, mid_mask, edge_mask)
+        name="smooth",
+    )(theta, mid, mid_energy, edge_grad, mid_mask, edge_mask)
+
+    return pl.pallas_call(
+        finish_kernel,
+        out_shape=pltpu.HBM((ROWS, CX * PLANE), BF16),
+        in_specs=[WHOLE] * 4 + [FAR],
+        out_specs=FAR,
+        scratch_shapes=[pltpu.VMEM((2, 2 * ORB, PLANE), BF16), pltpu.SemaphoreType.DMA((2, PLANE // TILE))],
+        input_output_aliases={4: 0},
+        compiler_params=PARAMS,
+        cost_estimate=cost(10**7, 10**7),
+        name="finish",
+    )(other_side, mate_side, part, edge_mask, inner)
 
 
 def solution(mesh):

time: 27 us -> 26.7 us (0.989)
  blocking collectives: 10.2 us -> 5.46 us
  starting transfers between devices: 5.64 us -> 9.44 us
  Pallas kernels: 9.21 us -> 10.1 us
    all_gather x2 -> x1, blocking collectives: 10.2 us -> 5.46 us  [gathered(): return lax.all_gather(value, ('grp', 'sx'), axis_index_groups=pairs)]
    ppermute x4, starting transfers between devices: 4.98 us -> 8.12 us  [to_mate(): return lax.ppermute(value, 'sx', mates)]
    pallas_call x2 -> x3, Pallas kernels: 3.44 us -> 4.35 us  [the longest x1 2.24 us: per_device(): pl.pallas_call(smooth_kernel, out_shape=(pltpu.HBM((ROWS, CX * PLANE), BF...]
    ppermute x1 -> x2, starting transfers between devices: 0.66 us -> 1.33 us  [across(): return lax.ppermute(value, 'sx', others)]
  transfers between devices with their start and end apart: 5 -> 6, of which waited for: 2 -> 2; matrix products, arithmetic and copies ran while one was open for 0% -> 0% of each run, Pallas kernels for 12% -> 20%
where the time goes in v9:
time: 26.7 us; the launch traced here: 26.5 us
  Pallas kernels  10.1 us (38%)
  starting transfers between devices  9.44 us (35%)
  blocking collectives  5.46 us (20%)
  waiting for transfers between devices  1.43 us (5%)
    ppermute x4, starting transfers between devices, to_mate(): return lax.ppermute(value, 'sx', mates)  8.12 us
    all_gather x1, blocking collectives, gathered(): return lax.all_gather(value, ('grp', 'sx'), axis_index_groups=pairs)  5.46 us
    pallas_call x1, Pallas kernels, per_device(): pl.pallas_call(smooth_kernel, out_shape=(pltpu.HBM((ROWS, CX * PLANE), BF...  2.24 us
    pallas_call x1, Pallas kernels, per_device(): pl.pallas_call(energy_kernel, out_shape=(pair, pair, pair, shape(2, ROWS,...  2.03 us
    pallas_call x1, Pallas kernels, per_device(): pl.pallas_call(edges_kernel, out_shape=(pair, pair, shape(ROWS, 16), shap...  1.51 us
    ppermute x4, waiting for transfers between devices, to_mate(): return lax.ppermute(value, 'sx', mates)  1.43 us
    pallas_call x1, Pallas kernels, per_device(): pl.pallas_call(gradient_kernel, out_shape=(pair, shape(ROWS, ROWS), shape...  1.36 us
    ppermute x2, starting transfers between devices, across(): return lax.ppermute(value, 'sx', others)  1.33 us
  transfers between devices with their start and end apart: 6, of which 2 were waited for; matrix products, arithmetic and copies ran while one was open for 0% of the time, Pallas kernels for 20%

profile of v9, /device:TPU:0, one launch (start us, length us, event | category | flops | bytes accessed | tf_op | source)
XLA Modules:
  0.0 26.5 jit_solution(10083369815040062450)
XLA Ops:
  0.0 1.5 %edges.1 = (bf16[2,192,1024]{2,1,0:T(8,128)(2,1)S(1)}, bf16[2,192,1024]{2,1,0:T(8,128)(2,1)S(1)}, bf16[192,16]{1,0:T(8,128)(2,1)S(1)}, f32[192,1024]{1,0:T(8,128...) custom-call(s32[4,1024]{1,0:T(4,128)} %bitcast.6, bf16[192,4096]{1,0:T(8,128)(2,1)} %pieces_ref.3), custom_call_target="tpu_custom_call" | custom-call | flops 100000000 | bytes 1000000 | tf_op jit(solution)/shard_map/edges/pallas_call | solution.py:513
  1.5 0.7 %collective-permute-start = (bf16[192,128]{1,0:T(8,128)(2,1)S(1)}, bf16[192,128]{1,0:T(8,128)(2,1)S(1)}, u32[]{:S(2)}, u32[]{:S(2)}) collective-permute-start(bf16[192,128]{1,0:T(8,128)(2,1)S(1)} %get-tuple-element.31), channel_id=1, source_target_pairs={{1,2},{2,1},{3,4},{4,3},{5,6},{6,5},{7,8},{8,7},{9,10},{10,9},{11,... | collective-permute-start | bytes 147464 | tf_op jit(solution)/shard_map/ppermute | solution.py:505
  2.2 4.4 %collective-permute-start.1 = (bf16[192,128]{1,0:T(8,128)(2,1)S(1)}, bf16[192,128]{1,0:T(8,128)(2,1)S(1)}, u32[]{:S(2)}, u32[]{:S(2)}) collective-permute-start(bf16[192,128]{1,0:T(8,128)(2,1)S(1)} %get-tuple-element.32), channel_id=1, source_target_pairs={{0,1},{1,0},{2,3},{3,2},{4,5},{5,4},{6,7},{7,6},{8,9},{9,8},{10,11... | collective-permute-start | bytes 147464 | tf_op jit(solution)/shard_map/ppermute | solution.py:502
  6.6 0.0 copy-done
  6.6 2.0 %energy.1 = (bf16[2,192,1024]{2,1,0:T(8,128)(2,1)S(1)}, bf16[2,192,1024]{2,1,0:T(8,128)(2,1)S(1)}, bf16[2,192,1024]{2,1,0:T(8,128)(2,1)S(1)}, f32[2,192,1024]{2,...) custom-call(bf16[192,16]{1,0:T(8,128)(2,1)S(1)} %get-tuple-element.33.rows_ref, ...), custom_call_target="tpu_custom_call" | custom-call | flops 4000000000 | bytes 10000000 | tf_op jit(solution)/shard_map/energy/pallas_call | solution.py:532
  8.6 0.0 collective-permute-done.across_ref
  8.6 0.0 collective-permute-done.1.mate_ref
  8.7 0.0 copy-start.2
  8.7 0.6 %bands.1 = (bf16[2,192,1024]{2,1,0:T(8,128)(2,1)S(1)}, f32[2,192,256]{2,1,0:T(8,128)S(1)}, bf16[3,128,128]{2,1,0:T(8,128)(2,1)S(1)}) custom-call(bf16[192,128]{1,0:T(8,128)(2,1)S(1)} %collective-permute-done.across_ref, bf16[192,128]{1,0:T(8,128)(2,1)S(1)} %collective-permute-done.1.mate_ref, ...), custom_call_target="tpu_custom_call", output_to_operand_aliasing={{0}: (7, {})} | custom-call | flops 1000000000 | bytes 10000000 | tf_op jit(solution)/shard_map/bands/pallas_call | solution.py:545
  9.2 0.1 collective-permute-start.2
  9.3 1.3 %collective-permute-done.2.rows_ref = bf16[3,128,128]{2,1,0:T(8,128)(2,1)S(1)} collective-permute-done((bf16[3,128,128]{2,1,0:T(8,128)(2,1)S(1)}, bf16[3,128,128]{2,1,0:T(8,128)(2,1)S(1)}, u32[]{:S(2)}, u32[]{:S(2)}) %collective-permute-start.2) | collective-permute-done | bytes 98336 | tf_op jit(solution)/shard_map/ppermute | solution.py:502
  10.6 0.2 relay.1
  10.8 5.5 %all-gather = bf16[14,64,128]{2,1,0:T(8,128)(2,1)S(1)} all-gather(bf16[7,64,128]{2,1,0:T(8,128)(2,1)S(1)} %relay.1), channel_id=2, replica_groups={{1,2},{3,4},{5,6},{7,8},{9,10},{11,12},{13,14},{17,18},{19,20},{21,22},..., dimensions={0}, use_global_device_ids=true | all-gather | bytes 344064 | tf_op jit(solution)/shard_map/all_gather | solution.py:508
  16.3 0.1 collective-permute-start.3
  16.4 0.0 copy-done.2
  16.4 1.0 %theta.1 = (bf16[2,192,256]{2,1,0:T(8,128)(2,1)S(1)}, f32[192,192]{1,0:T(8,128)S(1)}) custom-call(s32[2,16]{1,0:T(2,128)S(1)} %bitcast.4, f32[2,192,256]{2,1,0:T(8,128)S(1)} %get-tuple-element.41.own_ref, bf16[3,128,128]{2,1,0:T(8,128)(2,1)S(1)} %collective-permute-done.2.rows_ref, bf16[7,64,128]{2,1,0:T(8,128)(2,1)S(1)} %get-tuple-element.44.other_ref), custom_call_target="tpu_custom_call" | custom-call | flops 1000000000 | bytes 4000000 | tf_op jit(solution)/shard_map/theta/pallas_call | solution.py:578
  17.4 0.1 collective-permute-done.3.relayed_ref
  17.6 1.4 %gradient.1 = (bf16[2,192,1024]{2,1,0:T(8,128)(2,1)S(1)}, bf16[192,192]{1,0:T(8,128)(2,1)S(1)}, bf16[192,128]{1,0:T(8,128)(2,1)S(1)}, bf16[192,128]{1,0:T(8,128)(2,1)S(1)}) custom-call(s32[2,16]{1,0:T(2,128)S(1)} %bitcast.5, bf16[3,64,128]{2,1,0:T(8,128)(2,1)S(1)} %collective-permute-done.3.relayed_ref, ...), custom_call_target="tpu_custom_call" | custom-call | flops 1000000000 | bytes 10000000 | tf_op jit(solution)/shard_map/gradient/pallas_call | solution.py:588
  19.0 0.7 %collective-permute-start.4 = (bf16[192,128]{1,0:T(8,128)(2,1)S(1)}, bf16[192,128]{1,0:T(8,128)(2,1)S(1)}, u32[]{:S(2)}, u32[]{:S(2)}) collective-permute-start(bf16[192,128]{1,0:T(8,128)(2,1)S(1)} %get-tuple-element.48), channel_id=1, source_target_pairs={{1,2},{2,1},{3,4},{4,3},{5,6},{6,5},{7,8},{8,7},{9,10},{10,9},{11,... | collective-permute-start | bytes 147464 | tf_op jit(solution)/shard_map/ppermute | solution.py:505
  19.6 3.6 %collective-permute-start.5 = (bf16[192,128]{1,0:T(8,128)(2,1)S(1)}, bf16[192,128]{1,0:T(8,128)(2,1)S(1)}, u32[]{:S(2)}, u32[]{:S(2)}) collective-permute-start(bf16[192,128]{1,0:T(8,128)(2,1)S(1)} %get-tuple-element.49), channel_id=1, source_target_pairs={{0,1},{1,0},{2,3},{3,2},{4,5},{5,4},{6,7},{7,6},{8,9},{9,8},{10,11... | collective-permute-start | bytes 147464 | tf_op jit(solution)/shard_map/ppermute | solution.py:502
  23.2 2.2 %smooth.1 = (bf16[192,4096]{1,0:T(8,128)(2,1)}, f32[2,192,1024]{2,1,0:T(8,128)S(1)}) custom-call(bf16[192,192]{1,0:T(8,128)(2,1)S(1)} %get-tuple-element.50.theta_ref, bf16[2,192,1024]{2,1,0:T(8,128)(2,1)S(1)} %get-tuple-element.51.phi_ref, bf16[2,192,1024]{2,1,0:T(8,128)(2,1)S(1)} %get-tuple-element.52.energy_ref, ...), custom_call_target="tpu_custom_call" | custom-call | flops 2000000000 | bytes 10000000 | tf_op jit(solution)/shard_map/smooth/pallas_call | solution.py:601
  25.4 0.0 collective-permute-done.4.across_ref
  25.5 0.0 collective-permute-done.5.mate_ref
  25.5 1.1 %finish.1 = bf16[192,4096]{1,0:T(8,128)(2,1)} custom-call(bf16[192,128]{1,0:T(8,128)(2,1)S(1)} %collective-permute-done.4.across_ref, bf16[192,128]{1,0:T(8,128)(2,1)S(1)} %collective-permute-done.5.mate_ref, f32[2,192,1024]{2,1,0:T(8,128)S(1)} %get-tuple-element.55.part_ref, ...), custom_call_target="tpu_custom_call", output_to_operand_aliasing={{}: (4, {})} | custom-call | flops 10000000 | bytes 10000000 | tf_op jit(solution)/shard_map/finish/pallas_call | solution.py:617
  (4 shorter events, 0.0 us)
Async XLA Ops:
  0.0 6.6 %copy-start = (bf16[192,4096]{1,0:T(8,128)(2,1)S(1)}, bf16[192,4096]{1,0:T(8,128)(2,1)}, u32[]{:S(2)}) copy-start(bf16[192,4096]{1,0:T(8,128)(2,1)} %pieces_ref.3) | copy-start | bytes 4718596
  0.0 6.6 %copy-start.1 = (f32[4,1024]{1,0:T(4,128)S(1)}, f32[4,1024]{1,0:T(4,128)}, u32[]{:S(2)}) copy-start(f32[4,1024]{1,0:T(4,128)} %pot_ref.1) | copy-start | bytes 49156
  1.5 7.1 %collective-permute-start = (bf16[192,128]{1,0:T(8,128)(2,1)S(1)}, bf16[192,128]{1,0:T(8,128)(2,1)S(1)}, u32[]{:S(2)}, u32[]{:S(2)}) collective-permute-start(bf16[192,128]{1,0:T(8,128)(2,1)S(1)} %get-tuple-element.31), channel_id=1, source_target_pairs={{1,2},{2,1},{3,4},{4,3},{5,6},{6,5},{7,8},{8,7},{9,10},{10,9},{11,... | collective-permute-start | bytes 147464 | tf_op jit(solution)/shard_map/ppermute | solution.py:505
  2.2 6.4 %collective-permute-start.1 = (bf16[192,128]{1,0:T(8,128)(2,1)S(1)}, bf16[192,128]{1,0:T(8,128)(2,1)S(1)}, u32[]{:S(2)}, u32[]{:S(2)}) collective-permute-start(bf16[192,128]{1,0:T(8,128)(2,1)S(1)} %get-tuple-element.32), channel_id=1, source_target_pairs={{0,1},{1,0},{2,3},{3,2},{4,5},{5,4},{6,7},{7,6},{8,9},{9,8},{10,11... | collective-permute-start | bytes 147464 | tf_op jit(solution)/shard_map/ppermute | solution.py:502
  8.7 7.7 %copy-start.2 = (s32[16,2]{0,1:T(2,128)S(1)}, s32[16,2]{0,1:T(2,128)}, u32[]{:S(2)}) copy-start(s32[16,2]{0,1:T(2,128)} %param.7) | copy-start | bytes 388
  9.2 1.4 %collective-permute-start.2 = (bf16[3,128,128]{2,1,0:T(8,128)(2,1)S(1)}, bf16[3,128,128]{2,1,0:T(8,128)(2,1)S(1)}, u32[]{:S(2)}, u32[]{:S(2)}) collective-permute-start(bf16[3,128,128]{2,1,0:T(8,128)(2,1)S(1)} %get-tuple-element.42), channel_id=1, source_target_pairs={{0,1},{1,0},{2,3},{3,2},{4,5},{5,4},{6,7},{7,6},{8,9},{9,8},{10,11... | collective-permute-start | bytes 294920 | tf_op jit(solution)/shard_map/ppermute | solution.py:502
  16.3 1.3 %collective-permute-start.3 = (bf16[3,64,128]{2,1,0:T(8,128)(2,1)S(1)}, bf16[3,64,128]{2,1,0:T(8,128)(2,1)S(1)}, u32[]{:S(2)}, u32[]{:S(2)}) collective-permute-start(bf16[3,64,128]{2,1,0:T(8,128)(2,1)S(1)} %get-tuple-element.43), channel_id=1, source_target_pairs={{0,1},{1,0},{2,3},{3,2},{4,5},{5,4},{6,7},{7,6},{8,9},{9,8},{10,11... | collective-permute-start | bytes 147464 | tf_op jit(solution)/shard_map/ppermute | solution.py:502
  19.0 6.5 %collective-permute-start.4 = (bf16[192,128]{1,0:T(8,128)(2,1)S(1)}, bf16[192,128]{1,0:T(8,128)(2,1)S(1)}, u32[]{:S(2)}, u32[]{:S(2)}) collective-permute-start(bf16[192,128]{1,0:T(8,128)(2,1)S(1)} %get-tuple-element.48), channel_id=1, source_target_pairs={{1,2},{2,1},{3,4},{4,3},{5,6},{6,5},{7,8},{8,7},{9,10},{10,9},{11,... | collective-permute-start | bytes 147464 | tf_op jit(solution)/shard_map/ppermute | solution.py:505
  19.6 5.8 %collective-permute-start.5 = (bf16[192,128]{1,0:T(8,128)(2,1)S(1)}, bf16[192,128]{1,0:T(8,128)(2,1)S(1)}, u32[]{:S(2)}, u32[]{:S(2)}) collective-permute-start(bf16[192,128]{1,0:T(8,128)(2,1)S(1)} %get-tuple-element.49), channel_id=1, source_target_pairs={{0,1},{1,0},{2,3},{3,2},{4,5},{5,4},{6,7},{7,6},{8,9},{9,8},{10,11... | collective-permute-start | bytes 147464 | tf_op jit(solution)/shard_map/ppermute | solution.py:502

commit v10 on v9

--- a/solution.py
+++ b/solution.py
@@ -150,14 +150,32 @@
     return (slab == 0) | (slab == lax.axis_size("sx") - 1)
 
 
+def kept(pattern_ref, r, q):
+    slab = lax.axis_index("sx")
+    last = pattern_ref.shape[1] - 1
+    values = []
+    for col in (2 * q, 2 * q + 1):
+        apart = abs(col - r - 2)
+        if apart == 0:
+            values.append(1.0)
+        elif apart > 2:
+            values.append(0.0)
+        else:
+            at = jnp.clip(slab - 3 + min(col, r + 2), 0, last)
+            values.append(pattern_ref[apart - 1, at].astype(F32))
+    return jnp.where(low_half(), values[0], values[1])
+
+
 def edges_kernel(
-    table_ref, pieces_ref,
-    phi_ref, mask_ref, rows_ref, reach_ref, mate_ref, across_ref,
-    window_ref, raw_ref, sems,
+    table_ref, pattern_ref, pieces_ref,
+    phi_ref, mask_ref, rows_ref, reach_ref, keep_ref, mate_ref, across_ref,
+    window_ref, raw_ref, scalar_ref, sems,
 ):
     first = window_start(table_ref.shape[1])
     table_copy = pltpu.make_async_copy(table_ref.at[:, pl.ds(first, 4 * ORB)], window_ref, sems.at[2])
     table_copy.start()
+    pattern_copy = pltpu.make_async_copy(pattern_ref, scalar_ref, sems.at[3])
+    pattern_copy.start()
     copies = []
     for i in range(2):
         start = (CX - 1) * PLANE * i
@@ -173,6 +191,10 @@
     reach_ref[...] = reach
     for i in range(2):
         mask_ref[i] = sphere(reach, rows, (CX - 1) * i)
+    pattern_copy.wait()
+    for r in range(3):
+        for q in range(4):
+            keep_ref[r : r + 1, 128 * q : 128 * q + 128] = kept(scalar_ref, r, q)
     for i in range(2):
         copies[i].wait()
         phi_ref[i] = raw_ref[i] * mask_ref[i]
@@ -315,22 +337,6 @@
             out_ref[i, :, lanes] = value.astype(BF16) * mask_ref[i, :, lanes]
 
 
-def kept(pattern_ref, r, q):
-    slab = lax.axis_index("sx")
-    last = pattern_ref.shape[1] - 1
-    values = []
-    for col in (2 * q, 2 * q + 1):
-        apart = abs(col - r - 2)
-        if apart == 0:
-            values.append(1.0)
-        elif apart > 2:
-            values.append(0.0)
-        else:
-            at = jnp.clip(slab - 3 + min(col, r + 2), 0, last)
-            values.append(pattern_ref[apart - 1, at].astype(F32))
-    return jnp.where(low_half(), values[0], values[1])
-
-
 def split(value):
     high = value.astype(BF16)
     return high, (value - high.astype(F32)).astype(BF16)
@@ -341,7 +347,7 @@
 
 
 def theta_kernel(
-    pattern_ref, own_ref, rows_ref, other_ref,
+    keep_ref, own_ref, rows_ref, other_ref,
     window_ref, theta_ref,
     ham_ref, inv_ref,
 ):
@@ -369,7 +375,7 @@
                 value = jnp.where(even, got_even[r][q], got_odd[r][q])
                 if q in (1, 2):
                     value = value + own_ref[which, ORB * r : ORB * r + ORB, 128 * q - 128 : 128 * q]
-                value = value * kept(pattern_ref, r, q)
+                value = value * keep_ref[r : r + 1, 128 * q : 128 * q + 128]
                 if which == 1:
                     on = iota((ORB, 128), 0) + (ORB * (r + 2) - 128 * q) == iota((ORB, 128), 1)
                     value = jnp.where(on, 2.0, 0.0) - value
@@ -381,7 +387,7 @@
 
 
 def gradient_kernel(
-    pattern_ref, relayed_ref, bands_ref, base_ref,
+    keep_ref, relayed_ref, bands_ref, base_ref,
     edge_ref, edge_energy_ref, edge_mask_ref,
     edge_grad_ref, theta_ref, mate_ref, across_ref,
     window_ref, total_ref,
@@ -394,7 +400,8 @@
         turned = swapped(relayed_ref[1 + which].astype(F32))
         tiles = []
         for q, value in enumerate((jnp.where(low, front, turned), jnp.where(low, turned, 0.0))):
-            tiles.append(value * jnp.where(even, kept(pattern_ref, 2, 2 + q), kept(pattern_ref, 0, q)))
+            at_even = keep_ref[2:3, 128 * q + 256 : 128 * q + 384]
+            tiles.append(value * jnp.where(even, at_even, keep_ref[0:1, 128 * q : 128 * q + 128]))
         more.append(jnp.concatenate(tiles, axis=1))
     first, third = slice(0, ORB), slice(2 * ORB, ROWS)
     window_ref[...] = bands_ref[0]
@@ -451,18 +458,18 @@
 def finish_kernel(across_ref, mate_ref, part_ref, mask_ref, inner_ref, out_ref, done_ref, sems):
     halos = [unfold(side) for side in sides(mate_ref[...].astype(F32), across_ref[...].astype(F32))]
     copies = []
-    for h in range(4):
-        for i in range(2):
-            for t in (2 * h, 2 * h + 1):
+    for i in range(2):
+        start = PLANE * (CX - 1) * i
+        for half in range(2):
+            rows = slice(ORB * (half + i), ORB * (half + i) + ORB)
+            got = slice(ORB * half, ORB * half + ORB)
+            for t in range(PLANE // 128):
                 lanes = slice(128 * t, 128 * t + 128)
-                value = (part_ref[i, halo_rows(i), lanes] + halos[i][t % 3]) * (1.0 / 32.0)
-                done_ref[i, :, lanes] = value.astype(BF16) * mask_ref[i, halo_rows(i), lanes]
-            start = PLANE * (CX - 1) * i + TILE * h
+                value = (part_ref[i, rows, lanes] + halos[i][t % 3][got]) * (1.0 / 32.0)
+                done_ref[i, got, lanes] = value.astype(BF16) * mask_ref[i, rows, lanes]
             copies.append(
                 pltpu.make_async_copy(
-                    done_ref.at[i, :, TILE * h : TILE * h + TILE],
-                    out_ref.at[halo_rows(i), start : start + TILE],
-                    sems.at[i, h],
+                    done_ref.at[i, got], out_ref.at[rows, start : start + PLANE], sems.at[i, half]
                 )
             )
             copies[-1].start()
@@ -508,24 +515,27 @@
         return lax.all_gather(value, ("grp", "sx"), axis_index_groups=pairs)
 
     table = centers.T
+    patterns = pattern.T
     pair = shape(2, ROWS, PLANE)
 
-    edge, edge_mask, rows, reach, for_mate, for_other = pl.pallas_call(
+    edge, edge_mask, rows, reach, keep, for_mate, for_other = pl.pallas_call(
         edges_kernel,
         out_shape=(
-            pair, pair, shape(ROWS, 16), shape(ROWS, PLANE, dtype=F32), shape(ROWS, 128), shape(ROWS, 128),
+            pair, pair, shape(ROWS, 16), shape(ROWS, PLANE, dtype=F32), shape(3, 8 * ORB, dtype=F32),
+            shape(ROWS, 128), shape(ROWS, 128),
         ),
-        in_specs=[FAR, FAR],
-        out_specs=(WHOLE,) * 6,
+        in_specs=[FAR, FAR, FAR],
+        out_specs=(WHOLE,) * 7,
         scratch_shapes=[
             pltpu.VMEM((4, 4 * ORB), jnp.int32),
             pltpu.VMEM((2, ROWS, PLANE), BF16),
-            pltpu.SemaphoreType.DMA((3,)),
+            pltpu.SMEM(patterns.shape, jnp.int32),
+            pltpu.SemaphoreType.DMA((4,)),
         ],
         compiler_params=PARAMS,
         cost_estimate=cost(10**8, 10**6),
         name="edges",
-    )(far(table), far(pieces))
+    )(far(table), far(patterns), far(pieces))
     other_side = across(for_other)
     mate_side = to_mate(for_mate)
 
@@ -573,28 +583,26 @@
     )(gathered(for_other))
     relayed = to_mate(forward)
 
-    patterns = pattern.T
-    scalars = pl.BlockSpec(memory_space=pltpu.SMEM)
     bands, base = pl.pallas_call(
         theta_kernel,
         out_shape=(shape(2, ROWS, TILE), shape(ROWS, ROWS, dtype=F32)),
-        in_specs=[scalars] + [WHOLE] * 3,
+        in_specs=[WHOLE] * 4,
         out_specs=(WHOLE,) * 2,
         scratch_shapes=[pltpu.VMEM((ROWS, 8 * ORB), F32), pltpu.VMEM((ROWS, 8 * ORB), F32)],
         compiler_params=PARAMS,
         cost_estimate=cost(10**9, 4 * 10**6),
         name="theta",
-    )(patterns, own, mate_rows, other_rows)
+    )(keep, own, mate_rows, other_rows)
     edge_grad, theta, for_mate, for_other = pl.pallas_call(
         gradient_kernel,
         out_shape=(pair, shape(ROWS, ROWS), shape(ROWS, 128), shape(ROWS, 128)),
-        in_specs=[scalars] + [WHOLE] * 6,
+        in_specs=[WHOLE] * 7,
         out_specs=(WHOLE,) * 4,
         scratch_shapes=[pltpu.VMEM((ROWS, TILE), BF16), pltpu.VMEM((ROWS, ROWS), F32)],
         compiler_params=PARAMS,
         cost_estimate=cost(10**9, 10**7),
         name="gradient",
-    )(patterns, relayed, bands, base, edge, edge_energy, edge_mask)
+    )(keep, relayed, bands, base, edge, edge_energy, edge_mask)
     other_side = across(for_other)
     mate_side = to_mate(for_mate)
 
@@ -619,7 +627,7 @@
         out_shape=pltpu.HBM((ROWS, CX * PLANE), BF16),
         in_specs=[WHOLE] * 4 + [FAR],
         out_specs=FAR,
-        scratch_shapes=[pltpu.VMEM((2, 2 * ORB, PLANE), BF16), pltpu.SemaphoreType.DMA((2, PLANE // TILE))],
+        scratch_shapes=[pltpu.VMEM((2, 2 * ORB, PLANE), BF16), pltpu.SemaphoreType.DMA((2, 2))],
         input_output_aliases={4: 0},
         compiler_params=PARAMS,
         cost_estimate=cost(10**7, 10**7),

time: 26.7 us -> 25.9 us (0.970)
  Pallas kernels: 10.1 us -> 8.93 us
  waiting for transfers between devices: 1.43 us -> 1.98 us
    pallas_call x1, Pallas kernels: 1.36 us -> 0.81 us  [per_device(): pl.pallas_call(gradient_kernel, out_shape=(pair, shape(ROWS, ROWS), shape...]
    ppermute x4, waiting for transfers between devices: 1.43 us -> 1.98 us  [to_mate(): return lax.ppermute(value, 'sx', mates)]
    pallas_call x1, Pallas kernels: 1.05 us -> 0.51 us  [per_device(): pl.pallas_call(theta_kernel, out_shape=(shape(2, ROWS, TILE), shape(ROWS,...]
  transfers between devices with their start and end apart: 6 -> 6, of which waited for: 2 -> 2; matrix products, arithmetic and copies ran while one was open for 0% -> 0% of each run, Pallas kernels for 20% -> 19%
where the time goes in v10:
time: 25.9 us; the launch traced here: 25.8 us
  starting transfers between devices  9.26 us (36%)
  Pallas kernels  8.93 us (34%)
  blocking collectives  5.46 us (21%)
  waiting for transfers between devices  1.98 us (8%)
    ppermute x4, starting transfers between devices, to_mate(): return lax.ppermute(value, 'sx', mates)  7.93 us
    all_gather x1, blocking collectives, gathered(): return lax.all_gather(value, ('grp', 'sx'), axis_index_groups=pairs)  5.46 us
    pallas_call x1, Pallas kernels, per_device(): pl.pallas_call(smooth_kernel, out_shape=(pltpu.HBM((ROWS, CX * PLANE), BF...  2.24 us
    pallas_call x1, Pallas kernels, per_device(): pl.pallas_call(energy_kernel, out_shape=(pair, pair, pair, shape(2, ROWS,...  2.04 us
    ppermute x4, waiting for transfers between devices, to_mate(): return lax.ppermute(value, 'sx', mates)  1.98 us
    pallas_call x1, Pallas kernels, per_device(): pl.pallas_call(edges_kernel, out_shape=(pair, pair, shape(ROWS, 16), shap...  1.55 us
    ppermute x2, starting transfers between devices, across(): return lax.ppermute(value, 'sx', others)  1.33 us
    pallas_call x1, Pallas kernels, per_device(): pl.pallas_call(finish_kernel, out_shape=pltpu.HBM((ROWS, CX * PLANE), BF1...  0.98 us
  transfers between devices with their start and end apart: 6, of which 2 were waited for; matrix products, arithmetic and copies ran while one was open for 0% of the time, Pallas kernels for 19%

profile of v10, /device:TPU:0, one launch (start us, length us, event | category | flops | bytes accessed | tf_op | source)
XLA Modules:
  0.0 25.8 jit_solution(5727821274956772832)
XLA Ops:
  0.0 0.0 copy-start
  0.0 1.5 %edges.1 = (bf16[2,192,1024]{2,1,0:T(8,128)(2,1)S(1)}, bf16[2,192,1024]{2,1,0:T(8,128)(2,1)S(1)}, bf16[192,16]{1,0:T(8,128)(2,1)S(1)}, f32[192,1024]{1,0:T(8,128...) custom-call(s32[4,1024]{1,0:T(4,128)} %bitcast.4, s32[2,16]{1,0:T(2,128)} %bitcast.5, ...), custom_call_target="tpu_custom_call" | custom-call | flops 100000000 | bytes 1000000 | tf_op jit(solution)/shard_map/edges/pallas_call | solution.py:521
  1.6 0.7 %collective-permute-start = (bf16[192,128]{1,0:T(8,128)(2,1)S(1)}, bf16[192,128]{1,0:T(8,128)(2,1)S(1)}, u32[]{:S(2)}, u32[]{:S(2)}) collective-permute-start(bf16[192,128]{1,0:T(8,128)(2,1)S(1)} %get-tuple-element.33), channel_id=1, source_target_pairs={{1,2},{2,1},{3,4},{4,3},{5,6},{6,5},{7,8},{8,7},{9,10},{10,9},{11,... | collective-permute-start | bytes 147464 | tf_op jit(solution)/shard_map/ppermute | solution.py:512
  2.2 4.4 %collective-permute-start.1 = (bf16[192,128]{1,0:T(8,128)(2,1)S(1)}, bf16[192,128]{1,0:T(8,128)(2,1)S(1)}, u32[]{:S(2)}, u32[]{:S(2)}) collective-permute-start(bf16[192,128]{1,0:T(8,128)(2,1)S(1)} %get-tuple-element.34), channel_id=1, source_target_pairs={{0,1},{1,0},{2,3},{3,2},{4,5},{5,4},{6,7},{7,6},{8,9},{9,8},{10,11... | collective-permute-start | bytes 147464 | tf_op jit(solution)/shard_map/ppermute | solution.py:509
  6.6 0.0 copy-done
  6.6 0.0 copy-done.1
  6.6 2.0 %energy.1 = (bf16[2,192,1024]{2,1,0:T(8,128)(2,1)S(1)}, bf16[2,192,1024]{2,1,0:T(8,128)(2,1)S(1)}, bf16[2,192,1024]{2,1,0:T(8,128)(2,1)S(1)}, f32[2,192,1024]{2,...) custom-call(bf16[192,16]{1,0:T(8,128)(2,1)S(1)} %get-tuple-element.35.rows_ref, ...), custom_call_target="tpu_custom_call" | custom-call | flops 4000000000 | bytes 10000000 | tf_op jit(solution)/shard_map/energy/pallas_call | solution.py:542
  8.7 0.0 collective-permute-done.across_ref
  8.7 0.0 collective-permute-done.1.mate_ref
  8.7 0.6 %bands.1 = (bf16[2,192,1024]{2,1,0:T(8,128)(2,1)S(1)}, f32[2,192,256]{2,1,0:T(8,128)S(1)}, bf16[3,128,128]{2,1,0:T(8,128)(2,1)S(1)}) custom-call(bf16[192,128]{1,0:T(8,128)(2,1)S(1)} %collective-permute-done.across_ref, bf16[192,128]{1,0:T(8,128)(2,1)S(1)} %collective-permute-done.1.mate_ref, ...), custom_call_target="tpu_custom_call", output_to_operand_aliasing={{0}: (7, {})} | custom-call | flops 1000000000 | bytes 10000000 | tf_op jit(solution)/shard_map/bands/pallas_call | solution.py:555
  9.3 0.1 collective-permute-start.2
  9.4 1.3 %collective-permute-done.2.rows_ref = bf16[3,128,128]{2,1,0:T(8,128)(2,1)S(1)} collective-permute-done((bf16[3,128,128]{2,1,0:T(8,128)(2,1)S(1)}, bf16[3,128,128]{2,1,0:T(8,128)(2,1)S(1)}, u32[]{:S(2)}, u32[]{:S(2)}) %collective-permute-start.2) | collective-permute-done | bytes 98336 | tf_op jit(solution)/shard_map/ppermute | solution.py:509
  10.6 0.2 relay.1
  10.8 5.5 %all-gather = bf16[14,64,128]{2,1,0:T(8,128)(2,1)S(1)} all-gather(bf16[7,64,128]{2,1,0:T(8,128)(2,1)S(1)} %relay.1), channel_id=2, replica_groups={{1,2},{3,4},{5,6},{7,8},{9,10},{11,12},{13,14},{17,18},{19,20},{21,22},..., dimensions={0}, use_global_device_ids=true | all-gather | bytes 344064 | tf_op jit(solution)/shard_map/all_gather | solution.py:515
  16.3 0.1 collective-permute-start.3
  16.4 0.5 %theta.1 = (bf16[2,192,256]{2,1,0:T(8,128)(2,1)S(1)}, f32[192,192]{1,0:T(8,128)S(1)}) custom-call(f32[3,512]{1,0:T(4,128)S(1)} %get-tuple-element.32.keep_ref, f32[2,192,256]{2,1,0:T(8,128)S(1)} %get-tuple-element.43.own_ref, bf16[3,128,128]{2,1,0:T(8,128)(2,1)S(1)} %collective-permute-done.2.rows_ref, bf16[7,64,128]{2,1,0:T(8,128)(2,1)S(1)} %get-tuple-element.46.other_ref), custom_call_target="tpu_custom_call" | custom-call | flops 1000000000 | bytes 4000000 | tf_op jit(solution)/shard_map/theta/pallas_call | solution.py:586
  16.9 0.7 %collective-permute-done.3.relayed_ref = bf16[3,64,128]{2,1,0:T(8,128)(2,1)S(1)} collective-permute-done((bf16[3,64,128]{2,1,0:T(8,128)(2,1)S(1)}, bf16[3,64,128]{2,1,0:T(8,128)(2,1)S(1)}, u32[]{:S(2)}, u32[]{:S(2)}) %collective-permute-start.3) | collective-permute-done | bytes 49184 | tf_op jit(solution)/shard_map/ppermute | solution.py:509
  17.6 0.8 %gradient.1 = (bf16[2,192,1024]{2,1,0:T(8,128)(2,1)S(1)}, bf16[192,192]{1,0:T(8,128)(2,1)S(1)}, bf16[192,128]{1,0:T(8,128)(2,1)S(1)}, bf16[192,128]{1,0:T(8,128)(2,1)S(1)}) custom-call(f32[3,512]{1,0:T(4,128)S(1)} %get-tuple-element.32.keep_ref, bf16[3,64,128]{2,1,0:T(8,128)(2,1)S(1)} %collective-permute-done.3.relayed_ref, ...), custom_call_target="tpu_custom_call" | custom-call | flops 1000000000 | bytes 10000000 | tf_op jit(solution)/shard_map/gradient/pallas_call | solution.py:596
  18.5 0.7 %collective-permute-start.4 = (bf16[192,128]{1,0:T(8,128)(2,1)S(1)}, bf16[192,128]{1,0:T(8,128)(2,1)S(1)}, u32[]{:S(2)}, u32[]{:S(2)}) collective-permute-start(bf16[192,128]{1,0:T(8,128)(2,1)S(1)} %get-tuple-element.50), channel_id=1, source_target_pairs={{1,2},{2,1},{3,4},{4,3},{5,6},{6,5},{7,8},{8,7},{9,10},{10,9},{11,... | collective-permute-start | bytes 147464 | tf_op jit(solution)/shard_map/ppermute | solution.py:512
  19.1 3.4 %collective-permute-start.5 = (bf16[192,128]{1,0:T(8,128)(2,1)S(1)}, bf16[192,128]{1,0:T(8,128)(2,1)S(1)}, u32[]{:S(2)}, u32[]{:S(2)}) collective-permute-start(bf16[192,128]{1,0:T(8,128)(2,1)S(1)} %get-tuple-element.51), channel_id=1, source_target_pairs={{0,1},{1,0},{2,3},{3,2},{4,5},{5,4},{6,7},{7,6},{8,9},{9,8},{10,11... | collective-permute-start | bytes 147464 | tf_op jit(solution)/shard_map/ppermute | solution.py:509
  22.5 2.2 %smooth.1 = (bf16[192,4096]{1,0:T(8,128)(2,1)}, f32[2,192,1024]{2,1,0:T(8,128)S(1)}) custom-call(bf16[192,192]{1,0:T(8,128)(2,1)S(1)} %get-tuple-element.52.theta_ref, bf16[2,192,1024]{2,1,0:T(8,128)(2,1)S(1)} %get-tuple-element.53.phi_ref, bf16[2,192,1024]{2,1,0:T(8,128)(2,1)S(1)} %get-tuple-element.54.energy_ref, ...), custom_call_target="tpu_custom_call" | custom-call | flops 2000000000 | bytes 10000000 | tf_op jit(solution)/shard_map/smooth/pallas_call | solution.py:609
  24.7 0.0 collective-permute-done.4.across_ref
  24.8 0.0 collective-permute-done.5.mate_ref
  24.8 1.0 %finish.1 = bf16[192,4096]{1,0:T(8,128)(2,1)} custom-call(bf16[192,128]{1,0:T(8,128)(2,1)S(1)} %collective-permute-done.4.across_ref, bf16[192,128]{1,0:T(8,128)(2,1)S(1)} %collective-permute-done.5.mate_ref, f32[2,192,1024]{2,1,0:T(8,128)S(1)} %get-tuple-element.57.part_ref, ...), custom_call_target="tpu_custom_call", output_to_operand_aliasing={{}: (4, {})} | custom-call | flops 10000000 | bytes 10000000 | tf_op jit(solution)/shard_map/finish/pallas_call | solution.py:625
  (2 shorter events, 0.0 us)
Async XLA Ops:
  0.0 6.6 %copy-start = (bf16[192,4096]{1,0:T(8,128)(2,1)S(1)}, bf16[192,4096]{1,0:T(8,128)(2,1)}, u32[]{:S(2)}) copy-start(bf16[192,4096]{1,0:T(8,128)(2,1)} %pieces_ref.3) | copy-start | bytes 4718596
  0.0 6.6 %copy-start.1 = (f32[4,1024]{1,0:T(4,128)S(1)}, f32[4,1024]{1,0:T(4,128)}, u32[]{:S(2)}) copy-start(f32[4,1024]{1,0:T(4,128)} %pot_ref.1) | copy-start | bytes 49156
  1.6 7.1 %collective-permute-start = (bf16[192,128]{1,0:T(8,128)(2,1)S(1)}, bf16[192,128]{1,0:T(8,128)(2,1)S(1)}, u32[]{:S(2)}, u32[]{:S(2)}) collective-permute-start(bf16[192,128]{1,0:T(8,128)(2,1)S(1)} %get-tuple-element.33), channel_id=1, source_target_pairs={{1,2},{2,1},{3,4},{4,3},{5,6},{6,5},{7,8},{8,7},{9,10},{10,9},{11,... | collective-permute-start | bytes 147464 | tf_op jit(solution)/shard_map/ppermute | solution.py:512
  2.2 6.5 %collective-permute-start.1 = (bf16[192,128]{1,0:T(8,128)(2,1)S(1)}, bf16[192,128]{1,0:T(8,128)(2,1)S(1)}, u32[]{:S(2)}, u32[]{:S(2)}) collective-permute-start(bf16[192,128]{1,0:T(8,128)(2,1)S(1)} %get-tuple-element.34), channel_id=1, source_target_pairs={{0,1},{1,0},{2,3},{3,2},{4,5},{5,4},{6,7},{7,6},{8,9},{9,8},{10,11... | collective-permute-start | bytes 147464 | tf_op jit(solution)/shard_map/ppermute | solution.py:509
  9.3 1.4 %collective-permute-start.2 = (bf16[3,128,128]{2,1,0:T(8,128)(2,1)S(1)}, bf16[3,128,128]{2,1,0:T(8,128)(2,1)S(1)}, u32[]{:S(2)}, u32[]{:S(2)}) collective-permute-start(bf16[3,128,128]{2,1,0:T(8,128)(2,1)S(1)} %get-tuple-element.44), channel_id=1, source_target_pairs={{0,1},{1,0},{2,3},{3,2},{4,5},{5,4},{6,7},{7,6},{8,9},{9,8},{10,11... | collective-permute-start | bytes 294920 | tf_op jit(solution)/shard_map/ppermute | solution.py:509
  16.3 1.3 %collective-permute-start.3 = (bf16[3,64,128]{2,1,0:T(8,128)(2,1)S(1)}, bf16[3,64,128]{2,1,0:T(8,128)(2,1)S(1)}, u32[]{:S(2)}, u32[]{:S(2)}) collective-permute-start(bf16[3,64,128]{2,1,0:T(8,128)(2,1)S(1)} %get-tuple-element.45), channel_id=1, source_target_pairs={{0,1},{1,0},{2,3},{3,2},{4,5},{5,4},{6,7},{7,6},{8,9},{9,8},{10,11... | collective-permute-start | bytes 147464 | tf_op jit(solution)/shard_map/ppermute | solution.py:509
  18.5 6.3 %collective-permute-start.4 = (bf16[192,128]{1,0:T(8,128)(2,1)S(1)}, bf16[192,128]{1,0:T(8,128)(2,1)S(1)}, u32[]{:S(2)}, u32[]{:S(2)}) collective-permute-start(bf16[192,128]{1,0:T(8,128)(2,1)S(1)} %get-tuple-element.50), channel_id=1, source_target_pairs={{1,2},{2,1},{3,4},{4,3},{5,6},{6,5},{7,8},{8,7},{9,10},{10,9},{11,... | collective-permute-start | bytes 147464 | tf_op jit(solution)/shard_map/ppermute | solution.py:512
  19.1 5.6 %collective-permute-start.5 = (bf16[192,128]{1,0:T(8,128)(2,1)S(1)}, bf16[192,128]{1,0:T(8,128)(2,1)S(1)}, u32[]{:S(2)}, u32[]{:S(2)}) collective-permute-start(bf16[192,128]{1,0:T(8,128)(2,1)S(1)} %get-tuple-element.51), channel_id=1, source_target_pairs={{0,1},{1,0},{2,3},{3,2},{4,5},{5,4},{6,7},{7,6},{8,9},{9,8},{10,11... | collective-permute-start | bytes 147464 | tf_op jit(solution)/shard_map/ppermute | solution.py:509

commit v11 on v10

--- a/solution.py
+++ b/solution.py
@@ -14,6 +14,8 @@
 ROWS = 3 * ORB
 PLANE = NY * NZ
 TILE = 256
+WINDOW = 6 * ORB
+FACE = ROWS + ROWS // 2
 F32 = jnp.float32
 BF16 = jnp.bfloat16
 
@@ -24,7 +26,7 @@
 
 def window_start(width):
     slab = lax.axis_index("sx")
-    first = jnp.clip(slab * ORB - ORB, 0, width - 4 * ORB) // 128 * 128
+    first = jnp.clip(slab * ORB - 2 * ORB, 0, width - WINDOW) // 128 * 128
     return pl.multiple_of(first, 128)
 
 
@@ -32,10 +34,10 @@
     slab = lax.axis_index("sx")
     count = lax.axis_size("sx")
     window = window_ref[...]
-    shift = slab * ORB - ORB - first
-    window = pltpu.roll(jnp.concatenate([window, window], axis=0), lax.rem(4 * ORB - shift, 4 * ORB), 1)
-    lane = iota((1, 4 * ORB), 1)
-    block = slab - 1 + lane // ORB
+    shift = slab * ORB - 2 * ORB - first
+    window = pltpu.roll(jnp.concatenate([window, window], axis=0), lax.rem(WINDOW - shift, WINDOW), 1)
+    lane = iota((1, WINDOW), 1)
+    block = slab - 2 + lane // ORB
     valid = (block >= 0) & (block < count)
     cx = window[0:1] - slab * CX
     cy = window[1:2]
@@ -46,7 +48,7 @@
     cx = jnp.where(valid, cx, 0)
     cy = jnp.where(valid, cy, 0)
     cz = jnp.where(valid, cz, 0)
-    k = iota((16, 4 * ORB), 0)
+    k = iota((16, WINDOW), 0)
     feats = jnp.where(k == 0, 1, 0)
     feats = jnp.where(k == 1, 256, feats)
     feats = jnp.where(k == 2, cy, feats)
@@ -54,7 +56,7 @@
     feats = jnp.where(k == 4, const & 255, feats)
     feats = jnp.where(k == 5, const >> 8, feats)
     feats = jnp.where(k == 6, cx, feats)
-    return jnp.transpose(feats.astype(F32))[:ROWS].astype(BF16)
+    return jnp.transpose(feats.astype(F32))[: 5 * ORB].astype(BF16)
 
 
 def cell_features():
@@ -108,7 +110,8 @@
     tiles = [values[:, 128 * t : 128 * t + 128] for t in range(PLANE // 128)]
     a, b, c = (sum(tiles[t::3][1:], tiles[t]) for t in range(3))
     low_z = (iota((1, 128), 1) & 31) < 16
-    top, bottom = c[:ORB], c[ORB:]
+    half = values.shape[0] // 2
+    top, bottom = c[:half], c[half:]
     return (
         jnp.where(low_z, a + pltpu.roll(a, 112, 1), b + pltpu.roll(b, 16, 1)),
         jnp.where(low_z, top + pltpu.roll(top, 112, 1), bottom + pltpu.roll(bottom, 16, 1)),
@@ -117,7 +120,8 @@
 
 def unfold(packed):
     low_z = (iota((1, 128), 1) & 31) < 16
-    p, q = packed[: 2 * ORB], packed[2 * ORB :]
+    count = packed.shape[0] // 3 * 2
+    p, q = packed[:count], packed[count:]
     return (
         jnp.where(low_z, p, pltpu.roll(p, 16, 1)),
         jnp.where(low_z, pltpu.roll(p, 112, 1), p),
@@ -172,7 +176,7 @@
     window_ref, raw_ref, scalar_ref, sems,
 ):
     first = window_start(table_ref.shape[1])
-    table_copy = pltpu.make_async_copy(table_ref.at[:, pl.ds(first, 4 * ORB)], window_ref, sems.at[2])
+    table_copy = pltpu.make_async_copy(table_ref.at[:, pl.ds(first, WINDOW)], window_ref, sems.at[2])
     table_copy.start()
     pattern_copy = pltpu.make_async_copy(pattern_ref, scalar_ref, sems.at[3])
     pattern_copy.start()
@@ -185,8 +189,9 @@
         copies[i].start()
     cells = cell_features()
     table_copy.wait()
-    rows = row_features(window_ref, first)
-    rows_ref[...] = rows
+    blocks = row_features(window_ref, first)
+    rows_ref[...] = blocks
+    rows = blocks[ORB : 4 * ORB]
     reach = jnp.dot(rows, cells, preferred_element_type=F32)
     reach_ref[...] = reach
     for i in range(2):
@@ -198,7 +203,11 @@
     for i in range(2):
         copies[i].wait()
         phi_ref[i] = raw_ref[i] * mask_ref[i]
-    put_messages(phi_ref, mate_ref, across_ref)
+    even = is_even()
+    face = jnp.where(even, phi_ref[1, ORB:].astype(F32), phi_ref[0, : 2 * ORB].astype(F32))
+    mate_ref[: 2 * ORB], mate_ref[2 * ORB :] = (value.astype(BF16) for value in fold(face))
+    face = jnp.where(even, phi_ref[0].astype(F32), phi_ref[1].astype(F32))
+    across_ref[:ROWS], across_ref[ROWS:] = (value.astype(BF16) for value in fold(face))
 
 
 def rows_product(a, b):
@@ -209,7 +218,7 @@
     rows_ref, reach_ref, pieces_ref, pot_ref, edge_ref, edge_mask_ref,
     phi_ref, mask_ref, energy_ref, part_ref, edge_energy_ref, corr_ref, ham_ref,
 ):
-    rows = rows_ref[...]
+    rows = rows_ref[ORB : 4 * ORB]
     for i in range(2):
         mask = sphere(reach_ref[...], rows, 1 + i)
         mask_ref[i] = mask
@@ -251,12 +260,13 @@
 
 
 def bands_kernel(
-    across_ref, mate_ref, part_ref, mask_ref, phi_ref, corr_ref, ham_ref, rest_ref,
+    mate_ref, part_ref, mask_ref, phi_ref, corr_ref, ham_ref, rest_ref,
     energy_ref, own_ref, rows_ref,
 ):
     volume = 1.0 / (4.0 * CX**3)
     gram = []
-    for i, side in enumerate(sides(mate_ref[...].astype(F32), across_ref[...].astype(F32))):
+    mate = mate_ref[...].astype(F32)
+    for i, side in enumerate(sides(mate, jnp.zeros_like(mate))):
         tiles = unfold(side)
         for t in range(PLANE // 128):
             lanes = slice(128 * t, 128 * t + 128)
@@ -295,20 +305,34 @@
     return jnp.where(low, 0.0, turned), jnp.where(low, turned, swapped(c2x))
 
 
-def relay_kernel(own_ref, rows_ref, out_ref):
+def relay_kernel(own_ref, rows_ref, face_ref, out_ref):
     even = is_even()
     heads = []
+
+    def put(i, value):
+        out_ref[ORB * i : ORB * i + ORB] = value.astype(BF16)
+
     for which in range(2):
         head, rest = shifted(own_ref[which, :, 0:128], own_ref[which, :, 128:256])
         c01, c2x = mate_blocks(rows_ref, which)
         c01 = jnp.where(even, c01[:ORB], c01[ORB:])
         c2x = jnp.where(even, c2x[:ORB], c2x[ORB:])
         own = slice(ORB, 2 * ORB)
-        out_ref[2 * which] = (head[own] + jnp.where(even, c2x, c01)).astype(BF16)
-        out_ref[2 * which + 1] = (rest[own] + jnp.where(even, c01, c2x)).astype(BF16)
-        out_ref[5 + which] = jnp.where(even, rest[:ORB], rest[2 * ORB :]).astype(BF16)
+        put(2 * which, head[own] + jnp.where(even, c2x, c01))
+        put(2 * which + 1, rest[own] + jnp.where(even, c01, c2x))
+        put(5 + which, jnp.where(even, rest[:ORB], rest[2 * ORB :]))
         heads.append(jnp.where(even, head[:ORB], head[2 * ORB :]))
-    out_ref[4] = jnp.where(low_half(), swapped(heads[1]), heads[0]).astype(BF16)
+    put(4, jnp.where(low_half(), swapped(heads[1]), heads[0]))
+    out_ref[7 * ORB :] = face_ref[...]
+
+
+def around_kernel(rows_ref, mask_ref):
+    even = is_even()
+    rows = jnp.where(even, rows_ref[:ROWS].astype(F32), rows_ref[2 * ORB :].astype(F32))
+    reach = jnp.dot(rows.astype(BF16), cell_features(), preferred_element_type=F32)
+    plane = jnp.where(even, -1.0, float(CX))
+    bound = rows[:, 6:7] * (2.0 * plane) - plane * plane
+    mask_ref[...] = jnp.where(reach <= bound, 1.0, 0.0).astype(BF16)
 
 
 def shared_head(tile, which):
@@ -318,14 +342,68 @@
     return jnp.where(low_half(), 0.0, tile)
 
 
-def pick_kernel(both_ref, other_ref, forward_ref):
-    even = is_even()
+def face_kernel(
+    both_ref, around_ref, phi_ref, mask_ref, part_ref, energy_in_ref,
+    energy_ref, other_ref, extra_ref, forward_ref,
+    beyond_ref, halo_ref, back_ref, work_ref,
+):
+    even = is_even()
+    low = low_half()
+    scale = -0.5 / (4.0 * CX**3)
+
+    def got(start, size):
+        rows = slice(start, start + size)
+        value = jnp.where(even, both_ref[0, rows].astype(F32), both_ref[1, rows].astype(F32))
+        return jnp.where(at_end(), 0.0, value)
+
+    tiles = [got(ORB * i, ORB) for i in range(7)]
     for i in range(7):
-        value = jnp.where(even, both_ref[0, i].astype(F32), both_ref[1, i].astype(F32))
-        value = jnp.where(at_end(), 0.0, value).astype(BF16)
-        other_ref[i] = value
-        if i >= 4:
-            forward_ref[i - 4] = value
+        other_ref[i] = tiles[i].astype(BF16)
+    spread = unfold(got(7 * ORB, FACE))
+    for t in range(PLANE // 128):
+        lanes = slice(128 * t, 128 * t + 128)
+        beyond_ref[:, lanes] = spread[t % 3].astype(BF16) * around_ref[:, lanes]
+    extra_ref[...] = jnp.zeros((ROWS, 8 * ORB), F32)
+    work_ref[:, :, ROWS:] = jnp.zeros((2, 2 * ORB, TILE - ROWS), F32)
+    head, tail = shared_head(tiles[4], 1), tiles[6]
+    forward_ref[2] = jnp.where(low, swapped(head), swapped(tail)).astype(BF16)
+    forward_ref[3] = jnp.where(low, swapped(tail), 0.0).astype(BF16)
+
+    def add_face(i):
+        here = halo_rows(i)
+        there = slice(ORB, ROWS) if i == 0 else slice(0, 2 * ORB)
+        for t in range(PLANE // 128):
+            lanes = slice(128 * t, 128 * t + 128)
+            value = spread[t % 3][there]
+            mask = mask_ref[i, here, lanes]
+            halo_ref[:, lanes] = value.astype(BF16) * mask
+            energy_ref[i, here, lanes] = (part_ref[i, here, lanes] - 0.5 * value).astype(BF16) * mask
+            back_ref[:, lanes] = phi_ref[i, here, lanes] * around_ref[there, lanes]
+        work_ref[0, :, :ROWS] = rows_product(halo_ref[...], phi_ref[i]) * scale
+        work_ref[1, :, :ROWS] = rows_product(back_ref[...], beyond_ref[...]) * scale
+        x, y = work_ref[0, :, 0:128], work_ref[0, :, 128:256]
+        a, b = shifted(work_ref[1, :, 0:128], work_ref[1, :, 128:256])
+        if i == 0:
+            extra_ref[here, 0:128] = a
+            extra_ref[here, 128:256] = b + x
+            extra_ref[here, 256:384] = y
+            own = slice(ORB, 2 * ORB)
+        else:
+            extra_ref[here, 128:256] = a + x
+            extra_ref[here, 256:384] = b + y
+            own = slice(0, ORB)
+        a = swapped(shared_head(tiles[4], 0) + a[own])
+        b = swapped(tiles[5] + b[own])
+        x, y = swapped(x[own]), swapped(y[own])
+        if i == 0:
+            forward_ref[0] = jnp.where(low, a, b + x).astype(BF16)
+            forward_ref[1] = jnp.where(low, b + x, y).astype(BF16)
+        else:
+            forward_ref[0] = jnp.where(low, a + x, b + y).astype(BF16)
+            forward_ref[1] = jnp.where(low, b, x).astype(BF16)
+
+    pl.when(even)(lambda: add_face(0))
+    pl.when(jnp.logical_not(even))(lambda: add_face(1))
 
 
 def put_gradient(theta, orbital_ref, energy_ref, mask_ref, out_ref):
@@ -347,7 +425,7 @@
 
 
 def theta_kernel(
-    keep_ref, own_ref, rows_ref, other_ref,
+    keep_ref, own_ref, rows_ref, other_ref, extra_ref,
     window_ref, theta_ref,
     ham_ref, inv_ref,
 ):
@@ -375,6 +453,8 @@
                 value = jnp.where(even, got_even[r][q], got_odd[r][q])
                 if q in (1, 2):
                     value = value + own_ref[which, ORB * r : ORB * r + ORB, 128 * q - 128 : 128 * q]
+                if which == 0:
+                    value = value + extra_ref[ORB * r : ORB * r + ORB, 128 * q : 128 * q + 128]
                 value = value * keep_ref[r : r + 1, 128 * q : 128 * q + 128]
                 if which == 1:
                     on = iota((ORB, 128), 0) + (ORB * (r + 2) - 128 * q) == iota((ORB, 128), 1)
@@ -383,7 +463,10 @@
     ham, inv = split(ham_ref[...]), split(inv_ref[...])
     theta_ref[...] = fine_product(ham, inv)
     for which, (high, _) in enumerate((ham, inv)):
-        window_ref[which] = jnp.where(even, high[:, 256:512].astype(F32), high[:, 0:256].astype(F32)).astype(BF16)
+        quarter = [high[:, 128 * q : 128 * q + 128].astype(F32) for q in range(4)]
+        window_ref[which, :, 0:128] = jnp.where(even, quarter[2], quarter[0]).astype(BF16)
+        last = jnp.where(even, jnp.where(low, quarter[3], quarter[1]), quarter[1])
+        window_ref[which, :, 128:256] = last.astype(BF16)
 
 
 def gradient_kernel(
@@ -395,13 +478,13 @@
     even = is_even()
     low = low_half()
     more = []
+    kept_even = (keep_ref[2:3, 256:384], jnp.where(low, keep_ref[2:3, 384:512], keep_ref[2:3, 128:256]))
+    kept_odd = (keep_ref[0:1, 0:128], keep_ref[0:1, 128:256])
     for which in range(2):
-        front = swapped(shared_head(relayed_ref[0], which))
-        turned = swapped(relayed_ref[1 + which].astype(F32))
         tiles = []
-        for q, value in enumerate((jnp.where(low, front, turned), jnp.where(low, turned, 0.0))):
-            at_even = keep_ref[2:3, 128 * q + 256 : 128 * q + 384]
-            tiles.append(value * jnp.where(even, at_even, keep_ref[0:1, 128 * q : 128 * q + 128]))
+        for q in range(2):
+            value = relayed_ref[2 * which + q].astype(F32)
+            tiles.append(value * jnp.where(even, kept_even[q], kept_odd[q]))
         more.append(jnp.concatenate(tiles, axis=1))
     first, third = slice(0, ORB), slice(2 * ORB, ROWS)
     window_ref[...] = bands_ref[0]
@@ -518,16 +601,16 @@
     patterns = pattern.T
     pair = shape(2, ROWS, PLANE)
 
-    edge, edge_mask, rows, reach, keep, for_mate, for_other = pl.pallas_call(
+    edge, edge_mask, rows, reach, keep, for_mate, face = pl.pallas_call(
         edges_kernel,
         out_shape=(
-            pair, pair, shape(ROWS, 16), shape(ROWS, PLANE, dtype=F32), shape(3, 8 * ORB, dtype=F32),
-            shape(ROWS, 128), shape(ROWS, 128),
+            pair, pair, shape(5 * ORB, 16), shape(ROWS, PLANE, dtype=F32), shape(3, 8 * ORB, dtype=F32),
+            shape(ROWS, 128), shape(FACE, 128),
         ),
         in_specs=[FAR, FAR, FAR],
         out_specs=(WHOLE,) * 7,
         scratch_shapes=[
-            pltpu.VMEM((4, 4 * ORB), jnp.int32),
+            pltpu.VMEM((4, WINDOW), jnp.int32),
             pltpu.VMEM((2, ROWS, PLANE), BF16),
             pltpu.SMEM(patterns.shape, jnp.int32),
             pltpu.SemaphoreType.DMA((4,)),
@@ -536,7 +619,6 @@
         cost_estimate=cost(10**8, 10**6),
         name="edges",
     )(far(table), far(patterns), far(pieces))
-    other_side = across(for_other)
     mate_side = to_mate(for_mate)
 
     mid, mid_mask, mid_energy, part, rest_energy, corr, ham = pl.pallas_call(
@@ -555,44 +637,60 @@
     edge_energy, own, for_mate = pl.pallas_call(
         bands_kernel,
         out_shape=(pair, shape(2, ROWS, TILE, dtype=F32), shape(3, 2 * ORB, 128)),
-        in_specs=[WHOLE] * 8,
+        in_specs=[WHOLE] * 7,
         out_specs=(WHOLE,) * 3,
-        input_output_aliases={7: 0},
+        input_output_aliases={6: 0},
         compiler_params=PARAMS,
         cost_estimate=cost(10**9, 10**7),
         name="bands",
-    )(other_side, mate_side, part, edge_mask, edge, corr, ham, rest_energy)
+    )(mate_side, part, edge_mask, edge, corr, ham, rest_energy)
     mate_rows = to_mate(for_mate)
+    around = pl.pallas_call(
+        around_kernel,
+        out_shape=shape(ROWS, PLANE),
+        in_specs=[WHOLE],
+        out_specs=WHOLE,
+        compiler_params=PARAMS,
+        cost_estimate=cost(10**8, 10**6),
+        name="around",
+    )(rows)
     for_other = pl.pallas_call(
         relay_kernel,
-        out_shape=shape(7, ORB, 128),
-        in_specs=[WHOLE] * 2,
+        out_shape=shape(7 * ORB + FACE, 128),
+        in_specs=[WHOLE] * 3,
         out_specs=WHOLE,
         compiler_params=PARAMS,
         cost_estimate=cost(10**6, 10**6),
         name="relay",
-    )(own, mate_rows)
-    other_rows, forward = pl.pallas_call(
-        pick_kernel,
-        out_shape=(shape(7, ORB, 128), shape(3, ORB, 128)),
-        in_specs=[WHOLE],
-        out_specs=(WHOLE,) * 2,
-        compiler_params=PARAMS,
-        cost_estimate=cost(10**6, 10**6),
-        name="pick",
-    )(gathered(for_other))
+    )(own, mate_rows, face)
+    edge_energy, other_rows, extra, forward = pl.pallas_call(
+        face_kernel,
+        out_shape=(pair, shape(7, ORB, 128), shape(ROWS, 8 * ORB, dtype=F32), shape(4, ORB, 128)),
+        in_specs=[WHOLE] * 6,
+        out_specs=(WHOLE,) * 4,
+        scratch_shapes=[
+            pltpu.VMEM((ROWS, PLANE), BF16),
+            pltpu.VMEM((2 * ORB, PLANE), BF16),
+            pltpu.VMEM((2 * ORB, PLANE), BF16),
+            pltpu.VMEM((2, 2 * ORB, TILE), F32),
+        ],
+        input_output_aliases={5: 0},
+        compiler_params=PARAMS,
+        cost_estimate=cost(10**8, 10**6),
+        name="face",
+    )(gathered(for_other), around, edge, edge_mask, part, edge_energy)
     relayed = to_mate(forward)
 
     bands, base = pl.pallas_call(
         theta_kernel,
         out_shape=(shape(2, ROWS, TILE), shape(ROWS, ROWS, dtype=F32)),
-        in_specs=[WHOLE] * 4,
+        in_specs=[WHOLE] * 5,
         out_specs=(WHOLE,) * 2,
         scratch_shapes=[pltpu.VMEM((ROWS, 8 * ORB), F32), pltpu.VMEM((ROWS, 8 * ORB), F32)],
         compiler_params=PARAMS,
         cost_estimate=cost(10**9, 4 * 10**6),
         name="theta",
-    )(keep, own, mate_rows, other_rows)
+    )(keep, own, mate_rows, other_rows, extra)
     edge_grad, theta, for_mate, for_other = pl.pallas_call(
         gradient_kernel,
         out_shape=(pair, shape(ROWS, ROWS), shape(ROWS, 128), shape(ROWS, 128)),

time: 25.9 us -> 25.1 us (0.969)
  starting transfers between devices: 9.26 us -> 6.65 us
  blocking collectives: 5.46 us -> 6.85 us
  Pallas kernels: 8.93 us -> 9.98 us
  waiting for transfers between devices: 1.98 us -> 1.37 us
    ppermute x4, starting transfers between devices: 7.93 us -> 5.99 us  [to_mate(): return lax.ppermute(value, 'sx', mates)]
    all_gather x1, blocking collectives: 5.46 us -> 6.85 us  [gathered(): return lax.all_gather(value, ('grp', 'sx'), axis_index_groups=pairs)]
    pallas_call x3 -> x4, Pallas kernels: 1.77 us -> 2.96 us  [the longest x1 1.66 us: per_device(): pl.pallas_call(edges_kernel, out_shape=(pair, pair, shape(5 * ORB, 16), s...]
    ppermute x2 -> x1, starting transfers between devices: 1.33 us -> 0.66 us  [across(): return lax.ppermute(value, 'sx', others)]
    ppermute x4, waiting for transfers between devices: 1.98 us -> 1.37 us  [to_mate(): return lax.ppermute(value, 'sx', mates)]
  transfers between devices with their start and end apart: 6 -> 5, of which waited for: 2 -> 2; matrix products, arithmetic and copies ran while one was open for 0% -> 0% of each run, Pallas kernels for 19% -> 20%
where the time goes in v11:
time: 25.1 us; the launch traced here: 25 us
  Pallas kernels  9.98 us (40%)
  blocking collectives  6.85 us (27%)
  starting transfers between devices  6.65 us (26%)
  waiting for transfers between devices  1.37 us (5%)
    all_gather x1, blocking collectives, gathered(): return lax.all_gather(value, ('grp', 'sx'), axis_index_groups=pairs)  6.85 us
    ppermute x4, starting transfers between devices, to_mate(): return lax.ppermute(value, 'sx', mates)  5.99 us
    pallas_call x1, Pallas kernels, per_device(): pl.pallas_call(smooth_kernel, out_shape=(pltpu.HBM((ROWS, CX * PLANE), BF...  2.23 us
    pallas_call x1, Pallas kernels, per_device(): pl.pallas_call(energy_kernel, out_shape=(pair, pair, pair, shape(2, ROWS,...  2.02 us
    pallas_call x1, Pallas kernels, per_device(): pl.pallas_call(edges_kernel, out_shape=(pair, pair, shape(5 * ORB, 16), s...  1.66 us
    ppermute x4, waiting for transfers between devices, to_mate(): return lax.ppermute(value, 'sx', mates)  1.37 us
    pallas_call x1, Pallas kernels, per_device(): pl.pallas_call(finish_kernel, out_shape=pltpu.HBM((ROWS, CX * PLANE), BF1...  0.98 us
    pallas_call x1, Pallas kernels, per_device(): pl.pallas_call(face_kernel, out_shape=(pair, shape(7, ORB, 128), shape(RO...  0.87 us
  transfers between devices with their start and end apart: 5, of which 2 were waited for; matrix products, arithmetic and copies ran while one was open for 0% of the time, Pallas kernels for 20%

profile of v11, /device:TPU:0, one launch (start us, length us, event | category | flops | bytes accessed | tf_op | source)
XLA Modules:
  0.0 25.0 jit_solution(3148163857378669267)
XLA Ops:
  0.0 0.0 copy-start
  0.0 1.7 %edges.1 = (bf16[2,192,1024]{2,1,0:T(8,128)(2,1)S(1)}, bf16[2,192,1024]{2,1,0:T(8,128)(2,1)S(1)}, bf16[320,16]{1,0:T(8,128)(2,1)S(1)}, f32[192,1024]{1,0:T(8,128...) custom-call(s32[4,1024]{1,0:T(4,128)} %bitcast.4, s32[2,16]{1,0:T(2,128)} %bitcast.5, ...), custom_call_target="tpu_custom_call" | custom-call | flops 100000000 | bytes 1000000 | tf_op jit(solution)/shard_map/edges/pallas_call | solution.py:604
  1.7 0.5 %collective-permute-start = (bf16[192,128]{1,0:T(8,128)(2,1)S(1)}, bf16[192,128]{1,0:T(8,128)(2,1)S(1)}, u32[]{:S(2)}, u32[]{:S(2)}) collective-permute-start(bf16[192,128]{1,0:T(8,128)(2,1)S(1)} %get-tuple-element.35), channel_id=1, source_target_pairs={{0,1},{1,0},{2,3},{3,2},{4,5},{5,4},{6,7},{7,6},{8,9},{9,8},{10,11... | collective-permute-start | bytes 147464 | tf_op jit(solution)/shard_map/ppermute | solution.py:592
  2.2 0.0 copy-done
  2.2 0.0 copy-done.1
  2.2 2.0 %energy.1 = (bf16[2,192,1024]{2,1,0:T(8,128)(2,1)S(1)}, bf16[2,192,1024]{2,1,0:T(8,128)(2,1)S(1)}, bf16[2,192,1024]{2,1,0:T(8,128)(2,1)S(1)}, f32[2,192,1024]{2,...) custom-call(bf16[320,16]{1,0:T(8,128)(2,1)S(1)} %get-tuple-element.36.rows_ref, ...), custom_call_target="tpu_custom_call" | custom-call | flops 4000000000 | bytes 10000000 | tf_op jit(solution)/shard_map/energy/pallas_call | solution.py:624
  4.2 0.0 collective-permute-done.mate_ref
  4.2 0.6 %bands.1 = (bf16[2,192,1024]{2,1,0:T(8,128)(2,1)S(1)}, f32[2,192,256]{2,1,0:T(8,128)S(1)}, bf16[3,128,128]{2,1,0:T(8,128)(2,1)S(1)}) custom-call(bf16[192,128]{1,0:T(8,128)(2,1)S(1)} %collective-permute-done.mate_ref, f32[2,192,1024]{2,1,0:T(8,128)S(1)} %get-tuple-element.40.part_ref, ...), custom_call_target="tpu_custom_call", output_to_operand_aliasing={{0}: (6, {})} | custom-call | flops 1000000000 | bytes 10000000 | tf_op jit(solution)/shard_map/bands/pallas_call | solution.py:637
  4.8 0.1 collective-permute-start.1
  4.9 0.3 %around.1.around_ref = bf16[192,1024]{1,0:T(8,128)(2,1)S(1)} custom-call(bf16[320,16]{1,0:T(8,128)(2,1)S(1)} %get-tuple-element.36.rows_ref), custom_call_target="tpu_custom_call" | custom-call | flops 100000000 | bytes 1000000 | tf_op jit(solution)/shard_map/around/pallas_call | solution.py:648
  5.2 1.0 %collective-permute-done.1.rows_ref = bf16[3,128,128]{2,1,0:T(8,128)(2,1)S(1)} collective-permute-done((bf16[3,128,128]{2,1,0:T(8,128)(2,1)S(1)}, bf16[3,128,128]{2,1,0:T(8,128)(2,1)S(1)}, u32[]{:S(2)}, u32[]{:S(2)}) %collective-permute-start.1) | collective-permute-done | bytes 98336 | tf_op jit(solution)/shard_map/ppermute | solution.py:592
  6.2 0.2 relay.1
  6.4 6.8 %all-gather = bf16[1472,128]{1,0:T(8,128)(2,1)S(1)} all-gather(bf16[736,128]{1,0:T(8,128)(2,1)S(1)} %relay.1), channel_id=2, replica_groups={{1,2},{3,4},{5,6},{7,8},{9,10},{11,12},{13,14},{17,18},{19,20},{21,22},..., dimensions={0}, use_global_device_ids=true | all-gather | bytes 565248 | tf_op jit(solution)/shard_map/all_gather | solution.py:598
  13.2 0.9 %face.1 = (bf16[2,192,1024]{2,1,0:T(8,128)(2,1)S(1)}, bf16[7,64,128]{2,1,0:T(8,128)(2,1)S(1)}, f32[192,512]{1,0:T(8,128)S(1)}, bf16[4,64,128]{2,1,0:T(8,128)(2,1)S(1)}) custom-call(bf16[2,736,128]{2,1,0:T(8,128)(2,1)S(1)} %bitcast.3, bf16[192,1024]{1,0:T(8,128)(2,1)S(1)} %around.1.around_ref, ...), custom_call_target="tpu_custom_call", output_to_operand_aliasing={{0}: (5, {})} | custom-call | flops 100000000 | bytes 1000000 | tf_op jit(solution)/shard_map/face/pallas_call | solution.py:666
  14.1 1.2 %collective-permute-start.2 = (bf16[4,64,128]{2,1,0:T(8,128)(2,1)S(1)}, bf16[4,64,128]{2,1,0:T(8,128)(2,1)S(1)}, u32[]{:S(2)}, u32[]{:S(2)}) collective-permute-start(bf16[4,64,128]{2,1,0:T(8,128)(2,1)S(1)} %get-tuple-element.48), channel_id=1, source_target_pairs={{0,1},{1,0},{2,3},{3,2},{4,5},{5,4},{6,7},{7,6},{8,9},{9,8},{10,11... | collective-permute-start | bytes 196616 | tf_op jit(solution)/shard_map/ppermute | solution.py:592
  15.3 0.5 %theta.1 = (bf16[2,192,256]{2,1,0:T(8,128)(2,1)S(1)}, f32[192,192]{1,0:T(8,128)S(1)}) custom-call(f32[3,512]{1,0:T(4,128)S(1)} %get-tuple-element.34.keep_ref, f32[2,192,256]{2,1,0:T(8,128)S(1)} %get-tuple-element.44.own_ref, bf16[3,128,128]{2,1,0:T(8,128)(2,1)S(1)} %collective-permute-done.1.rows_ref, bf16[7,64,128]{2,1,0:T(8,128)(2,1)S(1)} %get-tuple-element.49.other_ref, ...), custom_call_target="tpu_custom_call" | custom-call | flops 1000000000 | bytes 4000000 | tf_op jit(solution)/shard_map/theta/pallas_call | solution.py:684
  15.8 0.4 %collective-permute-done.2.relayed_ref = bf16[4,64,128]{2,1,0:T(8,128)(2,1)S(1)} collective-permute-done((bf16[4,64,128]{2,1,0:T(8,128)(2,1)S(1)}, bf16[4,64,128]{2,1,0:T(8,128)(2,1)S(1)}, u32[]{:S(2)}, u32[]{:S(2)}) %collective-permute-start.2) | collective-permute-done | bytes 65568 | tf_op jit(solution)/shard_map/ppermute | solution.py:592
  16.2 0.7 %gradient.1 = (bf16[2,192,1024]{2,1,0:T(8,128)(2,1)S(1)}, bf16[192,192]{1,0:T(8,128)(2,1)S(1)}, bf16[192,128]{1,0:T(8,128)(2,1)S(1)}, bf16[192,128]{1,0:T(8,128)(2,1)S(1)}) custom-call(f32[3,512]{1,0:T(4,128)S(1)} %get-tuple-element.34.keep_ref, bf16[4,64,128]{2,1,0:T(8,128)(2,1)S(1)} %collective-permute-done.2.relayed_ref, ...), custom_call_target="tpu_custom_call" | custom-call | flops 1000000000 | bytes 10000000 | tf_op jit(solution)/shard_map/gradient/pallas_call | solution.py:694
  16.9 0.7 %collective-permute-start.3 = (bf16[192,128]{1,0:T(8,128)(2,1)S(1)}, bf16[192,128]{1,0:T(8,128)(2,1)S(1)}, u32[]{:S(2)}, u32[]{:S(2)}) collective-permute-start(bf16[192,128]{1,0:T(8,128)(2,1)S(1)} %get-tuple-element.54), channel_id=1, source_target_pairs={{1,2},{2,1},{3,4},{4,3},{5,6},{6,5},{7,8},{8,7},{9,10},{10,9},{11,... | collective-permute-start | bytes 147464 | tf_op jit(solution)/shard_map/ppermute | solution.py:595
  17.6 4.2 %collective-permute-start.4 = (bf16[192,128]{1,0:T(8,128)(2,1)S(1)}, bf16[192,128]{1,0:T(8,128)(2,1)S(1)}, u32[]{:S(2)}, u32[]{:S(2)}) collective-permute-start(bf16[192,128]{1,0:T(8,128)(2,1)S(1)} %get-tuple-element.55), channel_id=1, source_target_pairs={{0,1},{1,0},{2,3},{3,2},{4,5},{5,4},{6,7},{7,6},{8,9},{9,8},{10,11... | collective-permute-start | bytes 147464 | tf_op jit(solution)/shard_map/ppermute | solution.py:592
  21.7 2.2 %smooth.1 = (bf16[192,4096]{1,0:T(8,128)(2,1)}, f32[2,192,1024]{2,1,0:T(8,128)S(1)}) custom-call(bf16[192,192]{1,0:T(8,128)(2,1)S(1)} %get-tuple-element.56.theta_ref, bf16[2,192,1024]{2,1,0:T(8,128)(2,1)S(1)} %get-tuple-element.57.phi_ref, bf16[2,192,1024]{2,1,0:T(8,128)(2,1)S(1)} %get-tuple-element.58.energy_ref, ...), custom_call_target="tpu_custom_call" | custom-call | flops 2000000000 | bytes 10000000 | tf_op jit(solution)/shard_map/smooth/pallas_call | solution.py:707
  24.0 0.0 collective-permute-done.3.across_ref
  24.0 0.0 collective-permute-done.4.mate_ref
  24.0 1.0 %finish.1 = bf16[192,4096]{1,0:T(8,128)(2,1)} custom-call(bf16[192,128]{1,0:T(8,128)(2,1)S(1)} %collective-permute-done.3.across_ref, bf16[192,128]{1,0:T(8,128)(2,1)S(1)} %collective-permute-done.4.mate_ref, f32[2,192,1024]{2,1,0:T(8,128)S(1)} %get-tuple-element.61.part_ref, ...), custom_call_target="tpu_custom_call", output_to_operand_aliasing={{}: (4, {})} | custom-call | flops 10000000 | bytes 10000000 | tf_op jit(solution)/shard_map/finish/pallas_call | solution.py:723
  (1 shorter events, 0.0 us)
Async XLA Ops:
  0.0 2.2 %copy-start = (bf16[192,4096]{1,0:T(8,128)(2,1)S(1)}, bf16[192,4096]{1,0:T(8,128)(2,1)}, u32[]{:S(2)}) copy-start(bf16[192,4096]{1,0:T(8,128)(2,1)} %pieces_ref.3) | copy-start | bytes 4718596
  0.0 2.2 %copy-start.1 = (f32[4,1024]{1,0:T(4,128)S(1)}, f32[4,1024]{1,0:T(4,128)}, u32[]{:S(2)}) copy-start(f32[4,1024]{1,0:T(4,128)} %pot_ref.1) | copy-start | bytes 49156
  1.7 2.5 %collective-permute-start = (bf16[192,128]{1,0:T(8,128)(2,1)S(1)}, bf16[192,128]{1,0:T(8,128)(2,1)S(1)}, u32[]{:S(2)}, u32[]{:S(2)}) collective-permute-start(bf16[192,128]{1,0:T(8,128)(2,1)S(1)} %get-tuple-element.35), channel_id=1, source_target_pairs={{0,1},{1,0},{2,3},{3,2},{4,5},{5,4},{6,7},{7,6},{8,9},{9,8},{10,11... | collective-permute-start | bytes 147464 | tf_op jit(solution)/shard_map/ppermute | solution.py:592
  4.8 1.4 %collective-permute-start.1 = (bf16[3,128,128]{2,1,0:T(8,128)(2,1)S(1)}, bf16[3,128,128]{2,1,0:T(8,128)(2,1)S(1)}, u32[]{:S(2)}, u32[]{:S(2)}) collective-permute-start(bf16[3,128,128]{2,1,0:T(8,128)(2,1)S(1)} %get-tuple-element.45), channel_id=1, source_target_pairs={{0,1},{1,0},{2,3},{3,2},{4,5},{5,4},{6,7},{7,6},{8,9},{9,8},{10,11... | collective-permute-start | bytes 294920 | tf_op jit(solution)/shard_map/ppermute | solution.py:592
  14.1 2.1 %collective-permute-start.2 = (bf16[4,64,128]{2,1,0:T(8,128)(2,1)S(1)}, bf16[4,64,128]{2,1,0:T(8,128)(2,1)S(1)}, u32[]{:S(2)}, u32[]{:S(2)}) collective-permute-start(bf16[4,64,128]{2,1,0:T(8,128)(2,1)S(1)} %get-tuple-element.48), channel_id=1, source_target_pairs={{0,1},{1,0},{2,3},{3,2},{4,5},{5,4},{6,7},{7,6},{8,9},{9,8},{10,11... | collective-permute-start | bytes 196616 | tf_op jit(solution)/shard_map/ppermute | solution.py:592
  16.9 7.1 %collective-permute-start.3 = (bf16[192,128]{1,0:T(8,128)(2,1)S(1)}, bf16[192,128]{1,0:T(8,128)(2,1)S(1)}, u32[]{:S(2)}, u32[]{:S(2)}) collective-permute-start(bf16[192,128]{1,0:T(8,128)(2,1)S(1)} %get-tuple-element.54), channel_id=1, source_target_pairs={{1,2},{2,1},{3,4},{4,3},{5,6},{6,5},{7,8},{8,7},{9,10},{10,9},{11,... | collective-permute-start | bytes 147464 | tf_op jit(solution)/shard_map/ppermute | solution.py:595
  17.6 6.4 %collective-permute-start.4 = (bf16[192,128]{1,0:T(8,128)(2,1)S(1)}, bf16[192,128]{1,0:T(8,128)(2,1)S(1)}, u32[]{:S(2)}, u32[]{:S(2)}) collective-permute-start(bf16[192,128]{1,0:T(8,128)(2,1)S(1)} %get-tuple-element.55), channel_id=1, source_target_pairs={{0,1},{1,0},{2,3},{3,2},{4,5},{5,4},{6,7},{7,6},{8,9},{9,8},{10,11... | collective-permute-start | bytes 147464 | tf_op jit(solution)/shard_map/ppermute | solution.py:592

commit v12 on v11

--- a/solution.py
+++ b/solution.py
@@ -15,7 +15,7 @@
 PLANE = NY * NZ
 TILE = 256
 WINDOW = 6 * ORB
-FACE = ROWS + ROWS // 2
+FACE = 2 * ORB + ORB // 4
 F32 = jnp.float32
 BF16 = jnp.bfloat16
 
@@ -106,29 +106,74 @@
     return jnp.concatenate([first, last], axis=2)
 
 
-def fold(values):
-    tiles = [values[:, 128 * t : 128 * t + 128] for t in range(PLANE // 128)]
+def low_lanes(width):
+    return (iota((1, 128), 1) & (2 * width - 1)) < width
+
+
+def pack(first, second, width):
+    return jnp.where(
+        low_lanes(width),
+        first + pltpu.roll(first, 128 - width, 1),
+        second + pltpu.roll(second, width, 1),
+    )
+
+
+def unpack(packed, width):
+    low = low_lanes(width)
+    return (
+        jnp.where(low, packed, pltpu.roll(packed, width, 1)),
+        jnp.where(low, pltpu.roll(packed, 128 - width, 1), packed),
+    )
+
+
+def lane_tiles(values):
+    return [values[:, 128 * t : 128 * t + 128] for t in range(PLANE // 128)]
+
+
+def halves(values):
+    half = values.shape[0] // 2
+    return values[:half], values[half:]
+
+
+def fold(full, side):
+    tiles = lane_tiles(full)
     a, b, c = (sum(tiles[t::3][1:], tiles[t]) for t in range(3))
-    low_z = (iota((1, 128), 1) & 31) < 16
-    half = values.shape[0] // 2
-    top, bottom = c[:half], c[half:]
-    return (
-        jnp.where(low_z, a + pltpu.roll(a, 112, 1), b + pltpu.roll(b, 16, 1)),
-        jnp.where(low_z, top + pltpu.roll(top, 112, 1), bottom + pltpu.roll(bottom, 16, 1)),
-    )
+    tiles = lane_tiles(side)
+    d, e = (sum(tiles[t::2][1:], tiles[t]) for t in range(2))
+    return pack(a, b, 16), pack(*halves(c), 16), pack(*halves(pack(d, e, 16)), 8)
 
 
 def unfold(packed):
-    low_z = (iota((1, 128), 1) & 31) < 16
-    count = packed.shape[0] // 3 * 2
-    p, q = packed[:count], packed[count:]
-    return (
-        jnp.where(low_z, p, pltpu.roll(p, 16, 1)),
-        jnp.where(low_z, pltpu.roll(p, 112, 1), p),
-        jnp.concatenate(
-            [jnp.where(low_z, q, pltpu.roll(q, 16, 1)), jnp.where(low_z, pltpu.roll(q, 112, 1), q)], axis=0
-        ),
-    )
+    a, b = unpack(packed[:ORB], 16)
+    c = jnp.concatenate(unpack(packed[ORB : ORB + ORB // 2], 16), axis=0)
+    d, e = unpack(jnp.concatenate(unpack(packed[ORB + ORB // 2 : 2 * ORB], 8), axis=0), 16)
+    return (a, b, c), (d, e)
+
+
+def fold_far(values):
+    tiles = lane_tiles(values)
+    return pack(*halves(pack(*halves(sum(tiles[1:], tiles[0])), 16)), 8)
+
+
+def unfold_far(packed):
+    half = jnp.concatenate(unpack(packed, 8), axis=0)
+    return jnp.concatenate(unpack(half, 16), axis=0)
+
+
+def put_fold(ref, parts):
+    start = 0
+    for part in parts:
+        ref[start : start + part.shape[0]] = part.astype(BF16)
+        start += part.shape[0]
+
+
+def side_by_side(unfolded, i):
+    full, side = unfolded
+    tiles = []
+    for t in range(PLANE // 128):
+        pair = [full[t % 3], side[t % 2]]
+        tiles.append(jnp.concatenate(pair if i == 0 else pair[::-1], axis=0))
+    return tiles
 
 
 def is_even():
@@ -136,12 +181,12 @@
 
 
 def put_messages(planes, mate_ref, across_ref):
-    down = fold(planes[0, : 2 * ORB].astype(F32))
-    up = fold(planes[1, ORB:].astype(F32))
-    even = is_even()
-    for i, rows in enumerate((slice(0, 2 * ORB), slice(2 * ORB, ROWS))):
-        mate_ref[rows] = jnp.where(even, up[i], down[i]).astype(BF16)
-        across_ref[rows] = jnp.where(even, down[i], up[i]).astype(BF16)
+    own = slice(ORB, 2 * ORB)
+    down = fold(planes[0, own].astype(F32), planes[0, :ORB].astype(F32))
+    up = fold(planes[1, own].astype(F32), planes[1, 2 * ORB :].astype(F32))
+    even = is_even()
+    put_fold(mate_ref, [jnp.where(even, u, d) for u, d in zip(up, down)])
+    put_fold(across_ref, [jnp.where(even, d, u) for u, d in zip(up, down)])
 
 
 def sides(mate, across):
@@ -204,10 +249,11 @@
         copies[i].wait()
         phi_ref[i] = raw_ref[i] * mask_ref[i]
     even = is_even()
-    face = jnp.where(even, phi_ref[1, ORB:].astype(F32), phi_ref[0, : 2 * ORB].astype(F32))
-    mate_ref[: 2 * ORB], mate_ref[2 * ORB :] = (value.astype(BF16) for value in fold(face))
-    face = jnp.where(even, phi_ref[0].astype(F32), phi_ref[1].astype(F32))
-    across_ref[:ROWS], across_ref[ROWS:] = (value.astype(BF16) for value in fold(face))
+    own = slice(ORB, 2 * ORB)
+    lower, upper = phi_ref[0].astype(F32), phi_ref[1].astype(F32)
+    put_fold(mate_ref, fold(jnp.where(even, upper[own], lower[own]), jnp.where(even, upper[2 * ORB :], lower[:ORB])))
+    parts = fold(jnp.where(even, lower[own], upper[own]), jnp.where(even, lower[:ORB], upper[2 * ORB :]))
+    put_fold(across_ref, parts + (fold_far(jnp.where(even, lower[2 * ORB :], upper[:ORB])),))
 
 
 def rows_product(a, b):
@@ -238,17 +284,18 @@
             part_ref[i, :, lanes] = value
             rest = rest_rows(i)
             edge_energy_ref[i, rest, lanes] = value[rest].astype(BF16) * edge_mask_ref[i, rest, lanes]
-    mid = jnp.concatenate([phi_ref[0], phi_ref[1]], axis=1)
-    both = jnp.concatenate([energy_ref[0], energy_ref[1]], axis=1)
-    gram = rows_product(jnp.concatenate([mid, both], axis=0), mid)
-    corr = gram[:ROWS]
-    ham_ref[...] = gram[ROWS:]
+        orbitals = jnp.concatenate([phi_ref[0, :, lanes], phi_ref[1, :, lanes]], axis=1)
+        energies = jnp.concatenate([energy_ref[0, :, lanes], energy_ref[1, :, lanes]], axis=1)
+        grams = [rows_product(jnp.concatenate([orbitals, energies], axis=0), orbitals)]
+        for i in range(2):
+            orbitals = edge_ref[i, :, lanes]
+            energies = edge_energy_ref[i, rest_rows(i), lanes]
+            grams.append(rows_product(jnp.concatenate([orbitals, energies], axis=0), orbitals))
+        total = grams if t == 0 else [a + b for a, b in zip(total, grams)]
+    corr_ref[...] = total[0][:ROWS] + (total[1][:ROWS] + total[2][:ROWS])
+    ham_ref[...] = total[0][ROWS:]
     for i in range(2):
-        rest = rest_rows(i)
-        gram = rows_product(jnp.concatenate([edge_ref[i], edge_energy_ref[i, rest]], axis=0), edge_ref[i])
-        corr = corr + gram[:ROWS]
-        ham_ref[rest] += gram[ROWS:]
-    corr_ref[...] = corr
+        ham_ref[rest_rows(i)] += total[1 + i][ROWS:]
 
 
 def halo_rows(i):
@@ -267,10 +314,10 @@
     gram = []
     mate = mate_ref[...].astype(F32)
     for i, side in enumerate(sides(mate, jnp.zeros_like(mate))):
-        tiles = unfold(side)
+        tiles = side_by_side(unfold(side), i)
         for t in range(PLANE // 128):
             lanes = slice(128 * t, 128 * t + 128)
-            value = part_ref[i, halo_rows(i), lanes] - 0.5 * tiles[t % 3]
+            value = part_ref[i, halo_rows(i), lanes] - 0.5 * tiles[t]
             energy_ref[i, halo_rows(i), lanes] = value.astype(BF16) * mask_ref[i, halo_rows(i), lanes]
         gram.append(rows_product(energy_ref[i, halo_rows(i)], phi_ref[i]))
     own_ref[:, :, ROWS:] = jnp.zeros((2, ROWS, TILE - ROWS), F32)
@@ -359,10 +406,8 @@
     tiles = [got(ORB * i, ORB) for i in range(7)]
     for i in range(7):
         other_ref[i] = tiles[i].astype(BF16)
-    spread = unfold(got(7 * ORB, FACE))
-    for t in range(PLANE // 128):
-        lanes = slice(128 * t, 128 * t + 128)
-        beyond_ref[:, lanes] = spread[t % 3].astype(BF16) * around_ref[:, lanes]
+    beside = unfold(got(7 * ORB, 2 * ORB))
+    far_off = unfold_far(got(9 * ORB, ORB // 4)).astype(BF16)
     extra_ref[...] = jnp.zeros((ROWS, 8 * ORB), F32)
     work_ref[:, :, ROWS:] = jnp.zeros((2, 2 * ORB, TILE - ROWS), F32)
     head, tail = shared_head(tiles[4], 1), tiles[6]
@@ -372,9 +417,11 @@
     def add_face(i):
         here = halo_rows(i)
         there = slice(ORB, ROWS) if i == 0 else slice(0, 2 * ORB)
-        for t in range(PLANE // 128):
+        outer = slice(0, ORB) if i == 0 else slice(2 * ORB, ROWS)
+        for t, value in enumerate(side_by_side(beside, i)):
             lanes = slice(128 * t, 128 * t + 128)
-            value = spread[t % 3][there]
+            beyond_ref[there, lanes] = value.astype(BF16) * around_ref[there, lanes]
+            beyond_ref[outer, lanes] = far_off * around_ref[outer, lanes]
             mask = mask_ref[i, here, lanes]
             halo_ref[:, lanes] = value.astype(BF16) * mask
             energy_ref[i, here, lanes] = (part_ref[i, here, lanes] - 0.5 * value).astype(BF16) * mask
@@ -539,7 +586,10 @@
 
 
 def finish_kernel(across_ref, mate_ref, part_ref, mask_ref, inner_ref, out_ref, done_ref, sems):
-    halos = [unfold(side) for side in sides(mate_ref[...].astype(F32), across_ref[...].astype(F32))]
+    halos = [
+        side_by_side(unfold(side), i)
+        for i, side in enumerate(sides(mate_ref[...].astype(F32), across_ref[...].astype(F32)))
+    ]
     copies = []
     for i in range(2):
         start = PLANE * (CX - 1) * i
@@ -548,7 +598,7 @@
             got = slice(ORB * half, ORB * half + ORB)
             for t in range(PLANE // 128):
                 lanes = slice(128 * t, 128 * t + 128)
-                value = (part_ref[i, rows, lanes] + halos[i][t % 3][got]) * (1.0 / 32.0)
+                value = (part_ref[i, rows, lanes] + halos[i][t][got]) * (1.0 / 32.0)
                 done_ref[i, got, lanes] = value.astype(BF16) * mask_ref[i, rows, lanes]
             copies.append(
                 pltpu.make_async_copy(
@@ -605,7 +655,7 @@
         edges_kernel,
         out_shape=(
             pair, pair, shape(5 * ORB, 16), shape(ROWS, PLANE, dtype=F32), shape(3, 8 * ORB, dtype=F32),
-            shape(ROWS, 128), shape(FACE, 128),
+            shape(2 * ORB, 128), shape(FACE, 128),
         ),
         in_specs=[FAR, FAR, FAR],
         out_specs=(WHOLE,) * 7,
@@ -693,7 +743,7 @@
     )(keep, own, mate_rows, other_rows, extra)
     edge_grad, theta, for_mate, for_other = pl.pallas_call(
         gradient_kernel,
-        out_shape=(pair, shape(ROWS, ROWS), shape(ROWS, 128), shape(ROWS, 128)),
+        out_shape=(pair, shape(ROWS, ROWS), shape(2 * ORB, 128), shape(2 * ORB, 128)),
         in_specs=[WHOLE] * 7,
         out_specs=(WHOLE,) * 4,
         scratch_shapes=[pltpu.VMEM((ROWS, TILE), BF16), pltpu.VMEM((ROWS, ROWS), F32)],

time: 25.1 us -> 24.7 us (0.984)
  starting transfers between devices: 6.65 us -> 6.02 us
  Pallas kernels: 9.98 us -> 10.4 us
  blocking collectives: 6.85 us -> 6.45 us
    ppermute x4, starting transfers between devices: 5.99 us -> 5.36 us  [to_mate(): return lax.ppermute(value, 'sx', mates)]
    all_gather x1, blocking collectives: 6.85 us -> 6.45 us  [gathered(): return lax.all_gather(value, ('grp', 'sx'), axis_index_groups=pairs)]
  transfers between devices with their start and end apart: 5 -> 5, of which waited for: 2 -> 2; matrix products, arithmetic and copies ran while one was open for 0% -> 0% of each run, Pallas kernels for 20% -> 21%
where the time goes in v12:
time: 24.7 us; the launch traced here: 24.6 us
  Pallas kernels  10.4 us (42%)
  blocking collectives  6.45 us (26%)
  starting transfers between devices  6.02 us (24%)
  waiting for transfers between devices  1.61 us (7%)
    all_gather x1, blocking collectives, gathered(): return lax.all_gather(value, ('grp', 'sx'), axis_index_groups=pairs)  6.45 us
    ppermute x4, starting transfers between devices, to_mate(): return lax.ppermute(value, 'sx', mates)  5.36 us
    pallas_call x1, Pallas kernels, per_device(): pl.pallas_call(energy_kernel, out_shape=(pair, pair, pair, shape(2, ROWS,...  2.24 us
    pallas_call x1, Pallas kernels, per_device(): pl.pallas_call(smooth_kernel, out_shape=(pltpu.HBM((ROWS, CX * PLANE), BF...  2.23 us
    pallas_call x1, Pallas kernels, per_device(): pl.pallas_call(edges_kernel, out_shape=(pair, pair, shape(5 * ORB, 16), s...  1.69 us
    ppermute x4, waiting for transfers between devices, to_mate(): return lax.ppermute(value, 'sx', mates)  1.61 us
    pallas_call x1, Pallas kernels, per_device(): pl.pallas_call(finish_kernel, out_shape=pltpu.HBM((ROWS, CX * PLANE), BF1...  1.03 us
    pallas_call x1, Pallas kernels, per_device(): pl.pallas_call(face_kernel, out_shape=(pair, shape(7, ORB, 128), shape(RO...  0.85 us
  transfers between devices with their start and end apart: 5, of which 2 were waited for; matrix products, arithmetic and copies ran while one was open for 0% of the time, Pallas kernels for 21%

profile of v12, /device:TPU:0, one launch (start us, length us, event | category | flops | bytes accessed | tf_op | source)
XLA Modules:
  0.0 24.6 jit_solution(17887089506534191532)
XLA Ops:
  0.0 0.0 copy-start
  0.0 1.7 %edges.1 = (bf16[2,192,1024]{2,1,0:T(8,128)(2,1)S(1)}, bf16[2,192,1024]{2,1,0:T(8,128)(2,1)S(1)}, bf16[320,16]{1,0:T(8,128)(2,1)S(1)}, f32[192,1024]{1,0:T(8,128...) custom-call(s32[4,1024]{1,0:T(4,128)} %bitcast.4, s32[2,16]{1,0:T(2,128)} %bitcast.5, ...), custom_call_target="tpu_custom_call" | custom-call | flops 100000000 | bytes 1000000 | tf_op jit(solution)/shard_map/edges/pallas_call | solution.py:654
  1.7 0.5 %collective-permute-start = (bf16[128,128]{1,0:T(8,128)(2,1)S(1)}, bf16[128,128]{1,0:T(8,128)(2,1)S(1)}, u32[]{:S(2)}, u32[]{:S(2)}) collective-permute-start(bf16[128,128]{1,0:T(8,128)(2,1)S(1)} %get-tuple-element.35), channel_id=1, source_target_pairs={{0,1},{1,0},{2,3},{3,2},{4,5},{5,4},{6,7},{7,6},{8,9},{9,8},{10,11... | collective-permute-start | bytes 98312 | tf_op jit(solution)/shard_map/ppermute | solution.py:642
  2.2 0.0 copy-done
  2.2 0.0 copy-done.1
  2.2 2.2 %energy.1 = (bf16[2,192,1024]{2,1,0:T(8,128)(2,1)S(1)}, bf16[2,192,1024]{2,1,0:T(8,128)(2,1)S(1)}, bf16[2,192,1024]{2,1,0:T(8,128)(2,1)S(1)}, f32[2,192,1024]{2,...) custom-call(bf16[320,16]{1,0:T(8,128)(2,1)S(1)} %get-tuple-element.36.rows_ref, ...), custom_call_target="tpu_custom_call" | custom-call | flops 4000000000 | bytes 10000000 | tf_op jit(solution)/shard_map/energy/pallas_call | solution.py:674
  4.5 0.0 collective-permute-done.mate_ref
  4.5 0.6 %bands.1 = (bf16[2,192,1024]{2,1,0:T(8,128)(2,1)S(1)}, f32[2,192,256]{2,1,0:T(8,128)S(1)}, bf16[3,128,128]{2,1,0:T(8,128)(2,1)S(1)}) custom-call(bf16[128,128]{1,0:T(8,128)(2,1)S(1)} %collective-permute-done.mate_ref, f32[2,192,1024]{2,1,0:T(8,128)S(1)} %get-tuple-element.40.part_ref, ...), custom_call_target="tpu_custom_call", output_to_operand_aliasing={{0}: (6, {})} | custom-call | flops 1000000000 | bytes 10000000 | tf_op jit(solution)/shard_map/bands/pallas_call | solution.py:687
  5.1 0.1 collective-permute-start.1
  5.2 0.3 %around.1.around_ref = bf16[192,1024]{1,0:T(8,128)(2,1)S(1)} custom-call(bf16[320,16]{1,0:T(8,128)(2,1)S(1)} %get-tuple-element.36.rows_ref), custom_call_target="tpu_custom_call" | custom-call | flops 100000000 | bytes 1000000 | tf_op jit(solution)/shard_map/around/pallas_call | solution.py:698
  5.5 1.0 %collective-permute-done.1.rows_ref = bf16[3,128,128]{2,1,0:T(8,128)(2,1)S(1)} collective-permute-done((bf16[3,128,128]{2,1,0:T(8,128)(2,1)S(1)}, bf16[3,128,128]{2,1,0:T(8,128)(2,1)S(1)}, u32[]{:S(2)}, u32[]{:S(2)}) %collective-permute-start.1) | collective-permute-done | bytes 98336 | tf_op jit(solution)/shard_map/ppermute | solution.py:642
  6.5 0.2 relay.1
  6.7 6.5 %all-gather = bf16[1184,128]{1,0:T(8,128)(2,1)S(1)} all-gather(bf16[592,128]{1,0:T(8,128)(2,1)S(1)} %relay.1), channel_id=2, replica_groups={{1,2},{3,4},{5,6},{7,8},{9,10},{11,12},{13,14},{17,18},{19,20},{21,22},..., dimensions={0}, use_global_device_ids=true | all-gather | bytes 454656 | tf_op jit(solution)/shard_map/all_gather | solution.py:648
  13.1 0.8 %face.1 = (bf16[2,192,1024]{2,1,0:T(8,128)(2,1)S(1)}, bf16[7,64,128]{2,1,0:T(8,128)(2,1)S(1)}, f32[192,512]{1,0:T(8,128)S(1)}, bf16[4,64,128]{2,1,0:T(8,128)(2,1)S(1)}) custom-call(bf16[2,592,128]{2,1,0:T(8,128)(2,1)S(1)} %bitcast.3, bf16[192,1024]{1,0:T(8,128)(2,1)S(1)} %around.1.around_ref, ...), custom_call_target="tpu_custom_call", output_to_operand_aliasing={{0}: (5, {})} | custom-call | flops 100000000 | bytes 1000000 | tf_op jit(solution)/shard_map/face/pallas_call | solution.py:716
  14.0 0.2 collective-permute-start.2
  14.2 0.5 %theta.1 = (bf16[2,192,256]{2,1,0:T(8,128)(2,1)S(1)}, f32[192,192]{1,0:T(8,128)S(1)}) custom-call(f32[3,512]{1,0:T(4,128)S(1)} %get-tuple-element.34.keep_ref, f32[2,192,256]{2,1,0:T(8,128)S(1)} %get-tuple-element.44.own_ref, bf16[3,128,128]{2,1,0:T(8,128)(2,1)S(1)} %collective-permute-done.1.rows_ref, bf16[7,64,128]{2,1,0:T(8,128)(2,1)S(1)} %get-tuple-element.49.other_ref, ...), custom_call_target="tpu_custom_call" | custom-call | flops 1000000000 | bytes 4000000 | tf_op jit(solution)/shard_map/theta/pallas_call | solution.py:734
  14.7 0.6 %collective-permute-done.2.relayed_ref = bf16[4,64,128]{2,1,0:T(8,128)(2,1)S(1)} collective-permute-done((bf16[4,64,128]{2,1,0:T(8,128)(2,1)S(1)}, bf16[4,64,128]{2,1,0:T(8,128)(2,1)S(1)}, u32[]{:S(2)}, u32[]{:S(2)}) %collective-permute-start.2) | collective-permute-done | bytes 65568 | tf_op jit(solution)/shard_map/ppermute | solution.py:642
  15.3 0.7 %gradient.1 = (bf16[2,192,1024]{2,1,0:T(8,128)(2,1)S(1)}, bf16[192,192]{1,0:T(8,128)(2,1)S(1)}, bf16[128,128]{1,0:T(8,128)(2,1)S(1)}, bf16[128,128]{1,0:T(8,128)(2,1)S(1)}) custom-call(f32[3,512]{1,0:T(4,128)S(1)} %get-tuple-element.34.keep_ref, bf16[4,64,128]{2,1,0:T(8,128)(2,1)S(1)} %collective-permute-done.2.relayed_ref, ...), custom_call_target="tpu_custom_call" | custom-call | flops 1000000000 | bytes 10000000 | tf_op jit(solution)/shard_map/gradient/pallas_call | solution.py:744
  16.0 0.7 %collective-permute-start.3 = (bf16[128,128]{1,0:T(8,128)(2,1)S(1)}, bf16[128,128]{1,0:T(8,128)(2,1)S(1)}, u32[]{:S(2)}, u32[]{:S(2)}) collective-permute-start(bf16[128,128]{1,0:T(8,128)(2,1)S(1)} %get-tuple-element.54), channel_id=1, source_target_pairs={{1,2},{2,1},{3,4},{4,3},{5,6},{6,5},{7,8},{8,7},{9,10},{10,9},{11,... | collective-permute-start | bytes 98312 | tf_op jit(solution)/shard_map/ppermute | solution.py:645
  16.7 4.5 %collective-permute-start.4 = (bf16[128,128]{1,0:T(8,128)(2,1)S(1)}, bf16[128,128]{1,0:T(8,128)(2,1)S(1)}, u32[]{:S(2)}, u32[]{:S(2)}) collective-permute-start(bf16[128,128]{1,0:T(8,128)(2,1)S(1)} %get-tuple-element.55), channel_id=1, source_target_pairs={{0,1},{1,0},{2,3},{3,2},{4,5},{5,4},{6,7},{7,6},{8,9},{9,8},{10,11... | collective-permute-start | bytes 98312 | tf_op jit(solution)/shard_map/ppermute | solution.py:642
  21.3 2.2 %smooth.1 = (bf16[192,4096]{1,0:T(8,128)(2,1)}, f32[2,192,1024]{2,1,0:T(8,128)S(1)}) custom-call(bf16[192,192]{1,0:T(8,128)(2,1)S(1)} %get-tuple-element.56.theta_ref, bf16[2,192,1024]{2,1,0:T(8,128)(2,1)S(1)} %get-tuple-element.57.phi_ref, bf16[2,192,1024]{2,1,0:T(8,128)(2,1)S(1)} %get-tuple-element.58.energy_ref, ...), custom_call_target="tpu_custom_call" | custom-call | flops 2000000000 | bytes 10000000 | tf_op jit(solution)/shard_map/smooth/pallas_call | solution.py:757
  23.5 0.0 collective-permute-done.3.across_ref
  23.5 0.0 collective-permute-done.4.mate_ref
  23.5 1.0 %finish.1 = bf16[192,4096]{1,0:T(8,128)(2,1)} custom-call(bf16[128,128]{1,0:T(8,128)(2,1)S(1)} %collective-permute-done.3.across_ref, bf16[128,128]{1,0:T(8,128)(2,1)S(1)} %collective-permute-done.4.mate_ref, f32[2,192,1024]{2,1,0:T(8,128)S(1)} %get-tuple-element.61.part_ref, ...), custom_call_target="tpu_custom_call", output_to_operand_aliasing={{}: (4, {})} | custom-call | flops 10000000 | bytes 10000000 | tf_op jit(solution)/shard_map/finish/pallas_call | solution.py:773
  (1 shorter events, 0.0 us)
Async XLA Ops:
  0.0 2.2 %copy-start = (bf16[192,4096]{1,0:T(8,128)(2,1)S(1)}, bf16[192,4096]{1,0:T(8,128)(2,1)}, u32[]{:S(2)}) copy-start(bf16[192,4096]{1,0:T(8,128)(2,1)} %pieces_ref.3) | copy-start | bytes 4718596
  0.0 2.2 %copy-start.1 = (f32[4,1024]{1,0:T(4,128)S(1)}, f32[4,1024]{1,0:T(4,128)}, u32[]{:S(2)}) copy-start(f32[4,1024]{1,0:T(4,128)} %pot_ref.1) | copy-start | bytes 49156
  1.7 2.8 %collective-permute-start = (bf16[128,128]{1,0:T(8,128)(2,1)S(1)}, bf16[128,128]{1,0:T(8,128)(2,1)S(1)}, u32[]{:S(2)}, u32[]{:S(2)}) collective-permute-start(bf16[128,128]{1,0:T(8,128)(2,1)S(1)} %get-tuple-element.35), channel_id=1, source_target_pairs={{0,1},{1,0},{2,3},{3,2},{4,5},{5,4},{6,7},{7,6},{8,9},{9,8},{10,11... | collective-permute-start | bytes 98312 | tf_op jit(solution)/shard_map/ppermute | solution.py:642
  5.1 1.4 %collective-permute-start.1 = (bf16[3,128,128]{2,1,0:T(8,128)(2,1)S(1)}, bf16[3,128,128]{2,1,0:T(8,128)(2,1)S(1)}, u32[]{:S(2)}, u32[]{:S(2)}) collective-permute-start(bf16[3,128,128]{2,1,0:T(8,128)(2,1)S(1)} %get-tuple-element.45), channel_id=1, source_target_pairs={{0,1},{1,0},{2,3},{3,2},{4,5},{5,4},{6,7},{7,6},{8,9},{9,8},{10,11... | collective-permute-start | bytes 294920 | tf_op jit(solution)/shard_map/ppermute | solution.py:642
  14.0 1.3 %collective-permute-start.2 = (bf16[4,64,128]{2,1,0:T(8,128)(2,1)S(1)}, bf16[4,64,128]{2,1,0:T(8,128)(2,1)S(1)}, u32[]{:S(2)}, u32[]{:S(2)}) collective-permute-start(bf16[4,64,128]{2,1,0:T(8,128)(2,1)S(1)} %get-tuple-element.48), channel_id=1, source_target_pairs={{0,1},{1,0},{2,3},{3,2},{4,5},{5,4},{6,7},{7,6},{8,9},{9,8},{10,11... | collective-permute-start | bytes 196616 | tf_op jit(solution)/shard_map/ppermute | solution.py:642
  16.0 7.5 %collective-permute-start.3 = (bf16[128,128]{1,0:T(8,128)(2,1)S(1)}, bf16[128,128]{1,0:T(8,128)(2,1)S(1)}, u32[]{:S(2)}, u32[]{:S(2)}) collective-permute-start(bf16[128,128]{1,0:T(8,128)(2,1)S(1)} %get-tuple-element.54), channel_id=1, source_target_pairs={{1,2},{2,1},{3,4},{4,3},{5,6},{6,5},{7,8},{8,7},{9,10},{10,9},{11,... | collective-permute-start | bytes 98312 | tf_op jit(solution)/shard_map/ppermute | solution.py:645
  16.7 6.8 %collective-permute-start.4 = (bf16[128,128]{1,0:T(8,128)(2,1)S(1)}, bf16[128,128]{1,0:T(8,128)(2,1)S(1)}, u32[]{:S(2)}, u32[]{:S(2)}) collective-permute-start(bf16[128,128]{1,0:T(8,128)(2,1)S(1)} %get-tuple-element.55), channel_id=1, source_target_pairs={{0,1},{1,0},{2,3},{3,2},{4,5},{5,4},{6,7},{7,6},{8,9},{9,8},{10,11... | collective-permute-start | bytes 98312 | tf_op jit(solution)/shard_map/ppermute | solution.py:642

commit v13 on v12

--- a/solution.py
+++ b/solution.py
@@ -216,15 +216,13 @@
 
 
 def edges_kernel(
-    table_ref, pattern_ref, pieces_ref,
-    phi_ref, mask_ref, rows_ref, reach_ref, keep_ref, mate_ref, across_ref,
-    window_ref, raw_ref, scalar_ref, sems,
+    table_ref, pieces_ref,
+    phi_ref, mask_ref, rows_ref, reach_ref, mate_ref,
+    window_ref, raw_ref, sems,
 ):
     first = window_start(table_ref.shape[1])
     table_copy = pltpu.make_async_copy(table_ref.at[:, pl.ds(first, WINDOW)], window_ref, sems.at[2])
     table_copy.start()
-    pattern_copy = pltpu.make_async_copy(pattern_ref, scalar_ref, sems.at[3])
-    pattern_copy.start()
     copies = []
     for i in range(2):
         start = (CX - 1) * PLANE * i
@@ -241,10 +239,6 @@
     reach_ref[...] = reach
     for i in range(2):
         mask_ref[i] = sphere(reach, rows, (CX - 1) * i)
-    pattern_copy.wait()
-    for r in range(3):
-        for q in range(4):
-            keep_ref[r : r + 1, 128 * q : 128 * q + 128] = kept(scalar_ref, r, q)
     for i in range(2):
         copies[i].wait()
         phi_ref[i] = raw_ref[i] * mask_ref[i]
@@ -252,8 +246,6 @@
     own = slice(ORB, 2 * ORB)
     lower, upper = phi_ref[0].astype(F32), phi_ref[1].astype(F32)
     put_fold(mate_ref, fold(jnp.where(even, upper[own], lower[own]), jnp.where(even, upper[2 * ORB :], lower[:ORB])))
-    parts = fold(jnp.where(even, lower[own], upper[own]), jnp.where(even, lower[:ORB], upper[2 * ORB :]))
-    put_fold(across_ref, parts + (fold_far(jnp.where(even, lower[2 * ORB :], upper[:ORB])),))
 
 
 def rows_product(a, b):
@@ -284,18 +276,17 @@
             part_ref[i, :, lanes] = value
             rest = rest_rows(i)
             edge_energy_ref[i, rest, lanes] = value[rest].astype(BF16) * edge_mask_ref[i, rest, lanes]
-        orbitals = jnp.concatenate([phi_ref[0, :, lanes], phi_ref[1, :, lanes]], axis=1)
-        energies = jnp.concatenate([energy_ref[0, :, lanes], energy_ref[1, :, lanes]], axis=1)
-        grams = [rows_product(jnp.concatenate([orbitals, energies], axis=0), orbitals)]
-        for i in range(2):
-            orbitals = edge_ref[i, :, lanes]
-            energies = edge_energy_ref[i, rest_rows(i), lanes]
-            grams.append(rows_product(jnp.concatenate([orbitals, energies], axis=0), orbitals))
-        total = grams if t == 0 else [a + b for a, b in zip(total, grams)]
-    corr_ref[...] = total[0][:ROWS] + (total[1][:ROWS] + total[2][:ROWS])
-    ham_ref[...] = total[0][ROWS:]
+    mid = jnp.concatenate([phi_ref[0], phi_ref[1]], axis=1)
+    both = jnp.concatenate([energy_ref[0], energy_ref[1]], axis=1)
+    gram = rows_product(jnp.concatenate([mid, both], axis=0), mid)
+    corr = gram[:ROWS]
+    ham_ref[...] = gram[ROWS:]
     for i in range(2):
-        ham_ref[rest_rows(i)] += total[1 + i][ROWS:]
+        rest = rest_rows(i)
+        gram = rows_product(jnp.concatenate([edge_ref[i], edge_energy_ref[i, rest]], axis=0), edge_ref[i])
+        corr = corr + gram[:ROWS]
+        ham_ref[rest] += gram[ROWS:]
+    corr_ref[...] = corr
 
 
 def halo_rows(i):
@@ -373,13 +364,23 @@
     out_ref[7 * ORB :] = face_ref[...]
 
 
-def around_kernel(rows_ref, mask_ref):
+def around_kernel(pattern_ref, rows_ref, phi_ref, mask_ref, keep_ref, face_ref, scalar_ref, sem):
+    pattern_copy = pltpu.make_async_copy(pattern_ref, scalar_ref, sem)
+    pattern_copy.start()
     even = is_even()
+    own = slice(ORB, 2 * ORB)
+    lower, upper = phi_ref[0].astype(F32), phi_ref[1].astype(F32)
+    parts = fold(jnp.where(even, lower[own], upper[own]), jnp.where(even, lower[:ORB], upper[2 * ORB :]))
+    put_fold(face_ref, parts + (fold_far(jnp.where(even, lower[2 * ORB :], upper[:ORB])),))
     rows = jnp.where(even, rows_ref[:ROWS].astype(F32), rows_ref[2 * ORB :].astype(F32))
     reach = jnp.dot(rows.astype(BF16), cell_features(), preferred_element_type=F32)
     plane = jnp.where(even, -1.0, float(CX))
     bound = rows[:, 6:7] * (2.0 * plane) - plane * plane
     mask_ref[...] = jnp.where(reach <= bound, 1.0, 0.0).astype(BF16)
+    pattern_copy.wait()
+    for r in range(3):
+        for q in range(4):
+            keep_ref[r : r + 1, 128 * q : 128 * q + 128] = kept(scalar_ref, r, q)
 
 
 def shared_head(tile, which):
@@ -390,9 +391,9 @@
 
 
 def face_kernel(
-    both_ref, around_ref, phi_ref, mask_ref, part_ref, energy_in_ref,
-    energy_ref, other_ref, extra_ref, forward_ref,
-    beyond_ref, halo_ref, back_ref, work_ref,
+    both_ref, around_ref, phi_ref, mask_ref,
+    halo_ref, other_ref, extra_ref, forward_ref,
+    beyond_ref, back_ref, work_ref,
 ):
     even = is_even()
     low = low_half()
@@ -422,9 +423,7 @@
             lanes = slice(128 * t, 128 * t + 128)
             beyond_ref[there, lanes] = value.astype(BF16) * around_ref[there, lanes]
             beyond_ref[outer, lanes] = far_off * around_ref[outer, lanes]
-            mask = mask_ref[i, here, lanes]
-            halo_ref[:, lanes] = value.astype(BF16) * mask
-            energy_ref[i, here, lanes] = (part_ref[i, here, lanes] - 0.5 * value).astype(BF16) * mask
+            halo_ref[:, lanes] = value.astype(BF16) * mask_ref[i, here, lanes]
             back_ref[:, lanes] = phi_ref[i, here, lanes] * around_ref[there, lanes]
         work_ref[0, :, :ROWS] = rows_product(halo_ref[...], phi_ref[i]) * scale
         work_ref[1, :, :ROWS] = rows_product(back_ref[...], beyond_ref[...]) * scale
@@ -453,6 +452,12 @@
     pl.when(jnp.logical_not(even))(lambda: add_face(1))
 
 
+def add_halo(i, halo_ref, part_ref, mask_ref, energy_ref):
+    here = halo_rows(i)
+    value = part_ref[i, here] - 0.5 * halo_ref[...].astype(F32)
+    energy_ref[i, here] = value.astype(BF16) * mask_ref[i, here]
+
+
 def put_gradient(theta, orbital_ref, energy_ref, mask_ref, out_ref):
     for i in range(2):
         for t in range(PLANE // TILE):
@@ -472,8 +477,8 @@
 
 
 def theta_kernel(
-    keep_ref, own_ref, rows_ref, other_ref, extra_ref,
-    window_ref, theta_ref,
+    keep_ref, own_ref, rows_ref, other_ref, extra_ref, halo_ref, part_ref, edge_mask_ref, energy_in_ref,
+    window_ref, theta_ref, energy_ref,
     ham_ref, inv_ref,
 ):
     even = is_even()
@@ -514,6 +519,8 @@
         window_ref[which, :, 0:128] = jnp.where(even, quarter[2], quarter[0]).astype(BF16)
         last = jnp.where(even, jnp.where(low, quarter[3], quarter[1]), quarter[1])
         window_ref[which, :, 128:256] = last.astype(BF16)
+    pl.when(even)(lambda: add_halo(0, halo_ref, part_ref, edge_mask_ref, energy_ref))
+    pl.when(jnp.logical_not(even))(lambda: add_halo(1, halo_ref, part_ref, edge_mask_ref, energy_ref))
 
 
 def gradient_kernel(
@@ -651,24 +658,22 @@
     patterns = pattern.T
     pair = shape(2, ROWS, PLANE)
 
-    edge, edge_mask, rows, reach, keep, for_mate, face = pl.pallas_call(
+    edge, edge_mask, rows, reach, for_mate = pl.pallas_call(
         edges_kernel,
         out_shape=(
-            pair, pair, shape(5 * ORB, 16), shape(ROWS, PLANE, dtype=F32), shape(3, 8 * ORB, dtype=F32),
-            shape(2 * ORB, 128), shape(FACE, 128),
+            pair, pair, shape(5 * ORB, 16), shape(ROWS, PLANE, dtype=F32), shape(2 * ORB, 128),
         ),
-        in_specs=[FAR, FAR, FAR],
-        out_specs=(WHOLE,) * 7,
+        in_specs=[FAR, FAR],
+        out_specs=(WHOLE,) * 5,
         scratch_shapes=[
             pltpu.VMEM((4, WINDOW), jnp.int32),
             pltpu.VMEM((2, ROWS, PLANE), BF16),
-            pltpu.SMEM(patterns.shape, jnp.int32),
-            pltpu.SemaphoreType.DMA((4,)),
+            pltpu.SemaphoreType.DMA((3,)),
         ],
         compiler_params=PARAMS,
         cost_estimate=cost(10**8, 10**6),
         name="edges",
-    )(far(table), far(patterns), far(pieces))
+    )(far(table), far(pieces))
     mate_side = to_mate(for_mate)
 
     mid, mid_mask, mid_energy, part, rest_energy, corr, ham = pl.pallas_call(
@@ -695,15 +700,16 @@
         name="bands",
     )(mate_side, part, edge_mask, edge, corr, ham, rest_energy)
     mate_rows = to_mate(for_mate)
-    around = pl.pallas_call(
+    around, keep, face = pl.pallas_call(
         around_kernel,
-        out_shape=shape(ROWS, PLANE),
-        in_specs=[WHOLE],
-        out_specs=WHOLE,
+        out_shape=(shape(ROWS, PLANE), shape(3, 8 * ORB, dtype=F32), shape(FACE, 128)),
+        in_specs=[FAR, WHOLE, WHOLE],
+        out_specs=(WHOLE,) * 3,
+        scratch_shapes=[pltpu.SMEM(patterns.shape, jnp.int32), pltpu.SemaphoreType.DMA],
         compiler_params=PARAMS,
         cost_estimate=cost(10**8, 10**6),
         name="around",
-    )(rows)
+    )(far(patterns), rows, edge)
     for_other = pl.pallas_call(
         relay_kernel,
         out_shape=shape(7 * ORB + FACE, 128),
@@ -713,34 +719,35 @@
         cost_estimate=cost(10**6, 10**6),
         name="relay",
     )(own, mate_rows, face)
-    edge_energy, other_rows, extra, forward = pl.pallas_call(
+    halo, other_rows, extra, forward = pl.pallas_call(
         face_kernel,
-        out_shape=(pair, shape(7, ORB, 128), shape(ROWS, 8 * ORB, dtype=F32), shape(4, ORB, 128)),
-        in_specs=[WHOLE] * 6,
+        out_shape=(
+            shape(2 * ORB, PLANE), shape(7, ORB, 128), shape(ROWS, 8 * ORB, dtype=F32), shape(4, ORB, 128),
+        ),
+        in_specs=[WHOLE] * 4,
         out_specs=(WHOLE,) * 4,
         scratch_shapes=[
             pltpu.VMEM((ROWS, PLANE), BF16),
             pltpu.VMEM((2 * ORB, PLANE), BF16),
-            pltpu.VMEM((2 * ORB, PLANE), BF16),
             pltpu.VMEM((2, 2 * ORB, TILE), F32),
         ],
-        input_output_aliases={5: 0},
         compiler_params=PARAMS,
         cost_estimate=cost(10**8, 10**6),
         name="face",
-    )(gathered(for_other), around, edge, edge_mask, part, edge_energy)
+    )(gathered(for_other), around, edge, edge_mask)
     relayed = to_mate(forward)
 
-    bands, base = pl.pallas_call(
+    bands, base, edge_energy = pl.pallas_call(
         theta_kernel,
-        out_shape=(shape(2, ROWS, TILE), shape(ROWS, ROWS, dtype=F32)),
-        in_specs=[WHOLE] * 5,
-        out_specs=(WHOLE,) * 2,
+        out_shape=(shape(2, ROWS, TILE), shape(ROWS, ROWS, dtype=F32), pair),
+        in_specs=[WHOLE] * 9,
+        out_specs=(WHOLE,) * 3,
         scratch_shapes=[pltpu.VMEM((ROWS, 8 * ORB), F32), pltpu.VMEM((ROWS, 8 * ORB), F32)],
+        input_output_aliases={8: 2},
         compiler_params=PARAMS,
         cost_estimate=cost(10**9, 4 * 10**6),
         name="theta",
-    )(keep, own, mate_rows, other_rows, extra)
+    )(keep, own, mate_rows, other_rows, extra, halo, part, edge_mask, edge_energy)
     edge_grad, theta, for_mate, for_other = pl.pallas_call(
         gradient_kernel,
         out_shape=(pair, shape(ROWS, ROWS), shape(2 * ORB, 128), shape(2 * ORB, 128)),

time: 24.7 us -> 24.3 us (0.984)
  waiting for transfers between devices: 1.61 us -> 0.93 us
  Pallas kernels: 10.4 us -> 10.7 us
    ppermute x4, waiting for transfers between devices: 1.61 us -> 0.92 us  [to_mate(): return lax.ppermute(value, 'sx', mates)]
    pallas_call x2, Pallas kernels: 1.1 us -> 1.66 us  [the longest x1 0.85 us: per_device(): pl.pallas_call(around_kernel, out_shape=(shape(ROWS, PLANE), shape(3, 8 *...]
  transfers between devices with their start and end apart: 5 -> 5, of which waited for: 2 -> 2; matrix products, arithmetic and copies ran while one was open for 0% -> 0% of each run, Pallas kernels for 21% -> 24%
where the time goes in v13:
time: 24.3 us; the launch traced here: 24.2 us
  Pallas kernels  10.7 us (44%)
  blocking collectives  6.46 us (27%)
  starting transfers between devices  6.01 us (25%)
  waiting for transfers between devices  0.93 us (4%)
    all_gather x1, blocking collectives, gathered(): return lax.all_gather(value, ('grp', 'sx'), axis_index_groups=pairs)  6.46 us
    ppermute x4, starting transfers between devices, to_mate(): return lax.ppermute(value, 'sx', mates)  5.35 us
    pallas_call x1, Pallas kernels, per_device(): pl.pallas_call(smooth_kernel, out_shape=(pltpu.HBM((ROWS, CX * PLANE), BF...  2.24 us
    pallas_call x1, Pallas kernels, per_device(): pl.pallas_call(energy_kernel, out_shape=(pair, pair, pair, shape(2, ROWS,...  2.01 us
    pallas_call x1, Pallas kernels, per_device(): pl.pallas_call(edges_kernel, out_shape=(pair, pair, shape(5 * ORB, 16), s...  1.54 us
    pallas_call x1, Pallas kernels, per_device(): pl.pallas_call(finish_kernel, out_shape=pltpu.HBM((ROWS, CX * PLANE), BF1...  1.03 us
    ppermute x4, waiting for transfers between devices, to_mate(): return lax.ppermute(value, 'sx', mates)  0.92 us
    pallas_call x1, Pallas kernels, per_device(): pl.pallas_call(around_kernel, out_shape=(shape(ROWS, PLANE), shape(3, 8 *...  0.85 us
  transfers between devices with their start and end apart: 5, of which 2 were waited for; matrix products, arithmetic and copies ran while one was open for 0% of the time, Pallas kernels for 24%

profile of v13, /device:TPU:0, one launch (start us, length us, event | category | flops | bytes accessed | tf_op | source)
XLA Modules:
  0.0 24.2 jit_solution(5342060633683507127)
XLA Ops:
  0.0 0.0 copy-start
  0.0 1.5 %edges.1 = (bf16[2,192,1024]{2,1,0:T(8,128)(2,1)S(1)}, bf16[2,192,1024]{2,1,0:T(8,128)(2,1)S(1)}, bf16[320,16]{1,0:T(8,128)(2,1)S(1)}, f32[192,1024]{1,0:T(8,128)S(1)}, bf16[128,128]{1,0:T(8,128)(2,1)S(1)}) custom-call(s32[4,1024]{1,0:T(4,128)} %bitcast.4, bf16[192,4096]{1,0:T(8,128)(2,1)} %pieces_ref.3), custom_call_target="tpu_custom_call" | custom-call | flops 100000000 | bytes 1000000 | tf_op jit(solution)/shard_map/edges/pallas_call | solution.py:661
  1.6 0.5 %collective-permute-start = (bf16[128,128]{1,0:T(8,128)(2,1)S(1)}, bf16[128,128]{1,0:T(8,128)(2,1)S(1)}, u32[]{:S(2)}, u32[]{:S(2)}) collective-permute-start(bf16[128,128]{1,0:T(8,128)(2,1)S(1)} %get-tuple-element.39), channel_id=1, source_target_pairs={{0,1},{1,0},{2,3},{3,2},{4,5},{5,4},{6,7},{7,6},{8,9},{9,8},{10,11... | collective-permute-start | bytes 98312 | tf_op jit(solution)/shard_map/ppermute | solution.py:649
  2.1 0.0 copy-done
  2.1 0.0 copy-done.1
  2.1 2.0 %energy.1 = (bf16[2,192,1024]{2,1,0:T(8,128)(2,1)S(1)}, bf16[2,192,1024]{2,1,0:T(8,128)(2,1)S(1)}, bf16[2,192,1024]{2,1,0:T(8,128)(2,1)S(1)}, f32[2,192,1024]{2,...) custom-call(bf16[320,16]{1,0:T(8,128)(2,1)S(1)} %get-tuple-element.36.rows_ref, ...), custom_call_target="tpu_custom_call" | custom-call | flops 4000000000 | bytes 10000000 | tf_op jit(solution)/shard_map/energy/pallas_call | solution.py:679
  4.1 0.0 collective-permute-done.mate_ref
  4.1 0.6 %bands.1 = (bf16[2,192,1024]{2,1,0:T(8,128)(2,1)S(1)}, f32[2,192,256]{2,1,0:T(8,128)S(1)}, bf16[3,128,128]{2,1,0:T(8,128)(2,1)S(1)}) custom-call(bf16[128,128]{1,0:T(8,128)(2,1)S(1)} %collective-permute-done.mate_ref, f32[2,192,1024]{2,1,0:T(8,128)S(1)} %get-tuple-element.42.part_ref, ...), custom_call_target="tpu_custom_call", output_to_operand_aliasing={{0}: (6, {})} | custom-call | flops 1000000000 | bytes 10000000 | tf_op jit(solution)/shard_map/bands/pallas_call | solution.py:692
  4.8 0.1 collective-permute-start.1
  4.9 0.9 %around.1 = (bf16[192,1024]{1,0:T(8,128)(2,1)S(1)}, f32[3,512]{1,0:T(4,128)S(1)}, bf16[144,128]{1,0:T(8,128)(2,1)S(1)}) custom-call(s32[2,16]{1,0:T(2,128)} %bitcast.5, bf16[320,16]{1,0:T(8,128)(2,1)S(1)} %get-tuple-element.36.rows_ref, bf16[2,192,1024]{2,1,0:T(8,128)(2,1)S(1)} %get-tuple-element.37.phi_ref.edge_ref), custom_call_target="tpu_custom_call" | custom-call | flops 100000000 | bytes 1000000 | tf_op jit(solution)/shard_map/around/pallas_call | solution.py:703
  5.7 0.4 %collective-permute-done.1.rows_ref = bf16[3,128,128]{2,1,0:T(8,128)(2,1)S(1)} collective-permute-done((bf16[3,128,128]{2,1,0:T(8,128)(2,1)S(1)}, bf16[3,128,128]{2,1,0:T(8,128)(2,1)S(1)}, u32[]{:S(2)}, u32[]{:S(2)}) %collective-permute-start.1) | collective-permute-done | bytes 98336 | tf_op jit(solution)/shard_map/ppermute | solution.py:649
  6.1 0.2 relay.1
  6.3 6.5 %all-gather = bf16[1184,128]{1,0:T(8,128)(2,1)S(1)} all-gather(bf16[592,128]{1,0:T(8,128)(2,1)S(1)} %relay.1), channel_id=2, replica_groups={{1,2},{3,4},{5,6},{7,8},{9,10},{11,12},{13,14},{17,18},{19,20},{21,22},..., dimensions={0}, use_global_device_ids=true | all-gather | bytes 454656 | tf_op jit(solution)/shard_map/all_gather | solution.py:655
  12.8 0.8 %face.1 = (bf16[128,1024]{1,0:T(8,128)(2,1)S(1)}, bf16[7,64,128]{2,1,0:T(8,128)(2,1)S(1)}, f32[192,512]{1,0:T(8,128)S(1)}, bf16[4,64,128]{2,1,0:T(8,128)(2,1)S(1)}) custom-call(bf16[2,592,128]{2,1,0:T(8,128)(2,1)S(1)} %bitcast.3, bf16[192,1024]{1,0:T(8,128)(2,1)S(1)} %get-tuple-element.49.around_ref, ...), custom_call_target="tpu_custom_call" | custom-call | flops 100000000 | bytes 1000000 | tf_op jit(solution)/shard_map/face/pallas_call | solution.py:722
  13.6 0.2 collective-permute-start.2
  13.8 0.6 %theta.1 = (bf16[2,192,256]{2,1,0:T(8,128)(2,1)S(1)}, f32[192,192]{1,0:T(8,128)S(1)}, bf16[2,192,1024]{2,1,0:T(8,128)(2,1)S(1)}) custom-call(f32[3,512]{1,0:T(4,128)S(1)} %get-tuple-element.38.keep_ref, f32[2,192,256]{2,1,0:T(8,128)S(1)} %get-tuple-element.46.own_ref, ...), custom_call_target="tpu_custom_call", output_to_operand_aliasing={{2}: (8, {})} | custom-call | flops 1000000000 | bytes 4000000 | tf_op jit(solution)/shard_map/theta/pallas_call | solution.py:740
  14.4 0.5 %collective-permute-done.2.relayed_ref = bf16[4,64,128]{2,1,0:T(8,128)(2,1)S(1)} collective-permute-done((bf16[4,64,128]{2,1,0:T(8,128)(2,1)S(1)}, bf16[4,64,128]{2,1,0:T(8,128)(2,1)S(1)}, u32[]{:S(2)}, u32[]{:S(2)}) %collective-permute-start.2) | collective-permute-done | bytes 65568 | tf_op jit(solution)/shard_map/ppermute | solution.py:649
  14.9 0.7 %gradient.1 = (bf16[2,192,1024]{2,1,0:T(8,128)(2,1)S(1)}, bf16[192,192]{1,0:T(8,128)(2,1)S(1)}, bf16[128,128]{1,0:T(8,128)(2,1)S(1)}, bf16[128,128]{1,0:T(8,128)(2,1)S(1)}) custom-call(f32[3,512]{1,0:T(4,128)S(1)} %get-tuple-element.38.keep_ref, bf16[4,64,128]{2,1,0:T(8,128)(2,1)S(1)} %collective-permute-done.2.relayed_ref, ...), custom_call_target="tpu_custom_call" | custom-call | flops 1000000000 | bytes 10000000 | tf_op jit(solution)/shard_map/gradient/pallas_call | solution.py:751
  15.7 0.7 %collective-permute-start.3 = (bf16[128,128]{1,0:T(8,128)(2,1)S(1)}, bf16[128,128]{1,0:T(8,128)(2,1)S(1)}, u32[]{:S(2)}, u32[]{:S(2)}) collective-permute-start(bf16[128,128]{1,0:T(8,128)(2,1)S(1)} %get-tuple-element.58), channel_id=1, source_target_pairs={{1,2},{2,1},{3,4},{4,3},{5,6},{6,5},{7,8},{8,7},{9,10},{10,9},{11,... | collective-permute-start | bytes 98312 | tf_op jit(solution)/shard_map/ppermute | solution.py:652
  16.3 4.5 %collective-permute-start.4 = (bf16[128,128]{1,0:T(8,128)(2,1)S(1)}, bf16[128,128]{1,0:T(8,128)(2,1)S(1)}, u32[]{:S(2)}, u32[]{:S(2)}) collective-permute-start(bf16[128,128]{1,0:T(8,128)(2,1)S(1)} %get-tuple-element.59), channel_id=1, source_target_pairs={{0,1},{1,0},{2,3},{3,2},{4,5},{5,4},{6,7},{7,6},{8,9},{9,8},{10,11... | collective-permute-start | bytes 98312 | tf_op jit(solution)/shard_map/ppermute | solution.py:649
  20.9 2.2 %smooth.1 = (bf16[192,4096]{1,0:T(8,128)(2,1)}, f32[2,192,1024]{2,1,0:T(8,128)S(1)}) custom-call(bf16[192,192]{1,0:T(8,128)(2,1)S(1)} %get-tuple-element.60.theta_ref, bf16[2,192,1024]{2,1,0:T(8,128)(2,1)S(1)} %get-tuple-element.61.phi_ref, bf16[2,192,1024]{2,1,0:T(8,128)(2,1)S(1)} %get-tuple-element.62.energy_ref, ...), custom_call_target="tpu_custom_call" | custom-call | flops 2000000000 | bytes 10000000 | tf_op jit(solution)/shard_map/smooth/pallas_call | solution.py:764
  23.1 0.0 collective-permute-done.3.across_ref
  23.1 0.0 collective-permute-done.4.mate_ref
  23.1 1.0 %finish.1 = bf16[192,4096]{1,0:T(8,128)(2,1)} custom-call(bf16[128,128]{1,0:T(8,128)(2,1)S(1)} %collective-permute-done.3.across_ref, bf16[128,128]{1,0:T(8,128)(2,1)S(1)} %collective-permute-done.4.mate_ref, f32[2,192,1024]{2,1,0:T(8,128)S(1)} %get-tuple-element.65.part_ref, ...), custom_call_target="tpu_custom_call", output_to_operand_aliasing={{}: (4, {})} | custom-call | flops 10000000 | bytes 10000000 | tf_op jit(solution)/shard_map/finish/pallas_call | solution.py:780
  (1 shorter events, 0.0 us)
Async XLA Ops:
  0.0 2.1 %copy-start = (bf16[192,4096]{1,0:T(8,128)(2,1)S(1)}, bf16[192,4096]{1,0:T(8,128)(2,1)}, u32[]{:S(2)}) copy-start(bf16[192,4096]{1,0:T(8,128)(2,1)} %pieces_ref.3) | copy-start | bytes 4718596
  0.0 2.1 %copy-start.1 = (f32[4,1024]{1,0:T(4,128)S(1)}, f32[4,1024]{1,0:T(4,128)}, u32[]{:S(2)}) copy-start(f32[4,1024]{1,0:T(4,128)} %pot_ref.1) | copy-start | bytes 49156
  1.6 2.5 %collective-permute-start = (bf16[128,128]{1,0:T(8,128)(2,1)S(1)}, bf16[128,128]{1,0:T(8,128)(2,1)S(1)}, u32[]{:S(2)}, u32[]{:S(2)}) collective-permute-start(bf16[128,128]{1,0:T(8,128)(2,1)S(1)} %get-tuple-element.39), channel_id=1, source_target_pairs={{0,1},{1,0},{2,3},{3,2},{4,5},{5,4},{6,7},{7,6},{8,9},{9,8},{10,11... | collective-permute-start | bytes 98312 | tf_op jit(solution)/shard_map/ppermute | solution.py:649
  4.8 1.4 %collective-permute-start.1 = (bf16[3,128,128]{2,1,0:T(8,128)(2,1)S(1)}, bf16[3,128,128]{2,1,0:T(8,128)(2,1)S(1)}, u32[]{:S(2)}, u32[]{:S(2)}) collective-permute-start(bf16[3,128,128]{2,1,0:T(8,128)(2,1)S(1)} %get-tuple-element.47), channel_id=1, source_target_pairs={{0,1},{1,0},{2,3},{3,2},{4,5},{5,4},{6,7},{7,6},{8,9},{9,8},{10,11... | collective-permute-start | bytes 294920 | tf_op jit(solution)/shard_map/ppermute | solution.py:649
  13.6 1.3 %collective-permute-start.2 = (bf16[4,64,128]{2,1,0:T(8,128)(2,1)S(1)}, bf16[4,64,128]{2,1,0:T(8,128)(2,1)S(1)}, u32[]{:S(2)}, u32[]{:S(2)}) collective-permute-start(bf16[4,64,128]{2,1,0:T(8,128)(2,1)S(1)} %get-tuple-element.50), channel_id=1, source_target_pairs={{0,1},{1,0},{2,3},{3,2},{4,5},{5,4},{6,7},{7,6},{8,9},{9,8},{10,11... | collective-permute-start | bytes 196616 | tf_op jit(solution)/shard_map/ppermute | solution.py:649
  15.7 7.5 %collective-permute-start.3 = (bf16[128,128]{1,0:T(8,128)(2,1)S(1)}, bf16[128,128]{1,0:T(8,128)(2,1)S(1)}, u32[]{:S(2)}, u32[]{:S(2)}) collective-permute-start(bf16[128,128]{1,0:T(8,128)(2,1)S(1)} %get-tuple-element.58), channel_id=1, source_target_pairs={{1,2},{2,1},{3,4},{4,3},{5,6},{6,5},{7,8},{8,7},{9,10},{10,9},{11,... | collective-permute-start | bytes 98312 | tf_op jit(solution)/shard_map/ppermute | solution.py:652
  16.3 6.8 %collective-permute-start.4 = (bf16[128,128]{1,0:T(8,128)(2,1)S(1)}, bf16[128,128]{1,0:T(8,128)(2,1)S(1)}, u32[]{:S(2)}, u32[]{:S(2)}) collective-permute-start(bf16[128,128]{1,0:T(8,128)(2,1)S(1)} %get-tuple-element.59), channel_id=1, source_target_pairs={{0,1},{1,0},{2,3},{3,2},{4,5},{5,4},{6,7},{7,6},{8,9},{9,8},{10,11... | collective-permute-start | bytes 98312 | tf_op jit(solution)/shard_map/ppermute | solution.py:649

commit v14 on v13

--- a/solution.py
+++ b/solution.py
@@ -221,15 +221,19 @@
     window_ref, raw_ref, sems,
 ):
     first = window_start(table_ref.shape[1])
-    table_copy = pltpu.make_async_copy(table_ref.at[:, pl.ds(first, WINDOW)], window_ref, sems.at[2])
+    table_copy = pltpu.make_async_copy(table_ref.at[:, pl.ds(first, WINDOW)], window_ref, sems.at[6])
     table_copy.start()
     copies = []
     for i in range(2):
         start = (CX - 1) * PLANE * i
-        copies.append(
-            pltpu.make_async_copy(pieces_ref.at[:, start : start + PLANE], raw_ref.at[i], sems.at[i])
-        )
-        copies[i].start()
+        for j in range(3):
+            rows = slice(ORB * j, ORB * j + ORB)
+            copies.append(
+                pltpu.make_async_copy(
+                    pieces_ref.at[rows, start : start + PLANE], raw_ref.at[i, rows], sems.at[3 * i + j]
+                )
+            )
+            copies[-1].start()
     cells = cell_features()
     table_copy.wait()
     blocks = row_features(window_ref, first)
@@ -240,7 +244,8 @@
     for i in range(2):
         mask_ref[i] = sphere(reach, rows, (CX - 1) * i)
     for i in range(2):
-        copies[i].wait()
+        for j in range(3):
+            copies[3 * i + j].wait()
         phi_ref[i] = raw_ref[i] * mask_ref[i]
     even = is_even()
     own = slice(ORB, 2 * ORB)
@@ -303,12 +308,13 @@
 ):
     volume = 1.0 / (4.0 * CX**3)
     gram = []
-    mate = mate_ref[...].astype(F32)
-    for i, side in enumerate(sides(mate, jnp.zeros_like(mate))):
-        tiles = side_by_side(unfold(side), i)
+    unfolded = unfold(mate_ref[...].astype(F32))
+    for i in range(2):
+        factor = jnp.where(is_even() == (i == 1), 0.5, 0.0)
+        tiles = side_by_side(unfolded, i)
         for t in range(PLANE // 128):
             lanes = slice(128 * t, 128 * t + 128)
-            value = part_ref[i, halo_rows(i), lanes] - 0.5 * tiles[t]
+            value = part_ref[i, halo_rows(i), lanes] - factor * tiles[t]
             energy_ref[i, halo_rows(i), lanes] = value.astype(BF16) * mask_ref[i, halo_rows(i), lanes]
         gram.append(rows_product(energy_ref[i, halo_rows(i)], phi_ref[i]))
     own_ref[:, :, ROWS:] = jnp.zeros((2, ROWS, TILE - ROWS), F32)
@@ -668,7 +674,7 @@
         scratch_shapes=[
             pltpu.VMEM((4, WINDOW), jnp.int32),
             pltpu.VMEM((2, ROWS, PLANE), BF16),
-            pltpu.SemaphoreType.DMA((3,)),
+            pltpu.SemaphoreType.DMA((7,)),
         ],
         compiler_params=PARAMS,
         cost_estimate=cost(10**8, 10**6),

time: 24.3 us -> 24.3 us (level)
  no operation moved by 1% of the time
where the time goes in v14:
time: 24.3 us; the launch traced here: 24.2 us
  Pallas kernels  10.7 us (44%)
  blocking collectives  6.46 us (27%)
  starting transfers between devices  6.03 us (25%)
  waiting for transfers between devices  0.91 us (4%)
    all_gather x1, blocking collectives, gathered(): return lax.all_gather(value, ('grp', 'sx'), axis_index_groups=pairs)  6.46 us
    ppermute x4, starting transfers between devices, to_mate(): return lax.ppermute(value, 'sx', mates)  5.37 us
    pallas_call x1, Pallas kernels, per_device(): pl.pallas_call(smooth_kernel, out_shape=(pltpu.HBM((ROWS, CX * PLANE), BF...  2.23 us
    pallas_call x1, Pallas kernels, per_device(): pl.pallas_call(energy_kernel, out_shape=(pair, pair, pair, shape(2, ROWS,...  2.01 us
    pallas_call x1, Pallas kernels, per_device(): pl.pallas_call(edges_kernel, out_shape=(pair, pair, shape(5 * ORB, 16), s...  1.6 us
    pallas_call x1, Pallas kernels, per_device(): pl.pallas_call(finish_kernel, out_shape=pltpu.HBM((ROWS, CX * PLANE), BF1...  1.03 us
    ppermute x4, waiting for transfers between devices, to_mate(): return lax.ppermute(value, 'sx', mates)  0.91 us
    pallas_call x1, Pallas kernels, per_device(): pl.pallas_call(around_kernel, out_shape=(shape(ROWS, PLANE), shape(3, 8 *...  0.85 us
  transfers between devices with their start and end apart: 5, of which 2 were waited for; matrix products, arithmetic and copies ran while one was open for 0% of the time, Pallas kernels for 24%

profile of v14, /device:TPU:0, one launch (start us, length us, event | category | flops | bytes accessed | tf_op | source)
XLA Modules:
  0.0 24.2 jit_solution(18404877911903705852)
XLA Ops:
  0.0 0.0 copy-start
  0.0 1.6 %edges.1 = (bf16[2,192,1024]{2,1,0:T(8,128)(2,1)S(1)}, bf16[2,192,1024]{2,1,0:T(8,128)(2,1)S(1)}, bf16[320,16]{1,0:T(8,128)(2,1)S(1)}, f32[192,1024]{1,0:T(8,128)S(1)}, bf16[128,128]{1,0:T(8,128)(2,1)S(1)}) custom-call(s32[4,1024]{1,0:T(4,128)} %bitcast.4, bf16[192,4096]{1,0:T(8,128)(2,1)} %pieces_ref.3), custom_call_target="tpu_custom_call" | custom-call | flops 100000000 | bytes 1000000 | tf_op jit(solution)/shard_map/edges/pallas_call | solution.py:667
  1.6 0.5 %collective-permute-start = (bf16[128,128]{1,0:T(8,128)(2,1)S(1)}, bf16[128,128]{1,0:T(8,128)(2,1)S(1)}, u32[]{:S(2)}, u32[]{:S(2)}) collective-permute-start(bf16[128,128]{1,0:T(8,128)(2,1)S(1)} %get-tuple-element.39), channel_id=1, source_target_pairs={{0,1},{1,0},{2,3},{3,2},{4,5},{5,4},{6,7},{7,6},{8,9},{9,8},{10,11... | collective-permute-start | bytes 98312 | tf_op jit(solution)/shard_map/ppermute | solution.py:655
  2.1 0.0 copy-done
  2.1 0.0 copy-done.1
  2.1 2.0 %energy.1 = (bf16[2,192,1024]{2,1,0:T(8,128)(2,1)S(1)}, bf16[2,192,1024]{2,1,0:T(8,128)(2,1)S(1)}, bf16[2,192,1024]{2,1,0:T(8,128)(2,1)S(1)}, f32[2,192,1024]{2,...) custom-call(bf16[320,16]{1,0:T(8,128)(2,1)S(1)} %get-tuple-element.36.rows_ref, ...), custom_call_target="tpu_custom_call" | custom-call | flops 4000000000 | bytes 10000000 | tf_op jit(solution)/shard_map/energy/pallas_call | solution.py:685
  4.2 0.0 collective-permute-done.mate_ref
  4.2 0.6 %bands.1 = (bf16[2,192,1024]{2,1,0:T(8,128)(2,1)S(1)}, f32[2,192,256]{2,1,0:T(8,128)S(1)}, bf16[3,128,128]{2,1,0:T(8,128)(2,1)S(1)}) custom-call(bf16[128,128]{1,0:T(8,128)(2,1)S(1)} %collective-permute-done.mate_ref, f32[2,192,1024]{2,1,0:T(8,128)S(1)} %get-tuple-element.42.part_ref, ...), custom_call_target="tpu_custom_call", output_to_operand_aliasing={{0}: (6, {})} | custom-call | flops 1000000000 | bytes 10000000 | tf_op jit(solution)/shard_map/bands/pallas_call | solution.py:698
  4.8 0.1 collective-permute-start.1
  4.9 0.8 %around.1 = (bf16[192,1024]{1,0:T(8,128)(2,1)S(1)}, f32[3,512]{1,0:T(4,128)S(1)}, bf16[144,128]{1,0:T(8,128)(2,1)S(1)}) custom-call(s32[2,16]{1,0:T(2,128)} %bitcast.5, bf16[320,16]{1,0:T(8,128)(2,1)S(1)} %get-tuple-element.36.rows_ref, bf16[2,192,1024]{2,1,0:T(8,128)(2,1)S(1)} %get-tuple-element.37.phi_ref.edge_ref), custom_call_target="tpu_custom_call" | custom-call | flops 100000000 | bytes 1000000 | tf_op jit(solution)/shard_map/around/pallas_call | solution.py:709
  5.8 0.4 %collective-permute-done.1.rows_ref = bf16[3,128,128]{2,1,0:T(8,128)(2,1)S(1)} collective-permute-done((bf16[3,128,128]{2,1,0:T(8,128)(2,1)S(1)}, bf16[3,128,128]{2,1,0:T(8,128)(2,1)S(1)}, u32[]{:S(2)}, u32[]{:S(2)}) %collective-permute-start.1) | collective-permute-done | bytes 98336 | tf_op jit(solution)/shard_map/ppermute | solution.py:655
  6.1 0.2 relay.1
  6.3 6.5 %all-gather = bf16[1184,128]{1,0:T(8,128)(2,1)S(1)} all-gather(bf16[592,128]{1,0:T(8,128)(2,1)S(1)} %relay.1), channel_id=2, replica_groups={{1,2},{3,4},{5,6},{7,8},{9,10},{11,12},{13,14},{17,18},{19,20},{21,22},..., dimensions={0}, use_global_device_ids=true | all-gather | bytes 454656 | tf_op jit(solution)/shard_map/all_gather | solution.py:661
  12.8 0.8 %face.1 = (bf16[128,1024]{1,0:T(8,128)(2,1)S(1)}, bf16[7,64,128]{2,1,0:T(8,128)(2,1)S(1)}, f32[192,512]{1,0:T(8,128)S(1)}, bf16[4,64,128]{2,1,0:T(8,128)(2,1)S(1)}) custom-call(bf16[2,592,128]{2,1,0:T(8,128)(2,1)S(1)} %bitcast.3, bf16[192,1024]{1,0:T(8,128)(2,1)S(1)} %get-tuple-element.49.around_ref, ...), custom_call_target="tpu_custom_call" | custom-call | flops 100000000 | bytes 1000000 | tf_op jit(solution)/shard_map/face/pallas_call | solution.py:728
  13.6 0.2 collective-permute-start.2
  13.8 0.6 %theta.1 = (bf16[2,192,256]{2,1,0:T(8,128)(2,1)S(1)}, f32[192,192]{1,0:T(8,128)S(1)}, bf16[2,192,1024]{2,1,0:T(8,128)(2,1)S(1)}) custom-call(f32[3,512]{1,0:T(4,128)S(1)} %get-tuple-element.38.keep_ref, f32[2,192,256]{2,1,0:T(8,128)S(1)} %get-tuple-element.46.own_ref, ...), custom_call_target="tpu_custom_call", output_to_operand_aliasing={{2}: (8, {})} | custom-call | flops 1000000000 | bytes 4000000 | tf_op jit(solution)/shard_map/theta/pallas_call | solution.py:746
  14.4 0.5 %collective-permute-done.2.relayed_ref = bf16[4,64,128]{2,1,0:T(8,128)(2,1)S(1)} collective-permute-done((bf16[4,64,128]{2,1,0:T(8,128)(2,1)S(1)}, bf16[4,64,128]{2,1,0:T(8,128)(2,1)S(1)}, u32[]{:S(2)}, u32[]{:S(2)}) %collective-permute-start.2) | collective-permute-done | bytes 65568 | tf_op jit(solution)/shard_map/ppermute | solution.py:655
  14.9 0.7 %gradient.1 = (bf16[2,192,1024]{2,1,0:T(8,128)(2,1)S(1)}, bf16[192,192]{1,0:T(8,128)(2,1)S(1)}, bf16[128,128]{1,0:T(8,128)(2,1)S(1)}, bf16[128,128]{1,0:T(8,128)(2,1)S(1)}) custom-call(f32[3,512]{1,0:T(4,128)S(1)} %get-tuple-element.38.keep_ref, bf16[4,64,128]{2,1,0:T(8,128)(2,1)S(1)} %collective-permute-done.2.relayed_ref, ...), custom_call_target="tpu_custom_call" | custom-call | flops 1000000000 | bytes 10000000 | tf_op jit(solution)/shard_map/gradient/pallas_call | solution.py:757
  15.7 0.7 %collective-permute-start.3 = (bf16[128,128]{1,0:T(8,128)(2,1)S(1)}, bf16[128,128]{1,0:T(8,128)(2,1)S(1)}, u32[]{:S(2)}, u32[]{:S(2)}) collective-permute-start(bf16[128,128]{1,0:T(8,128)(2,1)S(1)} %get-tuple-element.58), channel_id=1, source_target_pairs={{1,2},{2,1},{3,4},{4,3},{5,6},{6,5},{7,8},{8,7},{9,10},{10,9},{11,... | collective-permute-start | bytes 98312 | tf_op jit(solution)/shard_map/ppermute | solution.py:658
  16.3 4.5 %collective-permute-start.4 = (bf16[128,128]{1,0:T(8,128)(2,1)S(1)}, bf16[128,128]{1,0:T(8,128)(2,1)S(1)}, u32[]{:S(2)}, u32[]{:S(2)}) collective-permute-start(bf16[128,128]{1,0:T(8,128)(2,1)S(1)} %get-tuple-element.59), channel_id=1, source_target_pairs={{0,1},{1,0},{2,3},{3,2},{4,5},{5,4},{6,7},{7,6},{8,9},{9,8},{10,11... | collective-permute-start | bytes 98312 | tf_op jit(solution)/shard_map/ppermute | solution.py:655
  20.9 2.2 %smooth.1 = (bf16[192,4096]{1,0:T(8,128)(2,1)}, f32[2,192,1024]{2,1,0:T(8,128)S(1)}) custom-call(bf16[192,192]{1,0:T(8,128)(2,1)S(1)} %get-tuple-element.60.theta_ref, bf16[2,192,1024]{2,1,0:T(8,128)(2,1)S(1)} %get-tuple-element.61.phi_ref, bf16[2,192,1024]{2,1,0:T(8,128)(2,1)S(1)} %get-tuple-element.62.energy_ref, ...), custom_call_target="tpu_custom_call" | custom-call | flops 2000000000 | bytes 10000000 | tf_op jit(solution)/shard_map/smooth/pallas_call | solution.py:770
  23.1 0.0 collective-permute-done.3.across_ref
  23.1 0.0 collective-permute-done.4.mate_ref
  23.1 1.0 %finish.1 = bf16[192,4096]{1,0:T(8,128)(2,1)} custom-call(bf16[128,128]{1,0:T(8,128)(2,1)S(1)} %collective-permute-done.3.across_ref, bf16[128,128]{1,0:T(8,128)(2,1)S(1)} %collective-permute-done.4.mate_ref, f32[2,192,1024]{2,1,0:T(8,128)S(1)} %get-tuple-element.65.part_ref, ...), custom_call_target="tpu_custom_call", output_to_operand_aliasing={{}: (4, {})} | custom-call | flops 10000000 | bytes 10000000 | tf_op jit(solution)/shard_map/finish/pallas_call | solution.py:786
  (1 shorter events, 0.0 us)
Async XLA Ops:
  0.0 2.1 %copy-start = (bf16[192,4096]{1,0:T(8,128)(2,1)S(1)}, bf16[192,4096]{1,0:T(8,128)(2,1)}, u32[]{:S(2)}) copy-start(bf16[192,4096]{1,0:T(8,128)(2,1)} %pieces_ref.3) | copy-start | bytes 4718596
  0.0 2.1 %copy-start.1 = (f32[4,1024]{1,0:T(4,128)S(1)}, f32[4,1024]{1,0:T(4,128)}, u32[]{:S(2)}) copy-start(f32[4,1024]{1,0:T(4,128)} %pot_ref.1) | copy-start | bytes 49156
  1.6 2.5 %collective-permute-start = (bf16[128,128]{1,0:T(8,128)(2,1)S(1)}, bf16[128,128]{1,0:T(8,128)(2,1)S(1)}, u32[]{:S(2)}, u32[]{:S(2)}) collective-permute-start(bf16[128,128]{1,0:T(8,128)(2,1)S(1)} %get-tuple-element.39), channel_id=1, source_target_pairs={{0,1},{1,0},{2,3},{3,2},{4,5},{5,4},{6,7},{7,6},{8,9},{9,8},{10,11... | collective-permute-start | bytes 98312 | tf_op jit(solution)/shard_map/ppermute | solution.py:655
  4.8 1.4 %collective-permute-start.1 = (bf16[3,128,128]{2,1,0:T(8,128)(2,1)S(1)}, bf16[3,128,128]{2,1,0:T(8,128)(2,1)S(1)}, u32[]{:S(2)}, u32[]{:S(2)}) collective-permute-start(bf16[3,128,128]{2,1,0:T(8,128)(2,1)S(1)} %get-tuple-element.47), channel_id=1, source_target_pairs={{0,1},{1,0},{2,3},{3,2},{4,5},{5,4},{6,7},{7,6},{8,9},{9,8},{10,11... | collective-permute-start | bytes 294920 | tf_op jit(solution)/shard_map/ppermute | solution.py:655
  13.6 1.3 %collective-permute-start.2 = (bf16[4,64,128]{2,1,0:T(8,128)(2,1)S(1)}, bf16[4,64,128]{2,1,0:T(8,128)(2,1)S(1)}, u32[]{:S(2)}, u32[]{:S(2)}) collective-permute-start(bf16[4,64,128]{2,1,0:T(8,128)(2,1)S(1)} %get-tuple-element.50), channel_id=1, source_target_pairs={{0,1},{1,0},{2,3},{3,2},{4,5},{5,4},{6,7},{7,6},{8,9},{9,8},{10,11... | collective-permute-start | bytes 196616 | tf_op jit(solution)/shard_map/ppermute | solution.py:655
  15.7 7.5 %collective-permute-start.3 = (bf16[128,128]{1,0:T(8,128)(2,1)S(1)}, bf16[128,128]{1,0:T(8,128)(2,1)S(1)}, u32[]{:S(2)}, u32[]{:S(2)}) collective-permute-start(bf16[128,128]{1,0:T(8,128)(2,1)S(1)} %get-tuple-element.58), channel_id=1, source_target_pairs={{1,2},{2,1},{3,4},{4,3},{5,6},{6,5},{7,8},{8,7},{9,10},{10,9},{11,... | collective-permute-start | bytes 98312 | tf_op jit(solution)/shard_map/ppermute | solution.py:658
  16.3 6.8 %collective-permute-start.4 = (bf16[128,128]{1,0:T(8,128)(2,1)S(1)}, bf16[128,128]{1,0:T(8,128)(2,1)S(1)}, u32[]{:S(2)}, u32[]{:S(2)}) collective-permute-start(bf16[128,128]{1,0:T(8,128)(2,1)S(1)} %get-tuple-element.59), channel_id=1, source_target_pairs={{0,1},{1,0},{2,3},{3,2},{4,5},{5,4},{6,7},{7,6},{8,9},{9,8},{10,11... | collective-permute-start | bytes 98312 | tf_op jit(solution)/shard_map/ppermute | solution.py:655

commit v15 on v13

--- a/solution.py
+++ b/solution.py
@@ -217,7 +217,7 @@
 
 def edges_kernel(
     table_ref, pieces_ref,
-    phi_ref, mask_ref, rows_ref, reach_ref, mate_ref,
+    phi_ref, mask_ref, rows_ref, mid_mask_ref, mate_ref,
     window_ref, raw_ref, sems,
 ):
     first = window_start(table_ref.shape[1])
@@ -236,9 +236,9 @@
     rows_ref[...] = blocks
     rows = blocks[ORB : 4 * ORB]
     reach = jnp.dot(rows, cells, preferred_element_type=F32)
-    reach_ref[...] = reach
     for i in range(2):
         mask_ref[i] = sphere(reach, rows, (CX - 1) * i)
+        mid_mask_ref[i] = sphere(reach, rows, 1 + i)
     for i in range(2):
         copies[i].wait()
         phi_ref[i] = raw_ref[i] * mask_ref[i]
@@ -253,14 +253,11 @@
 
 
 def energy_kernel(
-    rows_ref, reach_ref, pieces_ref, pot_ref, edge_ref, edge_mask_ref,
-    phi_ref, mask_ref, energy_ref, part_ref, edge_energy_ref, corr_ref, ham_ref,
+    mask_ref, pieces_ref, pot_ref, edge_ref, edge_mask_ref,
+    phi_ref, energy_ref, part_ref, edge_energy_ref, corr_ref, ham_ref,
 ):
-    rows = rows_ref[ORB : 4 * ORB]
     for i in range(2):
-        mask = sphere(reach_ref[...], rows, 1 + i)
-        mask_ref[i] = mask
-        phi_ref[i] = pieces_ref[:, PLANE * (1 + i) : PLANE * (2 + i)] * mask
+        phi_ref[i] = pieces_ref[:, PLANE * (1 + i) : PLANE * (2 + i)] * mask_ref[i]
     weights = in_plane(6, -1)
     for t in range(PLANE // TILE):
         lanes = slice(TILE * t, TILE * t + TILE)
@@ -303,12 +300,13 @@
 ):
     volume = 1.0 / (4.0 * CX**3)
     gram = []
-    mate = mate_ref[...].astype(F32)
-    for i, side in enumerate(sides(mate, jnp.zeros_like(mate))):
-        tiles = side_by_side(unfold(side), i)
+    unfolded = unfold(mate_ref[...].astype(F32))
+    for i in range(2):
+        factor = jnp.where(is_even() == (i == 1), 0.5, 0.0)
+        tiles = side_by_side(unfolded, i)
         for t in range(PLANE // 128):
             lanes = slice(128 * t, 128 * t + 128)
-            value = part_ref[i, halo_rows(i), lanes] - 0.5 * tiles[t]
+            value = part_ref[i, halo_rows(i), lanes] - factor * tiles[t]
             energy_ref[i, halo_rows(i), lanes] = value.astype(BF16) * mask_ref[i, halo_rows(i), lanes]
         gram.append(rows_product(energy_ref[i, halo_rows(i)], phi_ref[i]))
     own_ref[:, :, ROWS:] = jnp.zeros((2, ROWS, TILE - ROWS), F32)
@@ -392,8 +390,8 @@
 
 def face_kernel(
     both_ref, around_ref, phi_ref, mask_ref,
-    halo_ref, other_ref, extra_ref, forward_ref,
-    beyond_ref, back_ref, work_ref,
+    halo_ref, other_ref, work_ref, forward_ref,
+    beyond_ref, back_ref,
 ):
     even = is_even()
     low = low_half()
@@ -409,7 +407,6 @@
         other_ref[i] = tiles[i].astype(BF16)
     beside = unfold(got(7 * ORB, 2 * ORB))
     far_off = unfold_far(got(9 * ORB, ORB // 4)).astype(BF16)
-    extra_ref[...] = jnp.zeros((ROWS, 8 * ORB), F32)
     work_ref[:, :, ROWS:] = jnp.zeros((2, 2 * ORB, TILE - ROWS), F32)
     head, tail = shared_head(tiles[4], 1), tiles[6]
     forward_ref[2] = jnp.where(low, swapped(head), swapped(tail)).astype(BF16)
@@ -429,15 +426,7 @@
         work_ref[1, :, :ROWS] = rows_product(back_ref[...], beyond_ref[...]) * scale
         x, y = work_ref[0, :, 0:128], work_ref[0, :, 128:256]
         a, b = shifted(work_ref[1, :, 0:128], work_ref[1, :, 128:256])
-        if i == 0:
-            extra_ref[here, 0:128] = a
-            extra_ref[here, 128:256] = b + x
-            extra_ref[here, 256:384] = y
-            own = slice(ORB, 2 * ORB)
-        else:
-            extra_ref[here, 128:256] = a + x
-            extra_ref[here, 256:384] = b + y
-            own = slice(0, ORB)
+        own = slice(ORB, 2 * ORB) if i == 0 else slice(0, ORB)
         a = swapped(shared_head(tiles[4], 0) + a[own])
         b = swapped(tiles[5] + b[own])
         x, y = swapped(x[own]), swapped(y[own])
@@ -452,6 +441,19 @@
     pl.when(jnp.logical_not(even))(lambda: add_face(1))
 
 
+def add_terms(i, work_ref, extra_ref):
+    here = halo_rows(i)
+    x, y = work_ref[0, :, 0:128], work_ref[0, :, 128:256]
+    a, b = shifted(work_ref[1, :, 0:128], work_ref[1, :, 128:256])
+    if i == 0:
+        extra_ref[here, 0:128] = a
+        extra_ref[here, 128:256] = b + x
+        extra_ref[here, 256:384] = y
+    else:
+        extra_ref[here, 128:256] = a + x
+        extra_ref[here, 256:384] = b + y
+
+
 def add_halo(i, halo_ref, part_ref, mask_ref, energy_ref):
     here = halo_rows(i)
     value = part_ref[i, here] - 0.5 * halo_ref[...].astype(F32)
@@ -477,11 +479,14 @@
 
 
 def theta_kernel(
-    keep_ref, own_ref, rows_ref, other_ref, extra_ref, halo_ref, part_ref, edge_mask_ref, energy_in_ref,
+    keep_ref, own_ref, rows_ref, other_ref, work_ref, halo_ref, part_ref, edge_mask_ref, energy_in_ref,
     window_ref, theta_ref, energy_ref,
-    ham_ref, inv_ref,
+    ham_ref, inv_ref, extra_ref,
 ):
     even = is_even()
+    extra_ref[...] = jnp.zeros((ROWS, 8 * ORB), F32)
+    pl.when(even)(lambda: add_terms(0, work_ref, extra_ref))
+    pl.when(jnp.logical_not(even))(lambda: add_terms(1, work_ref, extra_ref))
     low = low_half()
     zero = jnp.zeros((ORB, 128), F32)
     for which, band_ref in enumerate((ham_ref, inv_ref)):
@@ -658,10 +663,10 @@
     patterns = pattern.T
     pair = shape(2, ROWS, PLANE)
 
-    edge, edge_mask, rows, reach, for_mate = pl.pallas_call(
+    edge, edge_mask, rows, mid_mask, for_mate = pl.pallas_call(
         edges_kernel,
         out_shape=(
-            pair, pair, shape(5 * ORB, 16), shape(ROWS, PLANE, dtype=F32), shape(2 * ORB, 128),
+            pair, pair, shape(5 * ORB, 16), pair, shape(2 * ORB, 128),
         ),
         in_specs=[FAR, FAR],
         out_specs=(WHOLE,) * 5,
@@ -676,18 +681,18 @@
     )(far(table), far(pieces))
     mate_side = to_mate(for_mate)
 
-    mid, mid_mask, mid_energy, part, rest_energy, corr, ham = pl.pallas_call(
+    mid, mid_energy, part, rest_energy, corr, ham = pl.pallas_call(
         energy_kernel,
         out_shape=(
-            pair, pair, pair, shape(2, ROWS, PLANE, dtype=F32), pair,
+            pair, pair, shape(2, ROWS, PLANE, dtype=F32), pair,
             shape(ROWS, ROWS, dtype=F32), shape(ROWS, ROWS, dtype=F32),
         ),
-        in_specs=[WHOLE] * 6,
-        out_specs=(WHOLE,) * 7,
+        in_specs=[WHOLE] * 5,
+        out_specs=(WHOLE,) * 6,
         compiler_params=PARAMS,
         cost_estimate=cost(4 * 10**9, 10**7),
         name="energy",
-    )(rows, reach, pieces, potential, edge, edge_mask)
+    )(mid_mask, pieces, potential, edge, edge_mask)
 
     edge_energy, own, for_mate = pl.pallas_call(
         bands_kernel,
@@ -719,17 +724,16 @@
         cost_estimate=cost(10**6, 10**6),
         name="relay",
     )(own, mate_rows, face)
-    halo, other_rows, extra, forward = pl.pallas_call(
+    halo, other_rows, face_terms, forward = pl.pallas_call(
         face_kernel,
         out_shape=(
-            shape(2 * ORB, PLANE), shape(7, ORB, 128), shape(ROWS, 8 * ORB, dtype=F32), shape(4, ORB, 128),
+            shape(2 * ORB, PLANE), shape(7, ORB, 128), shape(2, 2 * ORB, TILE, dtype=F32), shape(4, ORB, 128),
         ),
         in_specs=[WHOLE] * 4,
         out_specs=(WHOLE,) * 4,
         scratch_shapes=[
             pltpu.VMEM((ROWS, PLANE), BF16),
             pltpu.VMEM((2 * ORB, PLANE), BF16),
-            pltpu.VMEM((2, 2 * ORB, TILE), F32),
         ],
         compiler_params=PARAMS,
         cost_estimate=cost(10**8, 10**6),
@@ -742,12 +746,12 @@
         out_shape=(shape(2, ROWS, TILE), shape(ROWS, ROWS, dtype=F32), pair),
         in_specs=[WHOLE] * 9,
         out_specs=(WHOLE,) * 3,
-        scratch_shapes=[pltpu.VMEM((ROWS, 8 * ORB), F32), pltpu.VMEM((ROWS, 8 * ORB), F32)],
+        scratch_shapes=[pltpu.VMEM((ROWS, 8 * ORB), F32)] * 3,
         input_output_aliases={8: 2},
         compiler_params=PARAMS,
         cost_estimate=cost(10**9, 4 * 10**6),
         name="theta",
-    )(keep, own, mate_rows, other_rows, extra, halo, part, edge_mask, edge_energy)
+    )(keep, own, mate_rows, other_rows, face_terms, halo, part, edge_mask, edge_energy)
     edge_grad, theta, for_mate, for_other = pl.pallas_call(
         gradient_kernel,
         out_shape=(pair, shape(ROWS, ROWS), shape(2 * ORB, 128), shape(2 * ORB, 128)),

time: 24.3 us -> 24.4 us (level)
  no operation moved by 1% of the time
where the time goes in v15:
time: 24.4 us; the launch traced here: 24.2 us
  Pallas kernels  10.8 us (44%)
  blocking collectives  6.46 us (26%)
  starting transfers between devices  6.02 us (25%)
  waiting for transfers between devices  0.82 us (3%)
    all_gather x1, blocking collectives, gathered(): return lax.all_gather(value, ('grp', 'sx'), axis_index_groups=pairs)  6.46 us
    ppermute x4, starting transfers between devices, to_mate(): return lax.ppermute(value, 'sx', mates)  5.36 us
    pallas_call x1, Pallas kernels, per_device(): pl.pallas_call(smooth_kernel, out_shape=(pltpu.HBM((ROWS, CX * PLANE), BF...  2.25 us
    pallas_call x1, Pallas kernels, per_device(): pl.pallas_call(energy_kernel, out_shape=(pair, pair, shape(2, ROWS, PLANE...  1.93 us
    pallas_call x1, Pallas kernels, per_device(): pl.pallas_call(edges_kernel, out_shape=(pair, pair, shape(5 * ORB, 16), p...  1.67 us
    pallas_call x1, Pallas kernels, per_device(): pl.pallas_call(finish_kernel, out_shape=pltpu.HBM((ROWS, CX * PLANE), BF1...  1.03 us
    pallas_call x1, Pallas kernels, per_device(): pl.pallas_call(around_kernel, out_shape=(shape(ROWS, PLANE), shape(3, 8 *...  0.85 us
    ppermute x4, waiting for transfers between devices, to_mate(): return lax.ppermute(value, 'sx', mates)  0.82 us
  transfers between devices with their start and end apart: 5, of which 2 were waited for; matrix products, arithmetic and copies ran while one was open for 0% of the time, Pallas kernels for 24%

profile of v15, /device:TPU:0, one launch (start us, length us, event | category | flops | bytes accessed | tf_op | source)
XLA Modules:
  0.0 24.2 jit_solution(4753334257026567647)
XLA Ops:
  0.0 0.0 copy-start
  0.0 1.7 %edges.1 = (bf16[2,192,1024]{2,1,0:T(8,128)(2,1)S(1)}, bf16[2,192,1024]{2,1,0:T(8,128)(2,1)S(1)}, bf16[320,16]{1,0:T(8,128)(2,1)S(1)}, bf16[2,192,1024]{2,1,0:T(8,128)(2,1)S(1)}, bf16[128,128]{1,0:T(8,128)(2,1)S(1)}) custom-call(s32[4,1024]{1,0:T(4,128)} %bitcast.4, bf16[192,4096]{1,0:T(8,128)(2,1)} %pieces_ref.3), custom_call_target="tpu_custom_call" | custom-call | flops 100000000 | bytes 1000000 | tf_op jit(solution)/shard_map/edges/pallas_call | solution.py:666
  1.7 0.5 %collective-permute-start = (bf16[128,128]{1,0:T(8,128)(2,1)S(1)}, bf16[128,128]{1,0:T(8,128)(2,1)S(1)}, u32[]{:S(2)}, u32[]{:S(2)}) collective-permute-start(bf16[128,128]{1,0:T(8,128)(2,1)S(1)} %get-tuple-element.38), channel_id=1, source_target_pairs={{0,1},{1,0},{2,3},{3,2},{4,5},{5,4},{6,7},{7,6},{8,9},{9,8},{10,11... | collective-permute-start | bytes 98312 | tf_op jit(solution)/shard_map/ppermute | solution.py:654
  2.2 0.0 copy-done
  2.2 0.0 copy-done.1
  2.2 1.9 %energy.1 = (bf16[2,192,1024]{2,1,0:T(8,128)(2,1)S(1)}, bf16[2,192,1024]{2,1,0:T(8,128)(2,1)S(1)}, f32[2,192,1024]{2,1,0:T(8,128)S(1)}, bf16[2,192,1024]{2,1,0:T...) custom-call(bf16[2,192,1024]{2,1,0:T(8,128)(2,1)S(1)} %get-tuple-element.39.mask_ref, ...), custom_call_target="tpu_custom_call" | custom-call | flops 4000000000 | bytes 10000000 | tf_op jit(solution)/shard_map/energy/pallas_call | solution.py:684
  4.2 0.0 collective-permute-done.mate_ref
  4.2 0.6 %bands.1 = (bf16[2,192,1024]{2,1,0:T(8,128)(2,1)S(1)}, f32[2,192,256]{2,1,0:T(8,128)S(1)}, bf16[3,128,128]{2,1,0:T(8,128)(2,1)S(1)}) custom-call(bf16[128,128]{1,0:T(8,128)(2,1)S(1)} %collective-permute-done.mate_ref, f32[2,192,1024]{2,1,0:T(8,128)S(1)} %get-tuple-element.41.part_ref, ...), custom_call_target="tpu_custom_call", output_to_operand_aliasing={{0}: (6, {})} | custom-call | flops 1000000000 | bytes 10000000 | tf_op jit(solution)/shard_map/bands/pallas_call | solution.py:697
  4.8 0.1 collective-permute-start.1
  4.9 0.9 %around.1 = (bf16[192,1024]{1,0:T(8,128)(2,1)S(1)}, f32[3,512]{1,0:T(4,128)S(1)}, bf16[144,128]{1,0:T(8,128)(2,1)S(1)}) custom-call(s32[2,16]{1,0:T(2,128)} %bitcast.5, bf16[320,16]{1,0:T(8,128)(2,1)S(1)} %get-tuple-element.35.rows_ref, bf16[2,192,1024]{2,1,0:T(8,128)(2,1)S(1)} %get-tuple-element.36.phi_ref.edge_ref), custom_call_target="tpu_custom_call" | custom-call | flops 100000000 | bytes 1000000 | tf_op jit(solution)/shard_map/around/pallas_call | solution.py:708
  5.8 0.4 %collective-permute-done.1.rows_ref = bf16[3,128,128]{2,1,0:T(8,128)(2,1)S(1)} collective-permute-done((bf16[3,128,128]{2,1,0:T(8,128)(2,1)S(1)}, bf16[3,128,128]{2,1,0:T(8,128)(2,1)S(1)}, u32[]{:S(2)}, u32[]{:S(2)}) %collective-permute-start.1) | collective-permute-done | bytes 98336 | tf_op jit(solution)/shard_map/ppermute | solution.py:654
  6.1 0.2 relay.1
  6.3 6.5 %all-gather = bf16[1184,128]{1,0:T(8,128)(2,1)S(1)} all-gather(bf16[592,128]{1,0:T(8,128)(2,1)S(1)} %relay.1), channel_id=2, replica_groups={{1,2},{3,4},{5,6},{7,8},{9,10},{11,12},{13,14},{17,18},{19,20},{21,22},..., dimensions={0}, use_global_device_ids=true | all-gather | bytes 454656 | tf_op jit(solution)/shard_map/all_gather | solution.py:660
  12.8 0.8 %face.1 = (bf16[128,1024]{1,0:T(8,128)(2,1)S(1)}, bf16[7,64,128]{2,1,0:T(8,128)(2,1)S(1)}, f32[2,128,256]{2,1,0:T(8,128)S(1)}, bf16[4,64,128]{2,1,0:T(8,128)(2,1)S(1)}) custom-call(bf16[2,592,128]{2,1,0:T(8,128)(2,1)S(1)} %bitcast.3, bf16[192,1024]{1,0:T(8,128)(2,1)S(1)} %get-tuple-element.48.around_ref, ...), custom_call_target="tpu_custom_call" | custom-call | flops 100000000 | bytes 1000000 | tf_op jit(solution)/shard_map/face/pallas_call | solution.py:727
  13.6 0.2 collective-permute-start.2
  13.8 0.7 %theta.1 = (bf16[2,192,256]{2,1,0:T(8,128)(2,1)S(1)}, f32[192,192]{1,0:T(8,128)S(1)}, bf16[2,192,1024]{2,1,0:T(8,128)(2,1)S(1)}) custom-call(f32[3,512]{1,0:T(4,128)S(1)} %get-tuple-element.37.keep_ref, f32[2,192,256]{2,1,0:T(8,128)S(1)} %get-tuple-element.45.own_ref, ...), custom_call_target="tpu_custom_call", output_to_operand_aliasing={{2}: (8, {})} | custom-call | flops 1000000000 | bytes 4000000 | tf_op jit(solution)/shard_map/theta/pallas_call | solution.py:744
  14.5 0.4 %collective-permute-done.2.relayed_ref = bf16[4,64,128]{2,1,0:T(8,128)(2,1)S(1)} collective-permute-done((bf16[4,64,128]{2,1,0:T(8,128)(2,1)S(1)}, bf16[4,64,128]{2,1,0:T(8,128)(2,1)S(1)}, u32[]{:S(2)}, u32[]{:S(2)}) %collective-permute-start.2) | collective-permute-done | bytes 65568 | tf_op jit(solution)/shard_map/ppermute | solution.py:654
  14.9 0.7 %gradient.1 = (bf16[2,192,1024]{2,1,0:T(8,128)(2,1)S(1)}, bf16[192,192]{1,0:T(8,128)(2,1)S(1)}, bf16[128,128]{1,0:T(8,128)(2,1)S(1)}, bf16[128,128]{1,0:T(8,128)(2,1)S(1)}) custom-call(f32[3,512]{1,0:T(4,128)S(1)} %get-tuple-element.37.keep_ref, bf16[4,64,128]{2,1,0:T(8,128)(2,1)S(1)} %collective-permute-done.2.relayed_ref, ...), custom_call_target="tpu_custom_call" | custom-call | flops 1000000000 | bytes 10000000 | tf_op jit(solution)/shard_map/gradient/pallas_call | solution.py:755
  15.7 0.7 %collective-permute-start.3 = (bf16[128,128]{1,0:T(8,128)(2,1)S(1)}, bf16[128,128]{1,0:T(8,128)(2,1)S(1)}, u32[]{:S(2)}, u32[]{:S(2)}) collective-permute-start(bf16[128,128]{1,0:T(8,128)(2,1)S(1)} %get-tuple-element.57), channel_id=1, source_target_pairs={{1,2},{2,1},{3,4},{4,3},{5,6},{6,5},{7,8},{8,7},{9,10},{10,9},{11,... | collective-permute-start | bytes 98312 | tf_op jit(solution)/shard_map/ppermute | solution.py:657
  16.3 4.6 %collective-permute-start.4 = (bf16[128,128]{1,0:T(8,128)(2,1)S(1)}, bf16[128,128]{1,0:T(8,128)(2,1)S(1)}, u32[]{:S(2)}, u32[]{:S(2)}) collective-permute-start(bf16[128,128]{1,0:T(8,128)(2,1)S(1)} %get-tuple-element.58), channel_id=1, source_target_pairs={{0,1},{1,0},{2,3},{3,2},{4,5},{5,4},{6,7},{7,6},{8,9},{9,8},{10,11... | collective-permute-start | bytes 98312 | tf_op jit(solution)/shard_map/ppermute | solution.py:654
  20.9 2.2 %smooth.1 = (bf16[192,4096]{1,0:T(8,128)(2,1)}, f32[2,192,1024]{2,1,0:T(8,128)S(1)}) custom-call(bf16[192,192]{1,0:T(8,128)(2,1)S(1)} %get-tuple-element.59.theta_ref, bf16[2,192,1024]{2,1,0:T(8,128)(2,1)S(1)} %get-tuple-element.60.phi_ref, bf16[2,192,1024]{2,1,0:T(8,128)(2,1)S(1)} %get-tuple-element.61.energy_ref, ...), custom_call_target="tpu_custom_call" | custom-call | flops 2000000000 | bytes 10000000 | tf_op jit(solution)/shard_map/smooth/pallas_call | solution.py:768
  23.1 0.0 collective-permute-done.3.across_ref
  23.2 0.0 collective-permute-done.4.mate_ref
  23.2 1.0 %finish.1 = bf16[192,4096]{1,0:T(8,128)(2,1)} custom-call(bf16[128,128]{1,0:T(8,128)(2,1)S(1)} %collective-permute-done.3.across_ref, bf16[128,128]{1,0:T(8,128)(2,1)S(1)} %collective-permute-done.4.mate_ref, f32[2,192,1024]{2,1,0:T(8,128)S(1)} %get-tuple-element.63.part_ref, ...), custom_call_target="tpu_custom_call", output_to_operand_aliasing={{}: (4, {})} | custom-call | flops 10000000 | bytes 10000000 | tf_op jit(solution)/shard_map/finish/pallas_call | solution.py:784
  (1 shorter events, 0.0 us)
Async XLA Ops:
  0.0 2.2 %copy-start = (bf16[192,4096]{1,0:T(8,128)(2,1)S(1)}, bf16[192,4096]{1,0:T(8,128)(2,1)}, u32[]{:S(2)}) copy-start(bf16[192,4096]{1,0:T(8,128)(2,1)} %pieces_ref.3) | copy-start | bytes 4718596
  0.0 2.2 %copy-start.1 = (f32[4,1024]{1,0:T(4,128)S(1)}, f32[4,1024]{1,0:T(4,128)}, u32[]{:S(2)}) copy-start(f32[4,1024]{1,0:T(4,128)} %pot_ref.1) | copy-start | bytes 49156
  1.7 2.5 %collective-permute-start = (bf16[128,128]{1,0:T(8,128)(2,1)S(1)}, bf16[128,128]{1,0:T(8,128)(2,1)S(1)}, u32[]{:S(2)}, u32[]{:S(2)}) collective-permute-start(bf16[128,128]{1,0:T(8,128)(2,1)S(1)} %get-tuple-element.38), channel_id=1, source_target_pairs={{0,1},{1,0},{2,3},{3,2},{4,5},{5,4},{6,7},{7,6},{8,9},{9,8},{10,11... | collective-permute-start | bytes 98312 | tf_op jit(solution)/shard_map/ppermute | solution.py:654
  4.8 1.4 %collective-permute-start.1 = (bf16[3,128,128]{2,1,0:T(8,128)(2,1)S(1)}, bf16[3,128,128]{2,1,0:T(8,128)(2,1)S(1)}, u32[]{:S(2)}, u32[]{:S(2)}) collective-permute-start(bf16[3,128,128]{2,1,0:T(8,128)(2,1)S(1)} %get-tuple-element.46), channel_id=1, source_target_pairs={{0,1},{1,0},{2,3},{3,2},{4,5},{5,4},{6,7},{7,6},{8,9},{9,8},{10,11... | collective-permute-start | bytes 294920 | tf_op jit(solution)/shard_map/ppermute | solution.py:654
  13.6 1.3 %collective-permute-start.2 = (bf16[4,64,128]{2,1,0:T(8,128)(2,1)S(1)}, bf16[4,64,128]{2,1,0:T(8,128)(2,1)S(1)}, u32[]{:S(2)}, u32[]{:S(2)}) collective-permute-start(bf16[4,64,128]{2,1,0:T(8,128)(2,1)S(1)} %get-tuple-element.49), channel_id=1, source_target_pairs={{0,1},{1,0},{2,3},{3,2},{4,5},{5,4},{6,7},{7,6},{8,9},{9,8},{10,11... | collective-permute-start | bytes 196616 | tf_op jit(solution)/shard_map/ppermute | solution.py:654
  15.7 7.5 %collective-permute-start.3 = (bf16[128,128]{1,0:T(8,128)(2,1)S(1)}, bf16[128,128]{1,0:T(8,128)(2,1)S(1)}, u32[]{:S(2)}, u32[]{:S(2)}) collective-permute-start(bf16[128,128]{1,0:T(8,128)(2,1)S(1)} %get-tuple-element.57), channel_id=1, source_target_pairs={{1,2},{2,1},{3,4},{4,3},{5,6},{6,5},{7,8},{8,7},{9,10},{10,9},{11,... | collective-permute-start | bytes 98312 | tf_op jit(solution)/shard_map/ppermute | solution.py:657
  16.3 6.8 %collective-permute-start.4 = (bf16[128,128]{1,0:T(8,128)(2,1)S(1)}, bf16[128,128]{1,0:T(8,128)(2,1)S(1)}, u32[]{:S(2)}, u32[]{:S(2)}) collective-permute-start(bf16[128,128]{1,0:T(8,128)(2,1)S(1)} %get-tuple-element.58), channel_id=1, source_target_pairs={{0,1},{1,0},{2,3},{3,2},{4,5},{5,4},{6,7},{7,6},{8,9},{9,8},{10,11... | collective-permute-start | bytes 98312 | tf_op jit(solution)/shard_map/ppermute | solution.py:654

commit v16 on v13

--- a/solution.py
+++ b/solution.py
@@ -274,19 +274,18 @@
             plane = (CX - 1) * i
             value = 0.5 * (outer[i] - mid[i]) + pot_ref[plane : plane + 1, lanes] * edge[i]
             part_ref[i, :, lanes] = value
-            rest = rest_rows(i)
-            edge_energy_ref[i, rest, lanes] = value[rest].astype(BF16) * edge_mask_ref[i, rest, lanes]
+            edge_energy_ref[i, :, lanes] = value.astype(BF16) * edge_mask_ref[i, :, lanes]
     mid = jnp.concatenate([phi_ref[0], phi_ref[1]], axis=1)
     both = jnp.concatenate([energy_ref[0], energy_ref[1]], axis=1)
     gram = rows_product(jnp.concatenate([mid, both], axis=0), mid)
     corr = gram[:ROWS]
-    ham_ref[...] = gram[ROWS:]
+    ham = gram[ROWS:]
     for i in range(2):
-        rest = rest_rows(i)
-        gram = rows_product(jnp.concatenate([edge_ref[i], edge_energy_ref[i, rest]], axis=0), edge_ref[i])
+        gram = rows_product(jnp.concatenate([edge_ref[i], edge_energy_ref[i]], axis=0), edge_ref[i])
         corr = corr + gram[:ROWS]
-        ham_ref[rest] += gram[ROWS:]
+        ham = ham + gram[ROWS:]
     corr_ref[...] = corr
+    ham_ref[...] = ham
 
 
 def halo_rows(i):
@@ -300,21 +299,24 @@
 def bands_kernel(
     mate_ref, part_ref, mask_ref, phi_ref, corr_ref, ham_ref, rest_ref,
     energy_ref, own_ref, rows_ref,
+    halo_ref,
 ):
     volume = 1.0 / (4.0 * CX**3)
-    gram = []
-    mate = mate_ref[...].astype(F32)
-    for i, side in enumerate(sides(mate, jnp.zeros_like(mate))):
-        tiles = side_by_side(unfold(side), i)
-        for t in range(PLANE // 128):
+    unfolded = unfold(mate_ref[...].astype(F32))
+    own_ref[0, :, :ROWS] = ham_ref[...] * volume
+
+    def add_mate(i):
+        here = halo_rows(i)
+        for t, value in enumerate(side_by_side(unfolded, i)):
             lanes = slice(128 * t, 128 * t + 128)
-            value = part_ref[i, halo_rows(i), lanes] - 0.5 * tiles[t]
-            energy_ref[i, halo_rows(i), lanes] = value.astype(BF16) * mask_ref[i, halo_rows(i), lanes]
-        gram.append(rows_product(energy_ref[i, halo_rows(i)], phi_ref[i]))
+            mask = mask_ref[i, here, lanes]
+            halo_ref[:, lanes] = value.astype(BF16) * mask
+            energy_ref[i, here, lanes] = (part_ref[i, here, lanes] - 0.5 * value).astype(BF16) * mask
+        own_ref[0, here, :ROWS] += rows_product(halo_ref[...], phi_ref[i]) * (-0.5 * volume)
+
+    pl.when(is_even())(lambda: add_mate(1))
+    pl.when(jnp.logical_not(is_even()))(lambda: add_mate(0))
     own_ref[:, :, ROWS:] = jnp.zeros((2, ROWS, TILE - ROWS), F32)
-    own_ref[0, :ORB, :ROWS] = (ham_ref[:ORB] + gram[0][:ORB]) * volume
-    own_ref[0, ORB : 2 * ORB, :ROWS] = (ham_ref[ORB : 2 * ORB] + gram[0][ORB:] + gram[1][:ORB]) * volume
-    own_ref[0, 2 * ORB :, :ROWS] = (ham_ref[2 * ORB :] + gram[1][ORB:]) * volume
     own_ref[1, :, :ROWS] = corr_ref[...] * volume
     tail = jnp.where(low_half(), own_ref[0, :, 128:256], swapped(own_ref[1, :, 128:256]))
     even = is_even()
@@ -694,6 +696,7 @@
         out_shape=(pair, shape(2, ROWS, TILE, dtype=F32), shape(3, 2 * ORB, 128)),
         in_specs=[WHOLE] * 7,
         out_specs=(WHOLE,) * 3,
+        scratch_shapes=[pltpu.VMEM((2 * ORB, PLANE), BF16)],
         input_output_aliases={6: 0},
         compiler_params=PARAMS,
         cost_estimate=cost(10**9, 10**7),

time: 24.3 us -> 24.7 us (1.016)
  Pallas kernels: 10.7 us -> 11 us
    pallas_call x1, Pallas kernels: 2.01 us -> 2.41 us  [per_device(): pl.pallas_call(energy_kernel, out_shape=(pair, pair, pair, shape(2, ROWS,...]
  transfers between devices with their start and end apart: 5 -> 5, of which waited for: 2 -> 2; matrix products, arithmetic and copies ran while one was open for 0% -> 0% of each run, Pallas kernels for 24% -> 25%
where the time goes in v16:
time: 24.7 us; the launch traced here: 24.5 us
  Pallas kernels  11 us (45%)
  blocking collectives  6.46 us (26%)
  starting transfers between devices  6.01 us (24%)
  waiting for transfers between devices  0.93 us (4%)
    all_gather x1, blocking collectives, gathered(): return lax.all_gather(value, ('grp', 'sx'), axis_index_groups=pairs)  6.46 us
    ppermute x4, starting transfers between devices, to_mate(): return lax.ppermute(value, 'sx', mates)  5.35 us
    pallas_call x1, Pallas kernels, per_device(): pl.pallas_call(energy_kernel, out_shape=(pair, pair, pair, shape(2, ROWS,...  2.41 us
    pallas_call x1, Pallas kernels, per_device(): pl.pallas_call(smooth_kernel, out_shape=(pltpu.HBM((ROWS, CX * PLANE), BF...  2.24 us
    pallas_call x1, Pallas kernels, per_device(): pl.pallas_call(edges_kernel, out_shape=(pair, pair, shape(5 * ORB, 16), s...  1.54 us
    pallas_call x1, Pallas kernels, per_device(): pl.pallas_call(finish_kernel, out_shape=pltpu.HBM((ROWS, CX * PLANE), BF1...  1.03 us
    ppermute x4, waiting for transfers between devices, to_mate(): return lax.ppermute(value, 'sx', mates)  0.93 us
    pallas_call x1, Pallas kernels, per_device(): pl.pallas_call(around_kernel, out_shape=(shape(ROWS, PLANE), shape(3, 8 *...  0.85 us
  transfers between devices with their start and end apart: 5, of which 2 were waited for; matrix products, arithmetic and copies ran while one was open for 0% of the time, Pallas kernels for 25%

profile of v16, /device:TPU:0, one launch (start us, length us, event | category | flops | bytes accessed | tf_op | source)
XLA Modules:
  0.0 24.5 jit_solution(7827554690355000282)
XLA Ops:
  0.0 0.0 copy-start
  0.0 1.5 %edges.1 = (bf16[2,192,1024]{2,1,0:T(8,128)(2,1)S(1)}, bf16[2,192,1024]{2,1,0:T(8,128)(2,1)S(1)}, bf16[320,16]{1,0:T(8,128)(2,1)S(1)}, f32[192,1024]{1,0:T(8,128)S(1)}, bf16[128,128]{1,0:T(8,128)(2,1)S(1)}) custom-call(s32[4,1024]{1,0:T(4,128)} %bitcast.4, bf16[192,4096]{1,0:T(8,128)(2,1)} %pieces_ref.3), custom_call_target="tpu_custom_call" | custom-call | flops 100000000 | bytes 1000000 | tf_op jit(solution)/shard_map/edges/pallas_call | solution.py:663
  1.6 0.5 %collective-permute-start = (bf16[128,128]{1,0:T(8,128)(2,1)S(1)}, bf16[128,128]{1,0:T(8,128)(2,1)S(1)}, u32[]{:S(2)}, u32[]{:S(2)}) collective-permute-start(bf16[128,128]{1,0:T(8,128)(2,1)S(1)} %get-tuple-element.39), channel_id=1, source_target_pairs={{0,1},{1,0},{2,3},{3,2},{4,5},{5,4},{6,7},{7,6},{8,9},{9,8},{10,11... | collective-permute-start | bytes 98312 | tf_op jit(solution)/shard_map/ppermute | solution.py:651
  2.1 0.0 copy-done
  2.1 0.0 copy-done.1
  2.1 2.4 %energy.1 = (bf16[2,192,1024]{2,1,0:T(8,128)(2,1)S(1)}, bf16[2,192,1024]{2,1,0:T(8,128)(2,1)S(1)}, bf16[2,192,1024]{2,1,0:T(8,128)(2,1)S(1)}, f32[2,192,1024]{2,...) custom-call(bf16[320,16]{1,0:T(8,128)(2,1)S(1)} %get-tuple-element.36.rows_ref, ...), custom_call_target="tpu_custom_call" | custom-call | flops 4000000000 | bytes 10000000 | tf_op jit(solution)/shard_map/energy/pallas_call | solution.py:681
  4.5 0.0 collective-permute-done.mate_ref
  4.5 0.6 %bands.1 = (bf16[2,192,1024]{2,1,0:T(8,128)(2,1)S(1)}, f32[2,192,256]{2,1,0:T(8,128)S(1)}, bf16[3,128,128]{2,1,0:T(8,128)(2,1)S(1)}) custom-call(bf16[128,128]{1,0:T(8,128)(2,1)S(1)} %collective-permute-done.mate_ref, f32[2,192,1024]{2,1,0:T(8,128)S(1)} %get-tuple-element.42.part_ref, ...), custom_call_target="tpu_custom_call", output_to_operand_aliasing={{0}: (6, {})} | custom-call | flops 1000000000 | bytes 10000000 | tf_op jit(solution)/shard_map/bands/pallas_call | solution.py:694
  5.1 0.1 collective-permute-start.1
  5.2 0.8 %around.1 = (bf16[192,1024]{1,0:T(8,128)(2,1)S(1)}, f32[3,512]{1,0:T(4,128)S(1)}, bf16[144,128]{1,0:T(8,128)(2,1)S(1)}) custom-call(s32[2,16]{1,0:T(2,128)} %bitcast.5, bf16[320,16]{1,0:T(8,128)(2,1)S(1)} %get-tuple-element.36.rows_ref, bf16[2,192,1024]{2,1,0:T(8,128)(2,1)S(1)} %get-tuple-element.37.phi_ref.edge_ref), custom_call_target="tpu_custom_call" | custom-call | flops 100000000 | bytes 1000000 | tf_op jit(solution)/shard_map/around/pallas_call | solution.py:706
  6.1 0.4 %collective-permute-done.1.rows_ref = bf16[3,128,128]{2,1,0:T(8,128)(2,1)S(1)} collective-permute-done((bf16[3,128,128]{2,1,0:T(8,128)(2,1)S(1)}, bf16[3,128,128]{2,1,0:T(8,128)(2,1)S(1)}, u32[]{:S(2)}, u32[]{:S(2)}) %collective-permute-start.1) | collective-permute-done | bytes 98336 | tf_op jit(solution)/shard_map/ppermute | solution.py:651
  6.5 0.2 relay.1
  6.6 6.5 %all-gather = bf16[1184,128]{1,0:T(8,128)(2,1)S(1)} all-gather(bf16[592,128]{1,0:T(8,128)(2,1)S(1)} %relay.1), channel_id=2, replica_groups={{1,2},{3,4},{5,6},{7,8},{9,10},{11,12},{13,14},{17,18},{19,20},{21,22},..., dimensions={0}, use_global_device_ids=true | all-gather | bytes 454656 | tf_op jit(solution)/shard_map/all_gather | solution.py:657
  13.1 0.8 %face.1 = (bf16[128,1024]{1,0:T(8,128)(2,1)S(1)}, bf16[7,64,128]{2,1,0:T(8,128)(2,1)S(1)}, f32[192,512]{1,0:T(8,128)S(1)}, bf16[4,64,128]{2,1,0:T(8,128)(2,1)S(1)}) custom-call(bf16[2,592,128]{2,1,0:T(8,128)(2,1)S(1)} %bitcast.3, bf16[192,1024]{1,0:T(8,128)(2,1)S(1)} %get-tuple-element.49.around_ref, ...), custom_call_target="tpu_custom_call" | custom-call | flops 100000000 | bytes 1000000 | tf_op jit(solution)/shard_map/face/pallas_call | solution.py:725
  13.9 0.2 collective-permute-start.2
  14.1 0.6 %theta.1 = (bf16[2,192,256]{2,1,0:T(8,128)(2,1)S(1)}, f32[192,192]{1,0:T(8,128)S(1)}, bf16[2,192,1024]{2,1,0:T(8,128)(2,1)S(1)}) custom-call(f32[3,512]{1,0:T(4,128)S(1)} %get-tuple-element.38.keep_ref, f32[2,192,256]{2,1,0:T(8,128)S(1)} %get-tuple-element.46.own_ref, ...), custom_call_target="tpu_custom_call", output_to_operand_aliasing={{2}: (8, {})} | custom-call | flops 1000000000 | bytes 4000000 | tf_op jit(solution)/shard_map/theta/pallas_call | solution.py:743
  14.7 0.5 %collective-permute-done.2.relayed_ref = bf16[4,64,128]{2,1,0:T(8,128)(2,1)S(1)} collective-permute-done((bf16[4,64,128]{2,1,0:T(8,128)(2,1)S(1)}, bf16[4,64,128]{2,1,0:T(8,128)(2,1)S(1)}, u32[]{:S(2)}, u32[]{:S(2)}) %collective-permute-start.2) | collective-permute-done | bytes 65568 | tf_op jit(solution)/shard_map/ppermute | solution.py:651
  15.2 0.7 %gradient.1 = (bf16[2,192,1024]{2,1,0:T(8,128)(2,1)S(1)}, bf16[192,192]{1,0:T(8,128)(2,1)S(1)}, bf16[128,128]{1,0:T(8,128)(2,1)S(1)}, bf16[128,128]{1,0:T(8,128)(2,1)S(1)}) custom-call(f32[3,512]{1,0:T(4,128)S(1)} %get-tuple-element.38.keep_ref, bf16[4,64,128]{2,1,0:T(8,128)(2,1)S(1)} %collective-permute-done.2.relayed_ref, ...), custom_call_target="tpu_custom_call" | custom-call | flops 1000000000 | bytes 10000000 | tf_op jit(solution)/shard_map/gradient/pallas_call | solution.py:754
  16.0 0.7 %collective-permute-start.3 = (bf16[128,128]{1,0:T(8,128)(2,1)S(1)}, bf16[128,128]{1,0:T(8,128)(2,1)S(1)}, u32[]{:S(2)}, u32[]{:S(2)}) collective-permute-start(bf16[128,128]{1,0:T(8,128)(2,1)S(1)} %get-tuple-element.58), channel_id=1, source_target_pairs={{1,2},{2,1},{3,4},{4,3},{5,6},{6,5},{7,8},{8,7},{9,10},{10,9},{11,... | collective-permute-start | bytes 98312 | tf_op jit(solution)/shard_map/ppermute | solution.py:654
  16.7 4.5 %collective-permute-start.4 = (bf16[128,128]{1,0:T(8,128)(2,1)S(1)}, bf16[128,128]{1,0:T(8,128)(2,1)S(1)}, u32[]{:S(2)}, u32[]{:S(2)}) collective-permute-start(bf16[128,128]{1,0:T(8,128)(2,1)S(1)} %get-tuple-element.59), channel_id=1, source_target_pairs={{0,1},{1,0},{2,3},{3,2},{4,5},{5,4},{6,7},{7,6},{8,9},{9,8},{10,11... | collective-permute-start | bytes 98312 | tf_op jit(solution)/shard_map/ppermute | solution.py:651
  21.2 2.2 %smooth.1 = (bf16[192,4096]{1,0:T(8,128)(2,1)}, f32[2,192,1024]{2,1,0:T(8,128)S(1)}) custom-call(bf16[192,192]{1,0:T(8,128)(2,1)S(1)} %get-tuple-element.60.theta_ref, bf16[2,192,1024]{2,1,0:T(8,128)(2,1)S(1)} %get-tuple-element.61.phi_ref, bf16[2,192,1024]{2,1,0:T(8,128)(2,1)S(1)} %get-tuple-element.62.energy_ref, ...), custom_call_target="tpu_custom_call" | custom-call | flops 2000000000 | bytes 10000000 | tf_op jit(solution)/shard_map/smooth/pallas_call | solution.py:767
  23.5 0.0 collective-permute-done.3.across_ref
  23.5 0.0 collective-permute-done.4.mate_ref
  23.5 1.0 %finish.1 = bf16[192,4096]{1,0:T(8,128)(2,1)} custom-call(bf16[128,128]{1,0:T(8,128)(2,1)S(1)} %collective-permute-done.3.across_ref, bf16[128,128]{1,0:T(8,128)(2,1)S(1)} %collective-permute-done.4.mate_ref, f32[2,192,1024]{2,1,0:T(8,128)S(1)} %get-tuple-element.65.part_ref, ...), custom_call_target="tpu_custom_call", output_to_operand_aliasing={{}: (4, {})} | custom-call | flops 10000000 | bytes 10000000 | tf_op jit(solution)/shard_map/finish/pallas_call | solution.py:783
  (1 shorter events, 0.0 us)
Async XLA Ops:
  0.0 2.1 %copy-start = (bf16[192,4096]{1,0:T(8,128)(2,1)S(1)}, bf16[192,4096]{1,0:T(8,128)(2,1)}, u32[]{:S(2)}) copy-start(bf16[192,4096]{1,0:T(8,128)(2,1)} %pieces_ref.3) | copy-start | bytes 4718596
  0.0 2.1 %copy-start.1 = (f32[4,1024]{1,0:T(4,128)S(1)}, f32[4,1024]{1,0:T(4,128)}, u32[]{:S(2)}) copy-start(f32[4,1024]{1,0:T(4,128)} %pot_ref.1) | copy-start | bytes 49156
  1.6 2.9 %collective-permute-start = (bf16[128,128]{1,0:T(8,128)(2,1)S(1)}, bf16[128,128]{1,0:T(8,128)(2,1)S(1)}, u32[]{:S(2)}, u32[]{:S(2)}) collective-permute-start(bf16[128,128]{1,0:T(8,128)(2,1)S(1)} %get-tuple-element.39), channel_id=1, source_target_pairs={{0,1},{1,0},{2,3},{3,2},{4,5},{5,4},{6,7},{7,6},{8,9},{9,8},{10,11... | collective-permute-start | bytes 98312 | tf_op jit(solution)/shard_map/ppermute | solution.py:651
  5.1 1.4 %collective-permute-start.1 = (bf16[3,128,128]{2,1,0:T(8,128)(2,1)S(1)}, bf16[3,128,128]{2,1,0:T(8,128)(2,1)S(1)}, u32[]{:S(2)}, u32[]{:S(2)}) collective-permute-start(bf16[3,128,128]{2,1,0:T(8,128)(2,1)S(1)} %get-tuple-element.47), channel_id=1, source_target_pairs={{0,1},{1,0},{2,3},{3,2},{4,5},{5,4},{6,7},{7,6},{8,9},{9,8},{10,11... | collective-permute-start | bytes 294920 | tf_op jit(solution)/shard_map/ppermute | solution.py:651
  13.9 1.3 %collective-permute-start.2 = (bf16[4,64,128]{2,1,0:T(8,128)(2,1)S(1)}, bf16[4,64,128]{2,1,0:T(8,128)(2,1)S(1)}, u32[]{:S(2)}, u32[]{:S(2)}) collective-permute-start(bf16[4,64,128]{2,1,0:T(8,128)(2,1)S(1)} %get-tuple-element.50), channel_id=1, source_target_pairs={{0,1},{1,0},{2,3},{3,2},{4,5},{5,4},{6,7},{7,6},{8,9},{9,8},{10,11... | collective-permute-start | bytes 196616 | tf_op jit(solution)/shard_map/ppermute | solution.py:651
  16.0 7.5 %collective-permute-start.3 = (bf16[128,128]{1,0:T(8,128)(2,1)S(1)}, bf16[128,128]{1,0:T(8,128)(2,1)S(1)}, u32[]{:S(2)}, u32[]{:S(2)}) collective-permute-start(bf16[128,128]{1,0:T(8,128)(2,1)S(1)} %get-tuple-element.58), channel_id=1, source_target_pairs={{1,2},{2,1},{3,4},{4,3},{5,6},{6,5},{7,8},{8,7},{9,10},{10,9},{11,... | collective-permute-start | bytes 98312 | tf_op jit(solution)/shard_map/ppermute | solution.py:654
  16.7 6.8 %collective-permute-start.4 = (bf16[128,128]{1,0:T(8,128)(2,1)S(1)}, bf16[128,128]{1,0:T(8,128)(2,1)S(1)}, u32[]{:S(2)}, u32[]{:S(2)}) collective-permute-start(bf16[128,128]{1,0:T(8,128)(2,1)S(1)} %get-tuple-element.59), channel_id=1, source_target_pairs={{0,1},{1,0},{2,3},{3,2},{4,5},{5,4},{6,7},{7,6},{8,9},{9,8},{10,11... | collective-permute-start | bytes 98312 | tf_op jit(solution)/shard_map/ppermute | solution.py:651

commit v17 on v16

--- a/solution.py
+++ b/solution.py
@@ -275,17 +275,11 @@
             value = 0.5 * (outer[i] - mid[i]) + pot_ref[plane : plane + 1, lanes] * edge[i]
             part_ref[i, :, lanes] = value
             edge_energy_ref[i, :, lanes] = value.astype(BF16) * edge_mask_ref[i, :, lanes]
-    mid = jnp.concatenate([phi_ref[0], phi_ref[1]], axis=1)
-    both = jnp.concatenate([energy_ref[0], energy_ref[1]], axis=1)
-    gram = rows_product(jnp.concatenate([mid, both], axis=0), mid)
-    corr = gram[:ROWS]
-    ham = gram[ROWS:]
-    for i in range(2):
-        gram = rows_product(jnp.concatenate([edge_ref[i], edge_energy_ref[i]], axis=0), edge_ref[i])
-        corr = corr + gram[:ROWS]
-        ham = ham + gram[ROWS:]
-    corr_ref[...] = corr
-    ham_ref[...] = ham
+    orbitals = jnp.concatenate([phi_ref[0], phi_ref[1], edge_ref[0], edge_ref[1]], axis=1)
+    energies = jnp.concatenate([energy_ref[0], energy_ref[1], edge_energy_ref[0], edge_energy_ref[1]], axis=1)
+    gram = rows_product(jnp.concatenate([orbitals, energies], axis=0), orbitals)
+    corr_ref[...] = gram[:ROWS]
+    ham_ref[...] = gram[ROWS:]
 
 
 def halo_rows(i):

time: 24.7 us -> 24.7 us (level)
  no operation moved by 1% of the time
where the time goes in v17:
time: 24.7 us; the launch traced here: 24.5 us
  Pallas kernels  11 us (45%)
  blocking collectives  6.46 us (26%)
  starting transfers between devices  6.01 us (24%)
  waiting for transfers between devices  0.93 us (4%)
    all_gather x1, blocking collectives, gathered(): return lax.all_gather(value, ('grp', 'sx'), axis_index_groups=pairs)  6.46 us
    ppermute x4, starting transfers between devices, to_mate(): return lax.ppermute(value, 'sx', mates)  5.35 us
    pallas_call x1, Pallas kernels, per_device(): pl.pallas_call(energy_kernel, out_shape=(pair, pair, pair, shape(2, ROWS,...  2.41 us
    pallas_call x1, Pallas kernels, per_device(): pl.pallas_call(smooth_kernel, out_shape=(pltpu.HBM((ROWS, CX * PLANE), BF...  2.24 us
    pallas_call x1, Pallas kernels, per_device(): pl.pallas_call(edges_kernel, out_shape=(pair, pair, shape(5 * ORB, 16), s...  1.54 us
    pallas_call x1, Pallas kernels, per_device(): pl.pallas_call(finish_kernel, out_shape=pltpu.HBM((ROWS, CX * PLANE), BF1...  1.03 us
    ppermute x4, waiting for transfers between devices, to_mate(): return lax.ppermute(value, 'sx', mates)  0.93 us
    pallas_call x1, Pallas kernels, per_device(): pl.pallas_call(around_kernel, out_shape=(shape(ROWS, PLANE), shape(3, 8 *...  0.85 us
  transfers between devices with their start and end apart: 5, of which 2 were waited for; matrix products, arithmetic and copies ran while one was open for 0% of the time, Pallas kernels for 25%

profile of v17, /device:TPU:0, one launch (start us, length us, event | category | flops | bytes accessed | tf_op | source)
XLA Modules:
  0.0 24.5 jit_solution(7827554690355000282)
XLA Ops:
  0.0 0.0 copy-start
  0.0 1.5 %edges.1 = (bf16[2,192,1024]{2,1,0:T(8,128)(2,1)S(1)}, bf16[2,192,1024]{2,1,0:T(8,128)(2,1)S(1)}, bf16[320,16]{1,0:T(8,128)(2,1)S(1)}, f32[192,1024]{1,0:T(8,128)S(1)}, bf16[128,128]{1,0:T(8,128)(2,1)S(1)}) custom-call(s32[4,1024]{1,0:T(4,128)} %bitcast.4, bf16[192,4096]{1,0:T(8,128)(2,1)} %pieces_ref.3), custom_call_target="tpu_custom_call" | custom-call | flops 100000000 | bytes 1000000 | tf_op jit(solution)/shard_map/edges/pallas_call | solution.py:657
  1.6 0.5 %collective-permute-start = (bf16[128,128]{1,0:T(8,128)(2,1)S(1)}, bf16[128,128]{1,0:T(8,128)(2,1)S(1)}, u32[]{:S(2)}, u32[]{:S(2)}) collective-permute-start(bf16[128,128]{1,0:T(8,128)(2,1)S(1)} %get-tuple-element.39), channel_id=1, source_target_pairs={{0,1},{1,0},{2,3},{3,2},{4,5},{5,4},{6,7},{7,6},{8,9},{9,8},{10,11... | collective-permute-start | bytes 98312 | tf_op jit(solution)/shard_map/ppermute | solution.py:645
  2.1 0.0 copy-done
  2.1 0.0 copy-done.1
  2.1 2.4 %energy.1 = (bf16[2,192,1024]{2,1,0:T(8,128)(2,1)S(1)}, bf16[2,192,1024]{2,1,0:T(8,128)(2,1)S(1)}, bf16[2,192,1024]{2,1,0:T(8,128)(2,1)S(1)}, f32[2,192,1024]{2,...) custom-call(bf16[320,16]{1,0:T(8,128)(2,1)S(1)} %get-tuple-element.36.rows_ref, ...), custom_call_target="tpu_custom_call" | custom-call | flops 4000000000 | bytes 10000000 | tf_op jit(solution)/shard_map/energy/pallas_call | solution.py:675
  4.5 0.0 collective-permute-done.mate_ref
  4.5 0.6 %bands.1 = (bf16[2,192,1024]{2,1,0:T(8,128)(2,1)S(1)}, f32[2,192,256]{2,1,0:T(8,128)S(1)}, bf16[3,128,128]{2,1,0:T(8,128)(2,1)S(1)}) custom-call(bf16[128,128]{1,0:T(8,128)(2,1)S(1)} %collective-permute-done.mate_ref, f32[2,192,1024]{2,1,0:T(8,128)S(1)} %get-tuple-element.42.part_ref, ...), custom_call_target="tpu_custom_call", output_to_operand_aliasing={{0}: (6, {})} | custom-call | flops 1000000000 | bytes 10000000 | tf_op jit(solution)/shard_map/bands/pallas_call | solution.py:688
  5.1 0.1 collective-permute-start.1
  5.2 0.8 %around.1 = (bf16[192,1024]{1,0:T(8,128)(2,1)S(1)}, f32[3,512]{1,0:T(4,128)S(1)}, bf16[144,128]{1,0:T(8,128)(2,1)S(1)}) custom-call(s32[2,16]{1,0:T(2,128)} %bitcast.5, bf16[320,16]{1,0:T(8,128)(2,1)S(1)} %get-tuple-element.36.rows_ref, bf16[2,192,1024]{2,1,0:T(8,128)(2,1)S(1)} %get-tuple-element.37.phi_ref.edge_ref), custom_call_target="tpu_custom_call" | custom-call | flops 100000000 | bytes 1000000 | tf_op jit(solution)/shard_map/around/pallas_call | solution.py:700
  6.1 0.4 %collective-permute-done.1.rows_ref = bf16[3,128,128]{2,1,0:T(8,128)(2,1)S(1)} collective-permute-done((bf16[3,128,128]{2,1,0:T(8,128)(2,1)S(1)}, bf16[3,128,128]{2,1,0:T(8,128)(2,1)S(1)}, u32[]{:S(2)}, u32[]{:S(2)}) %collective-permute-start.1) | collective-permute-done | bytes 98336 | tf_op jit(solution)/shard_map/ppermute | solution.py:645
  6.5 0.2 relay.1
  6.6 6.5 %all-gather = bf16[1184,128]{1,0:T(8,128)(2,1)S(1)} all-gather(bf16[592,128]{1,0:T(8,128)(2,1)S(1)} %relay.1), channel_id=2, replica_groups={{1,2},{3,4},{5,6},{7,8},{9,10},{11,12},{13,14},{17,18},{19,20},{21,22},..., dimensions={0}, use_global_device_ids=true | all-gather | bytes 454656 | tf_op jit(solution)/shard_map/all_gather | solution.py:651
  13.1 0.8 %face.1 = (bf16[128,1024]{1,0:T(8,128)(2,1)S(1)}, bf16[7,64,128]{2,1,0:T(8,128)(2,1)S(1)}, f32[192,512]{1,0:T(8,128)S(1)}, bf16[4,64,128]{2,1,0:T(8,128)(2,1)S(1)}) custom-call(bf16[2,592,128]{2,1,0:T(8,128)(2,1)S(1)} %bitcast.3, bf16[192,1024]{1,0:T(8,128)(2,1)S(1)} %get-tuple-element.49.around_ref, ...), custom_call_target="tpu_custom_call" | custom-call | flops 100000000 | bytes 1000000 | tf_op jit(solution)/shard_map/face/pallas_call | solution.py:719
  13.9 0.2 collective-permute-start.2
  14.1 0.6 %theta.1 = (bf16[2,192,256]{2,1,0:T(8,128)(2,1)S(1)}, f32[192,192]{1,0:T(8,128)S(1)}, bf16[2,192,1024]{2,1,0:T(8,128)(2,1)S(1)}) custom-call(f32[3,512]{1,0:T(4,128)S(1)} %get-tuple-element.38.keep_ref, f32[2,192,256]{2,1,0:T(8,128)S(1)} %get-tuple-element.46.own_ref, ...), custom_call_target="tpu_custom_call", output_to_operand_aliasing={{2}: (8, {})} | custom-call | flops 1000000000 | bytes 4000000 | tf_op jit(solution)/shard_map/theta/pallas_call | solution.py:737
  14.7 0.5 %collective-permute-done.2.relayed_ref = bf16[4,64,128]{2,1,0:T(8,128)(2,1)S(1)} collective-permute-done((bf16[4,64,128]{2,1,0:T(8,128)(2,1)S(1)}, bf16[4,64,128]{2,1,0:T(8,128)(2,1)S(1)}, u32[]{:S(2)}, u32[]{:S(2)}) %collective-permute-start.2) | collective-permute-done | bytes 65568 | tf_op jit(solution)/shard_map/ppermute | solution.py:645
  15.2 0.7 %gradient.1 = (bf16[2,192,1024]{2,1,0:T(8,128)(2,1)S(1)}, bf16[192,192]{1,0:T(8,128)(2,1)S(1)}, bf16[128,128]{1,0:T(8,128)(2,1)S(1)}, bf16[128,128]{1,0:T(8,128)(2,1)S(1)}) custom-call(f32[3,512]{1,0:T(4,128)S(1)} %get-tuple-element.38.keep_ref, bf16[4,64,128]{2,1,0:T(8,128)(2,1)S(1)} %collective-permute-done.2.relayed_ref, ...), custom_call_target="tpu_custom_call" | custom-call | flops 1000000000 | bytes 10000000 | tf_op jit(solution)/shard_map/gradient/pallas_call | solution.py:748
  16.0 0.7 %collective-permute-start.3 = (bf16[128,128]{1,0:T(8,128)(2,1)S(1)}, bf16[128,128]{1,0:T(8,128)(2,1)S(1)}, u32[]{:S(2)}, u32[]{:S(2)}) collective-permute-start(bf16[128,128]{1,0:T(8,128)(2,1)S(1)} %get-tuple-element.58), channel_id=1, source_target_pairs={{1,2},{2,1},{3,4},{4,3},{5,6},{6,5},{7,8},{8,7},{9,10},{10,9},{11,... | collective-permute-start | bytes 98312 | tf_op jit(solution)/shard_map/ppermute | solution.py:648
  16.7 4.5 %collective-permute-start.4 = (bf16[128,128]{1,0:T(8,128)(2,1)S(1)}, bf16[128,128]{1,0:T(8,128)(2,1)S(1)}, u32[]{:S(2)}, u32[]{:S(2)}) collective-permute-start(bf16[128,128]{1,0:T(8,128)(2,1)S(1)} %get-tuple-element.59), channel_id=1, source_target_pairs={{0,1},{1,0},{2,3},{3,2},{4,5},{5,4},{6,7},{7,6},{8,9},{9,8},{10,11... | collective-permute-start | bytes 98312 | tf_op jit(solution)/shard_map/ppermute | solution.py:645
  21.2 2.2 %smooth.1 = (bf16[192,4096]{1,0:T(8,128)(2,1)}, f32[2,192,1024]{2,1,0:T(8,128)S(1)}) custom-call(bf16[192,192]{1,0:T(8,128)(2,1)S(1)} %get-tuple-element.60.theta_ref, bf16[2,192,1024]{2,1,0:T(8,128)(2,1)S(1)} %get-tuple-element.61.phi_ref, bf16[2,192,1024]{2,1,0:T(8,128)(2,1)S(1)} %get-tuple-element.62.energy_ref, ...), custom_call_target="tpu_custom_call" | custom-call | flops 2000000000 | bytes 10000000 | tf_op jit(solution)/shard_map/smooth/pallas_call | solution.py:761
  23.5 0.0 collective-permute-done.3.across_ref
  23.5 0.0 collective-permute-done.4.mate_ref
  23.5 1.0 %finish.1 = bf16[192,4096]{1,0:T(8,128)(2,1)} custom-call(bf16[128,128]{1,0:T(8,128)(2,1)S(1)} %collective-permute-done.3.across_ref, bf16[128,128]{1,0:T(8,128)(2,1)S(1)} %collective-permute-done.4.mate_ref, f32[2,192,1024]{2,1,0:T(8,128)S(1)} %get-tuple-element.65.part_ref, ...), custom_call_target="tpu_custom_call", output_to_operand_aliasing={{}: (4, {})} | custom-call | flops 10000000 | bytes 10000000 | tf_op jit(solution)/shard_map/finish/pallas_call | solution.py:777
  (1 shorter events, 0.0 us)
Async XLA Ops:
  0.0 2.1 %copy-start = (bf16[192,4096]{1,0:T(8,128)(2,1)S(1)}, bf16[192,4096]{1,0:T(8,128)(2,1)}, u32[]{:S(2)}) copy-start(bf16[192,4096]{1,0:T(8,128)(2,1)} %pieces_ref.3) | copy-start | bytes 4718596
  0.0 2.1 %copy-start.1 = (f32[4,1024]{1,0:T(4,128)S(1)}, f32[4,1024]{1,0:T(4,128)}, u32[]{:S(2)}) copy-start(f32[4,1024]{1,0:T(4,128)} %pot_ref.1) | copy-start | bytes 49156
  1.6 2.9 %collective-permute-start = (bf16[128,128]{1,0:T(8,128)(2,1)S(1)}, bf16[128,128]{1,0:T(8,128)(2,1)S(1)}, u32[]{:S(2)}, u32[]{:S(2)}) collective-permute-start(bf16[128,128]{1,0:T(8,128)(2,1)S(1)} %get-tuple-element.39), channel_id=1, source_target_pairs={{0,1},{1,0},{2,3},{3,2},{4,5},{5,4},{6,7},{7,6},{8,9},{9,8},{10,11... | collective-permute-start | bytes 98312 | tf_op jit(solution)/shard_map/ppermute | solution.py:645
  5.1 1.4 %collective-permute-start.1 = (bf16[3,128,128]{2,1,0:T(8,128)(2,1)S(1)}, bf16[3,128,128]{2,1,0:T(8,128)(2,1)S(1)}, u32[]{:S(2)}, u32[]{:S(2)}) collective-permute-start(bf16[3,128,128]{2,1,0:T(8,128)(2,1)S(1)} %get-tuple-element.47), channel_id=1, source_target_pairs={{0,1},{1,0},{2,3},{3,2},{4,5},{5,4},{6,7},{7,6},{8,9},{9,8},{10,11... | collective-permute-start | bytes 294920 | tf_op jit(solution)/shard_map/ppermute | solution.py:645
  13.9 1.3 %collective-permute-start.2 = (bf16[4,64,128]{2,1,0:T(8,128)(2,1)S(1)}, bf16[4,64,128]{2,1,0:T(8,128)(2,1)S(1)}, u32[]{:S(2)}, u32[]{:S(2)}) collective-permute-start(bf16[4,64,128]{2,1,0:T(8,128)(2,1)S(1)} %get-tuple-element.50), channel_id=1, source_target_pairs={{0,1},{1,0},{2,3},{3,2},{4,5},{5,4},{6,7},{7,6},{8,9},{9,8},{10,11... | collective-permute-start | bytes 196616 | tf_op jit(solution)/shard_map/ppermute | solution.py:645
  16.0 7.5 %collective-permute-start.3 = (bf16[128,128]{1,0:T(8,128)(2,1)S(1)}, bf16[128,128]{1,0:T(8,128)(2,1)S(1)}, u32[]{:S(2)}, u32[]{:S(2)}) collective-permute-start(bf16[128,128]{1,0:T(8,128)(2,1)S(1)} %get-tuple-element.58), channel_id=1, source_target_pairs={{1,2},{2,1},{3,4},{4,3},{5,6},{6,5},{7,8},{8,7},{9,10},{10,9},{11,... | collective-permute-start | bytes 98312 | tf_op jit(solution)/shard_map/ppermute | solution.py:648
  16.7 6.8 %collective-permute-start.4 = (bf16[128,128]{1,0:T(8,128)(2,1)S(1)}, bf16[128,128]{1,0:T(8,128)(2,1)S(1)}, u32[]{:S(2)}, u32[]{:S(2)}) collective-permute-start(bf16[128,128]{1,0:T(8,128)(2,1)S(1)} %get-tuple-element.59), channel_id=1, source_target_pairs={{0,1},{1,0},{2,3},{3,2},{4,5},{5,4},{6,7},{7,6},{8,9},{9,8},{10,11... | collective-permute-start | bytes 98312 | tf_op jit(solution)/shard_map/ppermute | solution.py:645

commit v18 on v13

--- a/solution.py
+++ b/solution.py
@@ -303,12 +303,13 @@
 ):
     volume = 1.0 / (4.0 * CX**3)
     gram = []
-    mate = mate_ref[...].astype(F32)
-    for i, side in enumerate(sides(mate, jnp.zeros_like(mate))):
-        tiles = side_by_side(unfold(side), i)
+    unfolded = unfold(mate_ref[...].astype(F32))
+    for i in range(2):
+        factor = jnp.where(is_even() == (i == 1), 0.5, 0.0)
+        tiles = side_by_side(unfolded, i)
         for t in range(PLANE // 128):
             lanes = slice(128 * t, 128 * t + 128)
-            value = part_ref[i, halo_rows(i), lanes] - 0.5 * tiles[t]
+            value = part_ref[i, halo_rows(i), lanes] - factor * tiles[t]
             energy_ref[i, halo_rows(i), lanes] = value.astype(BF16) * mask_ref[i, halo_rows(i), lanes]
         gram.append(rows_product(energy_ref[i, halo_rows(i)], phi_ref[i]))
     own_ref[:, :, ROWS:] = jnp.zeros((2, ROWS, TILE - ROWS), F32)

time: 24.3 us -> 24.3 us (level)
  no operation moved by 1% of the time
where the time goes in v18:
time: 24.3 us; the launch traced here: 24.1 us
  Pallas kernels  10.6 us (44%)
  blocking collectives  6.45 us (27%)
  starting transfers between devices  6 us (25%)
  waiting for transfers between devices  0.94 us (4%)
    all_gather x1, blocking collectives, gathered(): return lax.all_gather(value, ('grp', 'sx'), axis_index_groups=pairs)  6.45 us
    ppermute x4, starting transfers between devices, to_mate(): return lax.ppermute(value, 'sx', mates)  5.33 us
    pallas_call x1, Pallas kernels, per_device(): pl.pallas_call(smooth_kernel, out_shape=(pltpu.HBM((ROWS, CX * PLANE), BF...  2.23 us
    pallas_call x1, Pallas kernels, per_device(): pl.pallas_call(energy_kernel, out_shape=(pair, pair, pair, shape(2, ROWS,...  2.01 us
    pallas_call x1, Pallas kernels, per_device(): pl.pallas_call(edges_kernel, out_shape=(pair, pair, shape(5 * ORB, 16), s...  1.54 us
    pallas_call x1, Pallas kernels, per_device(): pl.pallas_call(finish_kernel, out_shape=pltpu.HBM((ROWS, CX * PLANE), BF1...  1.03 us
    ppermute x4, waiting for transfers between devices, to_mate(): return lax.ppermute(value, 'sx', mates)  0.93 us
    pallas_call x1, Pallas kernels, per_device(): pl.pallas_call(around_kernel, out_shape=(shape(ROWS, PLANE), shape(3, 8 *...  0.85 us
  transfers between devices with their start and end apart: 5, of which 2 were waited for; matrix products, arithmetic and copies ran while one was open for 0% of the time, Pallas kernels for 24%

profile of v18, /device:TPU:0, one launch (start us, length us, event | category | flops | bytes accessed | tf_op | source)
XLA Modules:
  0.0 24.1 jit_solution(10880140415222406304)
XLA Ops:
  0.0 0.0 copy-start
  0.0 1.5 %edges.1 = (bf16[2,192,1024]{2,1,0:T(8,128)(2,1)S(1)}, bf16[2,192,1024]{2,1,0:T(8,128)(2,1)S(1)}, bf16[320,16]{1,0:T(8,128)(2,1)S(1)}, f32[192,1024]{1,0:T(8,128)S(1)}, bf16[128,128]{1,0:T(8,128)(2,1)S(1)}) custom-call(s32[4,1024]{1,0:T(4,128)} %bitcast.4, bf16[192,4096]{1,0:T(8,128)(2,1)} %pieces_ref.3), custom_call_target="tpu_custom_call" | custom-call | flops 100000000 | bytes 1000000 | tf_op jit(solution)/shard_map/edges/pallas_call | solution.py:662
  1.6 0.5 %collective-permute-start = (bf16[128,128]{1,0:T(8,128)(2,1)S(1)}, bf16[128,128]{1,0:T(8,128)(2,1)S(1)}, u32[]{:S(2)}, u32[]{:S(2)}) collective-permute-start(bf16[128,128]{1,0:T(8,128)(2,1)S(1)} %get-tuple-element.39), channel_id=1, source_target_pairs={{0,1},{1,0},{2,3},{3,2},{4,5},{5,4},{6,7},{7,6},{8,9},{9,8},{10,11... | collective-permute-start | bytes 98312 | tf_op jit(solution)/shard_map/ppermute | solution.py:650
  2.1 0.0 copy-done
  2.1 0.0 copy-done.1
  2.1 2.0 %energy.1 = (bf16[2,192,1024]{2,1,0:T(8,128)(2,1)S(1)}, bf16[2,192,1024]{2,1,0:T(8,128)(2,1)S(1)}, bf16[2,192,1024]{2,1,0:T(8,128)(2,1)S(1)}, f32[2,192,1024]{2,...) custom-call(bf16[320,16]{1,0:T(8,128)(2,1)S(1)} %get-tuple-element.36.rows_ref, ...), custom_call_target="tpu_custom_call" | custom-call | flops 4000000000 | bytes 10000000 | tf_op jit(solution)/shard_map/energy/pallas_call | solution.py:680
  4.1 0.0 collective-permute-done.mate_ref
  4.1 0.6 %bands.1 = (bf16[2,192,1024]{2,1,0:T(8,128)(2,1)S(1)}, f32[2,192,256]{2,1,0:T(8,128)S(1)}, bf16[3,128,128]{2,1,0:T(8,128)(2,1)S(1)}) custom-call(bf16[128,128]{1,0:T(8,128)(2,1)S(1)} %collective-permute-done.mate_ref, f32[2,192,1024]{2,1,0:T(8,128)S(1)} %get-tuple-element.42.part_ref, ...), custom_call_target="tpu_custom_call", output_to_operand_aliasing={{0}: (6, {})} | custom-call | flops 1000000000 | bytes 10000000 | tf_op jit(solution)/shard_map/bands/pallas_call | solution.py:693
  4.7 0.1 collective-permute-start.1
  4.8 0.8 %around.1 = (bf16[192,1024]{1,0:T(8,128)(2,1)S(1)}, f32[3,512]{1,0:T(4,128)S(1)}, bf16[144,128]{1,0:T(8,128)(2,1)S(1)}) custom-call(s32[2,16]{1,0:T(2,128)} %bitcast.5, bf16[320,16]{1,0:T(8,128)(2,1)S(1)} %get-tuple-element.36.rows_ref, bf16[2,192,1024]{2,1,0:T(8,128)(2,1)S(1)} %get-tuple-element.37.phi_ref.edge_ref), custom_call_target="tpu_custom_call" | custom-call | flops 100000000 | bytes 1000000 | tf_op jit(solution)/shard_map/around/pallas_call | solution.py:704
  5.7 0.4 %collective-permute-done.1.rows_ref = bf16[3,128,128]{2,1,0:T(8,128)(2,1)S(1)} collective-permute-done((bf16[3,128,128]{2,1,0:T(8,128)(2,1)S(1)}, bf16[3,128,128]{2,1,0:T(8,128)(2,1)S(1)}, u32[]{:S(2)}, u32[]{:S(2)}) %collective-permute-start.1) | collective-permute-done | bytes 98336 | tf_op jit(solution)/shard_map/ppermute | solution.py:650
  6.1 0.2 relay.1
  6.3 6.5 %all-gather = bf16[1184,128]{1,0:T(8,128)(2,1)S(1)} all-gather(bf16[592,128]{1,0:T(8,128)(2,1)S(1)} %relay.1), channel_id=2, replica_groups={{1,2},{3,4},{5,6},{7,8},{9,10},{11,12},{13,14},{17,18},{19,20},{21,22},..., dimensions={0}, use_global_device_ids=true | all-gather | bytes 454656 | tf_op jit(solution)/shard_map/all_gather | solution.py:656
  12.7 0.8 %face.1 = (bf16[128,1024]{1,0:T(8,128)(2,1)S(1)}, bf16[7,64,128]{2,1,0:T(8,128)(2,1)S(1)}, f32[192,512]{1,0:T(8,128)S(1)}, bf16[4,64,128]{2,1,0:T(8,128)(2,1)S(1)}) custom-call(bf16[2,592,128]{2,1,0:T(8,128)(2,1)S(1)} %bitcast.3, bf16[192,1024]{1,0:T(8,128)(2,1)S(1)} %get-tuple-element.49.around_ref, ...), custom_call_target="tpu_custom_call" | custom-call | flops 100000000 | bytes 1000000 | tf_op jit(solution)/shard_map/face/pallas_call | solution.py:723
  13.5 0.2 collective-permute-start.2
  13.7 0.6 %theta.1 = (bf16[2,192,256]{2,1,0:T(8,128)(2,1)S(1)}, f32[192,192]{1,0:T(8,128)S(1)}, bf16[2,192,1024]{2,1,0:T(8,128)(2,1)S(1)}) custom-call(f32[3,512]{1,0:T(4,128)S(1)} %get-tuple-element.38.keep_ref, f32[2,192,256]{2,1,0:T(8,128)S(1)} %get-tuple-element.46.own_ref, ...), custom_call_target="tpu_custom_call", output_to_operand_aliasing={{2}: (8, {})} | custom-call | flops 1000000000 | bytes 4000000 | tf_op jit(solution)/shard_map/theta/pallas_call | solution.py:741
  14.3 0.5 %collective-permute-done.2.relayed_ref = bf16[4,64,128]{2,1,0:T(8,128)(2,1)S(1)} collective-permute-done((bf16[4,64,128]{2,1,0:T(8,128)(2,1)S(1)}, bf16[4,64,128]{2,1,0:T(8,128)(2,1)S(1)}, u32[]{:S(2)}, u32[]{:S(2)}) %collective-permute-start.2) | collective-permute-done | bytes 65568 | tf_op jit(solution)/shard_map/ppermute | solution.py:650
  14.9 0.7 %gradient.1 = (bf16[2,192,1024]{2,1,0:T(8,128)(2,1)S(1)}, bf16[192,192]{1,0:T(8,128)(2,1)S(1)}, bf16[128,128]{1,0:T(8,128)(2,1)S(1)}, bf16[128,128]{1,0:T(8,128)(2,1)S(1)}) custom-call(f32[3,512]{1,0:T(4,128)S(1)} %get-tuple-element.38.keep_ref, bf16[4,64,128]{2,1,0:T(8,128)(2,1)S(1)} %collective-permute-done.2.relayed_ref, ...), custom_call_target="tpu_custom_call" | custom-call | flops 1000000000 | bytes 10000000 | tf_op jit(solution)/shard_map/gradient/pallas_call | solution.py:752
  15.6 0.7 %collective-permute-start.3 = (bf16[128,128]{1,0:T(8,128)(2,1)S(1)}, bf16[128,128]{1,0:T(8,128)(2,1)S(1)}, u32[]{:S(2)}, u32[]{:S(2)}) collective-permute-start(bf16[128,128]{1,0:T(8,128)(2,1)S(1)} %get-tuple-element.58), channel_id=1, source_target_pairs={{1,2},{2,1},{3,4},{4,3},{5,6},{6,5},{7,8},{8,7},{9,10},{10,9},{11,... | collective-permute-start | bytes 98312 | tf_op jit(solution)/shard_map/ppermute | solution.py:653
  16.3 4.5 %collective-permute-start.4 = (bf16[128,128]{1,0:T(8,128)(2,1)S(1)}, bf16[128,128]{1,0:T(8,128)(2,1)S(1)}, u32[]{:S(2)}, u32[]{:S(2)}) collective-permute-start(bf16[128,128]{1,0:T(8,128)(2,1)S(1)} %get-tuple-element.59), channel_id=1, source_target_pairs={{0,1},{1,0},{2,3},{3,2},{4,5},{5,4},{6,7},{7,6},{8,9},{9,8},{10,11... | collective-permute-start | bytes 98312 | tf_op jit(solution)/shard_map/ppermute | solution.py:650
  20.8 2.2 %smooth.1 = (bf16[192,4096]{1,0:T(8,128)(2,1)}, f32[2,192,1024]{2,1,0:T(8,128)S(1)}) custom-call(bf16[192,192]{1,0:T(8,128)(2,1)S(1)} %get-tuple-element.60.theta_ref, bf16[2,192,1024]{2,1,0:T(8,128)(2,1)S(1)} %get-tuple-element.61.phi_ref, bf16[2,192,1024]{2,1,0:T(8,128)(2,1)S(1)} %get-tuple-element.62.energy_ref, ...), custom_call_target="tpu_custom_call" | custom-call | flops 2000000000 | bytes 10000000 | tf_op jit(solution)/shard_map/smooth/pallas_call | solution.py:765
  23.1 0.0 collective-permute-done.3.across_ref
  23.1 0.0 collective-permute-done.4.mate_ref
  23.1 1.0 %finish.1 = bf16[192,4096]{1,0:T(8,128)(2,1)} custom-call(bf16[128,128]{1,0:T(8,128)(2,1)S(1)} %collective-permute-done.3.across_ref, bf16[128,128]{1,0:T(8,128)(2,1)S(1)} %collective-permute-done.4.mate_ref, f32[2,192,1024]{2,1,0:T(8,128)S(1)} %get-tuple-element.65.part_ref, ...), custom_call_target="tpu_custom_call", output_to_operand_aliasing={{}: (4, {})} | custom-call | flops 10000000 | bytes 10000000 | tf_op jit(solution)/shard_map/finish/pallas_call | solution.py:781
  (1 shorter events, 0.0 us)
Async XLA Ops:
  0.0 2.1 %copy-start = (bf16[192,4096]{1,0:T(8,128)(2,1)S(1)}, bf16[192,4096]{1,0:T(8,128)(2,1)}, u32[]{:S(2)}) copy-start(bf16[192,4096]{1,0:T(8,128)(2,1)} %pieces_ref.3) | copy-start | bytes 4718596
  0.0 2.1 %copy-start.1 = (f32[4,1024]{1,0:T(4,128)S(1)}, f32[4,1024]{1,0:T(4,128)}, u32[]{:S(2)}) copy-start(f32[4,1024]{1,0:T(4,128)} %pot_ref.1) | copy-start | bytes 49156
  1.6 2.5 %collective-permute-start = (bf16[128,128]{1,0:T(8,128)(2,1)S(1)}, bf16[128,128]{1,0:T(8,128)(2,1)S(1)}, u32[]{:S(2)}, u32[]{:S(2)}) collective-permute-start(bf16[128,128]{1,0:T(8,128)(2,1)S(1)} %get-tuple-element.39), channel_id=1, source_target_pairs={{0,1},{1,0},{2,3},{3,2},{4,5},{5,4},{6,7},{7,6},{8,9},{9,8},{10,11... | collective-permute-start | bytes 98312 | tf_op jit(solution)/shard_map/ppermute | solution.py:650
  4.7 1.4 %collective-permute-start.1 = (bf16[3,128,128]{2,1,0:T(8,128)(2,1)S(1)}, bf16[3,128,128]{2,1,0:T(8,128)(2,1)S(1)}, u32[]{:S(2)}, u32[]{:S(2)}) collective-permute-start(bf16[3,128,128]{2,1,0:T(8,128)(2,1)S(1)} %get-tuple-element.47), channel_id=1, source_target_pairs={{0,1},{1,0},{2,3},{3,2},{4,5},{5,4},{6,7},{7,6},{8,9},{9,8},{10,11... | collective-permute-start | bytes 294920 | tf_op jit(solution)/shard_map/ppermute | solution.py:650
  13.5 1.3 %collective-permute-start.2 = (bf16[4,64,128]{2,1,0:T(8,128)(2,1)S(1)}, bf16[4,64,128]{2,1,0:T(8,128)(2,1)S(1)}, u32[]{:S(2)}, u32[]{:S(2)}) collective-permute-start(bf16[4,64,128]{2,1,0:T(8,128)(2,1)S(1)} %get-tuple-element.50), channel_id=1, source_target_pairs={{0,1},{1,0},{2,3},{3,2},{4,5},{5,4},{6,7},{7,6},{8,9},{9,8},{10,11... | collective-permute-start | bytes 196616 | tf_op jit(solution)/shard_map/ppermute | solution.py:650
  15.6 7.5 %collective-permute-start.3 = (bf16[128,128]{1,0:T(8,128)(2,1)S(1)}, bf16[128,128]{1,0:T(8,128)(2,1)S(1)}, u32[]{:S(2)}, u32[]{:S(2)}) collective-permute-start(bf16[128,128]{1,0:T(8,128)(2,1)S(1)} %get-tuple-element.58), channel_id=1, source_target_pairs={{1,2},{2,1},{3,4},{4,3},{5,6},{6,5},{7,8},{8,7},{9,10},{10,9},{11,... | collective-permute-start | bytes 98312 | tf_op jit(solution)/shard_map/ppermute | solution.py:653
  16.3 6.8 %collective-permute-start.4 = (bf16[128,128]{1,0:T(8,128)(2,1)S(1)}, bf16[128,128]{1,0:T(8,128)(2,1)S(1)}, u32[]{:S(2)}, u32[]{:S(2)}) collective-permute-start(bf16[128,128]{1,0:T(8,128)(2,1)S(1)} %get-tuple-element.59), channel_id=1, source_target_pairs={{0,1},{1,0},{2,3},{3,2},{4,5},{5,4},{6,7},{7,6},{8,9},{9,8},{10,11... | collective-permute-start | bytes 98312 | tf_op jit(solution)/shard_map/ppermute | solution.py:650

commit v19 on v18

--- a/solution.py
+++ b/solution.py
@@ -229,7 +229,7 @@
         copies.append(
             pltpu.make_async_copy(pieces_ref.at[:, start : start + PLANE], raw_ref.at[i], sems.at[i])
         )
-        copies[i].start()
+        copies[i].start(priority=1)
     cells = cell_features()
     table_copy.wait()
     blocks = row_features(window_ref, first)

time: 24.3 us -> 24.3 us (level)
  no operation moved by 1% of the time
where the time goes in v19:
time: 24.3 us; the launch traced here: 24.1 us
  Pallas kernels  10.6 us (44%)
  blocking collectives  6.45 us (27%)
  starting transfers between devices  6 us (25%)
  waiting for transfers between devices  0.94 us (4%)
    all_gather x1, blocking collectives, gathered(): return lax.all_gather(value, ('grp', 'sx'), axis_index_groups=pairs)  6.45 us
    ppermute x4, starting transfers between devices, to_mate(): return lax.ppermute(value, 'sx', mates)  5.33 us
    pallas_call x1, Pallas kernels, per_device(): pl.pallas_call(smooth_kernel, out_shape=(pltpu.HBM((ROWS, CX * PLANE), BF...  2.23 us
    pallas_call x1, Pallas kernels, per_device(): pl.pallas_call(energy_kernel, out_shape=(pair, pair, pair, shape(2, ROWS,...  2.01 us
    pallas_call x1, Pallas kernels, per_device(): pl.pallas_call(edges_kernel, out_shape=(pair, pair, shape(5 * ORB, 16), s...  1.54 us
    pallas_call x1, Pallas kernels, per_device(): pl.pallas_call(finish_kernel, out_shape=pltpu.HBM((ROWS, CX * PLANE), BF1...  1.03 us
    ppermute x4, waiting for transfers between devices, to_mate(): return lax.ppermute(value, 'sx', mates)  0.93 us
    pallas_call x1, Pallas kernels, per_device(): pl.pallas_call(around_kernel, out_shape=(shape(ROWS, PLANE), shape(3, 8 *...  0.85 us
  transfers between devices with their start and end apart: 5, of which 2 were waited for; matrix products, arithmetic and copies ran while one was open for 0% of the time, Pallas kernels for 24%

profile of v19, /device:TPU:0, one launch (start us, length us, event | category | flops | bytes accessed | tf_op | source)
XLA Modules:
  0.0 24.1 jit_solution(10890343501499244189)
XLA Ops:
  0.0 0.0 copy-start
  0.0 1.5 %edges.1 = (bf16[2,192,1024]{2,1,0:T(8,128)(2,1)S(1)}, bf16[2,192,1024]{2,1,0:T(8,128)(2,1)S(1)}, bf16[320,16]{1,0:T(8,128)(2,1)S(1)}, f32[192,1024]{1,0:T(8,128)S(1)}, bf16[128,128]{1,0:T(8,128)(2,1)S(1)}) custom-call(s32[4,1024]{1,0:T(4,128)} %bitcast.4, bf16[192,4096]{1,0:T(8,128)(2,1)} %pieces_ref.3), custom_call_target="tpu_custom_call" | custom-call | flops 100000000 | bytes 1000000 | tf_op jit(solution)/shard_map/edges/pallas_call | solution.py:662
  1.6 0.5 %collective-permute-start = (bf16[128,128]{1,0:T(8,128)(2,1)S(1)}, bf16[128,128]{1,0:T(8,128)(2,1)S(1)}, u32[]{:S(2)}, u32[]{:S(2)}) collective-permute-start(bf16[128,128]{1,0:T(8,128)(2,1)S(1)} %get-tuple-element.39), channel_id=1, source_target_pairs={{0,1},{1,0},{2,3},{3,2},{4,5},{5,4},{6,7},{7,6},{8,9},{9,8},{10,11... | collective-permute-start | bytes 98312 | tf_op jit(solution)/shard_map/ppermute | solution.py:650
  2.1 0.0 copy-done
  2.1 0.0 copy-done.1
  2.1 2.0 %energy.1 = (bf16[2,192,1024]{2,1,0:T(8,128)(2,1)S(1)}, bf16[2,192,1024]{2,1,0:T(8,128)(2,1)S(1)}, bf16[2,192,1024]{2,1,0:T(8,128)(2,1)S(1)}, f32[2,192,1024]{2,...) custom-call(bf16[320,16]{1,0:T(8,128)(2,1)S(1)} %get-tuple-element.36.rows_ref, ...), custom_call_target="tpu_custom_call" | custom-call | flops 4000000000 | bytes 10000000 | tf_op jit(solution)/shard_map/energy/pallas_call | solution.py:680
  4.1 0.0 collective-permute-done.mate_ref
  4.1 0.6 %bands.1 = (bf16[2,192,1024]{2,1,0:T(8,128)(2,1)S(1)}, f32[2,192,256]{2,1,0:T(8,128)S(1)}, bf16[3,128,128]{2,1,0:T(8,128)(2,1)S(1)}) custom-call(bf16[128,128]{1,0:T(8,128)(2,1)S(1)} %collective-permute-done.mate_ref, f32[2,192,1024]{2,1,0:T(8,128)S(1)} %get-tuple-element.42.part_ref, ...), custom_call_target="tpu_custom_call", output_to_operand_aliasing={{0}: (6, {})} | custom-call | flops 1000000000 | bytes 10000000 | tf_op jit(solution)/shard_map/bands/pallas_call | solution.py:693
  4.7 0.1 collective-permute-start.1
  4.8 0.8 %around.1 = (bf16[192,1024]{1,0:T(8,128)(2,1)S(1)}, f32[3,512]{1,0:T(4,128)S(1)}, bf16[144,128]{1,0:T(8,128)(2,1)S(1)}) custom-call(s32[2,16]{1,0:T(2,128)} %bitcast.5, bf16[320,16]{1,0:T(8,128)(2,1)S(1)} %get-tuple-element.36.rows_ref, bf16[2,192,1024]{2,1,0:T(8,128)(2,1)S(1)} %get-tuple-element.37.phi_ref.edge_ref), custom_call_target="tpu_custom_call" | custom-call | flops 100000000 | bytes 1000000 | tf_op jit(solution)/shard_map/around/pallas_call | solution.py:704
  5.7 0.4 %collective-permute-done.1.rows_ref = bf16[3,128,128]{2,1,0:T(8,128)(2,1)S(1)} collective-permute-done((bf16[3,128,128]{2,1,0:T(8,128)(2,1)S(1)}, bf16[3,128,128]{2,1,0:T(8,128)(2,1)S(1)}, u32[]{:S(2)}, u32[]{:S(2)}) %collective-permute-start.1) | collective-permute-done | bytes 98336 | tf_op jit(solution)/shard_map/ppermute | solution.py:650
  6.1 0.2 relay.1
  6.3 6.5 %all-gather = bf16[1184,128]{1,0:T(8,128)(2,1)S(1)} all-gather(bf16[592,128]{1,0:T(8,128)(2,1)S(1)} %relay.1), channel_id=2, replica_groups={{1,2},{3,4},{5,6},{7,8},{9,10},{11,12},{13,14},{17,18},{19,20},{21,22},..., dimensions={0}, use_global_device_ids=true | all-gather | bytes 454656 | tf_op jit(solution)/shard_map/all_gather | solution.py:656
  12.7 0.8 %face.1 = (bf16[128,1024]{1,0:T(8,128)(2,1)S(1)}, bf16[7,64,128]{2,1,0:T(8,128)(2,1)S(1)}, f32[192,512]{1,0:T(8,128)S(1)}, bf16[4,64,128]{2,1,0:T(8,128)(2,1)S(1)}) custom-call(bf16[2,592,128]{2,1,0:T(8,128)(2,1)S(1)} %bitcast.3, bf16[192,1024]{1,0:T(8,128)(2,1)S(1)} %get-tuple-element.49.around_ref, ...), custom_call_target="tpu_custom_call" | custom-call | flops 100000000 | bytes 1000000 | tf_op jit(solution)/shard_map/face/pallas_call | solution.py:723
  13.5 0.2 collective-permute-start.2
  13.7 0.6 %theta.1 = (bf16[2,192,256]{2,1,0:T(8,128)(2,1)S(1)}, f32[192,192]{1,0:T(8,128)S(1)}, bf16[2,192,1024]{2,1,0:T(8,128)(2,1)S(1)}) custom-call(f32[3,512]{1,0:T(4,128)S(1)} %get-tuple-element.38.keep_ref, f32[2,192,256]{2,1,0:T(8,128)S(1)} %get-tuple-element.46.own_ref, ...), custom_call_target="tpu_custom_call", output_to_operand_aliasing={{2}: (8, {})} | custom-call | flops 1000000000 | bytes 4000000 | tf_op jit(solution)/shard_map/theta/pallas_call | solution.py:741
  14.3 0.5 %collective-permute-done.2.relayed_ref = bf16[4,64,128]{2,1,0:T(8,128)(2,1)S(1)} collective-permute-done((bf16[4,64,128]{2,1,0:T(8,128)(2,1)S(1)}, bf16[4,64,128]{2,1,0:T(8,128)(2,1)S(1)}, u32[]{:S(2)}, u32[]{:S(2)}) %collective-permute-start.2) | collective-permute-done | bytes 65568 | tf_op jit(solution)/shard_map/ppermute | solution.py:650
  14.9 0.7 %gradient.1 = (bf16[2,192,1024]{2,1,0:T(8,128)(2,1)S(1)}, bf16[192,192]{1,0:T(8,128)(2,1)S(1)}, bf16[128,128]{1,0:T(8,128)(2,1)S(1)}, bf16[128,128]{1,0:T(8,128)(2,1)S(1)}) custom-call(f32[3,512]{1,0:T(4,128)S(1)} %get-tuple-element.38.keep_ref, bf16[4,64,128]{2,1,0:T(8,128)(2,1)S(1)} %collective-permute-done.2.relayed_ref, ...), custom_call_target="tpu_custom_call" | custom-call | flops 1000000000 | bytes 10000000 | tf_op jit(solution)/shard_map/gradient/pallas_call | solution.py:752
  15.6 0.7 %collective-permute-start.3 = (bf16[128,128]{1,0:T(8,128)(2,1)S(1)}, bf16[128,128]{1,0:T(8,128)(2,1)S(1)}, u32[]{:S(2)}, u32[]{:S(2)}) collective-permute-start(bf16[128,128]{1,0:T(8,128)(2,1)S(1)} %get-tuple-element.58), channel_id=1, source_target_pairs={{1,2},{2,1},{3,4},{4,3},{5,6},{6,5},{7,8},{8,7},{9,10},{10,9},{11,... | collective-permute-start | bytes 98312 | tf_op jit(solution)/shard_map/ppermute | solution.py:653
  16.3 4.5 %collective-permute-start.4 = (bf16[128,128]{1,0:T(8,128)(2,1)S(1)}, bf16[128,128]{1,0:T(8,128)(2,1)S(1)}, u32[]{:S(2)}, u32[]{:S(2)}) collective-permute-start(bf16[128,128]{1,0:T(8,128)(2,1)S(1)} %get-tuple-element.59), channel_id=1, source_target_pairs={{0,1},{1,0},{2,3},{3,2},{4,5},{5,4},{6,7},{7,6},{8,9},{9,8},{10,11... | collective-permute-start | bytes 98312 | tf_op jit(solution)/shard_map/ppermute | solution.py:650
  20.8 2.2 %smooth.1 = (bf16[192,4096]{1,0:T(8,128)(2,1)}, f32[2,192,1024]{2,1,0:T(8,128)S(1)}) custom-call(bf16[192,192]{1,0:T(8,128)(2,1)S(1)} %get-tuple-element.60.theta_ref, bf16[2,192,1024]{2,1,0:T(8,128)(2,1)S(1)} %get-tuple-element.61.phi_ref, bf16[2,192,1024]{2,1,0:T(8,128)(2,1)S(1)} %get-tuple-element.62.energy_ref, ...), custom_call_target="tpu_custom_call" | custom-call | flops 2000000000 | bytes 10000000 | tf_op jit(solution)/shard_map/smooth/pallas_call | solution.py:765
  23.1 0.0 collective-permute-done.3.across_ref
  23.1 0.0 collective-permute-done.4.mate_ref
  23.1 1.0 %finish.1 = bf16[192,4096]{1,0:T(8,128)(2,1)} custom-call(bf16[128,128]{1,0:T(8,128)(2,1)S(1)} %collective-permute-done.3.across_ref, bf16[128,128]{1,0:T(8,128)(2,1)S(1)} %collective-permute-done.4.mate_ref, f32[2,192,1024]{2,1,0:T(8,128)S(1)} %get-tuple-element.65.part_ref, ...), custom_call_target="tpu_custom_call", output_to_operand_aliasing={{}: (4, {})} | custom-call | flops 10000000 | bytes 10000000 | tf_op jit(solution)/shard_map/finish/pallas_call | solution.py:781
  (1 shorter events, 0.0 us)
Async XLA Ops:
  0.0 2.1 %copy-start = (bf16[192,4096]{1,0:T(8,128)(2,1)S(1)}, bf16[192,4096]{1,0:T(8,128)(2,1)}, u32[]{:S(2)}) copy-start(bf16[192,4096]{1,0:T(8,128)(2,1)} %pieces_ref.3) | copy-start | bytes 4718596
  0.0 2.1 %copy-start.1 = (f32[4,1024]{1,0:T(4,128)S(1)}, f32[4,1024]{1,0:T(4,128)}, u32[]{:S(2)}) copy-start(f32[4,1024]{1,0:T(4,128)} %pot_ref.1) | copy-start | bytes 49156
  1.6 2.5 %collective-permute-start = (bf16[128,128]{1,0:T(8,128)(2,1)S(1)}, bf16[128,128]{1,0:T(8,128)(2,1)S(1)}, u32[]{:S(2)}, u32[]{:S(2)}) collective-permute-start(bf16[128,128]{1,0:T(8,128)(2,1)S(1)} %get-tuple-element.39), channel_id=1, source_target_pairs={{0,1},{1,0},{2,3},{3,2},{4,5},{5,4},{6,7},{7,6},{8,9},{9,8},{10,11... | collective-permute-start | bytes 98312 | tf_op jit(solution)/shard_map/ppermute | solution.py:650
  4.7 1.4 %collective-permute-start.1 = (bf16[3,128,128]{2,1,0:T(8,128)(2,1)S(1)}, bf16[3,128,128]{2,1,0:T(8,128)(2,1)S(1)}, u32[]{:S(2)}, u32[]{:S(2)}) collective-permute-start(bf16[3,128,128]{2,1,0:T(8,128)(2,1)S(1)} %get-tuple-element.47), channel_id=1, source_target_pairs={{0,1},{1,0},{2,3},{3,2},{4,5},{5,4},{6,7},{7,6},{8,9},{9,8},{10,11... | collective-permute-start | bytes 294920 | tf_op jit(solution)/shard_map/ppermute | solution.py:650
  13.5 1.3 %collective-permute-start.2 = (bf16[4,64,128]{2,1,0:T(8,128)(2,1)S(1)}, bf16[4,64,128]{2,1,0:T(8,128)(2,1)S(1)}, u32[]{:S(2)}, u32[]{:S(2)}) collective-permute-start(bf16[4,64,128]{2,1,0:T(8,128)(2,1)S(1)} %get-tuple-element.50), channel_id=1, source_target_pairs={{0,1},{1,0},{2,3},{3,2},{4,5},{5,4},{6,7},{7,6},{8,9},{9,8},{10,11... | collective-permute-start | bytes 196616 | tf_op jit(solution)/shard_map/ppermute | solution.py:650
  15.6 7.5 %collective-permute-start.3 = (bf16[128,128]{1,0:T(8,128)(2,1)S(1)}, bf16[128,128]{1,0:T(8,128)(2,1)S(1)}, u32[]{:S(2)}, u32[]{:S(2)}) collective-permute-start(bf16[128,128]{1,0:T(8,128)(2,1)S(1)} %get-tuple-element.58), channel_id=1, source_target_pairs={{1,2},{2,1},{3,4},{4,3},{5,6},{6,5},{7,8},{8,7},{9,10},{10,9},{11,... | collective-permute-start | bytes 98312 | tf_op jit(solution)/shard_map/ppermute | solution.py:653
  16.3 6.8 %collective-permute-start.4 = (bf16[128,128]{1,0:T(8,128)(2,1)S(1)}, bf16[128,128]{1,0:T(8,128)(2,1)S(1)}, u32[]{:S(2)}, u32[]{:S(2)}) collective-permute-start(bf16[128,128]{1,0:T(8,128)(2,1)S(1)} %get-tuple-element.59), channel_id=1, source_target_pairs={{0,1},{1,0},{2,3},{3,2},{4,5},{5,4},{6,7},{7,6},{8,9},{9,8},{10,11... | collective-permute-start | bytes 98312 | tf_op jit(solution)/shard_map/ppermute | solution.py:650
